TPU v7x, 32 devices: a whole 2x2x4 slice. The times are simulated.
32 devices in a mesh: fsdp: 8 (over y, x, core), ctx: 4 (over z).
Axes of the slice: x: 2, y: 2, z: 4, core: 2. Of those that a mesh axis runs over, the one named last changes fastest.
Arguments:
- tokens_in: bfloat16 [4096, 2048], P(('fsdp', 'ctx')), may hold values from -6 to 6
- cotangent: bfloat16 [4096, 2048], P(('fsdp', 'ctx')), may hold values from -6 to 6
- routes: int32 [4096, 6], P(('fsdp', 'ctx')), may hold values from 0 to 15, all different within a row; in each aligned block of 512 rows (0 to 511, 512 to 1023, ...) at most 240 rows name the same one
- segments: int32 [4096], P(('fsdp', 'ctx')), may hold values from 0 to 23, as said below
- norm_in: float32 [2048], replicated, may hold values from 0.5 to 1.5
- w_query: bfloat16 [2048, 3072], P('fsdp', 'ctx'), may hold values from -0.125 to 0.125
- w_latent: bfloat16 [2048, 576], P(('fsdp', 'ctx')), may hold values from -0.125 to 0.125
- latent_gain: float32 [512], replicated, may hold values from 0.5 to 1.5
- w_expand: bfloat16 [512, 4096], P('fsdp', 'ctx'), may hold values from -0.25 to 0.25
- w_output: bfloat16 [2048, 2048], P('ctx', 'fsdp'), may hold values from -2 to 2
- norm_mid: float32 [2048], replicated, may hold values from 0.5 to 1.5
- w_router: bfloat16 [2048, 16], P(('fsdp', 'ctx')), may hold values from -0.0625 to 0.0625
- shared_gate: bfloat16 [2048, 2816], P('fsdp', 'ctx'), may hold values from -0.125 to 0.125
- shared_up: bfloat16 [2048, 2816], P('fsdp', 'ctx'), may hold values from -0.125 to 0.125
- shared_down: bfloat16 [2816, 2048], P('ctx', 'fsdp'), may hold values from -0.109375 to 0.109375
- expert_gate: bfloat16 [16, 1408, 2048], P('fsdp', 'ctx'), may hold values from -0.125 to 0.125
- routed_up_weight: bfloat16 [16, 1408, 2048], P('fsdp', 'ctx'), may hold values from -0.125 to 0.125
- expert_down: bfloat16 [16, 1408, 2048], P('fsdp', 'ctx'), may hold values from -0.15625 to 0.15625
Outputs:
- block_out: bfloat16 [4096, 2048], P(('fsdp', 'ctx'))
- grad_input: bfloat16 [4096, 2048], P(('fsdp', 'ctx'))
- grad_norm_in: float32 [2048], P(('fsdp', 'ctx'))
- grad_query: float32 [2048, 3072], P('fsdp', 'ctx')
- grad_latent: float32 [2048, 576], P(('fsdp', 'ctx'))
- grad_latent_gain: float32 [512], P(('fsdp', 'ctx'))
- grad_expand: float32 [512, 4096], P('fsdp', 'ctx')
- grad_output: float32 [2048, 2048], P('ctx', 'fsdp')
- grad_norm_mid: float32 [2048], P(('fsdp', 'ctx'))
- grad_router: float32 [2048, 16], P(('fsdp', 'ctx'))
- grad_shared_gate: float32 [2048, 2816], P('fsdp', 'ctx')
- grad_shared_up: float32 [2048, 2816], P('fsdp', 'ctx')
- grad_shared_down: float32 [2816, 2048], P('ctx', 'fsdp')
- grad_expert_gate: float32 [16, 1408, 2048], P('fsdp', 'ctx')
- grad_expert_up: float32 [16, 1408, 2048], P('fsdp', 'ctx')
- grad_expert_down: float32 [16, 1408, 2048], P('fsdp', 'ctx')
Inputs may be any that keep to these rules, and one draw needn't show every extreme that they name: `routes`: in each aligned block of 512 rows (one group) no expert is named by more than 240 rows, a bound that some block reaches; each row names 6 different experts. `segments`: ids never fall; aligned block g of 512 rows holds the ids 3 g, 3 g + 1 and 3 g + 2, the first and the last of them on fewer than 128 rows.
All inputs are finite; a program needn't handle non-finite values.
Results may differ from a plain program's by a relative error of at most 0.02.
Values may be sent and summed in bfloat16 or wider, within the bound.
No kernel may reach another device: no remote copies, remote signals or barrier semaphores. Data moves between devices by JAX's collectives and lax.ppermute only.
A program may use at most 384 MiB of HBM per device.

v0:
```python
import jax
import jax.numpy as jnp
from jax import lax
from jax.sharding import PartitionSpec as P

NOPE = 128
ROPE = 64
VD = 128
LAT = 512


EPS = 1e-06
THETA = 50000.0
ROUTE_SCALE = 2.446
BLOCK_ROWS = 512
NEG_FILL = -1e30


def dot32(left, right):
    return jnp.dot(left, right, preferred_element_type=jnp.float32)


def dot_nt(left, right):
    return lax.dot_general(
        left, right, (((1,), (1,)), ((), ())), preferred_element_type=jnp.float32
    )


def dot_tn(left, right):
    return lax.dot_general(
        left, right, (((0,), (0,)), ((), ())), preferred_element_type=jnp.float32
    )


def precise_nt(left, right):
    return lax.dot_general(
        left,
        right,
        (((1,), (1,)), ((), ())),
        precision=lax.Precision.HIGHEST,
        preferred_element_type=jnp.float32,
    )


def precise_tn(left, right):
    return lax.dot_general(
        left,
        right,
        (((0,), (0,)), ((), ())),
        precision=lax.Precision.HIGHEST,
        preferred_element_type=jnp.float32,
    )


def norm_parts(value, gain):
    factor = lax.rsqrt(jnp.mean(value * value, axis=-1, keepdims=True) + EPS)
    unit = value * factor
    return (unit * gain, unit, factor)


def norm_back(grad_out, unit, factor, gain):
    grad_unit = grad_out * gain
    return factor * (grad_unit - unit * jnp.mean(grad_unit * unit, axis=-1, keepdims=True))


def turn(value, cosine, sine):
    half = value.shape[-1] // 2
    first, second = (value[..., :half], value[..., half:])
    return jnp.concatenate(
        [first * cosine - second * sine, second * cosine + first * sine], axis=-1
    )


def turn_back(grad, cosine, sine):
    half = grad.shape[-1] // 2
    first, second = (grad[..., :half], grad[..., half:])
    return jnp.concatenate(
        [first * cosine + second * sine, second * cosine - first * sine], axis=-1
    )


def silu_slope(value):
    sig = jax.nn.sigmoid(value)
    return (sig * (1.0 + value * (1.0 - sig)), value * sig)


def per_device(
    tokens_in,
    cotangent,
    routes,
    segments,
    norm_in,
    w_query,
    w_latent,
    latent_gain,
    w_expand,
    w_output,
    norm_mid,
    w_router,
    shared_gate,
    shared_up,
    shared_down,
    expert_gate,
    routed_up_weight,
    expert_down,
):
    single_float32, brain_float16 = (jnp.float32, jnp.bfloat16)
    tok_dev = tokens_in.shape[0]
    offset = lax.axis_index("ctx") * tok_dev
    groups = lax.axis_size("fsdp")
    model_w = tokens_in.shape[1]
    share = model_w // lax.axis_size("ctx")
    column = lax.axis_index("ctx") * share
    query_w, expand_w, output_w, sgate_w, sup_w, sdown_w = (
        lax.all_gather(w_query, "fsdp", axis=0, tiled=True),
        lax.all_gather(w_expand, "fsdp", axis=0, tiled=True),
        lax.all_gather(w_output, "fsdp", axis=1, tiled=True),
        lax.all_gather(shared_gate, "fsdp", axis=0, tiled=True),
        lax.all_gather(shared_up, "fsdp", axis=0, tiled=True),
        lax.all_gather(shared_down, "fsdp", axis=1, tiled=True),
    )
    latent_w, router_w = (
        lax.all_gather(w_latent, ("fsdp", "ctx"), axis=0, tiled=True),
        lax.all_gather(w_router, ("fsdp", "ctx"), axis=0, tiled=True),
    )
    x_all, seg_all, route_all = (
        lax.all_gather(tokens_in, "ctx", axis=0, tiled=True),
        lax.all_gather(segments, "ctx", axis=0, tiled=True),
        lax.all_gather(routes, "ctx", axis=0, tiled=True),
    )
    count = x_all.shape[0]
    width = query_w.shape[1] // (NOPE + ROPE)
    scale = (NOPE + ROPE) ** (-0.5)
    steps = jnp.arange(count, dtype=jnp.int32)
    fresh = jnp.concatenate([jnp.ones((1,), dtype=bool), seg_all[1:] != seg_all[:-1]])
    start = lax.cummax(jnp.where(fresh, steps, 0), axis=0)
    place = (steps - start).astype(single_float32)
    freq = THETA ** (-(jnp.arange(ROPE // 2, dtype=single_float32) * 2.0 / ROPE))
    angle = place[:, None] * freq[None, :]
    cosine, sine = (jnp.cos(angle), jnp.sin(angle))
    x_f = x_all.astype(single_float32)
    normed, unit_in, factor_in = norm_parts(x_f, norm_in)
    x_low = normed.astype(brain_float16)
    q_raw = dot32(x_low, query_w).reshape(count, width, NOPE + ROPE)
    q_low = jnp.concatenate(
        [q_raw[..., :NOPE], turn(q_raw[..., NOPE:], cosine[:, None], sine[:, None])], axis=-1
    ).astype(brain_float16)
    latent_raw = dot32(x_low, latent_w)
    latent_n, unit_lat, factor_lat = norm_parts(latent_raw[:, :LAT], latent_gain)
    latent_low = latent_n.astype(brain_float16)
    krope = turn(latent_raw[:, LAT:], cosine, sine).astype(brain_float16)
    kv_raw = dot32(latent_low, expand_w).reshape(count, width, NOPE + VD)
    knope = kv_raw[..., :NOPE].astype(brain_float16)
    values = kv_raw[..., NOPE:].astype(brain_float16)
    block = min(BLOCK_ROWS, count)
    firsts = jnp.arange(count // block, dtype=jnp.int32) * block

    def scores_of(first):
        q_blk = lax.dynamic_slice_in_dim(q_low, first, block, 0)
        seg_blk = lax.dynamic_slice_in_dim(seg_all, first, block, 0)
        rows_at = first + jnp.arange(block, dtype=jnp.int32)
        raw = jnp.einsum(
            "qhd,khd->hqk", q_blk[..., :NOPE], knope, preferred_element_type=single_float32
        )
        raw = raw + jnp.einsum(
            "qhd,kd->hqk", q_blk[..., NOPE:], krope, preferred_element_type=single_float32
        )
        keep = (seg_blk[:, None] == seg_all[None, :]) & (steps[None, :] <= rows_at[:, None])
        return (jnp.where(keep[None], raw * scale, NEG_FILL), q_blk)

    def forward_block(first):
        logits, _ = scores_of(first)
        peak = jnp.max(logits, axis=-1, keepdims=True)
        expo = jnp.exp(logits - peak)
        total = jnp.sum(expo, axis=-1, keepdims=True)
        probs = (expo / total).astype(brain_float16)
        heads_out = jnp.einsum("hqk,khd->qhd", probs, values, preferred_element_type=single_float32)
        return (heads_out.astype(brain_float16), (peak + jnp.log(total))[..., 0])

    out_blocks, lse_blocks = lax.map(forward_block, firsts)
    heads_low = out_blocks.reshape(count, width * VD)
    attn = lax.psum(dot32(heads_low, output_w), "ctx")
    resid = x_f + attn
    mid, unit_mid, factor_mid = norm_parts(resid, norm_mid)
    mid_low = mid.astype(brain_float16)
    experts_n = router_w.shape[1]
    exp_dev = expert_gate.shape[0]
    top_k = route_all.shape[1]
    cap = 5 * count * top_k // (4 * experts_n)
    sig = jax.nn.sigmoid(dot32(mid_low, router_w))
    pick = (route_all[:, :, None] == jnp.arange(experts_n, dtype=jnp.int32)[None, None, :]).astype(
        single_float32
    )
    chosen = jnp.einsum("gke,ge->gk", pick, sig)
    chosen_sum = jnp.sum(chosen, axis=-1, keepdims=True)
    gates = ROUTE_SCALE * chosen / chosen_sum
    flat = route_all.reshape(-1)
    hits = (flat[:, None] == jnp.arange(experts_n, dtype=jnp.int32)[None, :]).astype(jnp.int32)
    slot = jnp.sum(jnp.cumsum(hits, axis=0) * hits, axis=1) - 1
    index = flat * cap + slot
    pairs = jnp.arange(count * top_k, dtype=jnp.int32)
    slot_pair = jnp.zeros((experts_n * cap,), jnp.int32).at[index].set(pairs)
    filled = jnp.zeros((experts_n * cap,), dtype=bool).at[index].set(True)
    slot_token = slot_pair // top_k

    def send_rows(rows):
        moved = lax.all_to_all(rows, "fsdp", split_axis=0, concat_axis=0, tiled=True)
        return lax.all_gather(moved, "ctx", axis=3, tiled=True)

    def return_rows(partial_value):
        summed = lax.psum_scatter(
            partial_value.astype(jnp.bfloat16), "ctx", scatter_dimension=3, tiled=True
        ).astype(jnp.float32)
        moved = lax.all_to_all(
            summed.astype(jnp.bfloat16), "fsdp", split_axis=0, concat_axis=0, tiled=True
        ).astype(summed.dtype)
        return moved.reshape(experts_n * cap, -1)

    def place_columns(piece):
        return lax.dynamic_update_slice_in_dim(
            jnp.zeros((count, model_w), single_float32), piece, column, 1
        )

    mid_share = lax.dynamic_slice_in_dim(mid_low, column, share, 1)
    rows = jnp.where(filled[:, None], mid_share[slot_token], jnp.zeros((), brain_float16))
    received = send_rows(rows.reshape(groups, exp_dev, cap, share))
    gate = jnp.einsum(
        "sjcd,jfd->sjcf", received, expert_gate, preferred_element_type=single_float32
    )
    upper = jnp.einsum(
        "sjcd,jfd->sjcf", received, routed_up_weight, preferred_element_type=single_float32
    )
    act_e = (jax.nn.silu(gate) * upper).astype(brain_float16)
    out_e = lax.optimization_barrier(
        jnp.einsum(
            "huzm,umw->huzw", act_e, expert_down, preferred_element_type=single_float32
        ).astype(brain_float16)
    ).astype(single_float32)
    back = return_rows(out_e)
    picked = back[index].reshape(count, top_k, -1)
    routed_share = jnp.einsum("gk,gkd->gd", gates, picked)
    sgate = dot32(mid_low, sgate_w)
    sup = dot32(mid_low, sup_w)
    sact = (jax.nn.silu(sgate) * sup).astype(brain_float16)
    moe = lax.psum_scatter(
        (dot32(sact, sdown_w) + place_columns(routed_share)).astype(jnp.bfloat16),
        "ctx",
        scatter_dimension=0,
        tiled=True,
    ).astype(jnp.float32)
    block_out = (lax.dynamic_slice_in_dim(resid, offset, tok_dev, 0) + moe).astype(brain_float16)
    grad_top = lax.all_gather(cotangent, "ctx", axis=0, tiled=True)
    grad_top_f = grad_top.astype(single_float32)
    sdown_grad = dot_tn(sact, grad_top)
    sact_grad = dot_nt(grad_top, sdown_w)
    slope_s, silu_s = silu_slope(sgate)
    sgate_d = (sact_grad * sup * slope_s).astype(brain_float16)
    sup_d = (sact_grad * silu_s).astype(brain_float16)
    sgate_grad = dot_tn(mid_low, sgate_d)
    sup_grad = dot_tn(mid_low, sup_d)
    mid_grad = dot_nt(sgate_d, sgate_w) + dot_nt(sup_d, sup_w)
    grad_share = lax.dynamic_slice_in_dim(grad_top_f, column, share, 1)
    gate_grad = jnp.einsum("gd,gkd->gk", grad_share, picked)
    grad_rows = gates.reshape(-1)[slot_pair][:, None] * grad_share[slot_token]
    grad_rows = (
        jnp.where(filled[:, None], grad_rows, 0.0)
        .astype(brain_float16)
        .reshape(groups, exp_dev, cap, share)
    )
    grad_recv = send_rows(grad_rows)
    present_rows, gate_h, up_h, act_h = (received, gate, upper, act_e)
    down_grad = jnp.einsum(
        "qgha,qghy->gay", act_h, grad_recv, preferred_element_type=single_float32
    )
    activation_gradient = jnp.einsum(
        "sjcd,jfd->sjcf", grad_recv, expert_down, preferred_element_type=single_float32
    )
    slope_e, expert_swish_output = silu_slope(gate_h)
    egate_d = (activation_gradient * up_h * slope_e).astype(brain_float16)
    expert_up_delta = (activation_gradient * expert_swish_output).astype(brain_float16)
    egate_grad = jnp.einsum(
        "qgha,qghy->gay", egate_d, present_rows, preferred_element_type=single_float32
    )
    expert_up_gradient = jnp.einsum(
        "qgha,qghy->gay", expert_up_delta, present_rows, preferred_element_type=single_float32
    )
    rows_grad = jnp.einsum(
        "huzm,umw->huzw", egate_d, expert_gate, preferred_element_type=single_float32
    )
    rows_grad = rows_grad + jnp.einsum(
        "huzm,umw->huzw", expert_up_delta, routed_up_weight, preferred_element_type=single_float32
    )
    rows_grad = lax.optimization_barrier(rows_grad.astype(brain_float16)).astype(single_float32)
    rows_back = return_rows(rows_grad)
    mid_grad = mid_grad + place_columns(jnp.sum(rows_back[index].reshape(count, top_k, -1), axis=1))
    spread = jnp.sum(gate_grad * gates, axis=-1, keepdims=True)
    chosen_grad = (ROUTE_SCALE * gate_grad - spread) / chosen_sum
    logit_grad = jnp.einsum("gk,gke->ge", chosen_grad, pick) * sig * (1.0 - sig)
    router_grad = precise_tn(mid_low.astype(single_float32), logit_grad)
    mid_grad = mid_grad + precise_nt(logit_grad, router_w.astype(single_float32))
    mid_total = lax.psum(mid_grad.astype(jnp.bfloat16), "ctx").astype(jnp.float32)
    resid_grad = norm_back(mid_total, unit_mid, factor_mid, norm_mid) + grad_top_f
    mid_gain_grad = jnp.sum(
        lax.dynamic_slice_in_dim(mid_total * unit_mid, offset, tok_dev, 0), axis=0
    )
    attn_low = resid_grad.astype(brain_float16)
    output_grad = dot_tn(heads_low, attn_low)
    heads_grad = dot_nt(attn_low, output_w).astype(brain_float16).reshape(count, width, VD)

    def backward_block(carry, item):
        knope_grad, krope_grad, values_grad = carry
        first, lse = item
        logits, q_blk = scores_of(first)
        probs = jnp.exp(logits - lse[..., None])
        grad_blk = lax.dynamic_slice_in_dim(heads_grad, first, block, 0)
        prob_grad = jnp.einsum(
            "qhd,khd->hqk", grad_blk, values, preferred_element_type=single_float32
        )
        delta = jnp.sum(probs * prob_grad, axis=-1, keepdims=True)
        score_grad = (probs * (prob_grad - delta)).astype(brain_float16)
        q_nope = (
            jnp.einsum("hqk,khd->qhd", score_grad, knope, preferred_element_type=single_float32)
            * scale
        )
        q_rope = (
            jnp.einsum("hqk,kd->qhd", score_grad, krope, preferred_element_type=single_float32)
            * scale
        )
        knope_grad = (
            knope_grad
            + jnp.einsum(
                "hqk,qhd->khd", score_grad, q_blk[..., :NOPE], preferred_element_type=single_float32
            )
            * scale
        )
        krope_grad = (
            krope_grad
            + jnp.einsum(
                "hqk,qhd->kd", score_grad, q_blk[..., NOPE:], preferred_element_type=single_float32
            )
            * scale
        )
        values_grad = values_grad + jnp.einsum(
            "hqk,qhd->khd",
            probs.astype(brain_float16),
            grad_blk,
            preferred_element_type=single_float32,
        )
        return ((knope_grad, krope_grad, values_grad), jnp.concatenate([q_nope, q_rope], axis=-1))

    start_carry = (
        jnp.zeros((count, width, NOPE), single_float32),
        jnp.zeros((count, ROPE), single_float32),
        jnp.zeros((count, width, VD), single_float32),
    )
    (knope_grad, krope_grad, values_grad), q_blocks = lax.scan(
        backward_block, start_carry, (firsts, lse_blocks)
    )
    q_grad = q_blocks.reshape(count, width, NOPE + ROPE)
    q_raw_grad = (
        jnp.concatenate(
            [q_grad[..., :NOPE], turn_back(q_grad[..., NOPE:], cosine[:, None], sine[:, None])],
            axis=-1,
        )
        .astype(brain_float16)
        .reshape(count, -1)
    )
    query_grad = dot_tn(x_low, q_raw_grad)
    normed_grad = dot_nt(q_raw_grad, query_w)
    kv_grad = (
        jnp.concatenate([knope_grad, values_grad], axis=-1).astype(brain_float16).reshape(count, -1)
    )
    expand_grad = dot_tn(latent_low, kv_grad)
    latent_out_grad = dot_nt(kv_grad, expand_w)
    latent_gain_grad = jnp.sum(latent_out_grad * unit_lat, axis=0)
    latent_grad = norm_back(latent_out_grad, unit_lat, factor_lat, latent_gain)
    raw_grad = jnp.concatenate([latent_grad, turn_back(krope_grad, cosine, sine)], axis=-1).astype(
        brain_float16
    )
    latent_w_grad = dot_tn(x_low, raw_grad)
    normed_grad = normed_grad + dot_nt(raw_grad, latent_w)
    in_gain_grad = jnp.sum(normed_grad * unit_in, axis=0)
    input_part = norm_back(normed_grad, unit_in, factor_in, norm_in)
    grad_input = lax.psum_scatter(
        input_part.astype(jnp.bfloat16), "ctx", scatter_dimension=0, tiled=True
    ).astype(jnp.float32) + lax.dynamic_slice_in_dim(resid_grad, offset, tok_dev, 0)
    g_query, g_expand, g_output, g_sgate, g_sup, g_sdown = (
        lax.psum_scatter(
            query_grad.astype(jnp.bfloat16), "fsdp", scatter_dimension=0, tiled=True
        ).astype(jnp.float32),
        lax.psum_scatter(
            expand_grad.astype(jnp.bfloat16), "fsdp", scatter_dimension=0, tiled=True
        ).astype(jnp.float32),
        lax.psum_scatter(
            output_grad.astype(jnp.bfloat16), "fsdp", scatter_dimension=1, tiled=True
        ).astype(jnp.float32),
        lax.psum_scatter(
            sgate_grad.astype(jnp.bfloat16), "fsdp", scatter_dimension=0, tiled=True
        ).astype(jnp.float32),
        lax.psum_scatter(
            sup_grad.astype(jnp.bfloat16), "fsdp", scatter_dimension=0, tiled=True
        ).astype(jnp.float32),
        lax.psum_scatter(
            sdown_grad.astype(jnp.bfloat16), "fsdp", scatter_dimension=1, tiled=True
        ).astype(jnp.float32),
    )
    g_latent, g_router, g_in, g_lat_gain, g_mid = (
        lax.psum_scatter(latent_w_grad, ("fsdp", "ctx"), scatter_dimension=0, tiled=True),
        lax.psum_scatter(router_grad, ("fsdp", "ctx"), scatter_dimension=0, tiled=True),
        lax.psum_scatter(in_gain_grad, ("fsdp", "ctx"), scatter_dimension=0, tiled=True),
        lax.psum_scatter(latent_gain_grad, ("fsdp", "ctx"), scatter_dimension=0, tiled=True),
        lax.psum_scatter(mid_gain_grad, ("fsdp", "ctx"), scatter_dimension=0, tiled=True),
    )
    return (
        block_out,
        grad_input.astype(brain_float16),
        g_in,
        g_query,
        g_latent,
        g_lat_gain,
        g_expand,
        g_output,
        g_mid,
        g_router,
        g_sgate,
        g_sup,
        g_sdown,
        egate_grad,
        expert_up_gradient,
        down_grad,
    )


def solution(mesh):
    in_specs = (
        P(("fsdp", "ctx"), None),
        P(("fsdp", "ctx"), None),
        P(("fsdp", "ctx"), None),
        P(("fsdp", "ctx")),
        P(),
        P("fsdp", "ctx"),
        P(("fsdp", "ctx"), None),
        P(),
        P("fsdp", "ctx"),
        P("ctx", "fsdp"),
        P(),
        P(("fsdp", "ctx"), None),
        P("fsdp", "ctx"),
        P("fsdp", "ctx"),
        P("ctx", "fsdp"),
        P("fsdp", "ctx", None),
        P("fsdp", "ctx", None),
        P("fsdp", "ctx", None),
    )
    out_specs = (
        P(("fsdp", "ctx"), None),
        P(("fsdp", "ctx"), None),
        P(("fsdp", "ctx")),
        P("fsdp", "ctx"),
        P(("fsdp", "ctx"), None),
        P(("fsdp", "ctx")),
        P("fsdp", "ctx"),
        P("ctx", "fsdp"),
        P(("fsdp", "ctx")),
        P(("fsdp", "ctx"), None),
        P("fsdp", "ctx"),
        P("fsdp", "ctx"),
        P("ctx", "fsdp"),
        P("fsdp", "ctx", None),
        P("fsdp", "ctx", None),
        P("fsdp", "ctx", None),
    )
    return jax.shard_map(
        per_device, mesh=mesh, in_specs=in_specs, out_specs=out_specs, check_vma=False
    )
```

profile of v0, /device:TPU:0, one launch (start us, length us, event | category | flops | bytes accessed | tf_op | source)
XLA Modules:
  0.0 2727.7 jit_solution(3218974739021637824)
XLA Ops:
  11.2 12.7 all-gather
  25.5 32.7 %all-gather.14.cloned.1.call-done = bf16[512,2048]{1,0:T(8,128)(2,1)} async-done(((bf16[128,2048]{1,0:T(8,128)(2,1)}), bf16[512,2048]{1,0:T(8,128)(2,1)}) %all-gather.14.cloned.1.call-update) | async-done | bytes 2097168 | tf_op jit(solution)/shard_map/all_gather | solution.py:127
  60.4 57.6 %all-gather.16.cloned.1.call-done = bf16[2048,576]{1,0:T(8,128)(2,1)} async-done(((bf16[64,576]{1,0:T(8,128)(2,1)}), bf16[2048,576]{1,0:T(8,128)(2,1)}) %all-gather.16.cloned.1.call-update) | async-done | bytes 2359312 | tf_op jit(solution)/shard_map/all_gather | solution.py:123
  123.1 19.2 all-gather.18.cloned.1.call-done
  154.8 21.6 all-gather.20.cloned.1.call-done
  176.4 4.4 fusion.103
  186.8 19.6 all-gather.22.cloned.1.call-done
  206.3 4.9 fusion.109
  211.3 13.5 all_gather.51
  225.8 4.6 reduce-window.19
  231.2 13.4 scatter_custom_fusion
  244.7 11.8 scatter_custom_fusion.1
  256.6 109.9 %all-reduce.7.cloned.1.call-done = f32[512,2048]{1,0:T(8,128)} async-done(((f32[512,2048]{1,0:T(8,128)}), f32[512,2048]{1,0:T(8,128)}) %all-reduce.7.cloned.1.call-update) | async-done | bytes 4194320 | tf_op jit(solution)/shard_map/psum | solution.py:182
  374.6 11.7 gather_fusion
  388.8 49.8 %all_to_all.20 = bf16[8,2,240,512]{3,2,1,0:T(8,128)(2,1)S(1)} all-to-all(bf16[8,2,240,512]{3,2,1,0:T(8,128)(2,1)S(1)} %broadcast_select_fusion), channel_id=1, replica_groups=mesh['fsdp'=8,'ctx'=4] {'fsdp'}, dimensions={0} | all-to-all | bytes 7864320 | tf_op jit(solution)/shard_map/all_to_all | solution.py:207
  441.3 266.5 %all-gather.30.cloned.1.call-done = bf16[8,2,240,2048]{3,2,0,1:T(8,128)(2,1)} async-done(((bf16[8,2,240,512]{3,2,0,1:T(8,128)(2,1)}), bf16[8,2,240,2048]{3,2,0,1:T(8,128)(2,1)}) %all-gather.30.cloned.1.call-update) | async-done | bytes 15728656 | tf_op jit(solution)/shard_map/all_gather | solution.py:208
  707.8 12.1 fusion.30
  719.9 12.8 fusion.8
  732.8 13.5 convert_bitcast_fusion
  748.9 258.3 %reduce-scatter.15.cloned.1.call-done = bf16[8,2,240,512]{3,2,0,1:T(8,128)(2,1)} async-done(((bf16[8,2,240,2048]{3,2,0,1:T(8,128)(2,1)}), bf16[8,2,240,512]{3,2,0,1:T(8,128)(2,1)}) %reduce-scatter.15.cloned.1.call-update) | async-done | bytes 3932176 | tf_op jit(solution)/shard_map/reduce_scatter | solution.py:211
  1007.2 4.4 copy.130
  1011.6 4.7 all-to-all-start.1
  1016.4 72.0 %all-gather.1 = bf16[32,64,16]{1,2,0:T(8,128)(2,1)S(1)} all-gather(bf16[1,64,16]{1,2,0:T(8,128)(2,1)S(1)} %bitcast.243), channel_id=1, replica_groups=mesh['fsdp'=8,'ctx'=4] {'fsdp','ctx'}, dimensions={0}, use_global_device_ids=true | all-gather | bytes 67584 | tf_op jit(solution)/shard_map/all_gather | solution.py:124
  1088.7 4.3 convert_element_type.192
  1097.1 5.4 fusion.111
  1102.5 21.1 all-gather.24.cloned.1.call-done
  1123.6 5.2 fusion.110
  1128.9 28.3 %all-gather.28.cloned.1.call-done = bf16[704,2048]{1,0:T(8,128)(2,1)} async-done(((bf16[704,256]{1,0:T(8,128)(2,1)}), bf16[704,2048]{1,0:T(8,128)(2,1)}) %all-gather.28.cloned.1.call-update) | async-done | bytes 2883600 | tf_op jit(solution)/shard_map/all_gather | solution.py:120
  1157.2 6.7 multiply_convert_fusion.2
  1168.6 16.0 gather_fusion.1
  1184.6 6.4 reshape.333
  1195.7 4.4 fusion.113
  1200.1 20.1 gather_fusion.2
  1223.9 13.7 gather_fusion.3
  1237.6 4.4 select_convert_fusion
  1242.0 48.8 %all_to_all.21 = bf16[8,2,240,512]{3,2,1,0:T(8,128)(2,1)S(1)} all-to-all(bf16[8,2,240,512]{3,2,1,0:T(8,128)(2,1)S(1)} %select_convert_fusion), channel_id=1, replica_groups=mesh['fsdp'=8,'ctx'=4] {'fsdp'}, dimensions={0} | all-to-all | bytes 7864320 | tf_op jit(solution)/shard_map/all_to_all | solution.py:207
  1293.1 268.8 %all-gather.34.cloned.1.call-done = bf16[8,2,240,2048]{3,2,0,1:T(8,128)(2,1)} async-done(((bf16[8,2,240,512]{3,2,0,1:T(8,128)(2,1)}), bf16[8,2,240,2048]{3,2,0,1:T(8,128)(2,1)}) %all-gather.34.cloned.1.call-update) | async-done | bytes 15728656 | tf_op jit(solution)/shard_map/all_gather | solution.py:208
  1561.9 14.7 fusion.7
  1576.6 16.9 fusion.28
  1593.5 18.0 fusion
  1611.5 261.0 %reduce-scatter.19.cloned.1.call-done = bf16[8,2,240,512]{3,2,0,1:T(8,128)(2,1)} async-done(((bf16[8,2,240,2048]{3,2,0,1:T(8,128)(2,1)}), bf16[8,2,240,512]{3,2,0,1:T(8,128)(2,1)}) %reduce-scatter.19.cloned.1.call-update) | async-done | bytes 3932176 | tf_op jit(solution)/shard_map/reduce_scatter | solution.py:211
  1872.5 4.4 copy.132
  1876.9 4.5 all-to-all-start.3
  1890.4 37.4 %all-to-all-done.3 = bf16[8,2,240,512]{3,2,1,0:T(8,128)(2,1)} async-done(((bf16[8,2,240,512]{3,2,1,0:T(8,128)(2,1)}), bf16[8,2,240,512]{3,2,1,0:T(8,128)(2,1)}, u32[]{:S(2)}, u32[]{:S(2)}) %all-to-all-start.3) | async-done | bytes 3932192 | tf_op jit(solution)/shard_map/all_to_all | solution.py:214
  1927.7 6.3 bitcast_convert_fusion
  1934.1 17.0 gather_fusion.4
  1951.1 8.2 reshape.337
  1959.4 6.0 reduce_sum.143
  1967.8 5.5 add_convert_fusion.1
  1973.4 5.2 convolution_convert_fusion.3
  1982.1 4.4 convolution_convert_fusion.2
  1994.0 65.2 %all-reduce.9.cloned.1.call-done = bf16[512,2048]{1,0:T(8,128)(2,1)} async-done(((bf16[512,2048]{1,0:T(8,128)(2,1)}), bf16[512,2048]{1,0:T(8,128)(2,1)}) %all-reduce.9.cloned.1.call-update) | async-done | bytes 2097168 | tf_op jit(solution)/shard_map/psum | solution.py:301
  2101.2 4.4 fusion.66
  2108.3 47.0 %reduce-scatter.33.cloned.1.call-done = bf16[256,704]{0,1:T(8,128)(2,1)} async-done(((bf16[2048,704]{0,1:T(8,128)(2,1)}), bf16[256,704]{0,1:T(8,128)(2,1)}) %reduce-scatter.33.cloned.1.call-update) | async-done | bytes 360464 | tf_op jit(solution)/shard_map/reduce_scatter | solution.py:400
  2157.3 46.8 %reduce-scatter.31.cloned.1.call-done = bf16[256,704]{0,1:T(8,128)(2,1)} async-done(((bf16[2048,704]{0,1:T(8,128)(2,1)}), bf16[256,704]{0,1:T(8,128)(2,1)}) %reduce-scatter.31.cloned.1.call-update) | async-done | bytes 360464 | tf_op jit(solution)/shard_map/reduce_scatter | solution.py:397
  2206.0 135.8 %reduce-scatter.37.cloned.1.call-done = f32[64,16]{1,0:T(8,128)} async-done(((f32[2048,16]{1,0:T(8,128)}), f32[64,16]{1,0:T(8,128)}) %reduce-scatter.37.cloned.1.call-update) | async-done | bytes 4112
  2343.2 41.4 %reduce-scatter.17.cloned.1.call-done = bf16[128,2048]{1,0:T(8,128)(2,1)} async-done(((bf16[512,2048]{1,0:T(8,128)(2,1)}), bf16[128,2048]{1,0:T(8,128)(2,1)}) %reduce-scatter.17.cloned.1.call-update) | async-done | bytes 524304 | tf_op jit(solution)/shard_map/reduce_scatter | solution.py:245
  2386.9 13.7 convolution_bitcast_fusion
  2400.6 13.7 convolution_bitcast_fusion.1
  2414.3 8.1 convolution_bitcast_fusion.2
  2424.7 39.8 %all-reduce.3 = (f32[2048]{0:T(1024)S(1)}, f32[512]{0:T(512)S(1)}, f32[2048]{0:T(1024)S(1)}) all-reduce(f32[2048]{0:T(1024)S(1)} %get-tuple-element.69, f32[512]{0:T(512)S(1)} %get-tuple-element.71, f32[2048]{0:T(1024)S(1)} %fusion.56), channel_id=6, replica_groups=mesh['fsdp'=8,'ctx'=4] {'fsdp','ctx'}, use_global_device_ids=true, to_apply=%region_26.27.clone | all-reduce | flops 4608 | bytes 36864
  2470.2 44.4 %reduce-scatter.21.cloned.1.call-done = bf16[128,2048]{1,0:T(8,128)(2,1)} async-done(((bf16[512,2048]{1,0:T(8,128)(2,1)}), bf16[128,2048]{1,0:T(8,128)(2,1)}) %reduce-scatter.21.cloned.1.call-update) | async-done | bytes 524304 | tf_op jit(solution)/shard_map/reduce_scatter | solution.py:384
  2516.9 47.0 %reduce-scatter.23.cloned.1.call-done = bf16[256,768]{1,0:T(8,128)(2,1)} async-done(((bf16[2048,768]{1,0:T(8,128)(2,1)}), bf16[256,768]{1,0:T(8,128)(2,1)}) %reduce-scatter.23.cloned.1.call-update) | async-done | bytes 393232 | tf_op jit(solution)/shard_map/reduce_scatter | solution.py:388
  2565.8 154.9 %reduce-scatter.25.cloned.1.call-done = f32[64,576]{1,0:T(8,128)} async-done(((f32[2048,576]{1,0:T(8,128)}), f32[64,576]{1,0:T(8,128)}) %reduce-scatter.25.cloned.1.call-update) | async-done | bytes 147472 | tf_op jit(solution)/shard_map/reduce_scatter | solution.py:408
  (338 shorter events, 154.6 us)
Async XLA Ops:
  7.2 725.6 %copy-start = (bf16[2,352,2048]{2,1,0:T(8,128)(2,1)S(1)}, bf16[2,352,2048]{2,1,0:T(8,128)(2,1)}, u32[]{:S(2)}) copy-start(bf16[2,352,2048]{2,1,0:T(8,128)(2,1)} %param.35) | copy-start | bytes 8650756
  7.2 51.1 %all-gather.14.cloned.1.call-start = ((), (), s32[]{:S(2)}) async-start(), calls=%async_computation.16 | async-start | bytes 2621440 | tf_op jit(solution)/shard_map/all_gather | solution.py:127
  7.9 110.0 %all-gather.16.cloned.1.call-start = ((), (), s32[]{:S(2)}) async-start(), calls=%async_computation.17 | async-start | bytes 2703360 | tf_op jit(solution)/shard_map/all_gather | solution.py:123
  8.7 133.6 %all-gather.18.cloned.1.call-start = ((), (), s32[]{:S(2)}) async-start(), calls=%async_computation.18 | async-start | bytes 1179648 | tf_op jit(solution)/shard_map/all_gather | solution.py:116
  9.4 167.0 %all-gather.20.cloned.1.call-start = ((), (), s32[]{:S(2)}) async-start(), calls=%async_computation.19 | async-start | bytes 3538944 | tf_op jit(solution)/shard_map/all_gather | solution.py:115
  10.0 196.4 %all-gather.22.cloned.1.call-start = ((), (), s32[]{:S(2)}) async-start(), calls=%async_computation.20 | async-start | bytes 2359296 | tf_op jit(solution)/shard_map/all_gather | solution.py:117
  10.6 355.9 %all-reduce.7.cloned.1.call-start = ((), (), s32[]{:S(2)}) async-start(), calls=%async_computation.21 | async-start | bytes 8388608 | tf_op jit(solution)/shard_map/psum | solution.py:182
  25.5 127.4 %copy-start.62 = (f32[512]{0:T(512)}, f32[512]{0:T(512)S(1)}, u32[]{:S(2)}) copy-start(f32[512]{0:T(512)S(1)} %fusion.93) | copy-start | bytes 6148
  60.3 116.0 %copy-start.70 = (f32[512]{0:T(512)}, f32[512]{0:T(512)S(1)}, u32[]{:S(2)}) copy-start(f32[512]{0:T(512)S(1)} %add_rsqrt_fusion.2) | copy-start | bytes 6148
  60.3 82.0 %copy-start.72 = (f32[512]{0:T(512)S(1)}, f32[512]{0:T(512)}, u32[]{:S(2)}) copy-start(f32[512]{0:T(512)} %param.25) | copy-start | bytes 6148
  123.0 22.6 copy-start.66
  123.0 53.3 %copy-start.68 = (f32[2048]{0:T(1024)S(1)}, f32[2048]{0:T(1024)}, u32[]{:S(2)}) copy-start(f32[2048]{0:T(1024)} %param.22) | copy-start | bytes 24580
  150.6 30.4 %copy-start.18 = (bf16[512,4,128]{2,1,0:T(4,128)(2,1)}, bf16[512,4,128]{2,1,0:T(4,128)(2,1)S(1)}, u32[]{:S(2)}) copy-start(bf16[512,4,128]{2,1,0:T(4,128)(2,1)S(1)} %get-tuple-element.104) | copy-start | bytes 1572868
  154.8 26.1 copy-start.45
  154.8 26.1 copy-start.47
  186.8 24.5 copy-start.51
  206.3 5.0 copy-start.74
  211.3 496.5 %all-gather.30.cloned.1.call-start = ((), (), s32[]{:S(2)}) async-start(), calls=%async_computation.25 | async-start | bytes 19660800 | tf_op jit(solution)/shard_map/all_gather | solution.py:208
  256.6 113.5 %copy-start.56 = (f32[2048]{0:T(1024)S(1)}, f32[2048]{0:T(1024)}, u32[]{:S(2)}) copy-start(f32[2048]{0:T(1024)} %param.28) | copy-start | bytes 24580
  440.8 566.4 %reduce-scatter.15.cloned.1.call-start = ((), (), s32[]{:S(2)}) async-start(), calls=%async_computation.26 | async-start | bytes 19660800 | tf_op jit(solution)/shard_map/reduce_scatter | solution.py:211
  707.8 12.1 copy-start.23
  746.3 342.4 %all-gather.32.cloned.1.call-start = ((), (), s32[]{:S(2)}) async-start(), calls=%async_computation.28 | async-start | bytes 2621440 | tf_op jit(solution)/shard_map/all_gather | solution.py:252
  747.0 350.0 %all-gather.26.cloned.1.call-start = ((), (), s32[]{:S(2)}) async-start(), calls=%async_computation.23 | async-start | bytes 3244032 | tf_op jit(solution)/shard_map/all_gather | solution.py:119
  747.6 376.0 %all-gather.24.cloned.1.call-start = ((), (), s32[]{:S(2)}) async-start(), calls=%async_computation.22 | async-start | bytes 3244032 | tf_op jit(solution)/shard_map/all_gather | solution.py:118
  748.3 408.9 %all-gather.28.cloned.1.call-start = ((), (), s32[]{:S(2)}) async-start(), calls=%async_computation.24 | async-start | bytes 3244032 | tf_op jit(solution)/shard_map/all_gather | solution.py:120
  1011.6 4.7 copy-start.75
  1011.6 157.0 %all-to-all-start.1 = ((bf16[8,2,240,512]{3,2,1,0:T(8,128)(2,1)}), bf16[8,2,240,512]{3,2,1,0:T(8,128)(2,1)}, u32[]{:S(2)}, u32[]{:S(2)}) async-start(bf16[8,2,240,512]{3,2,1,0:T(8,128)(2,1)} %copy.130), calls=%async_computation.2 | async-start | bytes 7864320 | tf_op jit(solution)/shard_map/all_to_all | solution.py:214
  1016.3 545.6 %all-gather.34.cloned.1.call-start = ((), (), s32[]{:S(2)}) async-start(), calls=%async_computation.29 | async-start | bytes 19660800 | tf_op jit(solution)/shard_map/all_gather | solution.py:208
  1088.6 6.9 copy-start.43
  1088.7 6.1 copy-start.6
  1157.2 7.6 copy-start.28
  1191.0 4.2 copy-start.37
  1293.0 579.5 %reduce-scatter.19.cloned.1.call-start = ((), (), s32[]{:S(2)}) async-start(), calls=%async_computation.30 | async-start | bytes 19660800 | tf_op jit(solution)/shard_map/reduce_scatter | solution.py:211
  1576.6 16.9 copy-start.24
  1576.6 16.9 copy-start.25
  1876.9 50.9 %all-to-all-start.3 = ((bf16[8,2,240,512]{3,2,1,0:T(8,128)(2,1)}), bf16[8,2,240,512]{3,2,1,0:T(8,128)(2,1)}, u32[]{:S(2)}, u32[]{:S(2)}) async-start(bf16[8,2,240,512]{3,2,1,0:T(8,128)(2,1)} %copy.132), calls=%async_computation.6 | async-start | bytes 7864320 | tf_op jit(solution)/shard_map/all_to_all | solution.py:214
  1881.4 4.6 copy-start.27
  1881.4 177.8 %all-reduce.9.cloned.1.call-start = ((), (), s32[]{:S(2)}) async-start(), calls=%async_computation.31 | async-start | bytes 4194304 | tf_op jit(solution)/shard_map/psum | solution.py:301
  1959.4 8.4 copy-start.44
  1959.4 8.4 copy-start.50
  1973.3 5.5 copy-start.7
  1973.3 5.5 copy-start.41
  1973.3 133.0 %reduce-scatter.35.cloned.1.call-start = ((), (), s32[]{:S(2)}) async-start(), calls=%async_computation.39 | async-start | bytes 3244032 | tf_op jit(solution)/shard_map/reduce_scatter | solution.py:403
  1978.6 176.8 %reduce-scatter.33.cloned.1.call-start = ((), (), s32[]{:S(2)}) async-start(), calls=%async_computation.38 | async-start | bytes 3244032 | tf_op jit(solution)/shard_map/reduce_scatter | solution.py:400
  1982.1 222.0 %reduce-scatter.31.cloned.1.call-start = ((), (), s32[]{:S(2)}) async-start(), calls=%async_computation.37 | async-start | bytes 3244032 | tf_op jit(solution)/shard_map/reduce_scatter | solution.py:397
  1986.5 355.3 %reduce-scatter.37.cloned.1.call-start = ((), (), s32[]{:S(2)}) async-start(), calls=%async_computation.40 | async-start | bytes 1081344
  1989.9 394.7 %reduce-scatter.17.cloned.1.call-start = ((), (), s32[]{:S(2)}) async-start(), calls=%async_computation.27 | async-start | bytes 2621440 | tf_op jit(solution)/shard_map/reduce_scatter | solution.py:245
  1990.0 69.3 %copy-start.57 = (f32[2048]{0:T(1024)S(1)}, f32[2048]{0:T(1024)}, u32[]{:S(2)}) copy-start(f32[2048]{0:T(1024)} %param.28) | copy-start | bytes 24580
  1993.9 69.0 %copy-start.65 = (f32[512]{0:T(512)S(1)}, f32[512]{0:T(512)}, u32[]{:S(2)}) copy-start(f32[512]{0:T(512)} %copy-done.64) | copy-start | bytes 6148
  1993.9 472.4 %reduce-scatter.27.cloned.1.call-start = ((), (), s32[]{:S(2)}) async-start(), calls=%async_computation.35 | async-start | bytes 1179648 | tf_op jit(solution)/shard_map/reduce_scatter | solution.py:391
  2059.2 4.7 copy-start.9
  2078.0 390.4 %reduce-scatter.29.cloned.1.call-start = ((), (), s32[]{:S(2)}) async-start(), calls=%async_computation.36 | async-start | bytes 2359296 | tf_op jit(solution)/shard_map/reduce_scatter | solution.py:394
  2084.0 430.6 %reduce-scatter.21.cloned.1.call-start = ((), (), s32[]{:S(2)}) async-start(), calls=%async_computation.32 | async-start | bytes 2621440 | tf_op jit(solution)/shard_map/reduce_scatter | solution.py:384
  2097.1 466.8 %reduce-scatter.23.cloned.1.call-start = ((), (), s32[]{:S(2)}) async-start(), calls=%async_computation.33 | async-start | bytes 3538944 | tf_op jit(solution)/shard_map/reduce_scatter | solution.py:388
  2100.9 619.9 %reduce-scatter.25.cloned.1.call-start = ((), (), s32[]{:S(2)}) async-start(), calls=%async_computation.34 | async-start | bytes 5406720 | tf_op jit(solution)/shard_map/reduce_scatter | solution.py:408
  2105.6 281.3 %copy-start.79 = (bf16[8,2,240,352]{2,3,0,1:T(8,128)(2,1)S(1)}, bf16[8,2,240,352]{2,3,0,1:T(8,128)(2,1)}, u32[]{:S(2)}) copy-start(bf16[8,2,240,352]{2,3,0,1:T(8,128)(2,1)} %get-tuple-element.116) | copy-start | bytes 8110084
  2386.9 13.7 copy-start.26
  2386.9 27.4 %slice-start = ((s8[15728640]{0:T(1024)(128)(4,1)}), s8[4194304]{0:T(1024)(128)(4,1)S(1)}, s32[]{:S(2)}) async-start(s8[15728640]{0:T(1024)(128)(4,1)} %bitcast.245), calls=%async_computation.41 | async-start | bytes 8388608
  2386.9 27.4 %slice-start.1 = ((s8[15728640]{0:T(1024)(128)(4,1)}), s8[4194304]{0:T(1024)(128)(4,1)S(1)}, s32[]{:S(2)}) async-start(s8[15728640]{0:T(1024)(128)(4,1)} %bitcast.245), calls=%async_computation.42 | async-start | bytes 8388608
  2400.5 13.7 copy-start.17
  2400.6 13.7 slice-start.2
  2400.6 13.7 slice-start.3
  2414.3 8.2 copy-start.10
  2422.4 298.3 %copy-start.1 = (bf16[2,352,2048]{2,1,0:T(8,128)(2,1)S(1)}, bf16[2,352,2048]{2,1,0:T(8,128)(2,1)}, u32[]{:S(2)}) copy-start(bf16[2,352,2048]{2,1,0:T(8,128)(2,1)} %param.35) | copy-start | bytes 8650756
  (47 other events, 118.9 us)
Sparse Core Ops, SparseCore 0:
  9.6 48.6 all-gather.13
  61.1 56.8 all-gather.15
  119.9 22.3 all-gather.17
  144.0 32.2 all-gather.19
  178.1 28.2 all-gather.21
  211.4 155.0 all-reduce.6
  440.9 266.7 all-gather.29
  746.4 260.7 reduce-scatter.14
  1008.9 48.4 all-gather.31
  1059.2 30.6 all-gather.25
  1091.9 31.6 all-gather.23
  1125.5 31.6 all-gather.27
  1293.2 268.7 all-gather.33
  1611.6 260.8 reduce-scatter.18
  1973.4 85.7 all-reduce.8
  2062.4 43.8 reduce-scatter.34
  2110.5 44.8 reduce-scatter.32
  2159.2 44.8 reduce-scatter.30
  2206.5 135.3 reduce-scatter.36
  2344.0 40.5 reduce-scatter.16
  2388.1 35.3 reduce-scatter.26
  2427.1 41.2 reduce-scatter.28
  2470.7 43.8 reduce-scatter.20
  2518.2 45.5 reduce-scatter.22
  2566.7 153.9 reduce-scatter.24
where the time goes:
time: 2740 us; the launch traced here: 2730 us
  waiting for transfers between devices  1990 us (73%)
  blocking collectives  237 us (9%)
  matrix products  230 us (8%)
  local copies, waits for them, and re-layouts  161 us (6%)
  other arithmetic  80.8 us (3%)
    all_gather x2, waiting for transfers between devices, send_rows(): return lax.all_gather(moved, 'ctx', axis=3, tiled=True)  535 us
    reduce_scatter x2, waiting for transfers between devices, return_rows(): lax.psum_scatter(partial_value.astype(jnp.bfloat16), 'ctx', scatter_dimen...  519 us
    reduce_scatter x1, waiting for transfers between devices, per_device(): lax.psum_scatter(latent_w_grad, ('fsdp', 'ctx'), scatter_dimension=0, til...  155 us
    unnamed x26, waiting for transfers between devices  142 us
    psum x1, waiting for transfers between devices, per_device(): attn = lax.psum(dot32(heads_low, output_w), 'ctx')  110 us
    all_to_all x2, blocking collectives, send_rows(): lax.all_to_all(rows, 'fsdp', split_axis=0, concat_axis=0, tiled=True)  98.6 us
    all_gather x1, blocking collectives, per_device(): lax.all_gather(w_router, ('fsdp', 'ctx'), axis=0, tiled=True)  72 us
    psum x1, waiting for transfers between devices, per_device(): lax.psum(mid_grad.astype(jnp.bfloat16), 'ctx').astype(jnp.float32)  65.2 us
  transfers between devices with their start and end apart: 27, of which 23 were waited for; matrix products, arithmetic and copies ran while one was open for 8% of the time, Pallas kernels for 0%

commit v1 on v0

v1 whole, which is shorter than its diff:
```python
import functools

import jax
import jax.numpy as jnp
from jax import lax
from jax.experimental import pallas as pl
from jax.experimental.pallas import tpu as pltpu
from jax.sharding import PartitionSpec as P

NOPE = 128
ROPE = 64
VD = 128
LAT = 512


EPS = 1e-06
THETA = 50000.0
ROUTE_SCALE = 2.446
MIB = 1024 * 1024
NEG_FILL = -1e30


def dot32(left, right):
    return jnp.dot(left, right, preferred_element_type=jnp.float32)


def dot_nt(left, right):
    return lax.dot_general(
        left, right, (((1,), (1,)), ((), ())), preferred_element_type=jnp.float32
    )


def dot_tn(left, right):
    return lax.dot_general(
        left, right, (((0,), (0,)), ((), ())), preferred_element_type=jnp.float32
    )


def precise_nt(left, right):
    return lax.dot_general(
        left,
        right,
        (((1,), (1,)), ((), ())),
        precision=lax.Precision.HIGHEST,
        preferred_element_type=jnp.float32,
    )


def precise_tn(left, right):
    return lax.dot_general(
        left,
        right,
        (((0,), (0,)), ((), ())),
        precision=lax.Precision.HIGHEST,
        preferred_element_type=jnp.float32,
    )


def norm_parts(value, gain):
    factor = lax.rsqrt(jnp.mean(value * value, axis=-1, keepdims=True) + EPS)
    unit = value * factor
    return (unit * gain, unit, factor)


def norm_back(grad_out, unit, factor, gain):
    grad_unit = grad_out * gain
    return factor * (grad_unit - unit * jnp.mean(grad_unit * unit, axis=-1, keepdims=True))


def turn(value, cosine, sine):
    half = value.shape[-1] // 2
    first, second = (value[..., :half], value[..., half:])
    return jnp.concatenate(
        [first * cosine - second * sine, second * cosine + first * sine], axis=-1
    )


def turn_back(grad, cosine, sine):
    half = grad.shape[-1] // 2
    first, second = (grad[..., :half], grad[..., half:])
    return jnp.concatenate(
        [first * cosine + second * sine, second * cosine - first * sine], axis=-1
    )


def silu_slope(value):
    sig = jax.nn.sigmoid(value)
    return (sig * (1.0 + value * (1.0 - sig)), value * sig)


def after(value, *others):
    return lax.optimization_barrier((value,) + others)[0]


def gather_ctx(value):
    lanes, lane = (lax.axis_size("ctx"), lax.axis_index("ctx"))
    rows = value.shape[0]
    whole = jnp.zeros((lanes * rows,) + value.shape[1:], value.dtype)
    whole = lax.dynamic_update_slice_in_dim(whole, value, lane * rows, 0)
    for hop in range(1, lanes):
        got = lax.ppermute(value, "ctx", [(i, (i + hop) % lanes) for i in range(lanes)])
        source = lax.rem(lane + lanes - hop, lanes)
        whole = lax.dynamic_update_slice_in_dim(whole, got, source * rows, 0)
    return whole


def scatter_ctx(value):
    lanes, lane = (lax.axis_size("ctx"), lax.axis_index("ctx"))
    rows = value.shape[0] // lanes
    total = lax.dynamic_slice_in_dim(value, lane * rows, rows, 0).astype(jnp.float32)
    for hop in range(1, lanes):
        target = lax.rem(lane + hop, lanes)
        part = lax.dynamic_slice_in_dim(value, target * rows, rows, 0)
        got = lax.ppermute(part, "ctx", [(i, (i + hop) % lanes) for i in range(lanes)])
        total = total + got.astype(jnp.float32)
    return total


class Plan:
    def __init__(self, exp_dev, hidden, shared, experts, top):
        self.exp_dev, self.hidden, self.experts, self.top = (exp_dev, hidden, experts, top)
        self.units = exp_dev * hidden
        self.shared = -(-shared // 8) * 8
        at = self.units + self.shared
        if at // 128 != (at + experts - 1) // 128:
            at = -(-at // 128) * 128
        self.router = at
        self.cols = -(-(at + experts) // 128) * 128
        self.even = (self.cols - 1) // 256 * 256
        self.tail = self.cols - self.even
        self.block = at // 128 * 128
        assert self.block >= self.even and self.block + 128 >= at + experts

    def join(self, gate, upper):
        return jnp.concatenate(
            [gate[: self.even], gate[self.even :], upper[self.even :], upper[: self.even]]
        )


def back_kernel(plan, first_ref, mid_ref, dout_ref, meta_ref, w1_ref, wd_ref, *refs):
    f32, bf16 = (jnp.float32, jnp.bfloat16)
    even, tail, hidden = (plan.even, plan.tail, plan.hidden)
    rows, model = mid_ref.shape
    rows_ref, gud_ref, act_ref = refs[-3:]
    mid = mid_ref[...]
    dout = dout_ref[...].reshape(rows, model)
    lanes = lax.broadcasted_iota(jnp.int32, (rows, 128), 1)
    off = plan.router - plan.block
    first = first_ref[0]
    sums = [jnp.zeros((rows, 128), f32) for _ in range(plan.exp_dev)]

    def elements(own, at, gate, upper, act_grad, gate_at, up_at):
        for b in range(0, gate.shape[1], 128):
            low = at + b
            g, u, da = (gate[:, b : b + 128], upper[:, b : b + 128], act_grad[:, b : b + 128])
            sig = jax.nn.sigmoid(g)
            swish = g * sig
            act = swish * u
            weighted = act * da
            scale = None
            for e in range(plan.exp_dev):
                start, stop = (e * hidden, (e + 1) * hidden)
                if stop <= low or start >= low + 128:
                    continue
                if start <= low and stop >= low + 128:
                    scale = own[e]
                    sums[e] = sums[e] + weighted
                else:
                    mine = (low + lanes >= start) & (low + lanes < stop)
                    sums[e] = sums[e] + jnp.where(mine, weighted, 0.0)
                    rest = jnp.ones((rows, 128), f32) if scale is None else scale
                    scale = jnp.where(mine, own[e], rest)
            if scale is not None:
                act = act * scale
                da = da * scale
            act_ref[:, low : low + 128] = act.astype(bf16)
            slope = sig + swish * (1.0 - sig)
            gud_ref[:, gate_at + b : gate_at + b + 128] = (da * u * slope).astype(bf16)
            gud_ref[:, up_at + b : up_at + b + 128] = (da * swish).astype(bf16)

    joint = dot_nt(mid, w1_ref[even : even + 2 * tail, :])
    at_block = plan.block - even
    sig = jax.nn.sigmoid(joint[:, at_block : at_block + 128])
    named = meta_ref[...].reshape(rows, 128).astype(f32)
    expert = (lanes - off).astype(f32)
    member = jnp.zeros((rows, 128), f32)
    for k in range(plan.top):
        member = jnp.where(expert == named[:, k : k + 1], 1.0, member)
    member = jnp.where((lanes >= off) & (lanes < off + plan.experts), member, 0.0)
    chosen = sig * member
    gates = ROUTE_SCALE * chosen / jnp.sum(chosen, axis=1, keepdims=True)
    own = [
        jnp.sum(jnp.where(lanes - off == first + e, gates, 0.0), axis=1, keepdims=True)
        for e in range(plan.exp_dev)
    ]
    act_grad = dot_nt(dout, wd_ref[even : even + tail, :])
    elements(own, even, joint[:, :tail], joint[:, tail:], act_grad, even, even + tail)
    for at in range(0, even, 256):
        up_at = even + 2 * tail + at
        elements(
            own,
            at,
            dot_nt(mid, w1_ref[at : at + 256, :]),
            dot_nt(mid, w1_ref[up_at : up_at + 256, :]),
            dot_nt(dout, wd_ref[at : at + 256, :]),
            at,
            up_at,
        )
    step = 512
    for at in range(0, model, step):
        rows_ref[:, at : at + step] = dot32(gud_ref[...], w1_ref[:, at : at + step]).astype(bf16)
    ends = jnp.zeros((rows, 128), f32)
    for e in range(plan.exp_dev):
        grad = jnp.sum(sums[e], axis=1, keepdims=True)
        high = grad.astype(bf16).astype(f32)
        ends = jnp.where(lanes == first + e, high, ends)
        ends = jnp.where(lanes == plan.experts + first + e, grad - high, ends)
    rows_ref[:, model:] = ends.astype(bf16)


def experts_back(plan, chunk, first, mid, dout, w1, wd, *held):
    tokens, model = mid.shape
    _, chunks, rows, _ = dout.shape
    tile = min(512, tokens)

    def row(width):
        return pl.BlockSpec((tile, width), lambda i: (i, 0))

    def slot(width):
        return pl.BlockSpec((None, tile, width), lambda i: (chunk, i, 0))

    def whole(value):
        return pl.BlockSpec(value.shape, lambda i: (0, 0), pipeline_mode=pl.Buffered(1))

    def outer(width, at):
        return pl.BlockSpec((tile // rows, None, rows, width), lambda i: (i, chunk, 0, at))

    bf16 = jnp.bfloat16
    return pl.pallas_call(
        functools.partial(back_kernel, plan),
        grid=(tokens // tile,),
        in_specs=[
            pl.BlockSpec(memory_space=pltpu.SMEM),
            row(model),
            outer(model, 0),
            outer(128, model // 128),
            whole(w1),
            whole(wd),
        ]
        + [pl.BlockSpec(memory_space=pl.ANY) for _ in held],
        out_specs=[row(model + 128), slot(2 * plan.cols), slot(plan.cols)],
        out_shape=[
            jax.ShapeDtypeStruct((tokens, model + 128), bf16),
            jax.ShapeDtypeStruct((chunks, tokens, 2 * plan.cols), bf16),
            jax.ShapeDtypeStruct((chunks, tokens, plan.cols), bf16),
        ],
        input_output_aliases={6 + n: 1 + n for n in range(len(held))},
        compiler_params=pltpu.CompilerParams(
            dimension_semantics=("arbitrary",), vmem_limit_bytes=58 * MIB
        ),
        cost_estimate=pl.CostEstimate(
            flops=10 * tokens * plan.cols * model,
            bytes_accessed=tokens * 6 * (model + plan.cols),
            transcendentals=tokens * plan.cols,
        ),
        name="experts_back",
    )(first, mid, dout, dout, w1, wd, *held)


def out_kernel(act_ref, wd_ref, *refs):
    out_ref = refs[-1]
    rows, model = (act_ref.shape[0], wd_ref.shape[1])
    act = act_ref[...]
    for at in range(0, model, 512):
        part = dot32(act, wd_ref[:, at : at + 512]).astype(jnp.bfloat16)
        out_ref[:, :, at : at + 512] = part.reshape(out_ref.shape[0], out_ref.shape[1], 512)


def experts_out(plan, groups, lanes, start, chunks, act, wd, *others):
    _, tokens, cols = act.shape
    model = wd.shape[1]
    count = tokens // groups
    rows = count // lanes
    return pl.pallas_call(
        out_kernel,
        grid=(chunks, groups),
        in_specs=[
            pl.BlockSpec((None, count, cols), lambda h, g: (start + h, g, 0)),
            pl.BlockSpec(wd.shape, lambda h, g: (0, 0), pipeline_mode=pl.Buffered(1)),
        ]
        + [pl.BlockSpec(memory_space=pl.ANY) for _ in others],
        out_specs=pl.BlockSpec((None, lanes, None, rows, model), lambda h, g: (g, 0, h, 0, 0)),
        out_shape=jax.ShapeDtypeStruct((groups, lanes, chunks, rows, model), jnp.bfloat16),
        compiler_params=pltpu.CompilerParams(
            dimension_semantics=("arbitrary", "arbitrary"), vmem_limit_bytes=32 * MIB
        ),
        cost_estimate=pl.CostEstimate(
            flops=2 * chunks * tokens * cols * model,
            bytes_accessed=2 * chunks * tokens * (cols + model),
            transcendentals=0,
        ),
        name="experts_out",
    )(act, wd, *others).reshape(groups * lanes * chunks * rows, model)


def sum_kernel(plan, h_ref, z_ref, out_ref, shared_ref):
    @pl.when((pl.program_id(0) == 0) & (pl.program_id(1) == 0))
    def _():
        out_ref[...] = jnp.zeros_like(out_ref)
        shared_ref[...] = jnp.zeros_like(shared_ref)

    h = h_ref[...]
    rows, model = (h.shape[0], z_ref.shape[2])
    step = 512
    for at in range(0, model, step):
        part = dot_tn(h, z_ref[:, :, at : at + step].reshape(rows, step))
        out_ref[:, at : at + step] += part[: plan.units]
        shared_ref[:, at : at + step] += part[plan.units : plan.units + plan.shared]


def down_sum(plan, model, act, dout):
    chunks, tokens, cols = act.shape
    rows = dout.shape[2]
    tile = min(512, tokens)
    shapes = [(plan.units, model), (plan.shared, model)]
    return pl.pallas_call(
        functools.partial(sum_kernel, plan),
        grid=(chunks, tokens // tile),
        in_specs=[
            pl.BlockSpec((None, tile, cols), lambda h, i: (h, i, 0)),
            pl.BlockSpec((tile // rows, None, rows, model), lambda h, i: (i, h, 0, 0)),
        ],
        out_specs=[pl.BlockSpec(s, lambda h, i: (0, 0)) for s in shapes],
        out_shape=[jax.ShapeDtypeStruct(s, jnp.float32) for s in shapes],
        compiler_params=pltpu.CompilerParams(
            dimension_semantics=("arbitrary", "arbitrary"), vmem_limit_bytes=48 * MIB
        ),
        cost_estimate=pl.CostEstimate(
            flops=2 * chunks * tokens * cols * model,
            bytes_accessed=2 * chunks * tokens * (model + cols) + 4 * plan.units * model,
            transcendentals=0,
        ),
        name="down_sum",
    )(act, dout)


def pair_kernel(plan, h_ref, *refs):
    mid_refs, (gate_ref, up_ref, shared_ref) = (refs[:-3], refs[-3:])
    chunk = pl.program_id(0)

    @pl.when((chunk == 0) & (pl.program_id(1) == 0))
    def _():
        gate_ref[...] = jnp.zeros_like(gate_ref)
        up_ref[...] = jnp.zeros_like(up_ref)
        shared_ref[...] = jnp.zeros_like(shared_ref)

    even, tail, units, shared = (plan.even, plan.tail, plan.units, plan.shared)
    second = even + 2 * tail
    step = 256

    def add(z_ref):
        h = h_ref[...]
        for at in range(0, z_ref.shape[1], step):
            cut = slice(at, at + step)
            part = dot_tn(h, z_ref[:, cut])
            gate_ref[:, cut] += part[:units]
            lead = min(units, even)
            up_ref[:lead, cut] += part[second : second + lead]
            if units > even:
                up_ref[even:, cut] += part[even + tail : tail + units]
            joint = jnp.concatenate([part[second:], part[even + tail : second]])
            shared_ref[0, :, cut] += part[units : units + shared]
            shared_ref[1, :, cut] += joint[units : units + shared]

    for h, z_ref in enumerate(mid_refs):
        pl.when(chunk == h)(functools.partial(add, z_ref))


def pair_sum(plan, gud, mids):
    chunks, tokens, cols = gud.shape
    model = mids[0].shape[1]
    tile = min(512, tokens) if chunks <= 2 else 128
    steps = tokens // tile
    shapes = [(plan.units, model), (plan.units, model), (2, plan.shared, model)]

    def part(h):
        def place(c, i):
            return (jnp.where(c == h, i, jnp.where(c < h, 0, steps - 1)), 0)

        return pl.BlockSpec((tile, model), place)

    return pl.pallas_call(
        functools.partial(pair_kernel, plan),
        grid=(chunks, steps),
        in_specs=[pl.BlockSpec((None, tile, cols), lambda c, i: (c, i, 0))]
        + [part(h) for h in range(chunks)],
        out_specs=[
            pl.BlockSpec(s, lambda c, i, n=len(s): (0,) * n, pipeline_mode=pl.Buffered(1))
            for s in shapes
        ],
        out_shape=[jax.ShapeDtypeStruct(s, jnp.float32) for s in shapes],
        compiler_params=pltpu.CompilerParams(
            dimension_semantics=("arbitrary", "arbitrary"), vmem_limit_bytes=58 * MIB
        ),
        cost_estimate=pl.CostEstimate(
            flops=2 * chunks * tokens * cols * model,
            bytes_accessed=2 * chunks * tokens * (model + cols) + 8 * plan.units * model,
            transcendentals=0,
        ),
        name="pair_sum",
    )(gud, *mids)


def pack_kernel(lead, x_ref, heads_grad_ref, latent_ref, qr_ref, heads_ref, kv_ref, extra_ref, out_ref):
    bf16 = jnp.bfloat16
    first = dot_tn(x_ref[...], qr_ref[...])
    out_ref[:, : lead - 128] = first[:, : lead - 128].astype(bf16)
    out_ref[:, lead - 128 : lead] = (first[:, lead - 128 :] + extra_ref[...]).astype(bf16)
    latent = dot32(latent_ref[...], kv_ref[...])
    rows = latent.shape[0]
    pieces = out_ref.shape[0] // rows
    wide = kv_ref.shape[1] // pieces
    for k in range(pieces):
        out_ref[k * rows : (k + 1) * rows, lead : lead + wide] = latent[
            :, k * wide : (k + 1) * wide
        ].astype(bf16)
    out_ref[:, lead + wide :] = dot_tn(heads_grad_ref[...], heads_ref[...]).astype(bf16)


def packed_grads(groups, x_low, attn_low, latent_t, qr, heads_low, kv_grad, extra):
    count, model = x_low.shape
    depth = model // groups
    rows = latent_t.shape[0] // groups
    lead = qr.shape[1]
    wide = kv_grad.shape[1] * rows // depth
    cols = lead + wide + heads_low.shape[1]

    def whole(value):
        return pl.BlockSpec(value.shape, lambda i: (0, 0))

    return pl.pallas_call(
        functools.partial(pack_kernel, lead),
        grid=(groups,),
        in_specs=[
            pl.BlockSpec((count, depth), lambda i: (0, i)),
            pl.BlockSpec((count, depth), lambda i: (0, i)),
            pl.BlockSpec((rows, count), lambda i: (i, 0)),
            whole(qr),
            whole(heads_low),
            whole(kv_grad),
            pl.BlockSpec((depth, 128), lambda i: (i, 0)),
        ],
        out_specs=pl.BlockSpec((depth, cols), lambda i: (i, 0)),
        out_shape=jax.ShapeDtypeStruct((model, cols), jnp.bfloat16),
        compiler_params=pltpu.CompilerParams(
            dimension_semantics=("arbitrary",), vmem_limit_bytes=40 * MIB
        ),
        cost_estimate=pl.CostEstimate(
            flops=2 * count * model * cols, bytes_accessed=16 * MIB, transcendentals=0
        ),
        name="packed_grads",
    )(x_low, attn_low, latent_t, qr, heads_low, kv_grad, extra)


def per_device(
    tokens_in,
    cotangent,
    routes,
    segments,
    norm_in,
    w_query,
    w_latent,
    latent_gain,
    w_expand,
    w_output,
    norm_mid,
    w_router,
    shared_gate,
    shared_up,
    shared_down,
    expert_gate,
    routed_up_weight,
    expert_down,
):
    f32, bf16 = (jnp.float32, jnp.bfloat16)
    groups, lanes = (lax.axis_size("fsdp"), lax.axis_size("ctx"))
    group = lax.axis_index("fsdp")
    tok_dev, model_w = tokens_in.shape
    count = tok_dev * lanes
    depth = w_query.shape[0]
    query_c, expand_c, heads_c = (w_query.shape[1], w_expand.shape[1], w_output.shape[0])
    exp_dev, hidden, _ = expert_gate.shape
    experts_n, top_k = (w_router.shape[1], routes.shape[1])
    sh_units = shared_gate.shape[1] // groups
    plan = Plan(exp_dev, hidden, sh_units, experts_n, top_k)
    units = plan.units
    chunks = max(2, groups * count // 2048)
    width = query_c // (NOPE + ROPE)
    scale = (NOPE + ROPE) ** (-0.5)

    small_c = -(-(LAT + ROPE + experts_n + 3) // 128) * 128
    assert small_c - 128 <= LAT + ROPE
    at_router = LAT + ROPE
    at_seg = at_router + experts_n
    seg_cols = segments.astype(bf16).reshape(w_latent.shape[0], -1)
    spare = small_c - at_seg - seg_cols.shape[1]
    small = jnp.concatenate(
        [w_latent, w_router, seg_cols, jnp.zeros((w_latent.shape[0], spare), bf16)], axis=1
    )
    small = gather_ctx(small)
    seg_all = small[:, at_seg : at_seg + seg_cols.shape[1]].astype(jnp.int32).reshape(count)
    pieces = depth // w_expand.shape[0]
    wide = expand_c // pieces
    expand_blocks = [w_expand[:, k * wide : (k + 1) * wide] for k in range(pieces)]
    packed = jnp.concatenate(
        [w_query, small, jnp.concatenate(expand_blocks, axis=0), w_output.T], axis=1
    )
    packed = lax.all_gather(packed, "fsdp", axis=0, tiled=True)
    at_expand = query_c + small_c
    at_output = at_expand + wide
    query_w = packed[:, :query_c]
    latent_w = packed[:, query_c : query_c + LAT + ROPE]
    router_w = packed[:, query_c + LAT + ROPE : query_c + LAT + ROPE + experts_n]
    expand_w = (
        packed[:, at_expand:at_output]
        .reshape(groups, pieces, LAT // groups, wide)
        .transpose(0, 2, 1, 3)
        .reshape(LAT, expand_c)
    )
    output_wt = packed[:, at_output:]

    meta = jnp.concatenate(
        [routes.astype(bf16), jnp.zeros((tok_dev, 128 - top_k), bf16)], axis=1
    )
    dout_own, small = lax.optimization_barrier((jnp.concatenate([cotangent, meta], axis=1), small))
    dout_group = gather_ctx(dout_own)
    x_own, dout_group = lax.optimization_barrier((tokens_in, dout_group))
    x_all = gather_ctx(x_own)
    dout_all = lax.all_gather(dout_group, "fsdp", axis=0, tiled=True)
    dout_all = dout_all.reshape(groups * lanes, chunks, tok_dev // chunks, model_w + 128)

    shared = jnp.stack([shared_gate.T, shared_up.T, shared_down]).reshape(
        3, groups, sh_units, depth
    )
    shared = lax.all_to_all(shared, "fsdp", split_axis=1, concat_axis=1, tiled=True)
    shared = shared.transpose(0, 2, 1, 3).reshape(3, sh_units, model_w)
    x_all = after(x_all, shared)

    def hidden_rows(experts, mine, router):
        gap = jnp.zeros((plan.router - units - sh_units, model_w), bf16)
        end = jnp.zeros((plan.cols - plan.router - router.shape[0], model_w), bf16)
        return jnp.concatenate([experts.reshape(units, model_w), mine, gap, router, end])

    none = jnp.zeros((0, model_w), bf16)
    w1 = plan.join(
        hidden_rows(expert_gate, shared[0], router_w.T),
        hidden_rows(routed_up_weight, shared[1], none),
    )
    wd = hidden_rows(expert_down, shared[2], none)

    steps = jnp.arange(count, dtype=jnp.int32)
    same = seg_all[:, None] == seg_all[None, :]
    start = jnp.min(jnp.where(same, steps[None, :], count), axis=1)
    place = (steps - start).astype(f32)
    freq = THETA ** (-(jnp.arange(ROPE // 2, dtype=f32) * 2.0 / ROPE))
    angle = place[:, None] * freq[None, :]
    cosine, sine = (jnp.cos(angle), jnp.sin(angle))
    normed, unit_in, _ = norm_parts(x_all.astype(f32), norm_in)
    x_low = normed.astype(bf16)
    q_raw = dot32(x_low, query_w).reshape(count, width, NOPE + ROPE)
    q_nope = q_raw[..., :NOPE].astype(bf16)
    q_rope = turn(q_raw[..., NOPE:], cosine[:, None], sine[:, None]).astype(bf16)
    latent_raw = dot32(x_low, latent_w)
    latent_n, unit_lat, factor_lat = norm_parts(latent_raw[:, :LAT], latent_gain)
    latent_low = latent_n.astype(bf16)
    krope = turn(latent_raw[:, LAT:], cosine, sine).astype(bf16)
    kv_raw = dot32(latent_low, expand_w).astype(bf16).reshape(count, width, NOPE + VD)
    knope = kv_raw[..., :NOPE]
    values = kv_raw[..., NOPE:]
    raw = jnp.einsum("qhd,khd->hqk", q_nope, knope, preferred_element_type=f32)
    raw = raw + jnp.einsum("qhd,kd->hqk", q_rope, krope, preferred_element_type=f32)
    keep = same & (steps[None, :] <= steps[:, None])
    logits = jnp.where(keep[None], raw * scale, NEG_FILL)
    expo = jnp.exp(logits - jnp.max(logits, axis=-1, keepdims=True))
    probs = expo / jnp.sum(expo, axis=-1, keepdims=True)
    probs_low = probs.astype(bf16)
    heads_low = (
        jnp.einsum("hqk,khd->qhd", probs_low, values, preferred_element_type=f32)
        .astype(bf16)
        .reshape(count, heads_c)
    )
    resid = tokens_in.astype(f32) + scatter_ctx(dot_nt(heads_low, output_wt).astype(bf16))
    mid, unit_mid, factor_mid = norm_parts(resid, norm_mid)
    mid_low = mid.astype(bf16)

    first = (group * exp_dev).astype(jnp.int32)[None]
    part = tok_dev // chunks
    mids, rows_parts, rows_own, held = ([], [], [], ())
    last = dout_all
    for h in range(chunks):
        mid_part = gather_ctx(mid_low[h * part : (h + 1) * part])
        last = lax.all_gather(after(mid_part, last), "fsdp", axis=0, tiled=True)
        mids.append(last)
    for h in range(chunks):
        rows_part, *held = experts_back(plan, h, first, mids[h], dout_all, w1, wd, *held)
        rows_part = after(rows_part, last)
        last = lax.psum_scatter(rows_part, "fsdp", scatter_dimension=0, tiled=True)
        rows_parts.append(last)
    gud, act = held
    edown_grad, sdown_grad = down_sum(plan, model_w, act, dout_all)
    egate_grad, eup_grad, sgu_grad = pair_sum(plan, gud, mids)
    out_parts = [
        experts_out(plan, groups, lanes, h, 2, act, wd, edown_grad, egate_grad) for h in range(0, chunks, 2)
    ]
    rows_own = [scatter_ctx(rows) for rows in rows_parts]
    rows_grad = jnp.concatenate(rows_own)
    rows_grad = after(rows_grad, edown_grad, egate_grad, *out_parts)
    mid_grad = rows_grad[:, :model_w]
    gates_grad = (
        rows_grad[:, model_w : model_w + experts_n]
        + rows_grad[:, model_w + experts_n : model_w + 2 * experts_n]
    )

    sig = jax.nn.sigmoid(dot32(mid_low, router_w))
    hit = routes[:, :, None] == jnp.arange(experts_n, dtype=jnp.int32)[None, None, :]
    member = jnp.any(hit, axis=1).astype(f32)
    chosen_sum = jnp.sum(sig * member, axis=-1, keepdims=True)
    gates = ROUTE_SCALE * sig * member / chosen_sum
    spread = jnp.sum(gates_grad * gates, axis=-1, keepdims=True)
    chosen_grad = (ROUTE_SCALE * gates_grad - spread) / chosen_sum
    logit_grad = chosen_grad * member * sig * (1.0 - sig)
    router_grad = precise_tn(mid_low.astype(f32), logit_grad)
    mid_grad = mid_grad + precise_nt(logit_grad, router_w.astype(f32))
    resid_grad = norm_back(mid_grad, unit_mid, factor_mid, norm_mid) + cotangent.astype(f32)
    mid_gain_grad = jnp.sum(mid_grad * unit_mid, axis=0)
    attn_low = gather_ctx(resid_grad.astype(bf16))

    out_sums = []
    for out_part in out_parts:
        last = lax.psum_scatter(after(out_part, last), "fsdp", scatter_dimension=0, tiled=True)
        out_sums.append(last)
    moe = jnp.concatenate([scatter_ctx(rows) for rows in out_sums])
    block_out = (resid + moe).astype(bf16)
    shared_grad = jnp.concatenate([sgu_grad, sdown_grad[None]])[:, :sh_units].astype(bf16)
    shared_grad = shared_grad.reshape(3, sh_units, groups, depth).transpose(0, 2, 1, 3)
    shared_grad = lax.all_to_all(shared_grad, "fsdp", split_axis=1, concat_axis=1, tiled=True)
    shared_grad = shared_grad.reshape(3, sh_units * groups, depth).astype(f32)

    heads_grad = dot32(attn_low, output_wt).astype(bf16).reshape(count, width, VD)
    prob_grad = jnp.einsum("qhd,khd->hqk", heads_grad, values, preferred_element_type=f32)
    delta = jnp.sum(probs * prob_grad, axis=-1, keepdims=True)
    score_grad = (probs * (prob_grad - delta)).astype(bf16)
    q_nope_grad = jnp.einsum("hqk,khd->qhd", score_grad, knope, preferred_element_type=f32) * scale
    q_rope_grad = jnp.einsum("hqk,kd->qhd", score_grad, krope, preferred_element_type=f32) * scale
    knope_grad = jnp.einsum("hqk,qhd->khd", score_grad, q_nope, preferred_element_type=f32) * scale
    krope_grad = jnp.einsum("hqk,qhd->kd", score_grad, q_rope, preferred_element_type=f32) * scale
    values_grad = jnp.einsum("hqk,qhd->khd", probs_low, heads_grad, preferred_element_type=f32)
    q_raw_grad = (
        jnp.concatenate(
            [q_nope_grad, turn_back(q_rope_grad, cosine[:, None], sine[:, None])], axis=-1
        )
        .astype(bf16)
        .reshape(count, query_c)
    )
    kv_grad = (
        jnp.concatenate([knope_grad, values_grad], axis=-1).astype(bf16).reshape(count, expand_c)
    )
    latent_out_grad = dot_nt(kv_grad, expand_w)
    latent_gain_grad = jnp.sum(latent_out_grad * unit_lat, axis=0)
    latent_grad = norm_back(latent_out_grad, unit_lat, factor_lat, latent_gain)
    raw_grad = jnp.concatenate([latent_grad, turn_back(krope_grad, cosine, sine)], axis=-1).astype(
        bf16
    )
    qr_grad = jnp.concatenate(
        [q_raw_grad, raw_grad, jnp.zeros((count, small_c - LAT - ROPE), bf16)], axis=1
    )
    normed_grad = dot_nt(qr_grad, packed[:, :at_expand])
    in_gain_grad = jnp.sum(normed_grad * unit_in, axis=0)
    normed_own = scatter_ctx(normed_grad.astype(bf16))
    _, unit_own, factor_own = norm_parts(tokens_in.astype(f32), norm_in)
    grad_input = norm_back(normed_own, unit_own, factor_own, norm_in) + resid_grad

    latent_gain_col = jnp.pad(
        latent_gain_grad.reshape(groups * lanes, -1),
        ((0, 0), (0, depth // lanes - LAT // (groups * lanes))),
    ).reshape(model_w, 1)
    before = LAT + ROPE - (small_c - 128)
    extra = jnp.concatenate(
        [
            jnp.zeros((model_w, before), f32),
            router_grad,
            in_gain_grad[:, None],
            mid_gain_grad[:, None],
            latent_gain_col,
            jnp.zeros((model_w, 128 - before - experts_n - 3), f32),
        ],
        axis=1,
    )
    grads = packed_grads(
        groups, x_low, attn_low, latent_low.T, qr_grad, heads_low, kv_grad, extra
    )
    grads = lax.psum_scatter(after(grads, last), "fsdp", scatter_dimension=0, tiled=True)
    small_own = scatter_ctx(grads[:, query_c:at_expand])
    g_query = grads[:, :query_c].astype(f32)
    g_expand = grads[:, at_expand:at_output].astype(f32)
    g_expand = jnp.concatenate(
        [g_expand[k * w_expand.shape[0] : (k + 1) * w_expand.shape[0]] for k in range(pieces)],
        axis=1,
    )
    g_output = grads[:, at_output:].astype(f32).T
    at_gain = at_router + experts_n
    return (
        block_out,
        grad_input.astype(bf16),
        small_own[:, at_gain],
        g_query,
        small_own[:, :at_router],
        small_own[: LAT // (groups * lanes), at_gain + 2],
        g_expand,
        g_output,
        small_own[:, at_gain + 1],
        small_own[:, at_router:at_gain],
        shared_grad[0].T,
        shared_grad[1].T,
        shared_grad[2],
        egate_grad.reshape(expert_gate.shape),
        eup_grad.reshape(expert_gate.shape),
        edown_grad.reshape(expert_gate.shape),
    )


def solution(mesh):
    in_specs = (
        P(("fsdp", "ctx"), None),
        P(("fsdp", "ctx"), None),
        P(("fsdp", "ctx"), None),
        P(("fsdp", "ctx")),
        P(),
        P("fsdp", "ctx"),
        P(("fsdp", "ctx"), None),
        P(),
        P("fsdp", "ctx"),
        P("ctx", "fsdp"),
        P(),
        P(("fsdp", "ctx"), None),
        P("fsdp", "ctx"),
        P("fsdp", "ctx"),
        P("ctx", "fsdp"),
        P("fsdp", "ctx", None),
        P("fsdp", "ctx", None),
        P("fsdp", "ctx", None),
    )
    out_specs = (
        P(("fsdp", "ctx"), None),
        P(("fsdp", "ctx"), None),
        P(("fsdp", "ctx")),
        P("fsdp", "ctx"),
        P(("fsdp", "ctx"), None),
        P(("fsdp", "ctx")),
        P("fsdp", "ctx"),
        P("ctx", "fsdp"),
        P(("fsdp", "ctx")),
        P(("fsdp", "ctx"), None),
        P("fsdp", "ctx"),
        P("fsdp", "ctx"),
        P("ctx", "fsdp"),
        P("fsdp", "ctx", None),
        P("fsdp", "ctx", None),
        P("fsdp", "ctx", None),
    )
    return jax.shard_map(
        per_device, mesh=mesh, in_specs=in_specs, out_specs=out_specs, check_vma=False
    )
```

time: 2740 us -> 896 us (0.33)
  waiting for transfers between devices: 1990 us -> 376 us
  blocking collectives: 237 us -> 0 us
  Pallas kernels: 0 us -> 204 us
  matrix products: 230 us -> 53.7 us
  starting transfers between devices: 11.7 us -> 104 us
  local copies, waits for them, and re-layouts: 161 us -> 93.1 us
  other arithmetic: 80.8 us -> 39.9 us
    reduce_scatter x11 -> x4, waiting for transfers between devices: 902 us -> 17.8 us  [the longest x2 17.8 us: per_device(): last = lax.psum_scatter(rows_part, 'fsdp', scatter_dimension=0, tiled=True)]
    all_gather x11 -> x4, waiting for transfers between devices: 736 us -> 42.4 us  [the longest x2 42.4 us: per_device(): last = lax.all_gather(after(mid_part, last), 'fsdp', axis=0, tiled=True)]
    ppermute x0 -> x36, waiting for transfers between devices: none -> 293 us  [the longest x18 158 us: scatter_ctx(): lax.ppermute(part, 'ctx', [(i, (i + hop) % lanes) for i in range(lanes)])]
    pallas_call x0 -> x6, Pallas kernels: none -> 204 us  [the longest x2 110 us: experts_back(): pl.pallas_call(functools.partial(back_kernel, plan), grid=(tokens // tile...]
    psum x2 -> x0, waiting for transfers between devices: 175 us -> none  [the longest x1 110 us: per_device(): attn = lax.psum(dot32(heads_low, output_w), 'ctx')]
    unnamed x26 -> x8, waiting for transfers between devices: 142 us -> 0.13 us
    dot_general x27 -> x10, matrix products: 166 us -> 24.4 us  [the longest x1 5.81 us: per_device(): jnp.einsum('hqk,qhd->khd', probs_low, heads_grad, preferred_element_type=...]
    all_to_all x2 -> x0, blocking collectives: 98.6 us -> none  [send_rows(): lax.all_to_all(rows, 'fsdp', split_axis=0, concat_axis=0, tiled=True)]
  transfers between devices with their start and end apart: 27 -> 46, of which waited for: 23 -> 28; matrix products, arithmetic and copies ran while one was open for 8% -> 17% of each run, Pallas kernels for 0% -> 23%
where the time goes in v1:
time: 896 us; the launch traced here: 887 us
  waiting for transfers between devices  376 us (42%)
  Pallas kernels  204 us (23%)
  starting transfers between devices  104 us (12%)
  local copies, waits for them, and re-layouts  93.1 us (10%)
  matrix products  53.7 us (6%)
  other arithmetic  39.9 us (4%)
  between operations  16.2 us (2%)
    ppermute x18, waiting for transfers between devices, scatter_ctx(): lax.ppermute(part, 'ctx', [(i, (i + hop) % lanes) for i in range(lanes)])  158 us
    ppermute x18, waiting for transfers between devices, gather_ctx(): lax.ppermute(value, 'ctx', [(i, (i + hop) % lanes) for i in range(lanes)])  135 us
    pallas_call x2, Pallas kernels, experts_back(): pl.pallas_call(functools.partial(back_kernel, plan), grid=(tokens // tile...  110 us
    ppermute x18, starting transfers between devices, scatter_ctx(): lax.ppermute(part, 'ctx', [(i, (i + hop) % lanes) for i in range(lanes)])  53.4 us
    ppermute x18, starting transfers between devices, gather_ctx(): lax.ppermute(value, 'ctx', [(i, (i + hop) % lanes) for i in range(lanes)])  42.6 us
    all_gather x2, waiting for transfers between devices, per_device(): last = lax.all_gather(after(mid_part, last), 'fsdp', axis=0, tiled=True)  42.4 us
    pallas_call x1, Pallas kernels, pair_sum(): pl.pallas_call(functools.partial(pair_kernel, plan), grid=(chunks, steps)...  41.2 us
    unnamed x212, local copies, waits for them, and re-layouts  33 us
  transfers between devices with their start and end apart: 46, of which 28 were waited for; matrix products, arithmetic and copies ran while one was open for 17% of the time, Pallas kernels for 23%

profile of v1, /device:TPU:0, one launch (start us, length us, event | category | flops | bytes accessed | tf_op | source)
XLA Modules:
  0.0 887.5 jit_solution(7478057977501291694)
XLA Ops:
  10.1 5.1 collective-permute-start.2
  20.4 6.4 collective-permute-done
  38.3 3.4 collective-permute-start.4
  41.9 10.1 %collective-permute-done.3 = bf16[128,2176]{1,0:T(8,128)(2,1)} collective-permute-done((bf16[128,2176]{1,0:T(8,128)(2,1)S(1)}, bf16[128,2176]{1,0:T(8,128)(2,1)}, u32[]{:S(2)}, u32[]{:S(2)}) %collective-permute-start.3) | collective-permute-done | bytes 557088 | tf_op jit(solution)/shard_map/ppermute | solution.py:101
  53.1 33.1 %collective-permute-done.4 = bf16[128,2176]{1,0:T(8,128)(2,1)S(1)} collective-permute-done((bf16[128,2176]{1,0:T(8,128)(2,1)S(1)}, bf16[128,2176]{1,0:T(8,128)(2,1)S(1)}, u32[]{:S(2)}, u32[]{:S(2)}) %collective-permute-start.4) | collective-permute-done | bytes 557088 | tf_op jit(solution)/shard_map/ppermute | solution.py:101
  91.0 3.4 collective-permute-start.7
  94.8 11.7 %collective-permute-done.6 = bf16[128,2048]{1,0:T(8,128)(2,1)S(1)} collective-permute-done((bf16[128,2048]{1,0:T(8,128)(2,1)S(1)}, bf16[128,2048]{1,0:T(8,128)(2,1)S(1)}, u32[]{:S(2)}, u32[]{:S(2)}) %collective-permute-start.6) | collective-permute-done | bytes 524320 | tf_op jit(solution)/shard_map/ppermute | solution.py:101
  106.6 21.4 %collective-permute-done.7 = bf16[128,2048]{1,0:T(8,128)(2,1)S(1)} collective-permute-done((bf16[128,2048]{1,0:T(8,128)(2,1)S(1)}, bf16[128,2048]{1,0:T(8,128)(2,1)S(1)}, u32[]{:S(2)}, u32[]{:S(2)}) %collective-permute-start.7) | collective-permute-done | bytes 524320 | tf_op jit(solution)/shard_map/ppermute | solution.py:101
  130.1 3.0 slice.223
  136.8 3.5 fusion.17
  146.4 3.0 convolution_convert_fusion.1
  149.4 2.6 reshape.287
  154.7 3.7 fusion.15
  161.1 3.2 fusion.79
  164.3 4.9 convolution_convert_fusion.2
  169.3 3.1 convolution_convert_fusion
  172.5 11.0 %collective-permute-start.9 = (bf16[128,2048]{1,0:T(8,128)(2,1)S(1)}, bf16[128,2048]{1,0:T(8,128)(2,1)S(1)}, u32[]{:S(2)}, u32[]{:S(2)}) collective-permute-start(bf16[128,2048]{1,0:T(8,128)(2,1)S(1)} %get-tuple-element.156), channel_id=1, source_target_pairs={{0,1},{1,2},{2,3},{3,0},{4,5},{5,6},{6,7},{7,4},{8,9},{9,10},{10,1... | collective-permute-start | bytes 1572872 | tf_op jit(solution)/shard_map/ppermute | solution.py:114
  185.2 10.6 %collective-permute-done.9 = bf16[128,2048]{1,0:T(8,128)(2,1)S(1)} collective-permute-done((bf16[128,2048]{1,0:T(8,128)(2,1)S(1)}, bf16[128,2048]{1,0:T(8,128)(2,1)S(1)}, u32[]{:S(2)}, u32[]{:S(2)}) %collective-permute-start.9) | collective-permute-done | bytes 524320 | tf_op jit(solution)/shard_map/ppermute | solution.py:114
  195.8 11.3 %collective-permute-done.11 = bf16[128,2048]{1,0:T(8,128)(2,1)S(1)} collective-permute-done((bf16[128,2048]{1,0:T(8,128)(2,1)S(1)}, bf16[128,2048]{1,0:T(8,128)(2,1)S(1)}, u32[]{:S(2)}, u32[]{:S(2)}) %collective-permute-start.11) | collective-permute-done | bytes 524320 | tf_op jit(solution)/shard_map/ppermute | solution.py:114
  207.1 19.6 %collective-permute-done.10 = bf16[128,2048]{1,0:T(8,128)(2,1)S(1)} collective-permute-done((bf16[128,2048]{1,0:T(8,128)(2,1)S(1)}, bf16[128,2048]{1,0:T(8,128)(2,1)S(1)}, u32[]{:S(2)}, u32[]{:S(2)}) %collective-permute-start.10) | collective-permute-done | bytes 524320 | tf_op jit(solution)/shard_map/ppermute | solution.py:114
  228.2 5.0 collective-permute-start.15
  233.4 12.2 %collective-permute-done.15 = bf16[64,2048]{1,0:T(8,128)(2,1)S(1)} collective-permute-done((bf16[64,2048]{1,0:T(8,128)(2,1)S(1)}, bf16[64,2048]{1,0:T(8,128)(2,1)S(1)}, u32[]{:S(2)}, u32[]{:S(2)}) %collective-permute-start.15) | collective-permute-done | bytes 262176 | tf_op jit(solution)/shard_map/ppermute | solution.py:101
  245.6 3.8 collective-permute-done.16
  251.2 13.3 %collective-permute-start.12 = (bf16[64,2048]{1,0:T(8,128)(2,1)S(1)}, bf16[64,2048]{1,0:T(8,128)(2,1)S(1)}, u32[]{:S(2)}, u32[]{:S(2)}) collective-permute-start(bf16[64,2048]{1,0:T(8,128)(2,1)S(1)} %get-tuple-element.185), channel_id=1, source_target_pairs={{0,1},{1,2},{2,3},{3,0},{4,5},{5,6},{6,7},{7,4},{8,9},{9,10},{10,1... | collective-permute-start | bytes 786440 | tf_op jit(solution)/shard_map/ppermute | solution.py:101
  268.4 5.7 collective-permute-done.13
  274.2 42.4 %all-gather.9.cloned.1.call-done.mid_ref.refs_0_ = bf16[2048,2048]{1,0:T(8,128)(2,1)} async-done(((bf16[256,2048]{1,0:T(8,128)(2,1)}), bf16[2048,2048]{1,0:T(8,128)(2,1)}) %all-gather.9.cloned.1.call-update) | async-done | bytes 8388624 | tf_op jit(solution)/shard_map/all_gather | solution.py:602
  317.7 3.6 all-to-all-start
  321.5 22.5 %all-to-all-done = bf16[3,8,88,256]{3,2,0,1:T(8,128)(2,1)S(1)} async-done(((bf16[3,8,88,256]{3,2,0,1:T(8,128)(2,1)}), bf16[3,8,88,256]{3,2,0,1:T(8,128)(2,1)S(1)}, u32[]{:S(2)}, u32[]{:S(2)}) %all-to-all-start) | async-done | bytes 1081376 | tf_op jit(solution)/shard_map/all_to_all | solution.py:545
  345.8 4.3 maximum_maximum_fusion.wd_ref
  351.1 4.0 fusion.5.w1_ref
  355.1 54.8 %experts_back.2 = (bf16[2048,2176]{1,0:T(8,128)(2,1)}, bf16[2,2048,1792]{2,1,0:T(8,128)(2,1)}, bf16[2,2048,896]{2,1,0:T(8,128)(2,1)}) custom-call(s32[1]{0:T(128)} %bitcast.8.first_ref, bf16[2048,2048]{1,0:T(8,128)(2,1)} %all-gather.9.cloned.1.call-done.mid_ref.refs_0_, bf16[32,2,64,2176]{3,2,1,0:T(8,128)(2,1)} %bitcast.153, ...), custom_call_target="tpu_custom_call" | custom-call | flops 37580963840 | bytes 36175872 | tf_op jit(solution)/shard_map/experts_back/pallas_call | solution.py:239
  410.4 55.4 %experts_back.3 = (bf16[2048,2176]{1,0:T(8,128)(2,1)}, bf16[2,2048,1792]{2,1,0:T(8,128)(2,1)}, bf16[2,2048,896]{2,1,0:T(8,128)(2,1)}) custom-call(s32[1]{0:T(128)} %bitcast.8.first_ref, bf16[2048,2048]{1,0:T(8,128)(2,1)} %all-gather.11.cloned.1.call-done.mid_ref.refs_1_, ...), custom_call_target="tpu_custom_call", output_to_operand_aliasing={{1}: (6, {}), {2}: (7, {})} | custom-call | flops 37580963840 | bytes 36175872 | tf_op jit(solution)/shard_map/experts_back/pallas_call | solution.py:239
  465.8 17.8 %reduce-scatter.5.cloned.1.call-done = bf16[256,2176]{1,0:T(8,128)(2,1)} async-done(((bf16[2048,2176]{1,0:T(8,128)(2,1)}), bf16[256,2176]{1,0:T(8,128)(2,1)}) %reduce-scatter.5.cloned.1.call-update) | async-done | bytes 1114128 | tf_op jit(solution)/shard_map/reduce_scatter | solution.py:607
  483.8 22.5 %down_sum.1 = (f32[704,2048]{1,0:T(8,128)}, f32[88,2048]{1,0:T(8,128)S(1)}) custom-call(bf16[2,2048,896]{2,1,0:T(8,128)(2,1)} %get-tuple-element.44.h_ref.act_ref, bf16[32,2,64,2176]{3,2,1,0:T(8,128)(2,1)} %bitcast.157), custom_call_target="tpu_custom_call" | custom-call | flops 15032385536 | bytes 29884416 | tf_op jit(solution)/shard_map/down_sum/pallas_call | solution.py:326
  507.1 41.2 %pair_sum.1 = (f32[704,2048]{1,0:T(8,128)}, f32[704,2048]{1,0:T(8,128)}, f32[2,88,2048]{2,1,0:T(8,128)}) custom-call(bf16[2,2048,1792]{2,1,0:T(8,128)(2,1)} %get-tuple-element.46.h_ref, bf16[2048,2048]{1,0:T(8,128)(2,1)} %all-gather.9.cloned.1.call-done.mid_ref.refs_0_, bf16[2048,2048]{1,0:T(8,128)(2,1)} %all-gather.11.cloned.1.call-done.mid_ref.refs_1_), custom_call_target="tpu_custom_call" | custom-call | flops 30064771072 | bytes 42991616 | tf_op jit(solution)/shard_map/pair_sum/pallas_call | solution.py:392
  548.3 2.6 copy-done.9
  550.9 2.7 copy-done.10
  553.7 3.2 copy-done.11
  556.9 21.2 %experts_out.1 = bf16[8,4,2,64,2048]{4,3,2,1,0:T(8,128)(2,1)} custom-call(bf16[2,2048,896]{2,1,0:T(8,128)(2,1)S(1)} %copy-done.11, bf16[896,2048]{1,0:T(8,128)(2,1)S(1)} %copy-done.4, f32[704,2048]{1,0:T(8,128)S(1)} %copy-done.9, f32[704,2048]{1,0:T(8,128)S(1)} %copy-done.10), custom_call_target="tpu_custom_call" | custom-call | flops 15032385536 | bytes 24117248 | tf_op jit(solution)/shard_map/experts_out/pallas_call | solution.py:284
  586.5 2.5 collective-permute-start.26
  589.0 2.9 collective-permute-done.21
  591.9 12.4 %collective-permute-start.25 = (bf16[64,2176]{1,0:T(8,128)(2,1)S(1)}, bf16[64,2176]{1,0:T(8,128)(2,1)S(1)}, u32[]{:S(2)}, u32[]{:S(2)}) collective-permute-start(bf16[64,2176]{1,0:T(8,128)(2,1)S(1)} %get-tuple-element.169), channel_id=1, source_target_pairs={{0,2},{1,3},{2,0},{3,1},{4,6},{5,7},{6,4},{7,5},{8,10},{9,11},{10,... | collective-permute-start | bytes 835592 | tf_op jit(solution)/shard_map/ppermute | solution.py:114
  604.3 11.5 %collective-permute-done.22 = bf16[64,2176]{1,0:T(8,128)(2,1)S(1)} collective-permute-done((bf16[64,2176]{1,0:T(8,128)(2,1)S(1)}, bf16[64,2176]{1,0:T(8,128)(2,1)S(1)}, u32[]{:S(2)}, u32[]{:S(2)}) %collective-permute-start.22) | collective-permute-done | bytes 278560 | tf_op jit(solution)/shard_map/ppermute | solution.py:114
  616.0 16.5 %collective-permute-done.25 = bf16[64,2176]{1,0:T(8,128)(2,1)S(1)} collective-permute-done((bf16[64,2176]{1,0:T(8,128)(2,1)S(1)}, bf16[64,2176]{1,0:T(8,128)(2,1)S(1)}, u32[]{:S(2)}, u32[]{:S(2)}) %collective-permute-start.25) | collective-permute-done | bytes 278560 | tf_op jit(solution)/shard_map/ppermute | solution.py:114
  641.2 2.8 fusion.80
  645.3 8.1 collective-permute-done.27
  654.5 20.4 %collective-permute-done.28 = bf16[128,2048]{1,0:T(8,128)(2,1)} collective-permute-done((bf16[128,2048]{1,0:T(8,128)(2,1)}, bf16[128,2048]{1,0:T(8,128)(2,1)}, u32[]{:S(2)}, u32[]{:S(2)}) %collective-permute-start.28) | collective-permute-done | bytes 524320 | tf_op jit(solution)/shard_map/ppermute | solution.py:101
  676.1 2.9 fusion.23
  679.0 5.8 convolution_bitcast_fusion
  684.8 3.2 multiply_reduce_fusion
  709.0 2.7 reshape.305
  719.0 2.5 concatenate.87.qr_ref
  721.6 7.7 fusion.11
  732.7 5.0 concatenate.88.extra_ref
  743.9 9.1 %packed_grads.1 = bf16[2048,2176]{1,0:T(8,128)(2,1)} custom-call(bf16[512,2048]{1,0:T(8,128)(2,1)S(1)} %copy-done.1, bf16[512,2048]{1,0:T(8,128)(2,1)S(1)} %constant_dynamic-update-slice_fusion.heads_grad_ref, bf16[512,512]{1,0:T(8,128)(2,1)S(1)} %copy-done.6, bf16[512,1408]{1,0:T(8,128)(2,1)S(1)} %concatenate.87.qr_ref, bf16[512,512]{1,0:T(8,128)(2,1)S(1)} %copy-done.5, ...), custom_call_target="tpu_custom_call" | custom-call | flops 4563402752 | bytes 16777216 | tf_op jit(solution)/shard_map/packed_grads/pallas_call | solution.py:441
  755.8 3.7 all-to-all-start.1
  760.6 9.4 %collective-permute-start.30 = (bf16[128,2048]{1,0:T(8,128)(2,1)S(1)}, bf16[128,2048]{1,0:T(8,128)(2,1)S(1)}, u32[]{:S(2)}, u32[]{:S(2)}) collective-permute-start(bf16[128,2048]{1,0:T(8,128)(2,1)S(1)} %get-tuple-element.150), channel_id=1, source_target_pairs={{0,1},{1,2},{2,3},{3,0},{4,5},{5,6},{6,7},{7,4},{8,9},{9,10},{10,1... | collective-permute-start | bytes 1572872 | tf_op jit(solution)/shard_map/ppermute | solution.py:114
  776.6 6.5 collective-permute-done.30
  785.7 8.5 collective-permute-done.32
  794.1 33.9 %collective-permute-done.31 = bf16[128,2048]{1,0:T(8,128)(2,1)S(1)} collective-permute-done((bf16[128,2048]{1,0:T(8,128)(2,1)}, bf16[128,2048]{1,0:T(8,128)(2,1)S(1)}, u32[]{:S(2)}, u32[]{:S(2)}) %collective-permute-start.31) | collective-permute-done | bytes 524320 | tf_op jit(solution)/shard_map/ppermute | solution.py:114
  828.6 33.0 %collective-permute-done.19 = bf16[128,2048]{1,0:T(8,128)(2,1)} collective-permute-done((bf16[128,2048]{1,0:T(8,128)(2,1)}, bf16[128,2048]{1,0:T(8,128)(2,1)}, u32[]{:S(2)}, u32[]{:S(2)}) %collective-permute-start.19) | collective-permute-done | bytes 524320 | tf_op jit(solution)/shard_map/ppermute | solution.py:114
  861.5 3.8 fusion.39
  867.5 3.8 collective-permute-start.35
  874.6 3.4 collective-permute-done.34
  (406 shorter events, 137.2 us)
Async XLA Ops:
  7.2 122.9 %all-gather.5.cloned.1.call-start = ((), (), s32[]{:S(2)}) async-start(), calls=%async_computation.6 | async-start | bytes 10027008 | tf_op jit(solution)/shard_map/all_gather | solution.py:518
  10.1 20.2 %collective-permute-start.2 = (bf16[64,640]{0,1:T(8,128)(2,1)S(1)}, bf16[64,640]{0,1:T(8,128)(2,1)S(1)}, u32[]{:S(2)}, u32[]{:S(2)}) collective-permute-start(bf16[64,640]{0,1:T(8,128)(2,1)S(1)} %maximum_maximum_fusion.1), channel_id=1, source_target_pairs={{0,3},{1,0},{2,1},{3,2},{4,7},{5,4},{6,5},{7,6},{8,11},{9,8},{10,9... | collective-permute-start | bytes 245768 | tf_op jit(solution)/shard_map/ppermute | solution.py:101
  15.2 13.9 %collective-permute-start.1 = (bf16[64,640]{0,1:T(8,128)(2,1)S(1)}, bf16[64,640]{0,1:T(8,128)(2,1)S(1)}, u32[]{:S(2)}, u32[]{:S(2)}) collective-permute-start(bf16[64,640]{0,1:T(8,128)(2,1)S(1)} %maximum_maximum_fusion.1), channel_id=1, source_target_pairs={{0,2},{1,3},{2,0},{3,1},{4,6},{5,7},{6,4},{7,5},{8,10},{9,11},{10,... | collective-permute-start | bytes 245768 | tf_op jit(solution)/shard_map/ppermute | solution.py:101
  15.2 11.5 %collective-permute-start = (bf16[64,640]{0,1:T(8,128)(2,1)S(1)}, bf16[64,640]{0,1:T(8,128)(2,1)S(1)}, u32[]{:S(2)}, u32[]{:S(2)}) collective-permute-start(bf16[64,640]{0,1:T(8,128)(2,1)S(1)} %maximum_maximum_fusion.1), channel_id=1, source_target_pairs={{0,1},{1,2},{2,3},{3,0},{4,5},{5,6},{6,7},{7,4},{8,9},{9,10},{10,1... | collective-permute-start | bytes 245768 | tf_op jit(solution)/shard_map/ppermute | solution.py:101
  33.9 216.3 %all-gather.7.cloned.1.call-start = ((), (), s32[]{:S(2)}) async-start(), calls=%async_computation.7 | async-start | bytes 20054016 | tf_op jit(solution)/shard_map/all_gather | solution.py:539
  34.4 17.6 %collective-permute-start.3 = (bf16[128,2176]{1,0:T(8,128)(2,1)S(1)}, bf16[128,2176]{1,0:T(8,128)(2,1)}, u32[]{:S(2)}, u32[]{:S(2)}) collective-permute-start(bf16[128,2176]{1,0:T(8,128)(2,1)S(1)} %concatenate.72), channel_id=1, source_target_pairs={{0,1},{1,2},{2,3},{3,0},{4,5},{5,6},{6,7},{7,4},{8,9},{9,10},{10,1... | collective-permute-start | bytes 1671176 | tf_op jit(solution)/shard_map/ppermute | solution.py:101
  36.6 49.6 %collective-permute-start.5 = (bf16[128,2176]{1,0:T(8,128)(2,1)S(1)}, bf16[128,2176]{1,0:T(8,128)(2,1)S(1)}, u32[]{:S(2)}, u32[]{:S(2)}) collective-permute-start(bf16[128,2176]{1,0:T(8,128)(2,1)S(1)} %concatenate.72), channel_id=1, source_target_pairs={{0,3},{1,0},{2,1},{3,2},{4,7},{5,4},{6,5},{7,6},{8,11},{9,8},{10,9... | collective-permute-start | bytes 1671176 | tf_op jit(solution)/shard_map/ppermute | solution.py:101
  38.3 47.9 %collective-permute-start.4 = (bf16[128,2176]{1,0:T(8,128)(2,1)S(1)}, bf16[128,2176]{1,0:T(8,128)(2,1)S(1)}, u32[]{:S(2)}, u32[]{:S(2)}) collective-permute-start(bf16[128,2176]{1,0:T(8,128)(2,1)S(1)} %concatenate.72), channel_id=1, source_target_pairs={{0,2},{1,3},{2,0},{3,1},{4,6},{5,7},{6,4},{7,5},{8,10},{9,11},{10,... | collective-permute-start | bytes 1671176 | tf_op jit(solution)/shard_map/ppermute | solution.py:101
  53.1 36.6 %copy-start.23 = (bf16[128,2048]{1,0:T(8,128)(2,1)S(1)}, bf16[128,2048]{1,0:T(8,128)(2,1)}, u32[]{:S(2)}) copy-start(bf16[128,2048]{1,0:T(8,128)(2,1)} %param.18) | copy-start | bytes 1572868
  87.7 228.8 %all-gather.9.cloned.1.call-start = ((), (), s32[]{:S(2)}) async-start(), calls=%async_computation.8 | async-start | bytes 9437184 | tf_op jit(solution)/shard_map/all_gather | solution.py:602
  87.8 52.5 %copy-start.97 = (f32[32]{0:T(128)}, f32[32]{0:T(128)S(1)}, u32[]{:S(2)}) copy-start(f32[32]{0:T(128)S(1)} %negate_power_fusion) | copy-start | bytes 388
  89.7 16.8 %collective-permute-start.6 = (bf16[128,2048]{1,0:T(8,128)(2,1)S(1)}, bf16[128,2048]{1,0:T(8,128)(2,1)S(1)}, u32[]{:S(2)}, u32[]{:S(2)}) collective-permute-start(bf16[128,2048]{1,0:T(8,128)(2,1)S(1)} %copy-done.23), channel_id=1, source_target_pairs={{0,1},{1,2},{2,3},{3,0},{4,5},{5,6},{6,7},{7,4},{8,9},{9,10},{10,1... | collective-permute-start | bytes 1572872 | tf_op jit(solution)/shard_map/ppermute | solution.py:101
  91.0 37.0 %collective-permute-start.7 = (bf16[128,2048]{1,0:T(8,128)(2,1)S(1)}, bf16[128,2048]{1,0:T(8,128)(2,1)S(1)}, u32[]{:S(2)}, u32[]{:S(2)}) collective-permute-start(bf16[128,2048]{1,0:T(8,128)(2,1)S(1)} %copy-done.23), channel_id=1, source_target_pairs={{0,2},{1,3},{2,0},{3,1},{4,6},{5,7},{6,4},{7,5},{8,10},{9,11},{10,... | collective-permute-start | bytes 1572872 | tf_op jit(solution)/shard_map/ppermute | solution.py:101
  94.5 45.8 %copy-start.84 = (f32[512]{0:T(512)}, f32[512]{0:T(512)S(1)}, u32[]{:S(2)}) copy-start(f32[512]{0:T(512)S(1)} %subtract_convert_fusion.2) | copy-start | bytes 6148
  94.5 33.6 %collective-permute-start.8 = (bf16[128,2048]{1,0:T(8,128)(2,1)S(1)}, bf16[128,2048]{1,0:T(8,128)(2,1)S(1)}, u32[]{:S(2)}, u32[]{:S(2)}) collective-permute-start(bf16[128,2048]{1,0:T(8,128)(2,1)S(1)} %copy-done.23), channel_id=1, source_target_pairs={{0,3},{1,0},{2,1},{3,2},{4,7},{5,4},{6,5},{7,6},{8,11},{9,8},{10,9... | collective-permute-start | bytes 1572872 | tf_op jit(solution)/shard_map/ppermute | solution.py:101
  172.3 54.3 %copy-start.24 = (bf16[128,2048]{1,0:T(8,128)(2,1)S(1)}, bf16[128,2048]{1,0:T(8,128)(2,1)}, u32[]{:S(2)}) copy-start(bf16[128,2048]{1,0:T(8,128)(2,1)} %param.18) | copy-start | bytes 1572868
  172.5 55.2 %copy-start.78 = (f32[2048]{0:T(1024)S(1)}, f32[2048]{0:T(1024)}, u32[]{:S(2)}) copy-start(f32[2048]{0:T(1024)} %param.28) | copy-start | bytes 24580
  172.5 23.3 %collective-permute-start.9 = (bf16[128,2048]{1,0:T(8,128)(2,1)S(1)}, bf16[128,2048]{1,0:T(8,128)(2,1)S(1)}, u32[]{:S(2)}, u32[]{:S(2)}) collective-permute-start(bf16[128,2048]{1,0:T(8,128)(2,1)S(1)} %get-tuple-element.156), channel_id=1, source_target_pairs={{0,1},{1,2},{2,3},{3,0},{4,5},{5,6},{6,7},{7,4},{8,9},{9,10},{10,1... | collective-permute-start | bytes 1572872 | tf_op jit(solution)/shard_map/ppermute | solution.py:114
  183.4 23.7 %collective-permute-start.11 = (bf16[128,2048]{1,0:T(8,128)(2,1)S(1)}, bf16[128,2048]{1,0:T(8,128)(2,1)S(1)}, u32[]{:S(2)}, u32[]{:S(2)}) collective-permute-start(bf16[128,2048]{1,0:T(8,128)(2,1)S(1)} %get-tuple-element.157), channel_id=1, source_target_pairs={{0,3},{1,0},{2,1},{3,2},{4,7},{5,4},{6,5},{7,6},{8,11},{9,8},{10,9... | collective-permute-start | bytes 1572872 | tf_op jit(solution)/shard_map/ppermute | solution.py:114
  183.6 43.0 %collective-permute-start.10 = (bf16[128,2048]{1,0:T(8,128)(2,1)S(1)}, bf16[128,2048]{1,0:T(8,128)(2,1)S(1)}, u32[]{:S(2)}, u32[]{:S(2)}) collective-permute-start(bf16[128,2048]{1,0:T(8,128)(2,1)S(1)} %get-tuple-element.158), channel_id=1, source_target_pairs={{0,2},{1,3},{2,0},{3,1},{4,6},{5,7},{6,4},{7,5},{8,10},{9,11},{10,... | collective-permute-start | bytes 1572872 | tf_op jit(solution)/shard_map/ppermute | solution.py:114
  228.1 21.3 %collective-permute-start.16 = (bf16[64,2048]{1,0:T(8,128)(2,1)S(1)}, bf16[64,2048]{1,0:T(8,128)(2,1)S(1)}, u32[]{:S(2)}, u32[]{:S(2)}) collective-permute-start(bf16[64,2048]{1,0:T(8,128)(2,1)S(1)} %get-tuple-element.183), channel_id=1, source_target_pairs={{0,2},{1,3},{2,0},{3,1},{4,6},{5,7},{6,4},{7,5},{8,10},{9,11},{10,... | collective-permute-start | bytes 786440 | tf_op jit(solution)/shard_map/ppermute | solution.py:101
  228.2 17.4 %collective-permute-start.15 = (bf16[64,2048]{1,0:T(8,128)(2,1)S(1)}, bf16[64,2048]{1,0:T(8,128)(2,1)S(1)}, u32[]{:S(2)}, u32[]{:S(2)}) collective-permute-start(bf16[64,2048]{1,0:T(8,128)(2,1)S(1)} %get-tuple-element.183), channel_id=1, source_target_pairs={{0,1},{1,2},{2,3},{3,0},{4,5},{5,6},{6,7},{7,4},{8,9},{9,10},{10,1... | collective-permute-start | bytes 786440 | tf_op jit(solution)/shard_map/ppermute | solution.py:101
  233.2 17.0 %collective-permute-start.17 = (bf16[64,2048]{1,0:T(8,128)(2,1)S(1)}, bf16[64,2048]{1,0:T(8,128)(2,1)S(1)}, u32[]{:S(2)}, u32[]{:S(2)}) collective-permute-start(bf16[64,2048]{1,0:T(8,128)(2,1)S(1)} %get-tuple-element.183), channel_id=1, source_target_pairs={{0,3},{1,0},{2,1},{3,2},{4,7},{5,4},{6,5},{7,6},{8,11},{9,8},{10,9... | collective-permute-start | bytes 786440 | tf_op jit(solution)/shard_map/ppermute | solution.py:101
  249.4 67.2 %copy-start.72 = (bf16[704,256]{1,0:T(8,128)(2,1)S(1)}, bf16[704,256]{1,0:T(8,128)(2,1)}, u32[]{:S(2)}) copy-start(bf16[704,256]{1,0:T(8,128)(2,1)} %param.32) | copy-start | bytes 1081348
  249.4 67.2 %copy-start.73 = (bf16[256,704]{0,1:T(8,128)(2,1)S(1)}, bf16[256,704]{0,1:T(8,128)(2,1)}, u32[]{:S(2)}) copy-start(bf16[256,704]{0,1:T(8,128)(2,1)} %param.31) | copy-start | bytes 1081348
  249.5 67.2 %copy-start.74 = (bf16[256,704]{0,1:T(8,128)(2,1)S(1)}, bf16[256,704]{0,1:T(8,128)(2,1)}, u32[]{:S(2)}) copy-start(bf16[256,704]{0,1:T(8,128)(2,1)} %param.30) | copy-start | bytes 1081348
  251.2 158.8 %all-gather.11.cloned.1.call-start = ((), (), s32[]{:S(2)}) async-start(), calls=%async_computation.9 | async-start | bytes 9437184 | tf_op jit(solution)/shard_map/all_gather | solution.py:602
  251.2 17.2 %collective-permute-start.12 = (bf16[64,2048]{1,0:T(8,128)(2,1)S(1)}, bf16[64,2048]{1,0:T(8,128)(2,1)S(1)}, u32[]{:S(2)}, u32[]{:S(2)}) collective-permute-start(bf16[64,2048]{1,0:T(8,128)(2,1)S(1)} %get-tuple-element.185), channel_id=1, source_target_pairs={{0,1},{1,2},{2,3},{3,0},{4,5},{5,6},{6,7},{7,4},{8,9},{9,10},{10,1... | collective-permute-start | bytes 786440 | tf_op jit(solution)/shard_map/ppermute | solution.py:101
  264.5 9.6 %collective-permute-start.13 = (bf16[64,2048]{1,0:T(8,128)(2,1)S(1)}, bf16[64,2048]{1,0:T(8,128)(2,1)S(1)}, u32[]{:S(2)}, u32[]{:S(2)}) collective-permute-start(bf16[64,2048]{1,0:T(8,128)(2,1)S(1)} %get-tuple-element.185), channel_id=1, source_target_pairs={{0,2},{1,3},{2,0},{3,1},{4,6},{5,7},{6,4},{7,5},{8,10},{9,11},{10,... | collective-permute-start | bytes 786440 | tf_op jit(solution)/shard_map/ppermute | solution.py:101
  264.5 9.6 %collective-permute-start.14 = (bf16[64,2048]{1,0:T(8,128)(2,1)S(1)}, bf16[64,2048]{1,0:T(8,128)(2,1)S(1)}, u32[]{:S(2)}, u32[]{:S(2)}) collective-permute-start(bf16[64,2048]{1,0:T(8,128)(2,1)S(1)} %get-tuple-element.185), channel_id=1, source_target_pairs={{0,3},{1,0},{2,1},{3,2},{4,7},{5,4},{6,5},{7,6},{8,11},{9,8},{10,9... | collective-permute-start | bytes 786440 | tf_op jit(solution)/shard_map/ppermute | solution.py:101
  274.2 42.4 %copy-start.40 = (bf16[256,2048]{1,0:T(8,128)(2,1)}, bf16[256,2048]{1,0:T(8,128)(2,1)S(1)}, u32[]{:S(2)}) copy-start(bf16[256,2048]{1,0:T(8,128)(2,1)S(1)} %constant_dynamic-update-slice_fusion.8) | copy-start | bytes 3145732
  317.7 26.3 %all-to-all-start = ((bf16[3,8,88,256]{3,2,0,1:T(8,128)(2,1)}), bf16[3,8,88,256]{3,2,0,1:T(8,128)(2,1)S(1)}, u32[]{:S(2)}, u32[]{:S(2)}) async-start(bf16[3,8,88,256]{3,2,0,1:T(8,128)(2,1)} %pad_maximum_fusion.3), calls=%async_computation | async-start | bytes 2162688 | tf_op jit(solution)/shard_map/all_to_all | solution.py:545
  321.3 162.2 %reduce-scatter.5.cloned.1.call-start = ((), (), s32[]{:S(2)}) async-start(), calls=%async_computation.10 | async-start | bytes 10027008 | tf_op jit(solution)/shard_map/reduce_scatter | solution.py:607
  410.0 168.1 %reduce-scatter.7.cloned.1.call-start = ((), (), s32[]{:S(2)}) async-start(), calls=%async_computation.11 | async-start | bytes 10027008 | tf_op jit(solution)/shard_map/reduce_scatter | solution.py:607
  483.6 269.4 %reduce-scatter.9.cloned.1.call-start = ((), (), s32[]{:S(2)}) async-start(), calls=%async_computation.12 | async-start | bytes 18874368 | tf_op jit(solution)/shard_map/reduce_scatter | solution.py:640
  507.1 41.2 %copy-start.4 = (bf16[896,2048]{1,0:T(8,128)(2,1)S(1)}, bf16[896,2048]{1,0:T(8,128)(2,1)}, u32[]{:S(2)}) copy-start(bf16[896,2048]{1,0:T(8,128)(2,1)} %maximum_maximum_fusion.wd_ref) | copy-start | bytes 11010052
  578.1 287.3 %reduce-scatter.11.cloned.1.call-start = ((), (), s32[]{:S(2)}) async-start(), calls=%async_computation.13 | async-start | bytes 10027008 | tf_op jit(solution)/shard_map/reduce_scatter | solution.py:702
  580.4 11.4 %collective-permute-start.21 = (bf16[64,2176]{1,0:T(8,128)(2,1)S(1)}, bf16[64,2176]{1,0:T(8,128)(2,1)S(1)}, u32[]{:S(2)}, u32[]{:S(2)}) collective-permute-start(bf16[64,2176]{1,0:T(8,128)(2,1)S(1)} %get-tuple-element.164), channel_id=1, source_target_pairs={{0,1},{1,2},{2,3},{3,0},{4,5},{5,6},{6,7},{7,4},{8,9},{9,10},{10,1... | collective-permute-start | bytes 835592 | tf_op jit(solution)/shard_map/ppermute | solution.py:114
  581.9 22.4 %collective-permute-start.23 = (bf16[64,2176]{1,0:T(8,128)(2,1)S(1)}, bf16[64,2176]{1,0:T(8,128)(2,1)S(1)}, u32[]{:S(2)}, u32[]{:S(2)}) collective-permute-start(bf16[64,2176]{1,0:T(8,128)(2,1)S(1)} %get-tuple-element.165), channel_id=1, source_target_pairs={{0,3},{1,0},{2,1},{3,2},{4,7},{5,4},{6,5},{7,6},{8,11},{9,8},{10,9... | collective-permute-start | bytes 835592 | tf_op jit(solution)/shard_map/ppermute | solution.py:114
  584.3 31.5 %collective-permute-start.22 = (bf16[64,2176]{1,0:T(8,128)(2,1)S(1)}, bf16[64,2176]{1,0:T(8,128)(2,1)S(1)}, u32[]{:S(2)}, u32[]{:S(2)}) collective-permute-start(bf16[64,2176]{1,0:T(8,128)(2,1)S(1)} %get-tuple-element.166), channel_id=1, source_target_pairs={{0,2},{1,3},{2,0},{3,1},{4,6},{5,7},{6,4},{7,5},{8,10},{9,11},{10,... | collective-permute-start | bytes 835592 | tf_op jit(solution)/shard_map/ppermute | solution.py:114
  584.9 31.1 %collective-permute-start.24 = (bf16[64,2176]{1,0:T(8,128)(2,1)S(1)}, bf16[64,2176]{1,0:T(8,128)(2,1)S(1)}, u32[]{:S(2)}, u32[]{:S(2)}) collective-permute-start(bf16[64,2176]{1,0:T(8,128)(2,1)S(1)} %get-tuple-element.167), channel_id=1, source_target_pairs={{0,1},{1,2},{2,3},{3,0},{4,5},{5,6},{6,7},{7,4},{8,9},{9,10},{10,1... | collective-permute-start | bytes 835592 | tf_op jit(solution)/shard_map/ppermute | solution.py:114
  586.5 29.5 %collective-permute-start.26 = (bf16[64,2176]{1,0:T(8,128)(2,1)S(1)}, bf16[64,2176]{1,0:T(8,128)(2,1)S(1)}, u32[]{:S(2)}, u32[]{:S(2)}) collective-permute-start(bf16[64,2176]{1,0:T(8,128)(2,1)S(1)} %get-tuple-element.168), channel_id=1, source_target_pairs={{0,3},{1,0},{2,1},{3,2},{4,7},{5,4},{6,5},{7,6},{8,11},{9,8},{10,9... | collective-permute-start | bytes 835592 | tf_op jit(solution)/shard_map/ppermute | solution.py:114
  591.9 40.6 %collective-permute-start.25 = (bf16[64,2176]{1,0:T(8,128)(2,1)S(1)}, bf16[64,2176]{1,0:T(8,128)(2,1)S(1)}, u32[]{:S(2)}, u32[]{:S(2)}) collective-permute-start(bf16[64,2176]{1,0:T(8,128)(2,1)S(1)} %get-tuple-element.169), channel_id=1, source_target_pairs={{0,2},{1,3},{2,0},{3,1},{4,6},{5,7},{6,4},{7,5},{8,10},{9,11},{10,... | collective-permute-start | bytes 835592 | tf_op jit(solution)/shard_map/ppermute | solution.py:114
  636.3 17.0 %collective-permute-start.27 = (bf16[128,2048]{1,0:T(8,128)(2,1)}, bf16[128,2048]{1,0:T(8,128)(2,1)}, u32[]{:S(2)}, u32[]{:S(2)}) collective-permute-start(bf16[128,2048]{1,0:T(8,128)(2,1)} %get-tuple-element.145), channel_id=1, source_target_pairs={{0,1},{1,2},{2,3},{3,0},{4,5},{5,6},{6,7},{7,4},{8,9},{9,10},{10,1... | collective-permute-start | bytes 1572872 | tf_op jit(solution)/shard_map/ppermute | solution.py:101
  636.4 38.6 %collective-permute-start.28 = (bf16[128,2048]{1,0:T(8,128)(2,1)}, bf16[128,2048]{1,0:T(8,128)(2,1)}, u32[]{:S(2)}, u32[]{:S(2)}) collective-permute-start(bf16[128,2048]{1,0:T(8,128)(2,1)} %get-tuple-element.145), channel_id=1, source_target_pairs={{0,2},{1,3},{2,0},{3,1},{4,6},{5,7},{6,4},{7,5},{8,10},{9,11},{10,... | collective-permute-start | bytes 1572872 | tf_op jit(solution)/shard_map/ppermute | solution.py:101
  639.4 36.6 %collective-permute-start.29 = (bf16[128,2048]{1,0:T(8,128)(2,1)}, bf16[128,2048]{1,0:T(8,128)(2,1)S(1)}, u32[]{:S(2)}, u32[]{:S(2)}) collective-permute-start(bf16[128,2048]{1,0:T(8,128)(2,1)} %get-tuple-element.145), channel_id=1, source_target_pairs={{0,3},{1,0},{2,1},{3,2},{4,7},{5,4},{6,5},{7,6},{8,11},{9,8},{10,9... | collective-permute-start | bytes 1572872 | tf_op jit(solution)/shard_map/ppermute | solution.py:101
  755.8 28.4 %all-to-all-start.1 = ((bf16[3,8,88,256]{3,2,0,1:T(8,128)(2,1)}), bf16[3,8,88,256]{3,2,0,1:T(8,128)(2,1)S(1)}, u32[]{:S(2)}, u32[]{:S(2)}) async-start(bf16[3,8,88,256]{3,2,0,1:T(8,128)(2,1)} %maximum_bitcast_fusion), calls=%async_computation.5 | async-start | bytes 2162688 | tf_op jit(solution)/shard_map/all_to_all | solution.py:646
  760.6 22.5 %collective-permute-start.30 = (bf16[128,2048]{1,0:T(8,128)(2,1)S(1)}, bf16[128,2048]{1,0:T(8,128)(2,1)S(1)}, u32[]{:S(2)}, u32[]{:S(2)}) collective-permute-start(bf16[128,2048]{1,0:T(8,128)(2,1)S(1)} %get-tuple-element.150), channel_id=1, source_target_pairs={{0,1},{1,2},{2,3},{3,0},{4,5},{5,6},{6,7},{7,4},{8,9},{9,10},{10,1... | collective-permute-start | bytes 1572872 | tf_op jit(solution)/shard_map/ppermute | solution.py:114
  770.1 24.1 %collective-permute-start.32 = (bf16[128,2048]{1,0:T(8,128)(2,1)}, bf16[128,2048]{1,0:T(8,128)(2,1)S(1)}, u32[]{:S(2)}, u32[]{:S(2)}) collective-permute-start(bf16[128,2048]{1,0:T(8,128)(2,1)} %get-tuple-element.151), channel_id=1, source_target_pairs={{0,3},{1,0},{2,1},{3,2},{4,7},{5,4},{6,5},{7,6},{8,11},{9,8},{10,9... | collective-permute-start | bytes 1572872 | tf_op jit(solution)/shard_map/ppermute | solution.py:114
  770.4 57.6 %collective-permute-start.31 = (bf16[128,2048]{1,0:T(8,128)(2,1)}, bf16[128,2048]{1,0:T(8,128)(2,1)S(1)}, u32[]{:S(2)}, u32[]{:S(2)}) collective-permute-start(bf16[128,2048]{1,0:T(8,128)(2,1)} %get-tuple-element.152), channel_id=1, source_target_pairs={{0,2},{1,3},{2,0},{3,1},{4,6},{5,7},{6,4},{7,5},{8,10},{9,11},{10,... | collective-permute-start | bytes 1572872 | tf_op jit(solution)/shard_map/ppermute | solution.py:114
  772.8 55.3 %copy-start.25 = (bf16[128,2048]{1,0:T(8,128)(2,1)S(1)}, bf16[128,2048]{1,0:T(8,128)(2,1)}, u32[]{:S(2)}) copy-start(bf16[128,2048]{1,0:T(8,128)(2,1)} %param.18) | copy-start | bytes 1572868
  772.8 55.3 %copy-start.77 = (f32[2048]{0:T(1024)S(1)}, f32[2048]{0:T(1024)}, u32[]{:S(2)}) copy-start(f32[2048]{0:T(1024)} %param.22) | copy-start | bytes 24580
  772.8 55.8 %collective-permute-start.18 = (bf16[128,2048]{1,0:T(8,128)(2,1)}, bf16[128,2048]{1,0:T(8,128)(2,1)}, u32[]{:S(2)}, u32[]{:S(2)}) collective-permute-start(bf16[128,2048]{1,0:T(8,128)(2,1)} %get-tuple-element.153), channel_id=1, source_target_pairs={{0,1},{1,2},{2,3},{3,0},{4,5},{5,6},{6,7},{7,4},{8,9},{9,10},{10,1... | collective-permute-start | bytes 1572872 | tf_op jit(solution)/shard_map/ppermute | solution.py:114
  774.1 54.4 %collective-permute-start.20 = (bf16[128,2048]{1,0:T(8,128)(2,1)}, bf16[128,2048]{1,0:T(8,128)(2,1)}, u32[]{:S(2)}, u32[]{:S(2)}) collective-permute-start(bf16[128,2048]{1,0:T(8,128)(2,1)} %get-tuple-element.154), channel_id=1, source_target_pairs={{0,3},{1,0},{2,1},{3,2},{4,7},{5,4},{6,5},{7,6},{8,11},{9,8},{10,9... | collective-permute-start | bytes 1572872 | tf_op jit(solution)/shard_map/ppermute | solution.py:114
  783.1 78.4 %collective-permute-start.19 = (bf16[128,2048]{1,0:T(8,128)(2,1)}, bf16[128,2048]{1,0:T(8,128)(2,1)}, u32[]{:S(2)}, u32[]{:S(2)}) collective-permute-start(bf16[128,2048]{1,0:T(8,128)(2,1)} %get-tuple-element.155), channel_id=1, source_target_pairs={{0,2},{1,3},{2,0},{3,1},{4,6},{5,7},{6,4},{7,5},{8,10},{9,11},{10,... | collective-permute-start | bytes 1572872 | tf_op jit(solution)/shard_map/ppermute | solution.py:114
  784.3 43.8 %copy-start.43 = (bf16[512,2048]{1,0:T(8,128)(2,1)S(1)}, bf16[512,2048]{1,0:T(8,128)(2,1)}, u32[]{:S(2)}) copy-start(bf16[512,2048]{1,0:T(8,128)(2,1)} %get-tuple-element.149) | copy-start | bytes 6291460
  785.7 75.9 %copy-start.20 = (f32[128,2048]{1,0:T(8,128)S(1)}, f32[128,2048]{1,0:T(8,128)}, u32[]{:S(2)}) copy-start(f32[128,2048]{1,0:T(8,128)} %copy-done.18) | copy-start | bytes 3145732
  785.7 75.9 %copy-start.30 = (bf16[128,2048]{1,0:T(8,128)(2,1)S(1)}, bf16[128,2048]{1,0:T(8,128)(2,1)}, u32[]{:S(2)}) copy-start(bf16[128,2048]{1,0:T(8,128)(2,1)} %param.19) | copy-start | bytes 1572868
  785.7 75.9 %copy-start.36 = (f32[128,2048]{1,0:T(8,128)S(1)}, f32[128,2048]{1,0:T(8,128)}, u32[]{:S(2)}) copy-start(f32[128,2048]{1,0:T(8,128)} %copy-done.35) | copy-start | bytes 3145732
  785.7 75.9 %copy-start.94 = (f32[128]{0:T(128)S(1)}, f32[128]{0:T(128)}, u32[]{:S(2)}) copy-start(f32[128]{0:T(128)} %copy-done.92) | copy-start | bytes 1540
  785.7 75.9 %copy-start.96 = (f32[128]{0:T(128)S(1)}, f32[128]{0:T(128)}, u32[]{:S(2)}) copy-start(f32[128]{0:T(128)} %copy-done.95) | copy-start | bytes 1540
  867.5 7.2 collective-permute-start.33
  867.5 7.1 collective-permute-start.35
  871.3 6.6 collective-permute-start.34
  (81 other events, 426.1 us)
Sparse Core Ops, SparseCore 0:
  34.0 61.0 all-gather.4
  97.6 94.2 all-gather.6
  251.3 65.2 all-gather.8
  318.9 60.5 all-gather.10
  410.1 73.4 reduce-scatter.4
  487.0 73.7 reduce-scatter.6
  578.2 115.9 reduce-scatter.8
  753.1 80.0 reduce-scatter.10

commit v2 on v1

--- a/solution.py
+++ b/solution.py
@@ -344,8 +344,8 @@
     )(act, dout)
 
 
-def pair_kernel(plan, h_ref, *refs):
-    mid_refs, (gate_ref, up_ref, shared_ref) = (refs[:-3], refs[-3:])
+def pair_kernel(plan, chunks, h_ref, *refs):
+    mid_refs, (gate_ref, up_ref, shared_ref) = (refs[:chunks], refs[-3:])
     chunk = pl.program_id(0)
 
     @pl.when((chunk == 0) & (pl.program_id(1) == 0))
@@ -376,7 +376,7 @@
         pl.when(chunk == h)(functools.partial(add, z_ref))
 
 
-def pair_sum(plan, gud, mids):
+def pair_sum(plan, gud, mids, *others):
     chunks, tokens, cols = gud.shape
     model = mids[0].shape[1]
     tile = min(512, tokens) if chunks <= 2 else 128
@@ -390,10 +390,11 @@
         return pl.BlockSpec((tile, model), place)
 
     return pl.pallas_call(
-        functools.partial(pair_kernel, plan),
+        functools.partial(pair_kernel, plan, chunks),
         grid=(chunks, steps),
         in_specs=[pl.BlockSpec((None, tile, cols), lambda c, i: (c, i, 0))]
-        + [part(h) for h in range(chunks)],
+        + [part(h) for h in range(chunks)]
+        + [pl.BlockSpec(memory_space=pl.ANY) for _ in others],
         out_specs=[
             pl.BlockSpec(s, lambda c, i, n=len(s): (0,) * n, pipeline_mode=pl.Buffered(1))
             for s in shapes
@@ -408,14 +409,14 @@
             transcendentals=0,
         ),
         name="pair_sum",
-    )(gud, *mids)
+    )(gud, *mids, *others)
 
 
 def pack_kernel(lead, x_ref, heads_grad_ref, latent_ref, qr_ref, heads_ref, kv_ref, extra_ref, out_ref):
     bf16 = jnp.bfloat16
     first = dot_tn(x_ref[...], qr_ref[...])
     out_ref[:, : lead - 128] = first[:, : lead - 128].astype(bf16)
-    out_ref[:, lead - 128 : lead] = (first[:, lead - 128 :] + extra_ref[...]).astype(bf16)
+    out_ref[:, lead - 128 : lead] = (first[:, lead - 128 :] + extra_ref[...].T).astype(bf16)
     latent = dot32(latent_ref[...], kv_ref[...])
     rows = latent.shape[0]
     pieces = out_ref.shape[0] // rows
@@ -448,7 +449,7 @@
             whole(qr),
             whole(heads_low),
             whole(kv_grad),
-            pl.BlockSpec((depth, 128), lambda i: (i, 0)),
+            pl.BlockSpec((128, depth), lambda i: (0, i)),
         ],
         out_specs=pl.BlockSpec((depth, cols), lambda i: (i, 0)),
         out_shape=jax.ShapeDtypeStruct((model, cols), jnp.bfloat16),
@@ -460,6 +461,244 @@
         ),
         name="packed_grads",
     )(x_low, attn_low, latent_t, qr, heads_low, kv_grad, extra)
+
+
+class Heads:
+    def __init__(self, width, groups, depth, small_c, wide, heads_c):
+        self.width, self.groups, self.depth = (width, groups, depth)
+        self.half = ROPE // 2
+        self.flat = width * NOPE
+        self.query = self.flat + 256
+        self.lead = self.query + small_c
+        self.wide = wide
+        self.output = self.lead + wide
+        self.cols = self.output + heads_c
+        self.scale = (NOPE + ROPE) ** (-0.5)
+        assert width * self.half <= 128 and small_c == LAT + 128
+
+    def order(self):
+        at = jnp.arange(self.query)[None, :]
+        rotary = at - self.flat
+        head, within = (rotary % 128 // self.half, rotary % 128 % self.half)
+        turned = head * (NOPE + ROPE) + NOPE + rotary // 128 * self.half + within
+        plain = at // NOPE * (NOPE + ROPE) + at % NOPE
+        source = jnp.where(at < self.flat, plain, jnp.where(head < self.width, turned, -1))
+        return (jnp.arange(self.width * (NOPE + ROPE))[:, None] == source).astype(jnp.bfloat16)
+
+
+def expand_rows(heads, w_ref, expand_ref):
+    rows = LAT // heads.groups
+    for f in range(heads.groups):
+        for k in range(heads.depth // rows):
+            at = f * heads.depth + k * rows
+            expand_ref[f * rows : (f + 1) * rows, k * heads.wide : (k + 1) * heads.wide] = w_ref[
+                at : at + rows, heads.lead : heads.output
+            ]
+
+
+def head_parts(heads, h, lanes, q_ref, kv_ref, kr_ref):
+    mine = (lanes % 128 >= h * heads.half) & (lanes % 128 < (h + 1) * heads.half)
+    rotary = q_ref[:, heads.flat : heads.query]
+    rotary = jnp.where(mine, rotary, jnp.zeros_like(rotary))
+    query = jnp.concatenate([q_ref[:, h * NOPE : (h + 1) * NOPE], rotary], axis=1)
+    at = h * (NOPE + VD)
+    key = jnp.concatenate([kv_ref[:, at : at + NOPE], kr_ref[...]], axis=1)
+    return (mine, query, key, kv_ref[:, at + NOPE : at + NOPE + VD])
+
+
+def allowed(seg_col_ref, seg_row_ref):
+    count = seg_col_ref.shape[0]
+    rows = lax.broadcasted_iota(jnp.int32, (count, count), 0)
+    cols = lax.broadcasted_iota(jnp.int32, (count, count), 1)
+    return (seg_col_ref[...] == seg_row_ref[...]) & (cols <= rows)
+
+
+def attend_kernel(heads, extra, x_ref, w_ref, cos_ref, sin_ref, seg_col_ref, seg_row_ref, gain_ref, *refs):
+    q_ref, kv_ref, kr_ref, lat_ref, low_ref, lse_ref, heads_ref, attn_ref, expand_ref = refs[extra:]
+    f32, bf16 = (jnp.float32, jnp.bfloat16)
+    count = x_ref.shape[0]
+    x = x_ref[...]
+    cosine, sine = (cos_ref[...], sin_ref[...])
+    query = dot32(x, w_ref[:, : heads.query])
+    first = query[:, heads.flat : heads.flat + 128]
+    second = query[:, heads.flat + 128 :]
+    q_ref[:, : heads.flat] = query[:, : heads.flat].astype(bf16)
+    q_ref[:, heads.flat : heads.flat + 128] = (first * cosine - second * sine).astype(bf16)
+    q_ref[:, heads.flat + 128 :] = (second * cosine + first * sine).astype(bf16)
+    latent = dot32(x, w_ref[:, heads.query : heads.lead])
+    ends = latent[:, LAT:]
+    latent = latent[:, :LAT]
+    lat_ref[...] = latent
+    factor = lax.rsqrt(jnp.mean(latent * latent, axis=-1, keepdims=True) + EPS)
+    low_ref[...] = (latent * factor * gain_ref[...]).astype(bf16)
+    lanes = lax.broadcasted_iota(jnp.int32, (count, 128), 1)
+    half = heads.half
+
+    def repeated(value):
+        value = value + pltpu.roll(value, half, 1)
+        return value + pltpu.roll(value, 2 * half, 1)
+
+    first = repeated(jnp.where(lanes < half, ends, 0.0))
+    second = repeated(jnp.where((lanes >= half) & (lanes < 2 * half), ends, 0.0))
+    kr_ref[:, :128] = (first * cosine - second * sine).astype(bf16)
+    kr_ref[:, 128:] = (second * cosine + first * sine).astype(bf16)
+    expand_rows(heads, w_ref, expand_ref)
+    kv_ref[...] = dot32(low_ref[...], expand_ref[...]).astype(bf16)
+    keep = allowed(seg_col_ref, seg_row_ref)
+    wide_lanes = lax.broadcasted_iota(jnp.int32, (count, 256), 1)
+    lse = jnp.zeros((count, 128), f32)
+    for h in range(heads.width):
+        _, query, key, value = head_parts(heads, h, wide_lanes, q_ref, kv_ref, kr_ref)
+        scores = jnp.where(keep, dot_nt(query, key) * heads.scale, NEG_FILL)
+        peak = jnp.max(scores, axis=-1, keepdims=True)
+        expo = jnp.exp(scores - peak)
+        total = jnp.sum(expo, axis=-1, keepdims=True)
+        lse = jnp.where(lanes == h, peak + jnp.log(total), lse)
+        probs = (expo * (1.0 / total)).astype(bf16)
+        heads_ref[:, h * VD : (h + 1) * VD] = dot32(probs, value).astype(bf16)
+    lse_ref[...] = lse
+    out = heads_ref[...]
+    step = 512
+    for at in range(0, attn_ref.shape[1], step):
+        attn_ref[:, at : at + step] = dot_nt(out, w_ref[at : at + step, heads.output :]).astype(bf16)
+
+
+def attend(heads, x_low, packed, cosine, sine, seg_col, seg_row, gain, *others):
+    count, model = x_low.shape
+    kv_c, heads_c = (heads.width * (NOPE + VD), heads.width * VD)
+    f32, bf16 = (jnp.float32, jnp.bfloat16)
+    shapes = [
+        ((count, heads.query), bf16),
+        ((count, kv_c), bf16),
+        ((count, 256), bf16),
+        ((count, LAT), f32),
+        ((count, LAT), bf16),
+        ((count, 128), f32),
+        ((count, heads_c), bf16),
+        ((count, model), bf16),
+    ]
+    vmem = pl.BlockSpec(memory_space=pltpu.VMEM)
+    return pl.pallas_call(
+        functools.partial(attend_kernel, heads, len(others)),
+        in_specs=[vmem] * 7 + [pl.BlockSpec(memory_space=pl.ANY) for _ in others],
+        out_specs=[vmem] * len(shapes),
+        out_shape=[jax.ShapeDtypeStruct(*s) for s in shapes],
+        scratch_shapes=[pltpu.VMEM((LAT, kv_c), bf16)],
+        compiler_params=pltpu.CompilerParams(vmem_limit_bytes=58 * MIB),
+        cost_estimate=pl.CostEstimate(
+            flops=2 * count * (model * heads.cols + LAT * kv_c + heads.width * count * 512),
+            bytes_accessed=2 * (model * heads.cols + 4 * count * model),
+            transcendentals=heads.width * count * count,
+        ),
+        name="attend",
+    )(x_low, packed, cosine, sine, seg_col, seg_row, gain, *others)
+
+
+def attend_back_kernel(
+    heads,
+    extra,
+    dattn_ref,
+    x_ref,
+    factor_ref,
+    w_ref,
+    cos_ref,
+    sin_ref,
+    seg_col_ref,
+    seg_row_ref,
+    gain_ref,
+    q_ref,
+    kv_ref,
+    kr_ref,
+    lat_ref,
+    lse_ref,
+    *refs,
+):
+    qr_ref, kvg_ref, normed_ref, in_gain_ref, lat_gain_ref, expand_ref = refs[extra:]
+    f32, bf16 = (jnp.float32, jnp.bfloat16)
+    count, model = x_ref.shape
+    half = heads.half
+    cosine, sine = (cos_ref[...], sin_ref[...])
+    expand_rows(heads, w_ref, expand_ref)
+    dheads = dot32(dattn_ref[...], w_ref[:, heads.output :]).astype(bf16)
+    keep = allowed(seg_col_ref, seg_row_ref)
+    lanes = lax.broadcasted_iota(jnp.int32, (count, 128), 1)
+    wide_lanes = lax.broadcasted_iota(jnp.int32, (count, 256), 1)
+    lse = lse_ref[...]
+    dq_rot = jnp.zeros((count, 256), f32)
+    dk_rot = jnp.zeros((count, 256), f32)
+    for h in range(heads.width):
+        mine, query, key, value = head_parts(heads, h, wide_lanes, q_ref, kv_ref, kr_ref)
+        scores = jnp.where(keep, dot_nt(query, key) * heads.scale, NEG_FILL)
+        probs = jnp.exp(scores - lse[:, h : h + 1])
+        dhead = dheads[:, h * VD : (h + 1) * VD]
+        dprobs = dot_nt(dhead, value)
+        delta = jnp.sum(probs * dprobs, axis=-1, keepdims=True)
+        dscores = (probs * (dprobs - delta)).astype(bf16)
+        dquery = dot32(dscores, key) * heads.scale
+        dkey = dot_tn(dscores, query) * heads.scale
+        qr_ref[:, h * NOPE : (h + 1) * NOPE] = dquery[:, :NOPE].astype(bf16)
+        dq_rot = dq_rot + jnp.where(mine, dquery[:, NOPE:], 0.0)
+        dk_rot = dk_rot + dkey[:, NOPE:]
+        at = h * (NOPE + VD)
+        kvg_ref[:, at : at + NOPE] = dkey[:, :NOPE].astype(bf16)
+        kvg_ref[:, at + NOPE : at + NOPE + VD] = dot_tn(probs.astype(bf16), dhead).astype(bf16)
+    first, second = (dq_rot[:, :128], dq_rot[:, 128:])
+    qr_ref[:, heads.flat : heads.flat + 128] = (first * cosine + second * sine).astype(bf16)
+    qr_ref[:, heads.flat + 128 : heads.query] = (second * cosine - first * sine).astype(bf16)
+
+    def folded(part):
+        part = part + pltpu.roll(part, half, 1)
+        return part + pltpu.roll(part, 2 * half, 1)
+
+    first, second = (folded(dk_rot[:, :128]), folded(dk_rot[:, 128:]))
+    ends = jnp.where(
+        lanes < half,
+        first * cosine + second * sine,
+        jnp.where(lanes < 2 * half, second * cosine - first * sine, 0.0),
+    )
+    qr_ref[:, heads.query + LAT : heads.lead] = ends.astype(bf16)
+    dlow = dot_nt(kvg_ref[...], expand_ref[...])
+    latent = lat_ref[...]
+    factor = lax.rsqrt(jnp.mean(latent * latent, axis=-1, keepdims=True) + EPS)
+    unit = latent * factor
+    lat_gain_ref[...] = jnp.sum(dlow * unit, axis=0, keepdims=True)
+    dlatent = norm_back(dlow, unit, factor, gain_ref[...])
+    qr_ref[:, heads.query : heads.query + LAT] = dlatent.astype(bf16)
+    qr = qr_ref[...]
+    step = 512
+    for at in range(0, model, step):
+        part = dot_nt(qr, w_ref[at : at + step, : heads.lead])
+        normed_ref[:, at : at + step] = part.astype(bf16)
+        unit_in = x_ref[:, at : at + step].astype(f32) * factor_ref[...]
+        in_gain_ref[:, at : at + step] = jnp.sum(part * unit_in, axis=0, keepdims=True)
+
+
+def attend_back(heads, *operands, others=()):
+    count, model = operands[1].shape
+    kv_c = heads.width * (NOPE + VD)
+    f32, bf16 = (jnp.float32, jnp.bfloat16)
+    shapes = [
+        ((count, heads.lead), bf16),
+        ((count, kv_c), bf16),
+        ((count, model), bf16),
+        ((1, model), f32),
+        ((1, LAT), f32),
+    ]
+    vmem = pl.BlockSpec(memory_space=pltpu.VMEM)
+    return pl.pallas_call(
+        functools.partial(attend_back_kernel, heads, len(others)),
+        in_specs=[vmem] * len(operands) + [pl.BlockSpec(memory_space=pl.ANY) for _ in others],
+        out_specs=[vmem] * len(shapes),
+        out_shape=[jax.ShapeDtypeStruct(*s) for s in shapes],
+        scratch_shapes=[pltpu.VMEM((LAT, kv_c), bf16)],
+        compiler_params=pltpu.CompilerParams(vmem_limit_bytes=58 * MIB),
+        cost_estimate=pl.CostEstimate(
+            flops=2 * count * (model * heads.cols + LAT * kv_c + heads.width * count * 1600),
+            bytes_accessed=2 * (model * heads.cols + 4 * count * model),
+            transcendentals=heads.width * count * count,
+        ),
+        name="attend_back",
+    )(*operands, *others)
 
 
 def per_device(
@@ -496,7 +735,6 @@
     units = plan.units
     chunks = max(2, groups * count // 2048)
     width = query_c // (NOPE + ROPE)
-    scale = (NOPE + ROPE) ** (-0.5)
 
     small_c = -(-(LAT + ROPE + experts_n + 3) // 128) * 128
     assert small_c - 128 <= LAT + ROPE
@@ -512,30 +750,22 @@
     pieces = depth // w_expand.shape[0]
     wide = expand_c // pieces
     expand_blocks = [w_expand[:, k * wide : (k + 1) * wide] for k in range(pieces)]
+    heads = Heads(width, groups, depth, small_c, wide, heads_c)
+    order = heads.order()
     packed = jnp.concatenate(
-        [w_query, small, jnp.concatenate(expand_blocks, axis=0), w_output.T], axis=1
+        [dot32(w_query, order).astype(bf16), small, jnp.concatenate(expand_blocks, axis=0), w_output.T], axis=1
     )
     packed = lax.all_gather(packed, "fsdp", axis=0, tiled=True)
-    at_expand = query_c + small_c
-    at_output = at_expand + wide
-    query_w = packed[:, :query_c]
-    latent_w = packed[:, query_c : query_c + LAT + ROPE]
-    router_w = packed[:, query_c + LAT + ROPE : query_c + LAT + ROPE + experts_n]
-    expand_w = (
-        packed[:, at_expand:at_output]
-        .reshape(groups, pieces, LAT // groups, wide)
-        .transpose(0, 2, 1, 3)
-        .reshape(LAT, expand_c)
-    )
-    output_wt = packed[:, at_output:]
+    at_expand = heads.lead
+    at_output = heads.output
+    at_first = heads.query + at_router
+    router_w = packed[:, at_first : at_first + experts_n]
 
     meta = jnp.concatenate(
         [routes.astype(bf16), jnp.zeros((tok_dev, 128 - top_k), bf16)], axis=1
     )
     dout_own, small = lax.optimization_barrier((jnp.concatenate([cotangent, meta], axis=1), small))
     dout_group = gather_ctx(dout_own)
-    x_own, dout_group = lax.optimization_barrier((tokens_in, dout_group))
-    x_all = gather_ctx(x_own)
     dout_all = lax.all_gather(dout_group, "fsdp", axis=0, tiled=True)
     dout_all = dout_all.reshape(groups * lanes, chunks, tok_dev // chunks, model_w + 128)
 
@@ -544,7 +774,7 @@
     )
     shared = lax.all_to_all(shared, "fsdp", split_axis=1, concat_axis=1, tiled=True)
     shared = shared.transpose(0, 2, 1, 3).reshape(3, sh_units, model_w)
-    x_all = after(x_all, shared)
+    x_all = gather_ctx(after(tokens_in, shared))
 
     def hidden_rows(experts, mine, router):
         gap = jnp.zeros((plan.router - units - sh_units, model_w), bf16)
@@ -564,32 +794,14 @@
     place = (steps - start).astype(f32)
     freq = THETA ** (-(jnp.arange(ROPE // 2, dtype=f32) * 2.0 / ROPE))
     angle = place[:, None] * freq[None, :]
-    cosine, sine = (jnp.cos(angle), jnp.sin(angle))
-    normed, unit_in, _ = norm_parts(x_all.astype(f32), norm_in)
+    cosine, sine = (jnp.concatenate([f(angle)] * 4, axis=1) for f in (jnp.cos, jnp.sin))
+    normed, _, factor_in = norm_parts(x_all.astype(f32), norm_in)
     x_low = normed.astype(bf16)
-    q_raw = dot32(x_low, query_w).reshape(count, width, NOPE + ROPE)
-    q_nope = q_raw[..., :NOPE].astype(bf16)
-    q_rope = turn(q_raw[..., NOPE:], cosine[:, None], sine[:, None]).astype(bf16)
-    latent_raw = dot32(x_low, latent_w)
-    latent_n, unit_lat, factor_lat = norm_parts(latent_raw[:, :LAT], latent_gain)
-    latent_low = latent_n.astype(bf16)
-    krope = turn(latent_raw[:, LAT:], cosine, sine).astype(bf16)
-    kv_raw = dot32(latent_low, expand_w).astype(bf16).reshape(count, width, NOPE + VD)
-    knope = kv_raw[..., :NOPE]
-    values = kv_raw[..., NOPE:]
-    raw = jnp.einsum("qhd,khd->hqk", q_nope, knope, preferred_element_type=f32)
-    raw = raw + jnp.einsum("qhd,kd->hqk", q_rope, krope, preferred_element_type=f32)
-    keep = same & (steps[None, :] <= steps[:, None])
-    logits = jnp.where(keep[None], raw * scale, NEG_FILL)
-    expo = jnp.exp(logits - jnp.max(logits, axis=-1, keepdims=True))
-    probs = expo / jnp.sum(expo, axis=-1, keepdims=True)
-    probs_low = probs.astype(bf16)
-    heads_low = (
-        jnp.einsum("hqk,khd->qhd", probs_low, values, preferred_element_type=f32)
-        .astype(bf16)
-        .reshape(count, heads_c)
-    )
-    resid = tokens_in.astype(f32) + scatter_ctx(dot_nt(heads_low, output_wt).astype(bf16))
+    fixed = (cosine, sine, seg_all[:, None], seg_all[None, :], latent_gain[None, :])
+    q_low, kv_low, kr_low, latent_raw, latent_low, lse, heads_low, attn = attend(
+        heads, x_low, packed, *fixed, wd
+    )
+    resid = after(tokens_in.astype(f32) + scatter_ctx(attn), w1)
     mid, unit_mid, factor_mid = norm_parts(resid, norm_mid)
     mid_low = mid.astype(bf16)
 
@@ -608,13 +820,15 @@
         rows_parts.append(last)
     gud, act = held
     edown_grad, sdown_grad = down_sum(plan, model_w, act, dout_all)
-    egate_grad, eup_grad, sgu_grad = pair_sum(plan, gud, mids)
+    rows_own = [scatter_ctx(rows) for rows in rows_parts]
+
+    early = (rows_own[0],) if chunks == 2 else ()
+    egate_grad, eup_grad, sgu_grad = pair_sum(plan, gud, mids, edown_grad, *early)
     out_parts = [
-        experts_out(plan, groups, lanes, h, 2, act, wd, edown_grad, egate_grad) for h in range(0, chunks, 2)
+        experts_out(plan, groups, lanes, h, 2, act, wd, egate_grad) for h in range(0, chunks, 2)
     ]
-    rows_own = [scatter_ctx(rows) for rows in rows_parts]
     rows_grad = jnp.concatenate(rows_own)
-    rows_grad = after(rows_grad, edown_grad, egate_grad, *out_parts)
+    rows_grad = after(rows_grad, egate_grad, *out_parts)
     mid_grad = rows_grad[:, :model_w]
     gates_grad = (
         rows_grad[:, model_w : model_w + experts_n]
@@ -629,10 +843,10 @@
     spread = jnp.sum(gates_grad * gates, axis=-1, keepdims=True)
     chosen_grad = (ROUTE_SCALE * gates_grad - spread) / chosen_sum
     logit_grad = chosen_grad * member * sig * (1.0 - sig)
-    router_grad = precise_tn(mid_low.astype(f32), logit_grad)
+    router_grad = precise_tn(logit_grad, mid_low.astype(f32))
     mid_grad = mid_grad + precise_nt(logit_grad, router_w.astype(f32))
     resid_grad = norm_back(mid_grad, unit_mid, factor_mid, norm_mid) + cotangent.astype(f32)
-    mid_gain_grad = jnp.sum(mid_grad * unit_mid, axis=0)
+    mid_gain_grad = jnp.sum(mid_grad * unit_mid, axis=0, keepdims=True)
     attn_low = gather_ctx(resid_grad.astype(bf16))
 
     out_sums = []
@@ -641,67 +855,50 @@
         out_sums.append(last)
     moe = jnp.concatenate([scatter_ctx(rows) for rows in out_sums])
     block_out = (resid + moe).astype(bf16)
+
+    qr_grad, kv_grad, normed_grad, in_gain_grad, latent_gain_grad = attend_back(
+        heads,
+        attn_low,
+        x_all,
+        factor_in,
+        packed,
+        *fixed,
+        q_low,
+        kv_low,
+        kr_low,
+        latent_raw,
+        lse,
+    )
     shared_grad = jnp.concatenate([sgu_grad, sdown_grad[None]])[:, :sh_units].astype(bf16)
     shared_grad = shared_grad.reshape(3, sh_units, groups, depth).transpose(0, 2, 1, 3)
+    shared_grad = after(shared_grad, qr_grad)
     shared_grad = lax.all_to_all(shared_grad, "fsdp", split_axis=1, concat_axis=1, tiled=True)
     shared_grad = shared_grad.reshape(3, sh_units * groups, depth).astype(f32)
-
-    heads_grad = dot32(attn_low, output_wt).astype(bf16).reshape(count, width, VD)
-    prob_grad = jnp.einsum("qhd,khd->hqk", heads_grad, values, preferred_element_type=f32)
-    delta = jnp.sum(probs * prob_grad, axis=-1, keepdims=True)
-    score_grad = (probs * (prob_grad - delta)).astype(bf16)
-    q_nope_grad = jnp.einsum("hqk,khd->qhd", score_grad, knope, preferred_element_type=f32) * scale
-    q_rope_grad = jnp.einsum("hqk,kd->qhd", score_grad, krope, preferred_element_type=f32) * scale
-    knope_grad = jnp.einsum("hqk,qhd->khd", score_grad, q_nope, preferred_element_type=f32) * scale
-    krope_grad = jnp.einsum("hqk,qhd->kd", score_grad, q_rope, preferred_element_type=f32) * scale
-    values_grad = jnp.einsum("hqk,qhd->khd", probs_low, heads_grad, preferred_element_type=f32)
-    q_raw_grad = (
-        jnp.concatenate(
-            [q_nope_grad, turn_back(q_rope_grad, cosine[:, None], sine[:, None])], axis=-1
-        )
-        .astype(bf16)
-        .reshape(count, query_c)
-    )
-    kv_grad = (
-        jnp.concatenate([knope_grad, values_grad], axis=-1).astype(bf16).reshape(count, expand_c)
-    )
-    latent_out_grad = dot_nt(kv_grad, expand_w)
-    latent_gain_grad = jnp.sum(latent_out_grad * unit_lat, axis=0)
-    latent_grad = norm_back(latent_out_grad, unit_lat, factor_lat, latent_gain)
-    raw_grad = jnp.concatenate([latent_grad, turn_back(krope_grad, cosine, sine)], axis=-1).astype(
-        bf16
-    )
-    qr_grad = jnp.concatenate(
-        [q_raw_grad, raw_grad, jnp.zeros((count, small_c - LAT - ROPE), bf16)], axis=1
-    )
-    normed_grad = dot_nt(qr_grad, packed[:, :at_expand])
-    in_gain_grad = jnp.sum(normed_grad * unit_in, axis=0)
-    normed_own = scatter_ctx(normed_grad.astype(bf16))
+    normed_own = scatter_ctx(normed_grad)
     _, unit_own, factor_own = norm_parts(tokens_in.astype(f32), norm_in)
     grad_input = norm_back(normed_own, unit_own, factor_own, norm_in) + resid_grad
 
-    latent_gain_col = jnp.pad(
+    latent_gain_row = jnp.pad(
         latent_gain_grad.reshape(groups * lanes, -1),
         ((0, 0), (0, depth // lanes - LAT // (groups * lanes))),
-    ).reshape(model_w, 1)
+    ).reshape(1, model_w)
     before = LAT + ROPE - (small_c - 128)
     extra = jnp.concatenate(
         [
-            jnp.zeros((model_w, before), f32),
+            jnp.zeros((before, model_w), f32),
             router_grad,
-            in_gain_grad[:, None],
-            mid_gain_grad[:, None],
-            latent_gain_col,
-            jnp.zeros((model_w, 128 - before - experts_n - 3), f32),
-        ],
-        axis=1,
+            mid_gain_grad,
+            in_gain_grad,
+            latent_gain_row,
+            jnp.zeros((128 - before - experts_n - 3, model_w), f32),
+        ]
     )
     grads = packed_grads(
         groups, x_low, attn_low, latent_low.T, qr_grad, heads_low, kv_grad, extra
     )
     grads = lax.psum_scatter(after(grads, last), "fsdp", scatter_dimension=0, tiled=True)
-    small_own = scatter_ctx(grads[:, query_c:at_expand])
-    g_query = grads[:, :query_c].astype(f32)
+    small_own = scatter_ctx(grads[:, heads.query : at_expand])
+    g_query = dot_nt(grads[:, : heads.query], order)
     g_expand = grads[:, at_expand:at_output].astype(f32)
     g_expand = jnp.concatenate(
         [g_expand[k * w_expand.shape[0] : (k + 1) * w_expand.shape[0]] for k in range(pieces)],
@@ -712,13 +909,13 @@
     return (
         block_out,
         grad_input.astype(bf16),
-        small_own[:, at_gain],
+        small_own[:, at_gain + 1],
         g_query,
         small_own[:, :at_router],
         small_own[: LAT // (groups * lanes), at_gain + 2],
         g_expand,
         g_output,
-        small_own[:, at_gain + 1],
+        small_own[:, at_gain],
         small_own[:, at_router:at_gain],
         shared_grad[0].T,
         shared_grad[1].T,

time: 896 us -> 764 us (0.85)
  waiting for transfers between devices: 376 us -> 308 us
  matrix products: 53.7 us -> 8.62 us
  local copies, waits for them, and re-layouts: 93.1 us -> 54.2 us
  Pallas kernels: 204 us -> 236 us
    ppermute x18, waiting for transfers between devices: 158 us -> 113 us  [scatter_ctx(): lax.ppermute(part, 'ctx', [(i, (i + hop) % lanes) for i in range(lanes)])]
    pallas_call x1 -> x3, Pallas kernels: 41.2 us -> 73.1 us  [the longest x1 41.1 us: pair_sum(): pl.pallas_call(functools.partial(pair_kernel, plan, chunks), grid=(chunks...]
    all_to_all x1, waiting for transfers between devices: 22.5 us -> 0.01 us  [per_device(): lax.all_to_all(shared, 'fsdp', split_axis=1, concat_axis=1, tiled=True)]
    dot_general x9 -> x0, matrix products: 21.7 us -> none  [the longest x1 5.81 us: per_device(): jnp.einsum('hqk,qhd->khd', probs_low, heads_grad, preferred_element_type=...]
    dot_general x5 -> x2, matrix products: 14.3 us -> 2.14 us  [dot32(): return jnp.dot(left, right, preferred_element_type=jnp.float32)]
    dot_general x3 -> x1, matrix products: 13.1 us -> 1.48 us  [dot_nt(): lax.dot_general(left, right, (((1,), (1,)), ((), ())), preferred_element_...]
    ppermute x18, starting transfers between devices: 42.6 us -> 32.7 us  [gather_ctx(): lax.ppermute(value, 'ctx', [(i, (i + hop) % lanes) for i in range(lanes)])]
    unnamed x212 -> x140, local copies, waits for them, and re-layouts: 33 us -> 25.2 us
  transfers between devices with their start and end apart: 46 -> 46, of which waited for: 28 -> 28; matrix products, arithmetic and copies ran while one was open for 17% -> 9% of each run, Pallas kernels for 23% -> 31%
where the time goes in v2:
time: 764 us; the launch traced here: 757 us
  waiting for transfers between devices  308 us (40%)
  Pallas kernels  236 us (31%)
  starting transfers between devices  97.1 us (13%)
  local copies, waits for them, and re-layouts  54.2 us (7%)
  other arithmetic  37.3 us (5%)
  between operations  15.5 us (2%)
  matrix products  8.62 us (1%)
    ppermute x18, waiting for transfers between devices, gather_ctx(): lax.ppermute(value, 'ctx', [(i, (i + hop) % lanes) for i in range(lanes)])  136 us
    ppermute x18, waiting for transfers between devices, scatter_ctx(): lax.ppermute(part, 'ctx', [(i, (i + hop) % lanes) for i in range(lanes)])  113 us
    pallas_call x2, Pallas kernels, experts_back(): pl.pallas_call(functools.partial(back_kernel, plan), grid=(tokens // tile...  110 us
    ppermute x18, starting transfers between devices, scatter_ctx(): lax.ppermute(part, 'ctx', [(i, (i + hop) % lanes) for i in range(lanes)])  55.9 us
    pallas_call x1, Pallas kernels, pair_sum(): pl.pallas_call(functools.partial(pair_kernel, plan, chunks), grid=(chunks...  41.1 us
    all_gather x2, waiting for transfers between devices, per_device(): last = lax.all_gather(after(mid_part, last), 'fsdp', axis=0, tiled=True)  36.6 us
    ppermute x18, starting transfers between devices, gather_ctx(): lax.ppermute(value, 'ctx', [(i, (i + hop) % lanes) for i in range(lanes)])  32.7 us
    unnamed x140, local copies, waits for them, and re-layouts  25.2 us
  transfers between devices with their start and end apart: 46, of which 28 were waited for; matrix products, arithmetic and copies ran while one was open for 9% of the time, Pallas kernels for 31%

profile of v2, /device:TPU:0, one launch (start us, length us, event | category | flops | bytes accessed | tf_op | source)
XLA Modules:
  0.0 757.2 jit_solution(4220498386663950237)
XLA Ops:
  10.0 4.1 collective-permute-start.4
  14.1 1.6 collective-permute-start.3
  15.7 2.2 collective-permute-start.5
  24.3 2.7 collective-permute-start.17
  28.5 12.2 %collective-permute-done.15 = bf16[128,2176]{1,0:T(8,128)(2,1)} collective-permute-done((bf16[128,2176]{1,0:T(8,128)(2,1)S(1)}, bf16[128,2176]{1,0:T(8,128)(2,1)}, u32[]{:S(2)}, u32[]{:S(2)}) %collective-permute-start.15) | collective-permute-done | bytes 557088 | tf_op jit(solution)/shard_map/ppermute | solution.py:101
  41.9 33.0 %collective-permute-done.16 = bf16[128,2176]{1,0:T(8,128)(2,1)S(1)} collective-permute-done((bf16[128,2176]{1,0:T(8,128)(2,1)S(1)}, bf16[128,2176]{1,0:T(8,128)(2,1)S(1)}, u32[]{:S(2)}, u32[]{:S(2)}) %collective-permute-start.16) | collective-permute-done | bytes 557088 | tf_op jit(solution)/shard_map/ppermute | solution.py:101
  76.4 2.5 collective-permute-start.2
  79.6 2.3 pad_maximum_fusion.3
  81.9 4.2 all-to-all-start
  91.8 20.9 %collective-permute-done = bf16[128,2048]{1,0:T(8,128)(2,1)} collective-permute-done((bf16[128,2048]{1,0:T(8,128)(2,1)S(1)}, bf16[128,2048]{1,0:T(8,128)(2,1)}, u32[]{:S(2)}, u32[]{:S(2)}) %collective-permute-start) | collective-permute-done | bytes 524320 | tf_op jit(solution)/shard_map/ppermute | solution.py:101
  113.8 8.4 %collective-permute-done.1 = bf16[128,2048]{1,0:T(8,128)(2,1)} collective-permute-done((bf16[128,2048]{1,0:T(8,128)(2,1)S(1)}, bf16[128,2048]{1,0:T(8,128)(2,1)}, u32[]{:S(2)}, u32[]{:S(2)}) %collective-permute-start.1) | collective-permute-done | bytes 524320 | tf_op jit(solution)/shard_map/ppermute | solution.py:101
  123.9 2.0 fusion.7.x_ref
  128.0 4.6 maximum_maximum_fusion.refs_0_.wd_ref
  134.2 14.0 %attend.1 = (bf16[512,768]{1,0:T(8,128)(2,1)}, bf16[512,1024]{1,0:T(8,128)(2,1)}, bf16[512,256]{1,0:T(8,128)(2,1)}, f32[512,512]{1,0:T(8,128)}, bf16[512,512]{1,...) custom-call(bf16[512,2048]{1,0:T(8,128)(2,1)} %fusion.7.x_ref, ...), custom_call_target="tpu_custom_call" | custom-call | flops 6174015488 | bytes 17301504 | tf_op jit(solution)/shard_map/attend/pallas_call | solution.py:581
  148.2 1.7 constant_dynamic-slice_fusion.17
  149.9 2.6 collective-permute-start.6
  153.8 2.8 collective-permute-start.7
  156.7 5.6 fusion.4.w1_ref
  162.3 4.3 collective-permute-done.6
  166.7 9.6 %collective-permute-done.8 = bf16[128,2048]{1,0:T(8,128)(2,1)S(1)} collective-permute-done((bf16[128,2048]{1,0:T(8,128)(2,1)S(1)}, bf16[128,2048]{1,0:T(8,128)(2,1)S(1)}, u32[]{:S(2)}, u32[]{:S(2)}) %collective-permute-start.8) | collective-permute-done | bytes 524320 | tf_op jit(solution)/shard_map/ppermute | solution.py:114
  176.2 22.0 %collective-permute-done.7 = bf16[128,2048]{1,0:T(8,128)(2,1)S(1)} collective-permute-done((bf16[128,2048]{1,0:T(8,128)(2,1)S(1)}, bf16[128,2048]{1,0:T(8,128)(2,1)S(1)}, u32[]{:S(2)}, u32[]{:S(2)}) %collective-permute-start.7) | collective-permute-done | bytes 524320 | tf_op jit(solution)/shard_map/ppermute | solution.py:114
  198.2 2.0 fusion.24
  201.4 4.5 collective-permute-start.12
  206.1 12.2 %collective-permute-done.12 = bf16[64,2048]{1,0:T(8,128)(2,1)S(1)} collective-permute-done((bf16[64,2048]{1,0:T(8,128)(2,1)S(1)}, bf16[64,2048]{1,0:T(8,128)(2,1)S(1)}, u32[]{:S(2)}, u32[]{:S(2)}) %collective-permute-start.12) | collective-permute-done | bytes 262176 | tf_op jit(solution)/shard_map/ppermute | solution.py:101
  218.3 3.2 collective-permute-done.13
  224.1 4.6 collective-permute-start.9
  229.0 2.8 collective-permute-start.11
  231.8 3.6 collective-permute-done.9
  235.5 8.5 %collective-permute-done.10 = bf16[64,2048]{1,0:T(8,128)(2,1)S(1)} collective-permute-done((bf16[64,2048]{1,0:T(8,128)(2,1)S(1)}, bf16[64,2048]{1,0:T(8,128)(2,1)S(1)}, u32[]{:S(2)}, u32[]{:S(2)}) %collective-permute-start.10) | collective-permute-done | bytes 262176 | tf_op jit(solution)/shard_map/ppermute | solution.py:101
  244.0 1.8 collective-permute-done.11
  245.8 35.2 %all-gather.9.cloned.1.call-done.mid_ref.refs_0_ = bf16[2048,2048]{1,0:T(8,128)(2,1)} async-done(((bf16[256,2048]{1,0:T(8,128)(2,1)}), bf16[2048,2048]{1,0:T(8,128)(2,1)}) %all-gather.9.cloned.1.call-update) | async-done | bytes 8388624 | tf_op jit(solution)/shard_map/all_gather | solution.py:814
  281.1 55.2 %experts_back.2 = (bf16[2048,2176]{1,0:T(8,128)(2,1)}, bf16[2,2048,1792]{2,1,0:T(8,128)(2,1)}, bf16[2,2048,896]{2,1,0:T(8,128)(2,1)}) custom-call(s32[1]{0:T(128)} %bitcast.13.first_ref, bf16[2048,2048]{1,0:T(8,128)(2,1)} %all-gather.9.cloned.1.call-done.mid_ref.refs_0_, bf16[32,2,64,2176]{3,2,1,0:T(8,128)(2,1)} %bitcast.88, ...), custom_call_target="tpu_custom_call" | custom-call | flops 37580963840 | bytes 36175872 | tf_op jit(solution)/shard_map/experts_back/pallas_call | solution.py:239
  337.8 54.8 %experts_back.3 = (bf16[2048,2176]{1,0:T(8,128)(2,1)}, bf16[2,2048,1792]{2,1,0:T(8,128)(2,1)}, bf16[2,2048,896]{2,1,0:T(8,128)(2,1)}) custom-call(s32[1]{0:T(128)} %bitcast.13.first_ref, bf16[2048,2048]{1,0:T(8,128)(2,1)} %all-gather.11.cloned.1.call-done.mid_ref.refs_1_, ...), custom_call_target="tpu_custom_call", output_to_operand_aliasing={{1}: (6, {}), {2}: (7, {})} | custom-call | flops 37580963840 | bytes 36175872 | tf_op jit(solution)/shard_map/experts_back/pallas_call | solution.py:239
  392.6 22.4 %reduce-scatter.5.cloned.1.call-done = bf16[256,2176]{1,0:T(8,128)(2,1)} async-done(((bf16[2048,2176]{1,0:T(8,128)(2,1)}), bf16[256,2176]{1,0:T(8,128)(2,1)}) %reduce-scatter.5.cloned.1.call-update) | async-done | bytes 1114128 | tf_op jit(solution)/shard_map/reduce_scatter | solution.py:819
  417.9 2.3 collective-permute-start.20
  420.8 22.7 %down_sum.1 = (f32[704,2048]{1,0:T(8,128)}, f32[88,2048]{1,0:T(8,128)S(1)}) custom-call(bf16[2,2048,896]{2,1,0:T(8,128)(2,1)} %get-tuple-element.57.h_ref.act_ref, bf16[32,2,64,2176]{3,2,1,0:T(8,128)(2,1)} %bitcast.92), custom_call_target="tpu_custom_call" | custom-call | flops 15032385536 | bytes 29884416 | tf_op jit(solution)/shard_map/down_sum/pallas_call | solution.py:326
  445.4 41.1 %pair_sum.1 = (f32[704,2048]{1,0:T(8,128)}, f32[704,2048]{1,0:T(8,128)}, f32[2,88,2048]{2,1,0:T(8,128)}) custom-call(bf16[2,2048,1792]{2,1,0:T(8,128)(2,1)} %get-tuple-element.58.h_ref, bf16[2048,2048]{1,0:T(8,128)(2,1)} %all-gather.9.cloned.1.call-done.mid_ref.refs_0_, bf16[2048,2048]{1,0:T(8,128)(2,1)} %all-gather.11.cloned.1.call-done.mid_ref.refs_1_, ...), custom_call_target="tpu_custom_call" | custom-call | flops 30064771072 | bytes 42991616 | tf_op jit(solution)/shard_map/pair_sum/pallas_call | solution.py:392
  486.6 2.6 copy-done.12
  489.2 3.1 copy-done.13
  492.3 21.2 %experts_out.1 = bf16[8,4,2,64,2048]{4,3,2,1,0:T(8,128)(2,1)} custom-call(bf16[2,2048,896]{2,1,0:T(8,128)(2,1)S(1)} %copy-done.13, bf16[896,2048]{1,0:T(8,128)(2,1)S(1)} %copy-done.5, f32[704,2048]{1,0:T(8,128)S(1)} %copy-done.12), custom_call_target="tpu_custom_call" | custom-call | flops 15032385536 | bytes 24117248 | tf_op jit(solution)/shard_map/experts_out/pallas_call | solution.py:284
  515.7 3.0 collective-permute-start.26
  520.4 5.8 collective-permute-done.24
  526.2 3.4 collective-permute-done.26
  529.7 12.7 %collective-permute-done.25 = bf16[64,2176]{1,0:T(8,128)(2,1)S(1)} collective-permute-done((bf16[64,2176]{1,0:T(8,128)(2,1)S(1)}, bf16[64,2176]{1,0:T(8,128)(2,1)S(1)}, u32[]{:S(2)}, u32[]{:S(2)}) %collective-permute-start.25) | collective-permute-done | bytes 278560 | tf_op jit(solution)/shard_map/ppermute | solution.py:114
  543.8 2.9 multiply_reduce_fusion
  548.1 1.7 collective-permute-start.28
  551.7 2.5 collective-permute-start.29
  554.1 2.1 fusion.60
  556.3 8.9 %collective-permute-done.27 = bf16[128,2048]{1,0:T(8,128)(2,1)} collective-permute-done((bf16[128,2048]{1,0:T(8,128)(2,1)}, bf16[128,2048]{1,0:T(8,128)(2,1)}, u32[]{:S(2)}, u32[]{:S(2)}) %collective-permute-start.27) | collective-permute-done | bytes 524320 | tf_op jit(solution)/shard_map/ppermute | solution.py:101
  566.2 19.6 %collective-permute-done.28 = bf16[128,2048]{1,0:T(8,128)(2,1)} collective-permute-done((bf16[128,2048]{1,0:T(8,128)(2,1)}, bf16[128,2048]{1,0:T(8,128)(2,1)}, u32[]{:S(2)}, u32[]{:S(2)}) %collective-permute-start.28) | collective-permute-done | bytes 524320 | tf_op jit(solution)/shard_map/ppermute | solution.py:101
  588.3 18.0 %attend_back.1 = (bf16[512,1408]{1,0:T(8,128)(2,1)}, bf16[512,1024]{1,0:T(8,128)(2,1)}, bf16[512,2048]{1,0:T(8,128)(2,1)}, f32[1,2048]{1,0:T(1,128)}, f32[1,512]{1,0:T(1,128)}) custom-call(bf16[512,2048]{1,0:T(8,128)(2,1)} %copy-done.2, bf16[512,2048]{1,0:T(8,128)(2,1)} %copy-done.17, f32[512,1]{1,0:T(8,128)} %copy.102.factor_ref, ...), custom_call_target="tpu_custom_call" | custom-call | flops 8455716864 | bytes 17301504 | tf_op jit(solution)/shard_map/attend_back/pallas_call | solution.py:688
  609.4 3.1 concatenate.70.extra_ref
  612.4 1.6 copy-done.4
  618.8 9.2 %packed_grads.1 = bf16[2048,2176]{1,0:T(8,128)(2,1)} custom-call(bf16[512,2048]{1,0:T(8,128)(2,1)S(1)} %copy-done.4, bf16[512,2048]{1,0:T(8,128)(2,1)S(1)} %copy-done.3, bf16[512,512]{1,0:T(8,128)(2,1)S(1)} %bitcast.60, bf16[512,1408]{1,0:T(8,128)(2,1)S(1)} %copy-done.7, bf16[512,512]{1,0:T(8,128)(2,1)S(1)} %copy-done.11, bf16[512,1024]{1,0:T(8,128)(2,1)S(1)} %copy-done.8, ...), custom_call_target="tpu_custom_call" | custom-call | flops 4563402752 | bytes 16777216 | tf_op jit(solution)/shard_map/packed_grads/pallas_call | solution.py:442
  632.1 9.6 %collective-permute-start.30 = (bf16[128,2048]{1,0:T(8,128)(2,1)}, bf16[128,2048]{1,0:T(8,128)(2,1)S(1)}, u32[]{:S(2)}, u32[]{:S(2)}) collective-permute-start(bf16[128,2048]{1,0:T(8,128)(2,1)} %get-tuple-element.156), channel_id=1, source_target_pairs={{0,1},{1,2},{2,3},{3,0},{4,5},{5,6},{6,7},{7,4},{8,9},{9,10},{10,1... | collective-permute-start | bytes 1572872 | tf_op jit(solution)/shard_map/ppermute | solution.py:114
  644.2 3.9 all-to-all-start.1
  648.2 2.9 constant_dynamic-slice_fusion.11
  652.2 2.7 collective-permute-start.23
  654.9 22.1 %collective-permute-start.22 = (bf16[128,2048]{1,0:T(8,128)(2,1)}, bf16[128,2048]{1,0:T(8,128)(2,1)}, u32[]{:S(2)}, u32[]{:S(2)}) collective-permute-start(bf16[128,2048]{1,0:T(8,128)(2,1)} %get-tuple-element.161), channel_id=1, source_target_pairs={{0,2},{1,3},{2,0},{3,1},{4,6},{5,7},{6,4},{7,5},{8,10},{9,11},{10,... | collective-permute-start | bytes 1572872 | tf_op jit(solution)/shard_map/ppermute | solution.py:114
  677.1 22.6 %collective-permute-done.31 = bf16[128,2048]{1,0:T(8,128)(2,1)S(1)} collective-permute-done((bf16[128,2048]{1,0:T(8,128)(2,1)}, bf16[128,2048]{1,0:T(8,128)(2,1)S(1)}, u32[]{:S(2)}, u32[]{:S(2)}) %collective-permute-start.31) | collective-permute-done | bytes 524320 | tf_op jit(solution)/shard_map/ppermute | solution.py:114
  703.5 27.7 %collective-permute-done.22 = bf16[128,2048]{1,0:T(8,128)(2,1)} collective-permute-done((bf16[128,2048]{1,0:T(8,128)(2,1)}, bf16[128,2048]{1,0:T(8,128)(2,1)}, u32[]{:S(2)}, u32[]{:S(2)}) %collective-permute-start.22) | collective-permute-done | bytes 524320 | tf_op jit(solution)/shard_map/ppermute | solution.py:114
  731.3 4.0 fusion.23
  737.8 3.5 collective-permute-start.35
  744.5 3.4 collective-permute-done.34
  (299 shorter events, 77.3 us)
Async XLA Ops:
  7.2 125.4 %all-gather.5.cloned.1.call-start = ((), (), s32[]{:S(2)}) async-start(), calls=%async_computation.6 | async-start | bytes 10027008 | tf_op jit(solution)/shard_map/all_gather | solution.py:758
  10.0 10.9 %collective-permute-start.4 = (bf16[64,640]{1,0:T(8,128)(2,1)S(1)}, bf16[64,640]{1,0:T(8,128)(2,1)S(1)}, u32[]{:S(2)}, u32[]{:S(2)}) collective-permute-start(bf16[64,640]{1,0:T(8,128)(2,1)S(1)} %get-tuple-element.155), channel_id=1, source_target_pairs={{0,2},{1,3},{2,0},{3,1},{4,6},{5,7},{6,4},{7,5},{8,10},{9,11},{10,... | collective-permute-start | bytes 245768 | tf_op jit(solution)/shard_map/ppermute | solution.py:101
  14.1 6.7 collective-permute-start.3
  15.7 5.8 collective-permute-start.5
  22.7 200.5 %all-gather.7.cloned.1.call-start = ((), (), s32[]{:S(2)}) async-start(), calls=%async_computation.7 | async-start | bytes 20054016 | tf_op jit(solution)/shard_map/all_gather | solution.py:769
  23.2 17.6 %collective-permute-start.15 = (bf16[128,2176]{1,0:T(8,128)(2,1)S(1)}, bf16[128,2176]{1,0:T(8,128)(2,1)}, u32[]{:S(2)}, u32[]{:S(2)}) collective-permute-start(bf16[128,2176]{1,0:T(8,128)(2,1)S(1)} %concatenate.68), channel_id=1, source_target_pairs={{0,1},{1,2},{2,3},{3,0},{4,5},{5,6},{6,7},{7,4},{8,9},{9,10},{10,1... | collective-permute-start | bytes 1671176 | tf_op jit(solution)/shard_map/ppermute | solution.py:101
  24.3 50.6 %collective-permute-start.17 = (bf16[128,2176]{1,0:T(8,128)(2,1)S(1)}, bf16[128,2176]{1,0:T(8,128)(2,1)S(1)}, u32[]{:S(2)}, u32[]{:S(2)}) collective-permute-start(bf16[128,2176]{1,0:T(8,128)(2,1)S(1)} %concatenate.68), channel_id=1, source_target_pairs={{0,3},{1,0},{2,1},{3,2},{4,7},{5,4},{6,5},{7,6},{8,11},{9,8},{10,9... | collective-permute-start | bytes 1671176 | tf_op jit(solution)/shard_map/ppermute | solution.py:101
  27.1 47.8 %collective-permute-start.16 = (bf16[128,2176]{1,0:T(8,128)(2,1)S(1)}, bf16[128,2176]{1,0:T(8,128)(2,1)S(1)}, u32[]{:S(2)}, u32[]{:S(2)}) collective-permute-start(bf16[128,2176]{1,0:T(8,128)(2,1)S(1)} %concatenate.68), channel_id=1, source_target_pairs={{0,2},{1,3},{2,0},{3,1},{4,6},{5,7},{6,4},{7,5},{8,10},{9,11},{10,... | collective-permute-start | bytes 1671176 | tf_op jit(solution)/shard_map/ppermute | solution.py:101
  41.8 34.6 %copy-start.19 = (bf16[128,2048]{1,0:T(8,128)(2,1)S(1)}, bf16[128,2048]{1,0:T(8,128)(2,1)}, u32[]{:S(2)}) copy-start(bf16[128,2048]{1,0:T(8,128)(2,1)} %param.18) | copy-start | bytes 1572868
  76.4 46.9 %collective-permute-start.2 = (bf16[128,2048]{1,0:T(8,128)(2,1)S(1)}, bf16[128,2048]{1,0:T(8,128)(2,1)S(1)}, u32[]{:S(2)}, u32[]{:S(2)}) collective-permute-start(bf16[128,2048]{1,0:T(8,128)(2,1)S(1)} %copy-done.19), channel_id=1, source_target_pairs={{0,3},{1,0},{2,1},{3,2},{4,7},{5,4},{6,5},{7,6},{8,11},{9,8},{10,9... | collective-permute-start | bytes 1572872 | tf_op jit(solution)/shard_map/ppermute | solution.py:101
  79.0 43.3 %collective-permute-start.1 = (bf16[128,2048]{1,0:T(8,128)(2,1)S(1)}, bf16[128,2048]{1,0:T(8,128)(2,1)}, u32[]{:S(2)}, u32[]{:S(2)}) collective-permute-start(bf16[128,2048]{1,0:T(8,128)(2,1)S(1)} %copy-done.19), channel_id=1, source_target_pairs={{0,2},{1,3},{2,0},{3,1},{4,6},{5,7},{6,4},{7,5},{8,10},{9,11},{10,... | collective-permute-start | bytes 1572872 | tf_op jit(solution)/shard_map/ppermute | solution.py:101
  79.0 33.8 %collective-permute-start = (bf16[128,2048]{1,0:T(8,128)(2,1)S(1)}, bf16[128,2048]{1,0:T(8,128)(2,1)}, u32[]{:S(2)}, u32[]{:S(2)}) collective-permute-start(bf16[128,2048]{1,0:T(8,128)(2,1)S(1)} %copy-done.19), channel_id=1, source_target_pairs={{0,1},{1,2},{2,3},{3,0},{4,5},{5,6},{6,7},{7,4},{8,9},{9,10},{10,1... | collective-permute-start | bytes 1572872 | tf_op jit(solution)/shard_map/ppermute | solution.py:101
  81.9 44.0 %all-to-all-start = ((bf16[3,8,88,256]{3,2,0,1:T(8,128)(2,1)}), bf16[3,8,88,256]{3,2,0,1:T(8,128)(2,1)}, u32[]{:S(2)}, u32[]{:S(2)}) async-start(bf16[3,8,88,256]{3,2,0,1:T(8,128)(2,1)} %pad_maximum_fusion.3), calls=%async_computation | async-start | bytes 2162688 | tf_op jit(solution)/shard_map/all_to_all | solution.py:775
  86.1 194.9 %all-gather.9.cloned.1.call-start = ((), (), s32[]{:S(2)}) async-start(), calls=%async_computation.8 | async-start | bytes 9437184 | tf_op jit(solution)/shard_map/all_gather | solution.py:814
  149.9 16.8 %collective-permute-start.6 = (bf16[128,2048]{1,0:T(8,128)(2,1)S(1)}, bf16[128,2048]{1,0:T(8,128)(2,1)S(1)}, u32[]{:S(2)}, u32[]{:S(2)}) collective-permute-start(bf16[128,2048]{1,0:T(8,128)(2,1)S(1)} %get-tuple-element.162), channel_id=1, source_target_pairs={{0,1},{1,2},{2,3},{3,0},{4,5},{5,6},{6,7},{7,4},{8,9},{9,10},{10,1... | collective-permute-start | bytes 1572872 | tf_op jit(solution)/shard_map/ppermute | solution.py:114
  152.6 23.7 %collective-permute-start.8 = (bf16[128,2048]{1,0:T(8,128)(2,1)S(1)}, bf16[128,2048]{1,0:T(8,128)(2,1)S(1)}, u32[]{:S(2)}, u32[]{:S(2)}) collective-permute-start(bf16[128,2048]{1,0:T(8,128)(2,1)S(1)} %get-tuple-element.163), channel_id=1, source_target_pairs={{0,3},{1,0},{2,1},{3,2},{4,7},{5,4},{6,5},{7,6},{8,11},{9,8},{10,9... | collective-permute-start | bytes 1572872 | tf_op jit(solution)/shard_map/ppermute | solution.py:114
  153.8 44.5 %collective-permute-start.7 = (bf16[128,2048]{1,0:T(8,128)(2,1)S(1)}, bf16[128,2048]{1,0:T(8,128)(2,1)S(1)}, u32[]{:S(2)}, u32[]{:S(2)}) collective-permute-start(bf16[128,2048]{1,0:T(8,128)(2,1)S(1)} %get-tuple-element.164), channel_id=1, source_target_pairs={{0,2},{1,3},{2,0},{3,1},{4,6},{5,7},{6,4},{7,5},{8,10},{9,11},{10,... | collective-permute-start | bytes 1572872 | tf_op jit(solution)/shard_map/ppermute | solution.py:114
  162.3 38.1 %copy-start.52 = (f32[2048]{0:T(1024)S(1)}, f32[2048]{0:T(1024)}, u32[]{:S(2)}) copy-start(f32[2048]{0:T(1024)} %param.28) | copy-start | bytes 24580
  201.3 20.2 %collective-permute-start.13 = (bf16[64,2048]{1,0:T(8,128)(2,1)S(1)}, bf16[64,2048]{1,0:T(8,128)(2,1)S(1)}, u32[]{:S(2)}, u32[]{:S(2)}) collective-permute-start(bf16[64,2048]{1,0:T(8,128)(2,1)S(1)} %get-tuple-element.181), channel_id=1, source_target_pairs={{0,2},{1,3},{2,0},{3,1},{4,6},{5,7},{6,4},{7,5},{8,10},{9,11},{10,... | collective-permute-start | bytes 786440 | tf_op jit(solution)/shard_map/ppermute | solution.py:101
  201.4 16.9 %collective-permute-start.12 = (bf16[64,2048]{1,0:T(8,128)(2,1)S(1)}, bf16[64,2048]{1,0:T(8,128)(2,1)S(1)}, u32[]{:S(2)}, u32[]{:S(2)}) collective-permute-start(bf16[64,2048]{1,0:T(8,128)(2,1)S(1)} %get-tuple-element.181), channel_id=1, source_target_pairs={{0,1},{1,2},{2,3},{3,0},{4,5},{5,6},{6,7},{7,4},{8,9},{9,10},{10,1... | collective-permute-start | bytes 786440 | tf_op jit(solution)/shard_map/ppermute | solution.py:101
  205.9 17.1 %collective-permute-start.14 = (bf16[64,2048]{1,0:T(8,128)(2,1)S(1)}, bf16[64,2048]{1,0:T(8,128)(2,1)S(1)}, u32[]{:S(2)}, u32[]{:S(2)}) collective-permute-start(bf16[64,2048]{1,0:T(8,128)(2,1)S(1)} %get-tuple-element.181), channel_id=1, source_target_pairs={{0,3},{1,0},{2,1},{3,2},{4,7},{5,4},{6,5},{7,6},{8,11},{9,8},{10,9... | collective-permute-start | bytes 786440 | tf_op jit(solution)/shard_map/ppermute | solution.py:101
  224.1 113.7 %all-gather.11.cloned.1.call-start = ((), (), s32[]{:S(2)}) async-start(), calls=%async_computation.9 | async-start | bytes 9437184 | tf_op jit(solution)/shard_map/all_gather | solution.py:814
  224.1 11.3 %collective-permute-start.9 = (bf16[64,2048]{1,0:T(8,128)(2,1)S(1)}, bf16[64,2048]{1,0:T(8,128)(2,1)S(1)}, u32[]{:S(2)}, u32[]{:S(2)}) collective-permute-start(bf16[64,2048]{1,0:T(8,128)(2,1)S(1)} %get-tuple-element.183), channel_id=1, source_target_pairs={{0,1},{1,2},{2,3},{3,0},{4,5},{5,6},{6,7},{7,4},{8,9},{9,10},{10,1... | collective-permute-start | bytes 786440 | tf_op jit(solution)/shard_map/ppermute | solution.py:101
  228.8 15.2 %collective-permute-start.10 = (bf16[64,2048]{1,0:T(8,128)(2,1)S(1)}, bf16[64,2048]{1,0:T(8,128)(2,1)S(1)}, u32[]{:S(2)}, u32[]{:S(2)}) collective-permute-start(bf16[64,2048]{1,0:T(8,128)(2,1)S(1)} %get-tuple-element.183), channel_id=1, source_target_pairs={{0,2},{1,3},{2,0},{3,1},{4,6},{5,7},{6,4},{7,5},{8,10},{9,11},{10,... | collective-permute-start | bytes 786440 | tf_op jit(solution)/shard_map/ppermute | solution.py:101
  229.0 16.8 %collective-permute-start.11 = (bf16[64,2048]{1,0:T(8,128)(2,1)S(1)}, bf16[64,2048]{1,0:T(8,128)(2,1)S(1)}, u32[]{:S(2)}, u32[]{:S(2)}) collective-permute-start(bf16[64,2048]{1,0:T(8,128)(2,1)S(1)} %get-tuple-element.183), channel_id=1, source_target_pairs={{0,3},{1,0},{2,1},{3,2},{4,7},{5,4},{6,5},{7,6},{8,11},{9,8},{10,9... | collective-permute-start | bytes 786440 | tf_op jit(solution)/shard_map/ppermute | solution.py:101
  245.8 35.2 %copy-start.28 = (bf16[256,2048]{1,0:T(8,128)(2,1)}, bf16[256,2048]{1,0:T(8,128)(2,1)S(1)}, u32[]{:S(2)}) copy-start(bf16[256,2048]{1,0:T(8,128)(2,1)S(1)} %constant_dynamic-update-slice_fusion.12) | copy-start | bytes 3145732
  281.0 134.0 %reduce-scatter.5.cloned.1.call-start = ((), (), s32[]{:S(2)}) async-start(), calls=%async_computation.10 | async-start | bytes 10027008 | tf_op jit(solution)/shard_map/reduce_scatter | solution.py:819
  337.8 175.7 %reduce-scatter.7.cloned.1.call-start = ((), (), s32[]{:S(2)}) async-start(), calls=%async_computation.11 | async-start | bytes 10027008 | tf_op jit(solution)/shard_map/reduce_scatter | solution.py:819
  415.1 213.7 %reduce-scatter.9.cloned.1.call-start = ((), (), s32[]{:S(2)}) async-start(), calls=%async_computation.12 | async-start | bytes 18874368 | tf_op jit(solution)/shard_map/reduce_scatter | solution.py:854
  416.3 27.2 %collective-permute-start.18 = (bf16[64,2176]{1,0:T(8,128)(2,1)S(1)}, bf16[64,2176]{1,0:T(8,128)(2,1)S(1)}, u32[]{:S(2)}, u32[]{:S(2)}) collective-permute-start(bf16[64,2176]{1,0:T(8,128)(2,1)S(1)} %get-tuple-element.168), channel_id=1, source_target_pairs={{0,1},{1,2},{2,3},{3,0},{4,5},{5,6},{6,7},{7,4},{8,9},{9,10},{10,1... | collective-permute-start | bytes 835592 | tf_op jit(solution)/shard_map/ppermute | solution.py:114
  417.9 25.7 %collective-permute-start.20 = (bf16[64,2176]{1,0:T(8,128)(2,1)S(1)}, bf16[64,2176]{1,0:T(8,128)(2,1)S(1)}, u32[]{:S(2)}, u32[]{:S(2)}) collective-permute-start(bf16[64,2176]{1,0:T(8,128)(2,1)S(1)} %get-tuple-element.169), channel_id=1, source_target_pairs={{0,3},{1,0},{2,1},{3,2},{4,7},{5,4},{6,5},{7,6},{8,11},{9,8},{10,9... | collective-permute-start | bytes 835592 | tf_op jit(solution)/shard_map/ppermute | solution.py:114
  420.2 24.3 %collective-permute-start.19 = (bf16[64,2176]{1,0:T(8,128)(2,1)S(1)}, bf16[64,2176]{1,0:T(8,128)(2,1)S(1)}, u32[]{:S(2)}, u32[]{:S(2)}) collective-permute-start(bf16[64,2176]{1,0:T(8,128)(2,1)S(1)} %get-tuple-element.170), channel_id=1, source_target_pairs={{0,2},{1,3},{2,0},{3,1},{4,6},{5,7},{6,4},{7,5},{8,10},{9,11},{10,... | collective-permute-start | bytes 835592 | tf_op jit(solution)/shard_map/ppermute | solution.py:114
  445.4 41.1 %copy-start.5 = (bf16[896,2048]{1,0:T(8,128)(2,1)S(1)}, bf16[896,2048]{1,0:T(8,128)(2,1)}, u32[]{:S(2)}) copy-start(bf16[896,2048]{1,0:T(8,128)(2,1)} %maximum_maximum_fusion.refs_0_.wd_ref) | copy-start | bytes 11010052
  513.5 29.9 %copy-start.33 = (f32[64,2176]{1,0:T(8,128)S(1)}, f32[64,2176]{1,0:T(8,128)}, u32[]{:S(2)}) copy-start(f32[64,2176]{1,0:T(8,128)} %convert_add_fusion.3.refs_3_) | copy-start | bytes 1671172
  513.6 221.7 %reduce-scatter.11.cloned.1.call-start = ((), (), s32[]{:S(2)}) async-start(), calls=%async_computation.13 | async-start | bytes 10027008 | tf_op jit(solution)/shard_map/reduce_scatter | solution.py:899
  514.8 11.4 %collective-permute-start.24 = (bf16[64,2176]{1,0:T(8,128)(2,1)S(1)}, bf16[64,2176]{1,0:T(8,128)(2,1)S(1)}, u32[]{:S(2)}, u32[]{:S(2)}) collective-permute-start(bf16[64,2176]{1,0:T(8,128)(2,1)S(1)} %get-tuple-element.165), channel_id=1, source_target_pairs={{0,1},{1,2},{2,3},{3,0},{4,5},{5,6},{6,7},{7,4},{8,9},{9,10},{10,1... | collective-permute-start | bytes 835592 | tf_op jit(solution)/shard_map/ppermute | solution.py:114
  515.7 14.0 %collective-permute-start.26 = (bf16[64,2176]{1,0:T(8,128)(2,1)S(1)}, bf16[64,2176]{1,0:T(8,128)(2,1)S(1)}, u32[]{:S(2)}, u32[]{:S(2)}) collective-permute-start(bf16[64,2176]{1,0:T(8,128)(2,1)S(1)} %get-tuple-element.166), channel_id=1, source_target_pairs={{0,3},{1,0},{2,1},{3,2},{4,7},{5,4},{6,5},{7,6},{8,11},{9,8},{10,9... | collective-permute-start | bytes 835592 | tf_op jit(solution)/shard_map/ppermute | solution.py:114
  518.7 23.6 %collective-permute-start.25 = (bf16[64,2176]{1,0:T(8,128)(2,1)S(1)}, bf16[64,2176]{1,0:T(8,128)(2,1)S(1)}, u32[]{:S(2)}, u32[]{:S(2)}) collective-permute-start(bf16[64,2176]{1,0:T(8,128)(2,1)S(1)} %get-tuple-element.167), channel_id=1, source_target_pairs={{0,2},{1,3},{2,0},{3,1},{4,6},{5,7},{6,4},{7,5},{8,10},{9,11},{10,... | collective-permute-start | bytes 835592 | tf_op jit(solution)/shard_map/ppermute | solution.py:114
  520.4 23.4 %copy-start.15 = (f32[128,2048]{1,0:T(8,128)S(1)}, f32[128,2048]{1,0:T(8,128)}, u32[]{:S(2)}) copy-start(f32[128,2048]{1,0:T(8,128)} %copy-done.14) | copy-start | bytes 3145732
  520.4 23.4 %copy-start.53 = (f32[2048]{0:T(1024)S(1)}, f32[2048]{0:T(1024)}, u32[]{:S(2)}) copy-start(f32[2048]{0:T(1024)} %param.28) | copy-start | bytes 24580
  548.1 17.1 %collective-permute-start.27 = (bf16[128,2048]{1,0:T(8,128)(2,1)}, bf16[128,2048]{1,0:T(8,128)(2,1)}, u32[]{:S(2)}, u32[]{:S(2)}) collective-permute-start(bf16[128,2048]{1,0:T(8,128)(2,1)} %get-tuple-element.153), channel_id=1, source_target_pairs={{0,1},{1,2},{2,3},{3,0},{4,5},{5,6},{6,7},{7,4},{8,9},{9,10},{10,1... | collective-permute-start | bytes 1572872 | tf_op jit(solution)/shard_map/ppermute | solution.py:101
  548.1 37.7 %collective-permute-start.28 = (bf16[128,2048]{1,0:T(8,128)(2,1)}, bf16[128,2048]{1,0:T(8,128)(2,1)}, u32[]{:S(2)}, u32[]{:S(2)}) collective-permute-start(bf16[128,2048]{1,0:T(8,128)(2,1)} %get-tuple-element.153), channel_id=1, source_target_pairs={{0,2},{1,3},{2,0},{3,1},{4,6},{5,7},{6,4},{7,5},{8,10},{9,11},{10,... | collective-permute-start | bytes 1572872 | tf_op jit(solution)/shard_map/ppermute | solution.py:101
  551.7 35.3 %collective-permute-start.29 = (bf16[128,2048]{1,0:T(8,128)(2,1)}, bf16[128,2048]{1,0:T(8,128)(2,1)S(1)}, u32[]{:S(2)}, u32[]{:S(2)}) collective-permute-start(bf16[128,2048]{1,0:T(8,128)(2,1)} %get-tuple-element.153), channel_id=1, source_target_pairs={{0,3},{1,0},{2,1},{3,2},{4,7},{5,4},{6,5},{7,6},{8,11},{9,8},{10,9... | collective-permute-start | bytes 1572872 | tf_op jit(solution)/shard_map/ppermute | solution.py:101
  632.1 22.9 %collective-permute-start.30 = (bf16[128,2048]{1,0:T(8,128)(2,1)}, bf16[128,2048]{1,0:T(8,128)(2,1)S(1)}, u32[]{:S(2)}, u32[]{:S(2)}) collective-permute-start(bf16[128,2048]{1,0:T(8,128)(2,1)} %get-tuple-element.156), channel_id=1, source_target_pairs={{0,1},{1,2},{2,3},{3,0},{4,5},{5,6},{6,7},{7,4},{8,9},{9,10},{10,1... | collective-permute-start | bytes 1572872 | tf_op jit(solution)/shard_map/ppermute | solution.py:114
  641.6 35.4 %collective-permute-start.32 = (bf16[128,2048]{1,0:T(8,128)(2,1)}, bf16[128,2048]{1,0:T(8,128)(2,1)S(1)}, u32[]{:S(2)}, u32[]{:S(2)}) collective-permute-start(bf16[128,2048]{1,0:T(8,128)(2,1)} %get-tuple-element.157), channel_id=1, source_target_pairs={{0,3},{1,0},{2,1},{3,2},{4,7},{5,4},{6,5},{7,6},{8,11},{9,8},{10,9... | collective-permute-start | bytes 1572872 | tf_op jit(solution)/shard_map/ppermute | solution.py:114
  641.6 58.0 %collective-permute-start.31 = (bf16[128,2048]{1,0:T(8,128)(2,1)}, bf16[128,2048]{1,0:T(8,128)(2,1)S(1)}, u32[]{:S(2)}, u32[]{:S(2)}) collective-permute-start(bf16[128,2048]{1,0:T(8,128)(2,1)} %get-tuple-element.158), channel_id=1, source_target_pairs={{0,2},{1,3},{2,0},{3,1},{4,6},{5,7},{6,4},{7,5},{8,10},{9,11},{10,... | collective-permute-start | bytes 1572872 | tf_op jit(solution)/shard_map/ppermute | solution.py:114
  644.2 56.3 %copy-start.20 = (bf16[128,2048]{1,0:T(8,128)(2,1)S(1)}, bf16[128,2048]{1,0:T(8,128)(2,1)}, u32[]{:S(2)}) copy-start(bf16[128,2048]{1,0:T(8,128)(2,1)} %param.18) | copy-start | bytes 1572868
  644.2 56.3 %copy-start.51 = (f32[2048]{0:T(1024)S(1)}, f32[2048]{0:T(1024)}, u32[]{:S(2)}) copy-start(f32[2048]{0:T(1024)} %param.22) | copy-start | bytes 24580
  644.2 57.9 %all-to-all-start.1 = ((bf16[3,8,88,256]{3,2,0,1:T(8,128)(2,1)}), bf16[3,8,88,256]{3,2,0,1:T(8,128)(2,1)S(1)}, u32[]{:S(2)}, u32[]{:S(2)}) async-start(bf16[3,8,88,256]{3,2,0,1:T(8,128)(2,1)} %maximum_bitcast_fusion), calls=%async_computation.5 | async-start | bytes 2162688 | tf_op jit(solution)/shard_map/all_to_all | solution.py:875
  651.1 52.4 %collective-permute-start.21 = (bf16[128,2048]{1,0:T(8,128)(2,1)}, bf16[128,2048]{1,0:T(8,128)(2,1)}, u32[]{:S(2)}, u32[]{:S(2)}) collective-permute-start(bf16[128,2048]{1,0:T(8,128)(2,1)} %get-tuple-element.159), channel_id=1, source_target_pairs={{0,1},{1,2},{2,3},{3,0},{4,5},{5,6},{6,7},{7,4},{8,9},{9,10},{10,1... | collective-permute-start | bytes 1572872 | tf_op jit(solution)/shard_map/ppermute | solution.py:114
  652.2 51.3 %collective-permute-start.23 = (bf16[128,2048]{1,0:T(8,128)(2,1)}, bf16[128,2048]{1,0:T(8,128)(2,1)}, u32[]{:S(2)}, u32[]{:S(2)}) collective-permute-start(bf16[128,2048]{1,0:T(8,128)(2,1)} %get-tuple-element.160), channel_id=1, source_target_pairs={{0,3},{1,0},{2,1},{3,2},{4,7},{5,4},{6,5},{7,6},{8,11},{9,8},{10,9... | collective-permute-start | bytes 1572872 | tf_op jit(solution)/shard_map/ppermute | solution.py:114
  654.9 44.8 %copy-start.34 = (bf16[128,2048]{1,0:T(8,128)(2,1)}, bf16[128,2048]{1,0:T(8,128)(2,1)S(1)}, u32[]{:S(2)}) copy-start(bf16[128,2048]{1,0:T(8,128)(2,1)S(1)} %collective-permute-done.30) | copy-start | bytes 1572868
  654.9 76.3 %collective-permute-start.22 = (bf16[128,2048]{1,0:T(8,128)(2,1)}, bf16[128,2048]{1,0:T(8,128)(2,1)}, u32[]{:S(2)}, u32[]{:S(2)}) collective-permute-start(bf16[128,2048]{1,0:T(8,128)(2,1)} %get-tuple-element.161), channel_id=1, source_target_pairs={{0,2},{1,3},{2,0},{3,1},{4,6},{5,7},{6,4},{7,5},{8,10},{9,11},{10,... | collective-permute-start | bytes 1572872 | tf_op jit(solution)/shard_map/ppermute | solution.py:114
  702.0 29.2 %copy-start.16 = (f32[128,2048]{1,0:T(8,128)S(1)}, f32[128,2048]{1,0:T(8,128)}, u32[]{:S(2)}) copy-start(f32[128,2048]{1,0:T(8,128)} %copy-done.14) | copy-start | bytes 3145732
  702.0 29.2 %copy-start.25 = (bf16[128,2048]{1,0:T(8,128)(2,1)S(1)}, bf16[128,2048]{1,0:T(8,128)(2,1)}, u32[]{:S(2)}) copy-start(bf16[128,2048]{1,0:T(8,128)(2,1)} %param.19) | copy-start | bytes 1572868
  702.0 29.2 %copy-start.60 = (f32[128]{0:T(128)S(1)}, f32[128]{0:T(128)}, u32[]{:S(2)}) copy-start(f32[128]{0:T(128)} %copy-done.58) | copy-start | bytes 1540
  702.1 29.2 %copy-start.64 = (f32[128]{0:T(128)S(1)}, f32[128]{0:T(128)}, u32[]{:S(2)}) copy-start(f32[128]{0:T(128)} %copy-done.63) | copy-start | bytes 1540
  702.1 29.2 %copy-start.27 = (f32[128,2048]{1,0:T(8,128)S(1)}, f32[128,2048]{1,0:T(8,128)}, u32[]{:S(2)}) copy-start(f32[128,2048]{1,0:T(8,128)} %copy-done.26) | copy-start | bytes 3145732
  702.1 29.2 %copy-start.35 = (bf16[128,2048]{1,0:T(8,128)(2,1)S(1)}, bf16[128,2048]{1,0:T(8,128)(2,1)}, u32[]{:S(2)}) copy-start(bf16[128,2048]{1,0:T(8,128)(2,1)} %copy-done.34) | copy-start | bytes 1572868
  702.1 29.2 %copy-start.37 = (bf16[128,2048]{1,0:T(8,128)(2,1)S(1)}, bf16[128,2048]{1,0:T(8,128)(2,1)}, u32[]{:S(2)}) copy-start(bf16[128,2048]{1,0:T(8,128)(2,1)} %copy-done.36) | copy-start | bytes 1572868
  702.1 29.2 %copy-start.39 = (bf16[128,2048]{1,0:T(8,128)(2,1)S(1)}, bf16[128,2048]{1,0:T(8,128)(2,1)}, u32[]{:S(2)}) copy-start(bf16[128,2048]{1,0:T(8,128)(2,1)} %copy-done.38) | copy-start | bytes 1572868
  737.4 7.2 collective-permute-start.33
  737.8 6.8 collective-permute-start.35
  741.2 6.7 collective-permute-start.34
  (48 other events, 234.1 us)
Sparse Core Ops, SparseCore 0:
  22.8 57.2 all-gather.4
  82.6 100.0 all-gather.6
  224.2 56.7 all-gather.8
  283.3 54.3 all-gather.10
  341.2 73.7 reduce-scatter.4
  418.5 73.7 reduce-scatter.6
  513.7 115.0 reduce-scatter.8
  632.3 76.5 reduce-scatter.10

commit v3 on v2

--- a/solution.py
+++ b/solution.py
@@ -2,6 +2,7 @@
 
 import jax
 import jax.numpy as jnp
+import numpy as np
 from jax import lax
 from jax.experimental import pallas as pl
 from jax.experimental.pallas import tpu as pltpu
@@ -104,24 +105,42 @@
     return whole
 
 
-def scatter_ctx(value):
+def pieces_ctx(value):
     lanes, lane = (lax.axis_size("ctx"), lax.axis_index("ctx"))
     rows = value.shape[0] // lanes
-    total = lax.dynamic_slice_in_dim(value, lane * rows, rows, 0).astype(jnp.float32)
+    got = [lax.dynamic_slice_in_dim(value, lane * rows, rows, 0)]
     for hop in range(1, lanes):
         target = lax.rem(lane + hop, lanes)
         part = lax.dynamic_slice_in_dim(value, target * rows, rows, 0)
-        got = lax.ppermute(part, "ctx", [(i, (i + hop) % lanes) for i in range(lanes)])
-        total = total + got.astype(jnp.float32)
+        got.append(lax.ppermute(part, "ctx", [(i, (i + hop) % lanes) for i in range(lanes)]))
+    return got
+
+
+def total_of(pieces):
+    total = pieces[0].astype(jnp.float32)
+    for piece in pieces[1:]:
+        total = total + piece.astype(jnp.float32)
     return total
+
+
+def scatter_ctx(value):
+    return total_of(pieces_ctx(value))
+
+
+def spread_ctx(value):
+    lanes = lax.axis_size("ctx")
+    return [value] + [
+        lax.ppermute(value, "ctx", [(i, (i + hop) % lanes) for i in range(lanes)])
+        for hop in range(1, lanes)
+    ]
 
 
 class Plan:
     def __init__(self, exp_dev, hidden, shared, experts, top):
-        self.exp_dev, self.hidden, self.experts, self.top = (exp_dev, hidden, experts, top)
+        self.exp_dev, self.hidden, self.experts, self.top = (2 * exp_dev, hidden, experts, top)
         self.units = exp_dev * hidden
         self.shared = -(-shared // 8) * 8
-        at = self.units + self.shared
+        at = 2 * (self.units + self.shared)
         if at // 128 != (at + experts - 1) // 128:
             at = -(-at // 128) * 128
         self.router = at
@@ -146,7 +165,6 @@
     dout = dout_ref[...].reshape(rows, model)
     lanes = lax.broadcasted_iota(jnp.int32, (rows, 128), 1)
     off = plan.router - plan.block
-    first = first_ref[0]
     sums = [jnp.zeros((rows, 128), f32) for _ in range(plan.exp_dev)]
 
     def elements(own, at, gate, upper, act_grad, gate_at, up_at):
@@ -190,7 +208,7 @@
     chosen = sig * member
     gates = ROUTE_SCALE * chosen / jnp.sum(chosen, axis=1, keepdims=True)
     own = [
-        jnp.sum(jnp.where(lanes - off == first + e, gates, 0.0), axis=1, keepdims=True)
+        jnp.sum(jnp.where(lanes - off == first_ref[e], gates, 0.0), axis=1, keepdims=True)
         for e in range(plan.exp_dev)
     ]
     act_grad = dot_nt(dout, wd_ref[even : even + tail, :])
@@ -213,8 +231,8 @@
     for e in range(plan.exp_dev):
         grad = jnp.sum(sums[e], axis=1, keepdims=True)
         high = grad.astype(bf16).astype(f32)
-        ends = jnp.where(lanes == first + e, high, ends)
-        ends = jnp.where(lanes == plan.experts + first + e, grad - high, ends)
+        ends = jnp.where(lanes == first_ref[e], high, ends)
+        ends = jnp.where(lanes == plan.experts + first_ref[e], grad - high, ends)
     rows_ref[:, model:] = ends.astype(bf16)
 
 
@@ -292,7 +310,7 @@
         out_specs=pl.BlockSpec((None, lanes, None, rows, model), lambda h, g: (g, 0, h, 0, 0)),
         out_shape=jax.ShapeDtypeStruct((groups, lanes, chunks, rows, model), jnp.bfloat16),
         compiler_params=pltpu.CompilerParams(
-            dimension_semantics=("arbitrary", "arbitrary"), vmem_limit_bytes=32 * MIB
+            dimension_semantics=("arbitrary", "arbitrary"), vmem_limit_bytes=60 * MIB
         ),
         cost_estimate=pl.CostEstimate(
             flops=2 * chunks * tokens * cols * model,
@@ -303,120 +321,110 @@
     )(act, wd, *others).reshape(groups * lanes * chunks * rows, model)
 
 
-def sum_kernel(plan, h_ref, z_ref, out_ref, shared_ref):
-    @pl.when((pl.program_id(0) == 0) & (pl.program_id(1) == 0))
+def sum_kernel(plan, kind, chunks, h_ref, *refs):
+    z_refs = refs[:chunks]
+    out_ref, shared_ref, other_ref, other_shared_ref, total_ref = refs[-5:]
+    chunk = pl.program_id(0)
+
+    @pl.when((chunk == 0) & (pl.program_id(1) == 0))
     def _():
         out_ref[...] = jnp.zeros_like(out_ref)
         shared_ref[...] = jnp.zeros_like(shared_ref)
-
-    h = h_ref[...]
-    rows, model = (h.shape[0], z_ref.shape[2])
+        total_ref[...] = jnp.zeros_like(total_ref)
+
+    even, tail, units, shared = (plan.even, plan.tail, plan.units, plan.shared)
+    model = out_ref.shape[1]
     step = 512
-    for at in range(0, model, step):
-        part = dot_tn(h, z_ref[:, :, at : at + step].reshape(rows, step))
-        out_ref[:, at : at + step] += part[: plan.units]
-        shared_ref[:, at : at + step] += part[plan.units : plan.units + plan.shared]
-
-
-def down_sum(plan, model, act, dout):
-    chunks, tokens, cols = act.shape
-    rows = dout.shape[2]
-    tile = min(512, tokens)
-    shapes = [(plan.units, model), (plan.shared, model)]
+
+    def add(z_ref):
+        h = h_ref[...]
+        for at in range(0, model, step):
+            cut = slice(at, at + step)
+            if len(z_ref.shape) == 2:
+                z = z_ref[:, cut]
+            else:
+                z = z_ref[:, :, cut].reshape(h.shape[0], step)
+            part = dot_tn(h, z)
+            if kind == "up":
+                part = jnp.concatenate([part[tail:], part[:tail]])
+            out_ref[:, cut] += part[:units]
+            total_ref[:units, cut] += part[units : 2 * units]
+            shared_ref[:, cut] += part[2 * units : 2 * units + shared]
+            total_ref[units:, cut] += part[2 * units + shared : 2 * (units + shared)]
+
+    for h, z_ref in enumerate(z_refs):
+        pl.when(chunk == h)(functools.partial(add, z_ref))
+
+    @pl.when((chunk == chunks - 1) & (pl.program_id(1) == pl.num_programs(1) - 1))
+    def _():
+        other_ref[...] = total_ref[:units].astype(jnp.bfloat16)
+        other_shared_ref[...] = total_ref[units:].astype(jnp.bfloat16)
+
+
+def weight_sum(plan, kind, model, hidden, rows, *others):
+    chunks, tokens, width = hidden.shape
+    cols = plan.cols
+    tile = min(512, tokens) if chunks <= 2 else 256
+    steps = tokens // tile
+    shapes = [(plan.units, model), (plan.shared, model)] * 2
+    types = [jnp.float32] * 2 + [jnp.bfloat16] * 2
+    half = 1 if kind == "up" else 0
+
+    def turn_of(h, c, i):
+        return jnp.where(c == h, i, jnp.where(c < h, 0, steps - 1))
+
+    if isinstance(rows, list):
+        specs = [
+            pl.BlockSpec((tile, model), lambda c, i, h=h: (turn_of(h, c, i), 0))
+            for h in range(chunks)
+        ]
+    else:
+        part = rows.shape[2]
+        specs = [
+            pl.BlockSpec(
+                (tile // part, None, part, model), lambda c, i, h=h: (turn_of(h, c, i), h, 0, 0)
+            )
+            for h in range(chunks)
+        ]
+        rows = [rows] * chunks
     return pl.pallas_call(
-        functools.partial(sum_kernel, plan),
-        grid=(chunks, tokens // tile),
-        in_specs=[
-            pl.BlockSpec((None, tile, cols), lambda h, i: (h, i, 0)),
-            pl.BlockSpec((tile // rows, None, rows, model), lambda h, i: (i, h, 0, 0)),
+        functools.partial(sum_kernel, plan, kind, chunks),
+        grid=(chunks, steps),
+        in_specs=[pl.BlockSpec((None, tile, cols), lambda c, i: (c, i, half))]
+        + specs
+        + [pl.BlockSpec(memory_space=pl.ANY) for _ in others],
+        out_specs=[
+            pl.BlockSpec(s, lambda c, i: (0, 0), pipeline_mode=pl.Buffered(1)) for s in shapes
         ],
-        out_specs=[pl.BlockSpec(s, lambda h, i: (0, 0)) for s in shapes],
-        out_shape=[jax.ShapeDtypeStruct(s, jnp.float32) for s in shapes],
+        out_shape=[jax.ShapeDtypeStruct(*s) for s in zip(shapes, types)],
+        scratch_shapes=[pltpu.VMEM((plan.units + plan.shared, model), jnp.float32)],
         compiler_params=pltpu.CompilerParams(
-            dimension_semantics=("arbitrary", "arbitrary"), vmem_limit_bytes=48 * MIB
+            dimension_semantics=("arbitrary", "arbitrary"), vmem_limit_bytes=58 * MIB
         ),
         cost_estimate=pl.CostEstimate(
             flops=2 * chunks * tokens * cols * model,
             bytes_accessed=2 * chunks * tokens * (model + cols) + 4 * plan.units * model,
             transcendentals=0,
         ),
-        name="down_sum",
-    )(act, dout)
-
-
-def pair_kernel(plan, chunks, h_ref, *refs):
-    mid_refs, (gate_ref, up_ref, shared_ref) = (refs[:chunks], refs[-3:])
-    chunk = pl.program_id(0)
-
-    @pl.when((chunk == 0) & (pl.program_id(1) == 0))
-    def _():
-        gate_ref[...] = jnp.zeros_like(gate_ref)
-        up_ref[...] = jnp.zeros_like(up_ref)
-        shared_ref[...] = jnp.zeros_like(shared_ref)
-
-    even, tail, units, shared = (plan.even, plan.tail, plan.units, plan.shared)
-    second = even + 2 * tail
-    step = 256
-
-    def add(z_ref):
-        h = h_ref[...]
-        for at in range(0, z_ref.shape[1], step):
-            cut = slice(at, at + step)
-            part = dot_tn(h, z_ref[:, cut])
-            gate_ref[:, cut] += part[:units]
-            lead = min(units, even)
-            up_ref[:lead, cut] += part[second : second + lead]
-            if units > even:
-                up_ref[even:, cut] += part[even + tail : tail + units]
-            joint = jnp.concatenate([part[second:], part[even + tail : second]])
-            shared_ref[0, :, cut] += part[units : units + shared]
-            shared_ref[1, :, cut] += joint[units : units + shared]
-
-    for h, z_ref in enumerate(mid_refs):
-        pl.when(chunk == h)(functools.partial(add, z_ref))
-
-
-def pair_sum(plan, gud, mids, *others):
-    chunks, tokens, cols = gud.shape
-    model = mids[0].shape[1]
-    tile = min(512, tokens) if chunks <= 2 else 128
-    steps = tokens // tile
-    shapes = [(plan.units, model), (plan.units, model), (2, plan.shared, model)]
-
-    def part(h):
-        def place(c, i):
-            return (jnp.where(c == h, i, jnp.where(c < h, 0, steps - 1)), 0)
-
-        return pl.BlockSpec((tile, model), place)
-
-    return pl.pallas_call(
-        functools.partial(pair_kernel, plan, chunks),
-        grid=(chunks, steps),
-        in_specs=[pl.BlockSpec((None, tile, cols), lambda c, i: (c, i, 0))]
-        + [part(h) for h in range(chunks)]
-        + [pl.BlockSpec(memory_space=pl.ANY) for _ in others],
-        out_specs=[
-            pl.BlockSpec(s, lambda c, i, n=len(s): (0,) * n, pipeline_mode=pl.Buffered(1))
-            for s in shapes
-        ],
-        out_shape=[jax.ShapeDtypeStruct(s, jnp.float32) for s in shapes],
-        compiler_params=pltpu.CompilerParams(
-            dimension_semantics=("arbitrary", "arbitrary"), vmem_limit_bytes=58 * MIB
-        ),
-        cost_estimate=pl.CostEstimate(
-            flops=2 * chunks * tokens * cols * model,
-            bytes_accessed=2 * chunks * tokens * (model + cols) + 8 * plan.units * model,
-            transcendentals=0,
-        ),
-        name="pair_sum",
-    )(gud, *mids, *others)
-
-
-def pack_kernel(lead, x_ref, heads_grad_ref, latent_ref, qr_ref, heads_ref, kv_ref, extra_ref, out_ref):
+        name=kind + "_sum",
+    )(hidden, *rows, *others)
+
+
+def pack_kernel(lead, before, x_ref, heads_grad_ref, latent_ref, qr_ref, heads_ref, kv_ref, early_ref, gains_ref, *refs):
+    out_ref = refs[-1]
     bf16 = jnp.bfloat16
     first = dot_tn(x_ref[...], qr_ref[...])
     out_ref[:, : lead - 128] = first[:, : lead - 128].astype(bf16)
-    out_ref[:, lead - 128 : lead] = (first[:, lead - 128 :] + extra_ref[...].T).astype(bf16)
+    early, cols = early_ref.shape
+    small = jnp.concatenate(
+        [
+            jnp.zeros((before, cols), jnp.float32),
+            early_ref[...],
+            gains_ref[:2],
+            jnp.zeros((128 - before - early - 2, cols), jnp.float32),
+        ]
+    )
+    out_ref[:, lead - 128 : lead] = (first[:, lead - 128 :] + small.T).astype(bf16)
     latent = dot32(latent_ref[...], kv_ref[...])
     rows = latent.shape[0]
     pieces = out_ref.shape[0] // rows
@@ -428,7 +436,7 @@
     out_ref[:, lead + wide :] = dot_tn(heads_grad_ref[...], heads_ref[...]).astype(bf16)
 
 
-def packed_grads(groups, x_low, attn_low, latent_t, qr, heads_low, kv_grad, extra):
+def packed_grads(groups, before, x_low, attn_low, latent_t, qr, heads_low, kv_grad, early, gains, *others):
     count, model = x_low.shape
     depth = model // groups
     rows = latent_t.shape[0] // groups
@@ -440,7 +448,7 @@
         return pl.BlockSpec(value.shape, lambda i: (0, 0))
 
     return pl.pallas_call(
-        functools.partial(pack_kernel, lead),
+        functools.partial(pack_kernel, lead, before),
         grid=(groups,),
         in_specs=[
             pl.BlockSpec((count, depth), lambda i: (0, i)),
@@ -449,18 +457,74 @@
             whole(qr),
             whole(heads_low),
             whole(kv_grad),
-            pl.BlockSpec((128, depth), lambda i: (0, i)),
-        ],
+            pl.BlockSpec((early.shape[0], depth), lambda i: (0, i)),
+            pl.BlockSpec((8, depth), lambda i: (0, i)),
+        ]
+        + [pl.BlockSpec(memory_space=pl.ANY) for _ in others],
         out_specs=pl.BlockSpec((depth, cols), lambda i: (i, 0)),
         out_shape=jax.ShapeDtypeStruct((model, cols), jnp.bfloat16),
         compiler_params=pltpu.CompilerParams(
-            dimension_semantics=("arbitrary",), vmem_limit_bytes=40 * MIB
+            dimension_semantics=("arbitrary",), vmem_limit_bytes=60 * MIB
         ),
         cost_estimate=pl.CostEstimate(
             flops=2 * count * model * cols, bytes_accessed=16 * MIB, transcendentals=0
         ),
         name="packed_grads",
-    )(x_low, attn_low, latent_t, qr, heads_low, kv_grad, extra)
+    )(x_low, attn_low, latent_t, qr, heads_low, kv_grad, early, gains, *others)
+
+
+def finish_kernel(own_ref, other_ref, *refs):
+    refs[-1][...] = own_ref[...] + other_ref[...].astype(jnp.float32)
+
+
+def finished(own, other, *others):
+    rows, cols = own.shape
+    block = pl.BlockSpec((rows // 4, cols), lambda i: (i, 0))
+    return pl.pallas_call(
+        finish_kernel,
+        grid=(4,),
+        in_specs=[block, block] + [pl.BlockSpec(memory_space=pl.ANY) for _ in others],
+        out_specs=block,
+        out_shape=jax.ShapeDtypeStruct((rows, cols), jnp.float32),
+        input_output_aliases={0: 0},
+        compiler_params=pltpu.CompilerParams(
+            dimension_semantics=("arbitrary",), vmem_limit_bytes=48 * MIB
+        ),
+        cost_estimate=pl.CostEstimate(
+            flops=rows * cols, bytes_accessed=10 * rows * cols, transcendentals=0
+        ),
+        name="finished",
+    )(own, other, *others)
+
+
+def end_kernel(pieces_n, resid_ref, grad_ref, x_ref, gain_ref, *refs):
+    pieces, (out_ref, dx_ref) = (refs[:pieces_n], refs[-2:])
+    f32, bf16 = (jnp.float32, jnp.bfloat16)
+    model = x_ref.shape[1]
+    moe = pieces[0][:, :model].astype(f32)
+    dnormed = pieces[0][:, model:].astype(f32)
+    for piece in pieces[1:]:
+        moe = moe + piece[:, :model].astype(f32)
+        dnormed = dnormed + piece[:, model:].astype(f32)
+    out_ref[...] = (resid_ref[...] + moe).astype(bf16)
+    _, unit, factor = norm_parts(x_ref[...].astype(f32), gain_ref[...])
+    dx_ref[...] = (norm_back(dnormed, unit, factor, gain_ref[...]) + grad_ref[...]).astype(bf16)
+
+
+def ends(pieces, resid, resid_grad, x, gain, *others):
+    shape = jax.ShapeDtypeStruct(x.shape, jnp.bfloat16)
+    vmem = pl.BlockSpec(memory_space=pltpu.VMEM)
+    return pl.pallas_call(
+        functools.partial(end_kernel, len(pieces)),
+        in_specs=[vmem] * (4 + len(pieces)) + [pl.BlockSpec(memory_space=pl.ANY) for _ in others],
+        out_specs=[vmem] * 2,
+        out_shape=[shape] * 2,
+        compiler_params=pltpu.CompilerParams(vmem_limit_bytes=48 * MIB),
+        cost_estimate=pl.CostEstimate(
+            flops=20 * x.size, bytes_accessed=30 * x.size, transcendentals=0
+        ),
+        name="ends",
+    )(resid, resid_grad, x, gain, *pieces, *others)
 
 
 class Heads:
@@ -513,11 +577,24 @@
     return (seg_col_ref[...] == seg_row_ref[...]) & (cols <= rows)
 
 
-def attend_kernel(heads, extra, x_ref, w_ref, cos_ref, sin_ref, seg_col_ref, seg_row_ref, gain_ref, *refs):
-    q_ref, kv_ref, kr_ref, lat_ref, low_ref, lse_ref, heads_ref, attn_ref, expand_ref = refs[extra:]
+def attend_kernel(heads, lanes_n, chunks, extra, lane_ref, in_gain_ref, w_ref, cos_ref, sin_ref, seg_col_ref, seg_row_ref, gain_ref, *refs):
+    pieces = refs[:lanes_n]
+    refs = refs[lanes_n + extra :]
+    x_ref, x_low_ref, factor_ref, q_ref, kv_ref, kr_ref, lat_ref, low_t_ref, lse_ref, heads_ref = refs[:10]
+    attn_refs, expand_ref = (refs[10:-1], refs[-1])
     f32, bf16 = (jnp.float32, jnp.bfloat16)
     count = x_ref.shape[0]
-    x = x_ref[...]
+    block = count // lanes_n
+    for hop, piece in enumerate(pieces):
+        source = lax.rem(lane_ref[0] + lanes_n - hop, lanes_n)
+        rows = pl.ds(pl.multiple_of(source * block, block), block)
+        value = piece[...]
+        x_ref[rows, :] = value
+        value = value.astype(f32)
+        scale = lax.rsqrt(jnp.mean(value * value, axis=-1, keepdims=True) + EPS)
+        factor_ref[rows, :] = jnp.broadcast_to(scale, (block, 128))
+        x_low_ref[rows, :] = (value * scale * in_gain_ref[...]).astype(bf16)
+    x = x_low_ref[...]
     cosine, sine = (cos_ref[...], sin_ref[...])
     query = dot32(x, w_ref[:, : heads.query])
     first = query[:, heads.flat : heads.flat + 128]
@@ -530,7 +607,9 @@
     latent = latent[:, :LAT]
     lat_ref[...] = latent
     factor = lax.rsqrt(jnp.mean(latent * latent, axis=-1, keepdims=True) + EPS)
-    low_ref[...] = (latent * factor * gain_ref[...]).astype(bf16)
+    low = latent * factor * gain_ref[...]
+    low_t_ref[...] = low.T.astype(bf16)
+    low = low.astype(bf16)
     lanes = lax.broadcasted_iota(jnp.int32, (count, 128), 1)
     half = heads.half
 
@@ -543,7 +622,7 @@
     kr_ref[:, :128] = (first * cosine - second * sine).astype(bf16)
     kr_ref[:, 128:] = (second * cosine + first * sine).astype(bf16)
     expand_rows(heads, w_ref, expand_ref)
-    kv_ref[...] = dot32(low_ref[...], expand_ref[...]).astype(bf16)
+    kv_ref[...] = dot32(low, expand_ref[...]).astype(bf16)
     keep = allowed(seg_col_ref, seg_row_ref)
     wide_lanes = lax.broadcasted_iota(jnp.int32, (count, 256), 1)
     lse = jnp.zeros((count, 128), f32)
@@ -559,28 +638,40 @@
     lse_ref[...] = lse
     out = heads_ref[...]
     step = 512
-    for at in range(0, attn_ref.shape[1], step):
-        attn_ref[:, at : at + step] = dot_nt(out, w_ref[at : at + step, heads.output :]).astype(bf16)
-
-
-def attend(heads, x_low, packed, cosine, sine, seg_col, seg_row, gain, *others):
-    count, model = x_low.shape
+    rows, model = attn_refs[0].shape
+    part = rows // lanes_n
+    for at in range(0, model, step):
+        cut = slice(at, at + step)
+        piece = dot_nt(out, w_ref[cut, heads.output :]).astype(bf16)
+        for c in range(chunks):
+            for j in range(lanes_n):
+                start = (j * chunks + c) * part
+                attn_refs[c][j * part : (j + 1) * part, cut] = piece[start : start + part]
+
+
+def attend(heads, chunks, lane, in_gain, packed, cosine, sine, seg_col, seg_row, gain, pieces, *others):
+    lanes = len(pieces)
+    count, model = (seg_col.shape[0], packed.shape[0])
     kv_c, heads_c = (heads.width * (NOPE + VD), heads.width * VD)
     f32, bf16 = (jnp.float32, jnp.bfloat16)
     shapes = [
+        ((count, model), bf16),
+        ((count, model), bf16),
+        ((count, 128), f32),
         ((count, heads.query), bf16),
         ((count, kv_c), bf16),
         ((count, 256), bf16),
         ((count, LAT), f32),
-        ((count, LAT), bf16),
+        ((LAT, count), bf16),
         ((count, 128), f32),
         ((count, heads_c), bf16),
-        ((count, model), bf16),
-    ]
+    ] + [((count // chunks, model), bf16)] * chunks
     vmem = pl.BlockSpec(memory_space=pltpu.VMEM)
     return pl.pallas_call(
-        functools.partial(attend_kernel, heads, len(others)),
-        in_specs=[vmem] * 7 + [pl.BlockSpec(memory_space=pl.ANY) for _ in others],
+        functools.partial(attend_kernel, heads, lanes, chunks, len(others)),
+        in_specs=[pl.BlockSpec(memory_space=pltpu.SMEM)]
+        + [vmem] * (7 + lanes)
+        + [pl.BlockSpec(memory_space=pl.ANY) for _ in others],
         out_specs=[vmem] * len(shapes),
         out_shape=[jax.ShapeDtypeStruct(*s) for s in shapes],
         scratch_shapes=[pltpu.VMEM((LAT, kv_c), bf16)],
@@ -591,7 +682,7 @@
             transcendentals=heads.width * count * count,
         ),
         name="attend",
-    )(x_low, packed, cosine, sine, seg_col, seg_row, gain, *others)
+    )(lane, in_gain, packed, cosine, sine, seg_col, seg_row, gain, *pieces, *others)
 
 
 def attend_back_kernel(
@@ -613,7 +704,8 @@
     lse_ref,
     *refs,
 ):
-    qr_ref, kvg_ref, normed_ref, in_gain_ref, lat_gain_ref, expand_ref = refs[extra:]
+    spread_ref = refs[0]
+    qr_ref, kvg_ref, normed_ref, gains_ref, expand_ref = refs[1 + extra :]
     f32, bf16 = (jnp.float32, jnp.bfloat16)
     count, model = x_ref.shape
     half = heads.half
@@ -661,7 +753,13 @@
     latent = lat_ref[...]
     factor = lax.rsqrt(jnp.mean(latent * latent, axis=-1, keepdims=True) + EPS)
     unit = latent * factor
-    lat_gain_ref[...] = jnp.sum(dlow * unit, axis=0, keepdims=True)
+    lat_gain = jnp.broadcast_to(jnp.sum(dlow * unit, axis=0, keepdims=True), (8, LAT))
+    parts = []
+    for _ in range(3):
+        parts.append(lat_gain.astype(bf16).astype(f32))
+        lat_gain = lat_gain - parts[-1]
+    spread = dot32(jnp.concatenate(parts).astype(bf16), spread_ref[...])
+    gains_ref[...] = spread[:8] + spread[8:16] + spread[16:]
     dlatent = norm_back(dlow, unit, factor, gain_ref[...])
     qr_ref[:, heads.query : heads.query + LAT] = dlatent.astype(bf16)
     qr = qr_ref[...]
@@ -669,8 +767,8 @@
     for at in range(0, model, step):
         part = dot_nt(qr, w_ref[at : at + step, : heads.lead])
         normed_ref[:, at : at + step] = part.astype(bf16)
-        unit_in = x_ref[:, at : at + step].astype(f32) * factor_ref[...]
-        in_gain_ref[:, at : at + step] = jnp.sum(part * unit_in, axis=0, keepdims=True)
+        unit_in = x_ref[:, at : at + step].astype(f32) * factor_ref[:, :1]
+        gains_ref[:1, at : at + step] = jnp.sum(part * unit_in, axis=0, keepdims=True)
 
 
 def attend_back(heads, *operands, others=()):
@@ -681,8 +779,7 @@
         ((count, heads.lead), bf16),
         ((count, kv_c), bf16),
         ((count, model), bf16),
-        ((1, model), f32),
-        ((1, LAT), f32),
+        ((8, model), f32),
     ]
     vmem = pl.BlockSpec(memory_space=pltpu.VMEM)
     return pl.pallas_call(
@@ -691,7 +788,7 @@
         out_specs=[vmem] * len(shapes),
         out_shape=[jax.ShapeDtypeStruct(*s) for s in shapes],
         scratch_shapes=[pltpu.VMEM((LAT, kv_c), bf16)],
-        compiler_params=pltpu.CompilerParams(vmem_limit_bytes=58 * MIB),
+        compiler_params=pltpu.CompilerParams(vmem_limit_bytes=60 * MIB),
         cost_estimate=pl.CostEstimate(
             flops=2 * count * (model * heads.cols + LAT * kv_c + heads.width * count * 1600),
             bytes_accessed=2 * (model * heads.cols + 4 * count * model),
@@ -723,6 +820,20 @@
 ):
     f32, bf16 = (jnp.float32, jnp.bfloat16)
     groups, lanes = (lax.axis_size("fsdp"), lax.axis_size("ctx"))
+    halves = [list(range(k, groups, 2)) for k in (0, 1)]
+    half = groups // 2
+
+    def swap(value):
+        return lax.ppermute(value, "fsdp", [(i, i ^ 1) for i in range(groups)])
+
+    def gather_half(value):
+        return lax.all_gather(value, "fsdp", axis=0, tiled=True, axis_index_groups=halves)
+
+    def scatter_half(value):
+        return lax.psum_scatter(
+            value, "fsdp", scatter_dimension=0, tiled=True, axis_index_groups=halves
+        )
+
     group = lax.axis_index("fsdp")
     tok_dev, model_w = tokens_in.shape
     count = tok_dev * lanes
@@ -764,29 +875,12 @@
     meta = jnp.concatenate(
         [routes.astype(bf16), jnp.zeros((tok_dev, 128 - top_k), bf16)], axis=1
     )
-    dout_own, small = lax.optimization_barrier((jnp.concatenate([cotangent, meta], axis=1), small))
+    dout_own = after(jnp.concatenate([cotangent, meta], axis=1), small)
     dout_group = gather_ctx(dout_own)
-    dout_all = lax.all_gather(dout_group, "fsdp", axis=0, tiled=True)
-    dout_all = dout_all.reshape(groups * lanes, chunks, tok_dev // chunks, model_w + 128)
-
-    shared = jnp.stack([shared_gate.T, shared_up.T, shared_down]).reshape(
-        3, groups, sh_units, depth
-    )
-    shared = lax.all_to_all(shared, "fsdp", split_axis=1, concat_axis=1, tiled=True)
-    shared = shared.transpose(0, 2, 1, 3).reshape(3, sh_units, model_w)
-    x_all = gather_ctx(after(tokens_in, shared))
-
-    def hidden_rows(experts, mine, router):
-        gap = jnp.zeros((plan.router - units - sh_units, model_w), bf16)
-        end = jnp.zeros((plan.cols - plan.router - router.shape[0], model_w), bf16)
-        return jnp.concatenate([experts.reshape(units, model_w), mine, gap, router, end])
-
-    none = jnp.zeros((0, model_w), bf16)
-    w1 = plan.join(
-        hidden_rows(expert_gate, shared[0], router_w.T),
-        hidden_rows(routed_up_weight, shared[1], none),
-    )
-    wd = hidden_rows(expert_down, shared[2], none)
+    dout_all = gather_half(dout_group)
+    dout_all = dout_all.reshape(half * lanes, chunks, tok_dev // chunks, model_w + 128)
+
+    x_pieces = spread_ctx(after(tokens_in, dout_group))
 
     steps = jnp.arange(count, dtype=jnp.int32)
     same = seg_all[:, None] == seg_all[None, :]
@@ -795,68 +889,137 @@
     freq = THETA ** (-(jnp.arange(ROPE // 2, dtype=f32) * 2.0 / ROPE))
     angle = place[:, None] * freq[None, :]
     cosine, sine = (jnp.concatenate([f(angle)] * 4, axis=1) for f in (jnp.cos, jnp.sin))
-    normed, _, factor_in = norm_parts(x_all.astype(f32), norm_in)
-    x_low = normed.astype(bf16)
     fixed = (cosine, sine, seg_all[:, None], seg_all[None, :], latent_gain[None, :])
-    q_low, kv_low, kr_low, latent_raw, latent_low, lse, heads_low, attn = attend(
-        heads, x_low, packed, *fixed, wd
-    )
-    resid = after(tokens_in.astype(f32) + scatter_ctx(attn), w1)
-    mid, unit_mid, factor_mid = norm_parts(resid, norm_mid)
-    mid_low = mid.astype(bf16)
-
-    first = (group * exp_dev).astype(jnp.int32)[None]
+    lane = lax.axis_index("ctx").astype(jnp.int32)[None]
+    x_all, x_low, factor_in, q_low, kv_low, kr_low, latent_raw, latent_low_t, lse, heads_low, *attn = (
+        attend(heads, chunks, lane, norm_in[None, :], packed, *fixed, x_pieces)
+    )
+    def pair_weights(*others):
+        shared = jnp.stack([shared_gate.T, shared_up.T, shared_down]).reshape(
+            3, groups, sh_units, depth
+        )
+        shared, *pack = after((shared, expert_gate, routed_up_weight, expert_down), *others)
+        shared = lax.all_to_all(shared, "fsdp", split_axis=1, concat_axis=1, tiled=True)
+        shared = shared.transpose(0, 2, 1, 3).reshape(3, sh_units, model_w)
+
+        if plan.shared > sh_units:
+            shared = jnp.pad(shared, ((0, 0), (0, plan.shared - sh_units), (0, 0)))
+        shared_pair = swap(shared)
+
+        pack = [weights.reshape(units, model_w) for weights in pack]
+        pair = [swap(weights) for weights in pack]
+
+        def hidden_rows(k, router):
+            gap = jnp.zeros((plan.router - 2 * (units + plan.shared), model_w), bf16)
+            end = jnp.zeros((plan.cols - plan.router - router.shape[0], model_w), bf16)
+            return jnp.concatenate([pack[k], pair[k], shared[k], shared_pair[k], gap, router, end])
+
+        none = jnp.zeros((0, model_w), bf16)
+        w1 = plan.join(
+            hidden_rows(0, router_w.T),
+            hidden_rows(1, none),
+        )
+        wd = hidden_rows(2, none)
+        return (w1, wd)
+
+    w1, wd = pair_weights(lse)
+
+    own_experts = group * exp_dev + jnp.arange(exp_dev, dtype=jnp.int32)
+    pair_experts = (group ^ 1) * exp_dev + jnp.arange(exp_dev, dtype=jnp.int32)
+    first = jnp.concatenate([own_experts, pair_experts])
     part = tok_dev // chunks
-    mids, rows_parts, rows_own, held = ([], [], [], ())
-    last = dout_all
+    mids, rows_parts, held = ([], [], ())
+    resid, unit_mid, factor_mid, mid_low = ([], [], [], [])
+    last, sent = (dout_all, ())
     for h in range(chunks):
-        mid_part = gather_ctx(mid_low[h * part : (h + 1) * part])
-        last = lax.all_gather(after(mid_part, last), "fsdp", axis=0, tiled=True)
+        rows = tokens_in[h * part : (h + 1) * part].astype(f32)
+        attn_part = after(attn[h], *sent)
+        resid.append(rows + scatter_ctx(attn_part))
+        mid, unit, factor = norm_parts(resid[h], norm_mid)
+        unit_mid.append(unit)
+        factor_mid.append(factor)
+        mid_low.append(mid.astype(bf16))
+        mid_part = gather_ctx(mid_low[h])
+        sent = (mid_part,)
+        mid_part = after(mid_part, w1, wd)
+        last = gather_half(after(mid_part, last))
         mids.append(last)
     for h in range(chunks):
         rows_part, *held = experts_back(plan, h, first, mids[h], dout_all, w1, wd, *held)
         rows_part = after(rows_part, last)
-        last = lax.psum_scatter(rows_part, "fsdp", scatter_dimension=0, tiled=True)
+        last = scatter_half(rows_part)
         rows_parts.append(last)
     gud, act = held
-    edown_grad, sdown_grad = down_sum(plan, model_w, act, dout_all)
-    rows_own = [scatter_ctx(rows) for rows in rows_parts]
-
-    early = (rows_own[0],) if chunks == 2 else ()
-    egate_grad, eup_grad, sgu_grad = pair_sum(plan, gud, mids, edown_grad, *early)
-    out_parts = [
-        experts_out(plan, groups, lanes, h, 2, act, wd, egate_grad) for h in range(0, chunks, 2)
-    ]
-    rows_grad = jnp.concatenate(rows_own)
-    rows_grad = after(rows_grad, egate_grad, *out_parts)
-    mid_grad = rows_grad[:, :model_w]
-    gates_grad = (
-        rows_grad[:, model_w : model_w + experts_n]
-        + rows_grad[:, model_w + experts_n : model_w + 2 * experts_n]
-    )
-
-    sig = jax.nn.sigmoid(dot32(mid_low, router_w))
-    hit = routes[:, :, None] == jnp.arange(experts_n, dtype=jnp.int32)[None, None, :]
-    member = jnp.any(hit, axis=1).astype(f32)
-    chosen_sum = jnp.sum(sig * member, axis=-1, keepdims=True)
-    gates = ROUTE_SCALE * sig * member / chosen_sum
-    spread = jnp.sum(gates_grad * gates, axis=-1, keepdims=True)
-    chosen_grad = (ROUTE_SCALE * gates_grad - spread) / chosen_sum
-    logit_grad = chosen_grad * member * sig * (1.0 - sig)
-    router_grad = precise_tn(logit_grad, mid_low.astype(f32))
-    mid_grad = mid_grad + precise_nt(logit_grad, router_w.astype(f32))
-    resid_grad = norm_back(mid_grad, unit_mid, factor_mid, norm_mid) + cotangent.astype(f32)
-    mid_gain_grad = jnp.sum(mid_grad * unit_mid, axis=0, keepdims=True)
-    attn_low = gather_ctx(resid_grad.astype(bf16))
+
+    router_f = router_w.astype(f32)
+
+    def middle_back(h, pieces, *others):
+        own = total_of([after(pieces[0], *others)] + pieces[1:])
+        rows = slice(h * part, (h + 1) * part)
+        mid_grad = own[:, :model_w]
+        gates_grad = (
+            own[:, model_w : model_w + experts_n]
+            + own[:, model_w + experts_n : model_w + 2 * experts_n]
+        )
+        sig = jax.nn.sigmoid(dot32(mid_low[h], router_w))
+        hit = routes[rows, :, None] == jnp.arange(experts_n, dtype=jnp.int32)[None, None, :]
+        member = jnp.any(hit, axis=1).astype(f32)
+        chosen_sum = jnp.sum(sig * member, axis=-1, keepdims=True)
+        gates = ROUTE_SCALE * sig * member / chosen_sum
+        spread = jnp.sum(gates_grad * gates, axis=-1, keepdims=True)
+        chosen_grad = (ROUTE_SCALE * gates_grad - spread) / chosen_sum
+        logit_grad = chosen_grad * member * sig * (1.0 - sig)
+        mid_grad = mid_grad + precise_nt(logit_grad, router_f)
+        grad = norm_back(mid_grad, unit_mid[h], factor_mid[h], norm_mid)
+        grad = grad + cotangent[rows].astype(f32)
+        return (
+            grad,
+            grad.astype(bf16),
+            jnp.sum(mid_grad * unit_mid[h], axis=0, keepdims=True),
+            precise_tn(logit_grad, mid_low[h].astype(f32)),
+        )
+
+    def outputs(*others):
+        return [
+            experts_out(plan, half, lanes, h, 2, act, wd, *others) for h in range(0, chunks, 2)
+        ]
+
+    if chunks == 2:
+        back = [middle_back(0, pieces_ctx(rows_parts[0]))]
+        gate_sums = weight_sum(plan, "gate", model_w, gud, mids)
+        attn_low = [gather_ctx(back[0][1])]
+        out_parts = outputs(back[0][1], gate_sums[3])
+        out_parts = [after(out_parts[0], attn_low[0])]
+        back.append(middle_back(1, pieces_ctx(after(rows_parts[1], *out_parts))))
+        down_sums = weight_sum(plan, "down", model_w, act, dout_all, rows_parts[1])
+        attn_low.append(gather_ctx(back[1][1]))
+        up_sums = weight_sum(plan, "up", model_w, gud, mids, back[1][1])
+        early_swaps = [swap(gate_sums[2]), swap(down_sums[2])]
+    else:
+        gate_sums = weight_sum(plan, "gate", model_w, gud, mids)
+        down_sums = weight_sum(plan, "down", model_w, act, dout_all)
+        up_sums = weight_sum(plan, "up", model_w, gud, mids)
+        out_parts = outputs(down_sums[3], gate_sums[3], up_sums[3])
+        back = [middle_back(h, pieces_ctx(rows_parts[h])) for h in range(chunks)]
+        attn_low = [gather_ctx(grad[1]) for grad in back]
+        early_swaps = [swap(gate_sums[2]), swap(down_sums[2])]
+    attn_low = jnp.stack([a.reshape(lanes, part, model_w) for a in attn_low], axis=1)
+    attn_low = attn_low.reshape(count, model_w)
+    resid_grad = jnp.concatenate([grad[0] for grad in back])
+    mid_gain_grad = sum(grad[2] for grad in back)
+    router_grad = sum(grad[3] for grad in back)
 
     out_sums = []
     for out_part in out_parts:
-        last = lax.psum_scatter(after(out_part, last), "fsdp", scatter_dimension=0, tiled=True)
+        last = scatter_half(after(out_part, last))
         out_sums.append(last)
-    moe = jnp.concatenate([scatter_ctx(rows) for rows in out_sums])
-    block_out = (resid + moe).astype(bf16)
-
-    qr_grad, kv_grad, normed_grad, in_gain_grad, latent_gain_grad = attend_back(
+
+    share = LAT // (groups * lanes)
+    column = np.arange(model_w)[None, :]
+    spot = column * lanes * groups // model_w * share + column % (depth // lanes)
+    inside = column % (depth // lanes) < share
+    spread = jnp.asarray(((np.arange(LAT)[:, None] == spot) & inside).astype(np.float32), bf16)
+    qr_grad, kv_grad, normed_grad, gains = attend_back(
         heads,
         attn_low,
         x_all,
@@ -868,34 +1031,54 @@
         kr_low,
         latent_raw,
         lse,
-    )
-    shared_grad = jnp.concatenate([sgu_grad, sdown_grad[None]])[:, :sh_units].astype(bf16)
+        spread,
+        others=early_swaps + [up_sums[3]],
+    )
+    if chunks == 2:
+        end_pieces = pieces_ctx(jnp.concatenate([out_sums[0], normed_grad], axis=1))
+    else:
+        moe = jnp.concatenate([scatter_ctx(rows) for rows in out_sums])
+        end_pieces = pieces_ctx(normed_grad)
+        normed_own = total_of(end_pieces)
+        block_out = (jnp.concatenate(resid) + moe).astype(bf16)
+    before = LAT + ROPE - (small_c - 128)
+    early = jnp.concatenate([router_grad, mid_gain_grad])
+    grads = packed_grads(
+        groups,
+        before,
+        x_low,
+        attn_low,
+        latent_low_t,
+        qr_grad,
+        heads_low,
+        kv_grad,
+        early,
+        gains,
+    )
+    all_sums = (gate_sums, up_sums, down_sums)
+    swapped = (early_swaps[0], swap(up_sums[2]), early_swaps[1])
+    expert_grads = [
+        finished(sums[0], other, end_pieces[1]).reshape(expert_gate.shape)
+        for sums, other in zip(all_sums, swapped)
+    ]
+    shared_other = swap(after(jnp.stack([sums[3] for sums in all_sums]), end_pieces[1]))
+    shared_grad = jnp.stack([sums[1] for sums in all_sums]) + shared_other.astype(f32)
+    shared_grad = shared_grad[:, :sh_units].astype(bf16)
     shared_grad = shared_grad.reshape(3, sh_units, groups, depth).transpose(0, 2, 1, 3)
-    shared_grad = after(shared_grad, qr_grad)
     shared_grad = lax.all_to_all(shared_grad, "fsdp", split_axis=1, concat_axis=1, tiled=True)
     shared_grad = shared_grad.reshape(3, sh_units * groups, depth).astype(f32)
-    normed_own = scatter_ctx(normed_grad)
-    _, unit_own, factor_own = norm_parts(tokens_in.astype(f32), norm_in)
-    grad_input = norm_back(normed_own, unit_own, factor_own, norm_in) + resid_grad
-
-    latent_gain_row = jnp.pad(
-        latent_gain_grad.reshape(groups * lanes, -1),
-        ((0, 0), (0, depth // lanes - LAT // (groups * lanes))),
-    ).reshape(1, model_w)
-    before = LAT + ROPE - (small_c - 128)
-    extra = jnp.concatenate(
-        [
-            jnp.zeros((before, model_w), f32),
-            router_grad,
-            mid_gain_grad,
-            in_gain_grad,
-            latent_gain_row,
-            jnp.zeros((128 - before - experts_n - 3, model_w), f32),
-        ]
-    )
-    grads = packed_grads(
-        groups, x_low, attn_low, latent_low.T, qr_grad, heads_low, kv_grad, extra
-    )
+    if chunks == 2:
+        block_out, grad_input = ends(
+            end_pieces,
+            jnp.concatenate(resid),
+            resid_grad,
+            tokens_in,
+            norm_in[None, :],
+            *expert_grads,
+        )
+    else:
+        _, unit_own, factor_own = norm_parts(tokens_in.astype(f32), norm_in)
+        grad_input = norm_back(normed_own, unit_own, factor_own, norm_in) + resid_grad
     grads = lax.psum_scatter(after(grads, last), "fsdp", scatter_dimension=0, tiled=True)
     small_own = scatter_ctx(grads[:, heads.query : at_expand])
     g_query = dot_nt(grads[:, : heads.query], order)
@@ -920,9 +1103,7 @@
         shared_grad[0].T,
         shared_grad[1].T,
         shared_grad[2],
-        egate_grad.reshape(expert_gate.shape),
-        eup_grad.reshape(expert_gate.shape),
-        edown_grad.reshape(expert_gate.shape),
+        *expert_grads,
     )
 
 

time: 764 us -> 683 us (0.89)
  waiting for transfers between devices: 308 us -> 194 us
  starting transfers between devices: 97.1 us -> 118 us
  Pallas kernels: 236 us -> 255 us
    ppermute x18, waiting for transfers between devices: 136 us -> 62.4 us  [gather_ctx(): lax.ppermute(value, 'ctx', [(i, (i + hop) % lanes) for i in range(lanes)])]
    pallas_call x4 -> x9, Pallas kernels: 87 us -> 118 us  [the longest x3 69.2 us: weight_sum(): pl.pallas_call(functools.partial(sum_kernel, plan, kind, chunks), grid=(c...]
    all_gather x3, waiting for transfers between devices: 36.7 us -> 13.4 us  [gather_half(): lax.all_gather(value, 'fsdp', axis=0, tiled=True, axis_index_groups=halves)]
    ppermute x18 -> x29, starting transfers between devices: 55.9 us -> 73.5 us  [the longest x18 57.8 us: pieces_ctx(): lax.ppermute(part, 'ctx', [(i, (i + hop) % lanes) for i in range(lanes)])]
    pallas_call x2, Pallas kernels: 110 us -> 96 us  [experts_back(): pl.pallas_call(functools.partial(back_kernel, plan), grid=(tokens // tile...]
    reduce_scatter x3, waiting for transfers between devices: 23.2 us -> 9.85 us  [scatter_half(): lax.psum_scatter(value, 'fsdp', scatter_dimension=0, tiled=True, axis_ind...]
    ppermute x18 -> x29, waiting for transfers between devices: 113 us -> 108 us  [the longest x18 76.5 us: pieces_ctx(): lax.ppermute(part, 'ctx', [(i, (i + hop) % lanes) for i in range(lanes)])]
    unnamed x140 -> x108, local copies, waits for them, and re-layouts: 25.2 us -> 21.6 us
  transfers between devices with their start and end apart: 46 -> 57, of which waited for: 28 -> 23; matrix products, arithmetic and copies ran while one was open for 9% -> 12% of each run, Pallas kernels for 31% -> 38%
where the time goes in v3:
time: 683 us; the launch traced here: 678 us
  Pallas kernels  255 us (37%)
  waiting for transfers between devices  194 us (28%)
  starting transfers between devices  118 us (17%)
  local copies, waits for them, and re-layouts  50.2 us (7%)
  other arithmetic  31.6 us (5%)
  between operations  15.6 us (2%)
  matrix products  13.3 us (2%)
    pallas_call x2, Pallas kernels, experts_back(): pl.pallas_call(functools.partial(back_kernel, plan), grid=(tokens // tile...  96 us
    ppermute x18, waiting for transfers between devices, pieces_ctx(): lax.ppermute(part, 'ctx', [(i, (i + hop) % lanes) for i in range(lanes)])  76.5 us
    pallas_call x3, Pallas kernels, weight_sum(): pl.pallas_call(functools.partial(sum_kernel, plan, kind, chunks), grid=(c...  69.2 us
    ppermute x18, waiting for transfers between devices, gather_ctx(): lax.ppermute(value, 'ctx', [(i, (i + hop) % lanes) for i in range(lanes)])  62.4 us
    ppermute x18, starting transfers between devices, pieces_ctx(): lax.ppermute(part, 'ctx', [(i, (i + hop) % lanes) for i in range(lanes)])  57.8 us
    ppermute x18, starting transfers between devices, gather_ctx(): lax.ppermute(value, 'ctx', [(i, (i + hop) % lanes) for i in range(lanes)])  36.7 us
    ppermute x3, waiting for transfers between devices, spread_ctx(): lax.ppermute(value, 'ctx', [(i, (i + hop) % lanes) for i in range(lanes)])  29.7 us
    unnamed x108, local copies, waits for them, and re-layouts  21.6 us
  transfers between devices with their start and end apart: 57, of which 23 were waited for; matrix products, arithmetic and copies ran while one was open for 12% of the time, Pallas kernels for 38%

profile of v3, /device:TPU:0, one launch (start us, length us, event | category | flops | bytes accessed | tf_op | source)
XLA Modules:
  0.0 678.4 jit_solution(14897183263566750216)
XLA Ops:
  10.0 3.1 collective-permute-start
  13.1 2.6 collective-permute-start.1
  18.8 2.4 collective-permute-done.1
  23.7 2.0 collective-permute-start.3
  25.7 1.9 collective-permute-start.4
  29.5 12.0 %collective-permute-done.3 = bf16[128,2176]{1,0:T(8,128)(2,1)} collective-permute-done((bf16[128,2176]{1,0:T(8,128)(2,1)}, bf16[128,2176]{1,0:T(8,128)(2,1)}, u32[]{:S(2)}, u32[]{:S(2)}) %collective-permute-start.3) | collective-permute-done | bytes 557088 | tf_op jit(solution)/shard_map/ppermute | solution.py:102
  42.6 21.4 %collective-permute-done.4 = bf16[128,2176]{1,0:T(8,128)(2,1)S(1)} collective-permute-done((bf16[128,2176]{1,0:T(8,128)(2,1)}, bf16[128,2176]{1,0:T(8,128)(2,1)S(1)}, u32[]{:S(2)}, u32[]{:S(2)}) %collective-permute-start.4) | collective-permute-done | bytes 557088 | tf_op jit(solution)/shard_map/ppermute | solution.py:102
  65.6 2.2 pad_maximum_fusion.7
  69.8 12.4 %collective-permute-start.6 = (bf16[128,2048]{1,0:T(8,128)(2,1)S(1)}, bf16[128,2048]{1,0:T(8,128)(2,1)S(1)}, u32[]{:S(2)}, u32[]{:S(2)}) collective-permute-start(bf16[128,2048]{1,0:T(8,128)(2,1)S(1)} %copy-done.4), channel_id=1, source_target_pairs={{0,1},{1,2},{2,3},{3,0},{4,5},{5,6},{6,7},{7,4},{8,9},{9,10},{10,1... | collective-permute-start | bytes 1572872 | tf_op jit(solution)/shard_map/ppermute | solution.py:133
  87.1 8.7 %collective-permute-done.6.refs_1_ = bf16[128,2048]{1,0:T(8,128)(2,1)S(1)} collective-permute-done((bf16[128,2048]{1,0:T(8,128)(2,1)S(1)}, bf16[128,2048]{1,0:T(8,128)(2,1)S(1)}, u32[]{:S(2)}, u32[]{:S(2)}) %collective-permute-start.6) | collective-permute-done | bytes 524320 | tf_op jit(solution)/shard_map/ppermute | solution.py:133
  95.8 21.1 %collective-permute-done.7.refs_2_ = bf16[128,2048]{1,0:T(8,128)(2,1)S(1)} collective-permute-done((bf16[128,2048]{1,0:T(8,128)(2,1)S(1)}, bf16[128,2048]{1,0:T(8,128)(2,1)S(1)}, u32[]{:S(2)}, u32[]{:S(2)}) %collective-permute-start.7) | collective-permute-done | bytes 524320 | tf_op jit(solution)/shard_map/ppermute | solution.py:133
  117.8 15.0 %attend.1 = (bf16[512,2048]{1,0:T(8,128)(2,1)}, bf16[512,2048]{1,0:T(8,128)(2,1)}, f32[512,128]{1,0:T(8,128)}, bf16[512,768]{1,0:T(8,128)(2,1)}, bf16[512,1024]{...) custom-call(s32[1]{0:T(128)} %bitcast.lane_ref, ...), custom_call_target="tpu_custom_call" | custom-call | flops 6174015488 | bytes 17301504 | tf_op jit(solution)/shard_map/attend/pallas_call | solution.py:670
  132.9 3.7 all-to-all-start
  137.9 11.2 %collective-permute-start.10 = (bf16[64,2048]{1,0:T(8,128)(2,1)S(1)}, bf16[64,2048]{1,0:T(8,128)(2,1)S(1)}, u32[]{:S(2)}, u32[]{:S(2)}) collective-permute-start(bf16[64,2048]{1,0:T(8,128)(2,1)S(1)} %get-tuple-element.235), channel_id=1, source_target_pairs={{0,2},{1,3},{2,0},{3,1},{4,6},{5,7},{6,4},{7,5},{8,10},{9,11},{10,... | collective-permute-start | bytes 786440 | tf_op jit(solution)/shard_map/ppermute | solution.py:115
  149.0 2.8 collective-permute-start.11
  153.5 8.4 %collective-permute-done.10 = bf16[64,2048]{1,0:T(8,128)(2,1)S(1)} collective-permute-done((bf16[64,2048]{1,0:T(8,128)(2,1)S(1)}, bf16[64,2048]{1,0:T(8,128)(2,1)S(1)}, u32[]{:S(2)}, u32[]{:S(2)}) %collective-permute-start.10) | collective-permute-done | bytes 262176 | tf_op jit(solution)/shard_map/ppermute | solution.py:115
  161.9 8.1 %collective-permute-done.9 = bf16[64,2048]{1,0:T(8,128)(2,1)S(1)} collective-permute-done((bf16[64,2048]{1,0:T(8,128)(2,1)S(1)}, bf16[64,2048]{1,0:T(8,128)(2,1)S(1)}, u32[]{:S(2)}, u32[]{:S(2)}) %collective-permute-start.9) | collective-permute-done | bytes 262176 | tf_op jit(solution)/shard_map/ppermute | solution.py:115
  171.5 3.7 collective-permute-start.12
  175.2 2.8 collective-permute-start.13
  179.1 3.7 constant_dynamic-update-slice_fusion.2
  183.6 2.0 collective-permute-start.14
  187.3 5.4 collective-permute-done.13
  193.4 6.5 collective-permute-done.14
  202.9 3.8 constant_dynamic-update-slice_fusion.1
  207.4 1.8 fusion.20
  210.0 9.9 %fusion.4.w1_ref = bf16[3328,2048]{1,0:T(8,128)(2,1)} fusion(bf16[88,2048]{1,0:T(8,128)(2,1)S(1)} %get-tuple-element.229, bf16[88,2048]{1,0:T(8,128)(2,1)} %bitcast.108, bf16[704,2048]{1,0:T(8,128)(2,1)} %collective-permute-done.20, bf16[704,2048]{1,0:T(8,128)(2,1)} %bitcast.100, bf16[88,2048]{1,0:T(8,128)(2,1)S(1)} %get-tuple-element.228, ...), kind=kLoop, calls=%fused_computation.5 | loop fusion | flops 149946368 | bytes 27656192 | tf_op jit(solution)/shard_map/concatenate | solution.py:154
  221.1 3.4 collective-permute-start.15
  225.8 2.8 collective-permute-start.17
  228.6 3.9 collective-permute-done.15
  232.5 11.0 %collective-permute-done.16 = bf16[64,2048]{1,0:T(8,128)(2,1)S(1)} collective-permute-done((bf16[64,2048]{1,0:T(8,128)(2,1)S(1)}, bf16[64,2048]{1,0:T(8,128)(2,1)S(1)}, u32[]{:S(2)}, u32[]{:S(2)}) %collective-permute-start.16) | collective-permute-done | bytes 262176 | tf_op jit(solution)/shard_map/ppermute | solution.py:115
  245.1 6.1 collective-permute-start.22
  251.4 2.2 collective-permute-start.24
  253.6 4.2 collective-permute-done.22
  257.9 8.6 %collective-permute-done.23 = bf16[64,2048]{1,0:T(8,128)(2,1)S(1)} collective-permute-done((bf16[64,2048]{1,0:T(8,128)(2,1)S(1)}, bf16[64,2048]{1,0:T(8,128)(2,1)S(1)}, u32[]{:S(2)}, u32[]{:S(2)}) %collective-permute-start.23) | collective-permute-done | bytes 262176 | tf_op jit(solution)/shard_map/ppermute | solution.py:102
  268.3 6.7 all-gather.9.cloned.1.call-done.mid_ref.refs_0_
  275.6 47.6 %experts_back.2 = (bf16[1024,2176]{1,0:T(8,128)(2,1)}, bf16[2,1024,3328]{2,1,0:T(8,128)(2,1)}, bf16[2,1024,1664]{2,1,0:T(8,128)(2,1)}) custom-call(s32[4]{0:T(128)} %pad_add_fusion.first_ref, bf16[1024,2048]{1,0:T(8,128)(2,1)} %all-gather.9.cloned.1.call-done.mid_ref.refs_0_, bf16[16,2,64,2176]{3,2,1,0:T(8,128)(2,1)} %bitcast.124, ...), custom_call_target="tpu_custom_call" | custom-call | flops 34896609280 | bytes 22806528 | tf_op jit(solution)/shard_map/experts_back/pallas_call | solution.py:257
  323.2 6.8 all-gather.11.cloned.1.call-done.mid_ref.refs_1_
  330.0 48.5 %experts_back.3 = (bf16[1024,2176]{1,0:T(8,128)(2,1)}, bf16[2,1024,3328]{2,1,0:T(8,128)(2,1)}, bf16[2,1024,1664]{2,1,0:T(8,128)(2,1)}) custom-call(s32[4]{0:T(128)} %pad_add_fusion.first_ref, bf16[1024,2048]{1,0:T(8,128)(2,1)} %all-gather.11.cloned.1.call-done.mid_ref.refs_1_, ...), custom_call_target="tpu_custom_call", output_to_operand_aliasing={{1}: (6, {}), {2}: (7, {})} | custom-call | flops 34896609280 | bytes 22806528 | tf_op jit(solution)/shard_map/experts_back/pallas_call | solution.py:257
  378.5 9.8 %reduce-scatter.5.cloned.1.call-done = bf16[256,2176]{1,0:T(8,128)(2,1)} async-done(((bf16[1024,2176]{1,0:T(8,128)(2,1)}), bf16[256,2176]{1,0:T(8,128)(2,1)}) %reduce-scatter.5.cloned.1.call-update) | async-done | bytes 1114128 | tf_op jit(solution)/shard_map/reduce_scatter | solution.py:833
  391.8 2.4 collective-permute-start.26
  395.7 22.9 %gate_sum.1 = (f32[704,2048]{1,0:T(8,128)}, f32[88,2048]{1,0:T(8,128)}, bf16[704,2048]{1,0:T(8,128)(2,1)}, bf16[88,2048]{1,0:T(8,128)(2,1)}) custom-call(bf16[2,1024,3328]{2,1,0:T(8,128)(2,1)} %get-tuple-element.91.h_ref, bf16[1024,2048]{1,0:T(8,128)(2,1)} %all-gather.9.cloned.1.call-done.mid_ref.refs_0_, ...), custom_call_target="tpu_custom_call" | custom-call | flops 13958643712 | bytes 20971520 | tf_op jit(solution)/shard_map/gate_sum/pallas_call | solution.py:390
  419.0 2.0 multiply_reduce_fusion.1
  424.0 1.9 collective-permute-start.30
  425.9 20.9 %experts_out.1 = bf16[4,4,2,64,2048]{4,3,2,1,0:T(8,128)(2,1)} custom-call(bf16[2,1024,1664]{2,1,0:T(8,128)(2,1)} %get-tuple-element.90.act_ref.h_ref, bf16[1664,2048]{1,0:T(8,128)(2,1)} %broadcast_dynamic-update-slice_fusion.wd_ref, bf16[64,2048]{1,0:T(8,128)(2,1)} %copy-done.36, bf16[88,2048]{1,0:T(8,128)(2,1)} %get-tuple-element.92.refs_1_), custom_call_target="tpu_custom_call" | custom-call | flops 13958643712 | bytes 15204352 | tf_op jit(solution)/shard_map/experts_out/pallas_call | solution.py:302
  449.7 1.9 fusion.61
  451.5 2.0 constant_dynamic-slice_fusion.10
  453.5 2.0 collective-permute-start.31
  456.7 2.2 collective-permute-start.33
  458.9 22.9 %down_sum.1 = (f32[704,2048]{1,0:T(8,128)}, f32[88,2048]{1,0:T(8,128)}, bf16[704,2048]{1,0:T(8,128)(2,1)}, bf16[88,2048]{1,0:T(8,128)(2,1)}) custom-call(bf16[2,1024,1664]{2,1,0:T(8,128)(2,1)} %get-tuple-element.90.act_ref.h_ref, bf16[16,2,64,2176]{3,2,1,0:T(8,128)(2,1)} %bitcast.128, bf16[16,2,64,2176]{3,2,1,0:T(8,128)(2,1)} %bitcast.129, ...), custom_call_target="tpu_custom_call" | custom-call | flops 13958643712 | bytes 20971520 | tf_op jit(solution)/shard_map/down_sum/pallas_call | solution.py:390
  482.1 2.1 multiply_reduce_fusion
  489.7 23.4 %up_sum.1 = (f32[704,2048]{1,0:T(8,128)}, f32[88,2048]{1,0:T(8,128)}, bf16[704,2048]{1,0:T(8,128)(2,1)}, bf16[88,2048]{1,0:T(8,128)(2,1)}) custom-call(bf16[2,1024,3328]{2,1,0:T(8,128)(2,1)} %get-tuple-element.91.h_ref, bf16[1024,2048]{1,0:T(8,128)(2,1)} %all-gather.9.cloned.1.call-done.mid_ref.refs_0_, ...), custom_call_target="tpu_custom_call" | custom-call | flops 13958643712 | bytes 20971520 | tf_op jit(solution)/shard_map/up_sum/pallas_call | solution.py:390
  519.2 19.7 %attend_back.1 = (bf16[512,1408]{1,0:T(8,128)(2,1)}, bf16[512,1024]{1,0:T(8,128)(2,1)}, bf16[512,2048]{1,0:T(8,128)(2,1)}, f32[8,2048]{1,0:T(8,128)}) custom-call(bf16[512,2048]{1,0:T(8,128)(2,1)} %bitcast.93, bf16[512,2048]{1,0:T(8,128)(2,1)} %get-tuple-element.96.x_ref, f32[512,128]{1,0:T(8,128)} %get-tuple-element.97.factor_ref, ...), custom_call_target="tpu_custom_call" | custom-call | flops 8455716864 | bytes 17301504 | tf_op jit(solution)/shard_map/attend_back/pallas_call | solution.py:785
  538.9 12.4 %packed_grads.1 = bf16[2048,2176]{1,0:T(8,128)(2,1)} custom-call(bf16[512,2048]{1,0:T(8,128)(2,1)} %get-tuple-element.112.x_ref, bf16[512,2048]{1,0:T(8,128)(2,1)} %bitcast.94, bf16[512,512]{1,0:T(8,128)(2,1)} %get-tuple-element.113.latent_ref, bf16[512,1408]{1,0:T(8,128)(2,1)} %get-tuple-element.114.qr_ref, bf16[512,512]{1,0:T(8,128)(2,1)} %get-tuple-element.115.heads_ref, ...), custom_call_target="tpu_custom_call" | custom-call | flops 4563402752 | bytes 16777216 | tf_op jit(solution)/shard_map/packed_grads/pallas_call | solution.py:450
  554.7 1.8 constant_dynamic-slice_fusion.3
  557.1 25.8 %collective-permute-done.39.refs_0_.refs_1_ = bf16[128,4096]{1,0:T(8,128)(2,1)S(1)} collective-permute-done((bf16[128,4096]{1,0:T(8,128)(2,1)S(1)}, bf16[128,4096]{1,0:T(8,128)(2,1)S(1)}, u32[]{:S(2)}, u32[]{:S(2)}) %collective-permute-start.39) | collective-permute-done | bytes 1048608 | tf_op jit(solution)/shard_map/ppermute | solution.py:115
  587.0 4.2 all-to-all-start.1
  593.9 6.5 finished.5
  600.4 5.7 finished.3
  606.1 6.2 finished.4
  612.3 17.9 %collective-permute-done.40.refs_2_ = bf16[128,4096]{1,0:T(8,128)(2,1)S(1)} collective-permute-done((bf16[128,4096]{1,0:T(8,128)(2,1)}, bf16[128,4096]{1,0:T(8,128)(2,1)S(1)}, u32[]{:S(2)}, u32[]{:S(2)}) %collective-permute-start.40) | collective-permute-done | bytes 1048608 | tf_op jit(solution)/shard_map/ppermute | solution.py:115
  631.5 3.5 ends.1
  635.0 2.6 fusion.56
  640.3 21.1 %collective-permute-start.43 = (bf16[64,640]{1,0:T(8,128)(2,1)S(1)}, bf16[64,640]{1,0:T(8,128)(2,1)S(1)}, u32[]{:S(2)}, u32[]{:S(2)}) collective-permute-start(bf16[64,640]{1,0:T(8,128)(2,1)S(1)} %get-tuple-element.236), channel_id=1, source_target_pairs={{0,1},{1,2},{2,3},{3,0},{4,5},{5,6},{6,7},{7,4},{8,9},{9,10},{10,1... | collective-permute-start | bytes 245768 | tf_op jit(solution)/shard_map/ppermute | solution.py:115
  665.9 2.5 fusion.5
  (291 shorter events, 86.4 us)
Async XLA Ops:
  7.2 109.6 %all-gather.5.cloned.1.call-start = ((), (), s32[]{:S(2)}) async-start(), calls=%async_computation.6 | async-start | bytes 10027008 | tf_op jit(solution)/shard_map/all_gather | solution.py:869
  10.0 8.7 %collective-permute-start = (bf16[64,640]{1,0:T(8,128)(2,1)S(1)}, bf16[64,640]{1,0:T(8,128)(2,1)S(1)}, u32[]{:S(2)}, u32[]{:S(2)}) collective-permute-start(bf16[64,640]{1,0:T(8,128)(2,1)S(1)} %get-tuple-element.209), channel_id=1, source_target_pairs={{0,1},{1,2},{2,3},{3,0},{4,5},{5,6},{6,7},{7,4},{8,9},{9,10},{10,1... | collective-permute-start | bytes 245768 | tf_op jit(solution)/shard_map/ppermute | solution.py:102
  13.1 8.1 %collective-permute-start.1 = (bf16[64,640]{1,0:T(8,128)(2,1)S(1)}, bf16[64,640]{1,0:T(8,128)(2,1)S(1)}, u32[]{:S(2)}, u32[]{:S(2)}) collective-permute-start(bf16[64,640]{1,0:T(8,128)(2,1)S(1)} %get-tuple-element.209), channel_id=1, source_target_pairs={{0,2},{1,3},{2,0},{3,1},{4,6},{5,7},{6,4},{7,5},{8,10},{9,11},{10,... | collective-permute-start | bytes 245768 | tf_op jit(solution)/shard_map/ppermute | solution.py:102
  15.7 5.7 collective-permute-start.2
  22.5 197.3 %all-gather.7.cloned.1.call-start = ((), (), s32[]{:S(2)}) async-start(), calls=%async_computation.7 | async-start | bytes 11141120 | tf_op jit(solution)/shard_map/all_gather | solution.py:830
  23.7 17.8 %collective-permute-start.3 = (bf16[128,2176]{1,0:T(8,128)(2,1)}, bf16[128,2176]{1,0:T(8,128)(2,1)}, u32[]{:S(2)}, u32[]{:S(2)}) collective-permute-start(bf16[128,2176]{1,0:T(8,128)(2,1)} %concatenate.62), channel_id=1, source_target_pairs={{0,1},{1,2},{2,3},{3,0},{4,5},{5,6},{6,7},{7,4},{8,9},{9,10},{10,1... | collective-permute-start | bytes 1671176 | tf_op jit(solution)/shard_map/ppermute | solution.py:102
  25.7 38.3 %collective-permute-start.4 = (bf16[128,2176]{1,0:T(8,128)(2,1)}, bf16[128,2176]{1,0:T(8,128)(2,1)S(1)}, u32[]{:S(2)}, u32[]{:S(2)}) collective-permute-start(bf16[128,2176]{1,0:T(8,128)(2,1)} %concatenate.62), channel_id=1, source_target_pairs={{0,2},{1,3},{2,0},{3,1},{4,6},{5,7},{6,4},{7,5},{8,10},{9,11},{10,... | collective-permute-start | bytes 1671176 | tf_op jit(solution)/shard_map/ppermute | solution.py:102
  27.6 36.5 %collective-permute-start.5 = (bf16[128,2176]{1,0:T(8,128)(2,1)}, bf16[128,2176]{1,0:T(8,128)(2,1)S(1)}, u32[]{:S(2)}, u32[]{:S(2)}) collective-permute-start(bf16[128,2176]{1,0:T(8,128)(2,1)} %concatenate.62), channel_id=1, source_target_pairs={{0,3},{1,0},{2,1},{3,2},{4,7},{5,4},{6,5},{7,6},{8,11},{9,8},{10,9... | collective-permute-start | bytes 1671176 | tf_op jit(solution)/shard_map/ppermute | solution.py:102
  29.5 36.1 %copy-start.31 = (bf16[704,256]{1,0:T(8,128)(2,1)S(1)}, bf16[704,256]{1,0:T(8,128)(2,1)}, u32[]{:S(2)}) copy-start(bf16[704,256]{1,0:T(8,128)(2,1)} %param.33) | copy-start | bytes 1081348
  69.8 25.9 %collective-permute-start.6 = (bf16[128,2048]{1,0:T(8,128)(2,1)S(1)}, bf16[128,2048]{1,0:T(8,128)(2,1)S(1)}, u32[]{:S(2)}, u32[]{:S(2)}) collective-permute-start(bf16[128,2048]{1,0:T(8,128)(2,1)S(1)} %copy-done.4), channel_id=1, source_target_pairs={{0,1},{1,2},{2,3},{3,0},{4,5},{5,6},{6,7},{7,4},{8,9},{9,10},{10,1... | collective-permute-start | bytes 1572872 | tf_op jit(solution)/shard_map/ppermute | solution.py:133
  82.2 34.6 %collective-permute-start.7 = (bf16[128,2048]{1,0:T(8,128)(2,1)S(1)}, bf16[128,2048]{1,0:T(8,128)(2,1)S(1)}, u32[]{:S(2)}, u32[]{:S(2)}) collective-permute-start(bf16[128,2048]{1,0:T(8,128)(2,1)S(1)} %copy-done.4), channel_id=1, source_target_pairs={{0,2},{1,3},{2,0},{3,1},{4,6},{5,7},{6,4},{7,5},{8,10},{9,11},{10,... | collective-permute-start | bytes 1572872 | tf_op jit(solution)/shard_map/ppermute | solution.py:133
  83.4 33.5 %collective-permute-start.8 = (bf16[128,2048]{1,0:T(8,128)(2,1)S(1)}, bf16[128,2048]{1,0:T(8,128)(2,1)S(1)}, u32[]{:S(2)}, u32[]{:S(2)}) collective-permute-start(bf16[128,2048]{1,0:T(8,128)(2,1)S(1)} %copy-done.4), channel_id=1, source_target_pairs={{0,3},{1,0},{2,1},{3,2},{4,7},{5,4},{6,5},{7,6},{8,11},{9,8},{10,9... | collective-permute-start | bytes 1572872 | tf_op jit(solution)/shard_map/ppermute | solution.py:133
  132.8 37.2 %copy-start.5 = (bf16[128,2048]{1,0:T(8,128)(2,1)S(1)}, bf16[128,2048]{1,0:T(8,128)(2,1)}, u32[]{:S(2)}) copy-start(bf16[128,2048]{1,0:T(8,128)(2,1)} %x_ref.1) | copy-start | bytes 1572868
  132.8 70.1 %collective-permute-start.21 = (bf16[704,2048]{1,0:T(8,128)(2,1)}, bf16[704,2048]{1,0:T(8,128)(2,1)}, u32[]{:S(2)}, u32[]{:S(2)}) collective-permute-start(bf16[704,2048]{1,0:T(8,128)(2,1)} %bitcast.16), channel_id=1, source_target_pairs={{0,4},{4,0},{8,12},{12,8},{16,20},{20,16},{24,28},{28,24},{1,5},{5... | collective-permute-start | bytes 8650760 | tf_op jit(solution)/shard_map/ppermute | solution.py:827
  132.9 45.1 %all-to-all-start = ((bf16[3,8,88,256]{3,2,0,1:T(8,128)(2,1)}), bf16[3,8,88,256]{3,2,0,1:T(8,128)(2,1)S(1)}, u32[]{:S(2)}, u32[]{:S(2)}) async-start(bf16[3,8,88,256]{3,2,0,1:T(8,128)(2,1)} %pad_maximum_fusion.7), calls=%async_computation | async-start | bytes 2162688 | tf_op jit(solution)/shard_map/all_to_all | solution.py:902
  136.6 34.8 %copy-start.38 = (f32[2048]{0:T(1024)S(1)}, f32[2048]{0:T(1024)}, u32[]{:S(2)}) copy-start(f32[2048]{0:T(1024)} %param.29) | copy-start | bytes 24580
  136.6 138.3 %all-gather.9.cloned.1.call-start = ((), (), s32[]{:S(2)}) async-start(), calls=%async_computation.8 | async-start | bytes 5242880 | tf_op jit(solution)/shard_map/all_gather | solution.py:830
  137.9 24.0 %collective-permute-start.10 = (bf16[64,2048]{1,0:T(8,128)(2,1)S(1)}, bf16[64,2048]{1,0:T(8,128)(2,1)S(1)}, u32[]{:S(2)}, u32[]{:S(2)}) collective-permute-start(bf16[64,2048]{1,0:T(8,128)(2,1)S(1)} %get-tuple-element.235), channel_id=1, source_target_pairs={{0,2},{1,3},{2,0},{3,1},{4,6},{5,7},{6,4},{7,5},{8,10},{9,11},{10,... | collective-permute-start | bytes 786440 | tf_op jit(solution)/shard_map/ppermute | solution.py:115
  149.0 12.8 %collective-permute-start.11 = (bf16[64,2048]{1,0:T(8,128)(2,1)S(1)}, bf16[64,2048]{1,0:T(8,128)(2,1)S(1)}, u32[]{:S(2)}, u32[]{:S(2)}) collective-permute-start(bf16[64,2048]{1,0:T(8,128)(2,1)S(1)} %get-tuple-element.234), channel_id=1, source_target_pairs={{0,3},{1,0},{2,1},{3,2},{4,7},{5,4},{6,5},{7,6},{8,11},{9,8},{10,9... | collective-permute-start | bytes 786440 | tf_op jit(solution)/shard_map/ppermute | solution.py:115
  151.9 18.1 %collective-permute-start.9 = (bf16[64,2048]{1,0:T(8,128)(2,1)S(1)}, bf16[64,2048]{1,0:T(8,128)(2,1)S(1)}, u32[]{:S(2)}, u32[]{:S(2)}) collective-permute-start(bf16[64,2048]{1,0:T(8,128)(2,1)S(1)} %get-tuple-element.233), channel_id=1, source_target_pairs={{0,1},{1,2},{2,3},{3,0},{4,5},{5,6},{6,7},{7,4},{8,9},{9,10},{10,1... | collective-permute-start | bytes 786440 | tf_op jit(solution)/shard_map/ppermute | solution.py:115
  171.2 249.8 %copy-start.9 = (f32[64,2048]{1,0:T(8,128)}, f32[64,2048]{1,0:T(8,128)S(1)}, u32[]{:S(2)}) copy-start(f32[64,2048]{1,0:T(8,128)S(1)} %get-tuple-element.207) | copy-start | bytes 1572868
  171.5 12.1 %collective-permute-start.12 = (bf16[64,2048]{1,0:T(8,128)(2,1)S(1)}, bf16[64,2048]{1,0:T(8,128)(2,1)}, u32[]{:S(2)}, u32[]{:S(2)}) collective-permute-start(bf16[64,2048]{1,0:T(8,128)(2,1)S(1)} %get-tuple-element.205), channel_id=1, source_target_pairs={{0,1},{1,2},{2,3},{3,0},{4,5},{5,6},{6,7},{7,4},{8,9},{9,10},{10,1... | collective-permute-start | bytes 786440 | tf_op jit(solution)/shard_map/ppermute | solution.py:102
  175.2 17.5 %collective-permute-start.13 = (bf16[64,2048]{1,0:T(8,128)(2,1)S(1)}, bf16[64,2048]{1,0:T(8,128)(2,1)S(1)}, u32[]{:S(2)}, u32[]{:S(2)}) collective-permute-start(bf16[64,2048]{1,0:T(8,128)(2,1)S(1)} %get-tuple-element.205), channel_id=1, source_target_pairs={{0,2},{1,3},{2,0},{3,1},{4,6},{5,7},{6,4},{7,5},{8,10},{9,11},{10,... | collective-permute-start | bytes 786440 | tf_op jit(solution)/shard_map/ppermute | solution.py:102
  179.1 22.4 %collective-permute-start.19 = (bf16[3,88,2048]{2,1,0:T(8,128)(2,1)}, bf16[3,88,2048]{2,1,0:T(8,128)(2,1)}, u32[]{:S(2)}, u32[]{:S(2)}) collective-permute-start(bf16[3,88,2048]{2,1,0:T(8,128)(2,1)} %bitcast.51), channel_id=1, source_target_pairs={{0,4},{4,0},{8,12},{12,8},{16,20},{20,16},{24,28},{28,24},{1,5},{5... | collective-permute-start | bytes 3244040 | tf_op jit(solution)/shard_map/ppermute | solution.py:827
  183.0 26.9 %collective-permute-start.18 = (bf16[704,2048]{1,0:T(8,128)(2,1)}, bf16[704,2048]{1,0:T(8,128)(2,1)}, u32[]{:S(2)}, u32[]{:S(2)}) collective-permute-start(bf16[704,2048]{1,0:T(8,128)(2,1)} %bitcast.101), channel_id=1, source_target_pairs={{0,4},{4,0},{8,12},{12,8},{16,20},{20,16},{24,28},{28,24},{1,5},{5... | collective-permute-start | bytes 8650760 | tf_op jit(solution)/shard_map/ppermute | solution.py:827
  183.6 16.3 %collective-permute-start.14 = (bf16[64,2048]{1,0:T(8,128)(2,1)S(1)}, bf16[64,2048]{1,0:T(8,128)(2,1)S(1)}, u32[]{:S(2)}, u32[]{:S(2)}) collective-permute-start(bf16[64,2048]{1,0:T(8,128)(2,1)S(1)} %get-tuple-element.205), channel_id=1, source_target_pairs={{0,3},{1,0},{2,1},{3,2},{4,7},{5,4},{6,5},{7,6},{8,11},{9,8},{10,9... | collective-permute-start | bytes 786440 | tf_op jit(solution)/shard_map/ppermute | solution.py:102
  192.6 17.3 %collective-permute-start.20 = (bf16[704,2048]{1,0:T(8,128)(2,1)}, bf16[704,2048]{1,0:T(8,128)(2,1)}, u32[]{:S(2)}, u32[]{:S(2)}) collective-permute-start(bf16[704,2048]{1,0:T(8,128)(2,1)} %bitcast.99), channel_id=1, source_target_pairs={{0,4},{4,0},{8,12},{12,8},{16,20},{20,16},{24,28},{28,24},{1,5},{5... | collective-permute-start | bytes 8650760 | tf_op jit(solution)/shard_map/ppermute | solution.py:827
  219.9 110.1 %all-gather.11.cloned.1.call-start = ((), (), s32[]{:S(2)}) async-start(), calls=%async_computation.9 | async-start | bytes 5242880 | tf_op jit(solution)/shard_map/all_gather | solution.py:830
  221.1 11.4 %collective-permute-start.15 = (bf16[64,2048]{1,0:T(8,128)(2,1)S(1)}, bf16[64,2048]{1,0:T(8,128)(2,1)S(1)}, u32[]{:S(2)}, u32[]{:S(2)}) collective-permute-start(bf16[64,2048]{1,0:T(8,128)(2,1)S(1)} %get-tuple-element.230), channel_id=1, source_target_pairs={{0,1},{1,2},{2,3},{3,0},{4,5},{5,6},{6,7},{7,4},{8,9},{9,10},{10,1... | collective-permute-start | bytes 786440 | tf_op jit(solution)/shard_map/ppermute | solution.py:115
  224.5 19.1 %collective-permute-start.16 = (bf16[64,2048]{1,0:T(8,128)(2,1)S(1)}, bf16[64,2048]{1,0:T(8,128)(2,1)S(1)}, u32[]{:S(2)}, u32[]{:S(2)}) collective-permute-start(bf16[64,2048]{1,0:T(8,128)(2,1)S(1)} %get-tuple-element.232), channel_id=1, source_target_pairs={{0,2},{1,3},{2,0},{3,1},{4,6},{5,7},{6,4},{7,5},{8,10},{9,11},{10,... | collective-permute-start | bytes 786440 | tf_op jit(solution)/shard_map/ppermute | solution.py:115
  225.8 17.8 %collective-permute-start.17 = (bf16[64,2048]{1,0:T(8,128)(2,1)S(1)}, bf16[64,2048]{1,0:T(8,128)(2,1)S(1)}, u32[]{:S(2)}, u32[]{:S(2)}) collective-permute-start(bf16[64,2048]{1,0:T(8,128)(2,1)S(1)} %get-tuple-element.231), channel_id=1, source_target_pairs={{0,3},{1,0},{2,1},{3,2},{4,7},{5,4},{6,5},{7,6},{8,11},{9,8},{10,9... | collective-permute-start | bytes 786440 | tf_op jit(solution)/shard_map/ppermute | solution.py:115
  244.8 239.6 %copy-start.10 = (f32[64,2048]{1,0:T(8,128)}, f32[64,2048]{1,0:T(8,128)S(1)}, u32[]{:S(2)}) copy-start(f32[64,2048]{1,0:T(8,128)S(1)} %get-tuple-element.203) | copy-start | bytes 1572868
  245.1 78.1 %copy-start.21 = (bf16[64,2048]{1,0:T(8,128)(2,1)}, bf16[64,2048]{1,0:T(8,128)(2,1)S(1)}, u32[]{:S(2)}) copy-start(bf16[64,2048]{1,0:T(8,128)(2,1)S(1)} %get-tuple-element.201) | copy-start | bytes 786436
  245.1 12.8 %collective-permute-start.22 = (bf16[64,2048]{1,0:T(8,128)(2,1)S(1)}, bf16[64,2048]{1,0:T(8,128)(2,1)S(1)}, u32[]{:S(2)}, u32[]{:S(2)}) collective-permute-start(bf16[64,2048]{1,0:T(8,128)(2,1)S(1)} %get-tuple-element.201), channel_id=1, source_target_pairs={{0,1},{1,2},{2,3},{3,0},{4,5},{5,6},{6,7},{7,4},{8,9},{9,10},{10,1... | collective-permute-start | bytes 786440 | tf_op jit(solution)/shard_map/ppermute | solution.py:102
  251.2 15.3 %collective-permute-start.23 = (bf16[64,2048]{1,0:T(8,128)(2,1)S(1)}, bf16[64,2048]{1,0:T(8,128)(2,1)S(1)}, u32[]{:S(2)}, u32[]{:S(2)}) collective-permute-start(bf16[64,2048]{1,0:T(8,128)(2,1)S(1)} %get-tuple-element.201), channel_id=1, source_target_pairs={{0,2},{1,3},{2,0},{3,1},{4,6},{5,7},{6,4},{7,5},{8,10},{9,11},{10,... | collective-permute-start | bytes 786440 | tf_op jit(solution)/shard_map/ppermute | solution.py:102
  251.4 16.8 %collective-permute-start.24 = (bf16[64,2048]{1,0:T(8,128)(2,1)S(1)}, bf16[64,2048]{1,0:T(8,128)(2,1)S(1)}, u32[]{:S(2)}, u32[]{:S(2)}) collective-permute-start(bf16[64,2048]{1,0:T(8,128)(2,1)S(1)} %get-tuple-element.201), channel_id=1, source_target_pairs={{0,3},{1,0},{2,1},{3,2},{4,7},{5,4},{6,5},{7,6},{8,11},{9,8},{10,9... | collective-permute-start | bytes 786440 | tf_op jit(solution)/shard_map/ppermute | solution.py:102
  274.9 113.4 %reduce-scatter.5.cloned.1.call-start = ((), (), s32[]{:S(2)}) async-start(), calls=%async_computation.10 | async-start | bytes 5570560 | tf_op jit(solution)/shard_map/reduce_scatter | solution.py:833
  330.0 117.0 %reduce-scatter.7.cloned.1.call-start = ((), (), s32[]{:S(2)}) async-start(), calls=%async_computation.11 | async-start | bytes 5570560 | tf_op jit(solution)/shard_map/reduce_scatter | solution.py:833
  388.4 163.0 %reduce-scatter.9.cloned.1.call-start = ((), (), s32[]{:S(2)}) async-start(), calls=%async_computation.12 | async-start | bytes 10485760 | tf_op jit(solution)/shard_map/reduce_scatter | solution.py:833
  390.3 28.3 %collective-permute-start.25 = (bf16[64,2176]{1,0:T(8,128)(2,1)S(1)}, bf16[64,2176]{1,0:T(8,128)(2,1)S(1)}, u32[]{:S(2)}, u32[]{:S(2)}) collective-permute-start(bf16[64,2176]{1,0:T(8,128)(2,1)S(1)} %get-tuple-element.221), channel_id=1, source_target_pairs={{0,1},{1,2},{2,3},{3,0},{4,5},{5,6},{6,7},{7,4},{8,9},{9,10},{10,1... | collective-permute-start | bytes 835592 | tf_op jit(solution)/shard_map/ppermute | solution.py:115
  391.8 26.8 %collective-permute-start.26 = (bf16[64,2176]{1,0:T(8,128)(2,1)S(1)}, bf16[64,2176]{1,0:T(8,128)(2,1)S(1)}, u32[]{:S(2)}, u32[]{:S(2)}) collective-permute-start(bf16[64,2176]{1,0:T(8,128)(2,1)S(1)} %get-tuple-element.220), channel_id=1, source_target_pairs={{0,2},{1,3},{2,0},{3,1},{4,6},{5,7},{6,4},{7,5},{8,10},{9,11},{10,... | collective-permute-start | bytes 835592 | tf_op jit(solution)/shard_map/ppermute | solution.py:115
  394.2 24.4 %collective-permute-start.27 = (bf16[64,2176]{1,0:T(8,128)(2,1)S(1)}, bf16[64,2176]{1,0:T(8,128)(2,1)S(1)}, u32[]{:S(2)}, u32[]{:S(2)}) collective-permute-start(bf16[64,2176]{1,0:T(8,128)(2,1)S(1)} %get-tuple-element.219), channel_id=1, source_target_pairs={{0,3},{1,0},{2,1},{3,2},{4,7},{5,4},{6,5},{7,6},{8,11},{9,8},{10,9... | collective-permute-start | bytes 835592 | tf_op jit(solution)/shard_map/ppermute | solution.py:115
  422.1 24.7 %collective-permute-start.28 = (bf16[64,2048]{1,0:T(8,128)(2,1)S(1)}, bf16[64,2048]{1,0:T(8,128)(2,1)S(1)}, u32[]{:S(2)}, u32[]{:S(2)}) collective-permute-start(bf16[64,2048]{1,0:T(8,128)(2,1)S(1)} %get-tuple-element.198.refs_0_), channel_id=1, source_target_pairs={{0,1},{1,2},{2,3},{3,0},{4,5},{5,6},{6,7},{7,4},{8,9},{9,10},{10,1... | collective-permute-start | bytes 786440 | tf_op jit(solution)/shard_map/ppermute | solution.py:102
  422.6 24.2 %collective-permute-start.29 = (bf16[64,2048]{1,0:T(8,128)(2,1)S(1)}, bf16[64,2048]{1,0:T(8,128)(2,1)S(1)}, u32[]{:S(2)}, u32[]{:S(2)}) collective-permute-start(bf16[64,2048]{1,0:T(8,128)(2,1)S(1)} %get-tuple-element.198.refs_0_), channel_id=1, source_target_pairs={{0,2},{1,3},{2,0},{3,1},{4,6},{5,7},{6,4},{7,5},{8,10},{9,11},{10,... | collective-permute-start | bytes 786440 | tf_op jit(solution)/shard_map/ppermute | solution.py:102
  424.0 22.9 %collective-permute-start.30 = (bf16[64,2048]{1,0:T(8,128)(2,1)S(1)}, bf16[64,2048]{1,0:T(8,128)(2,1)S(1)}, u32[]{:S(2)}, u32[]{:S(2)}) collective-permute-start(bf16[64,2048]{1,0:T(8,128)(2,1)S(1)} %get-tuple-element.198.refs_0_), channel_id=1, source_target_pairs={{0,3},{1,0},{2,1},{3,2},{4,7},{5,4},{6,5},{7,6},{8,11},{9,8},{10,9... | collective-permute-start | bytes 786440 | tf_op jit(solution)/shard_map/ppermute | solution.py:102
  447.9 190.3 %reduce-scatter.11.cloned.1.call-start = ((), (), s32[]{:S(2)}) async-start(), calls=%async_computation.13 | async-start | bytes 10027008 | tf_op jit(solution)/shard_map/reduce_scatter | solution.py:1082
  449.6 32.5 %copy-start.43 = (f32[64]{0:T(128)}, f32[64]{0:T(128)S(1)}, u32[]{:S(2)}) copy-start(f32[64]{0:T(128)S(1)} %get-tuple-element.254) | copy-start | bytes 772
  449.6 68.0 %collective-permute-start.37 = (bf16[704,2048]{1,0:T(8,128)(2,1)}, bf16[704,2048]{1,0:T(8,128)(2,1)S(1)}, u32[]{:S(2)}, u32[]{:S(2)}) collective-permute-start(bf16[704,2048]{1,0:T(8,128)(2,1)} %get-tuple-element.102), channel_id=1, source_target_pairs={{0,4},{4,0},{8,12},{12,8},{16,20},{20,16},{24,28},{28,24},{1,5},{5... | collective-permute-start | bytes 8650760 | tf_op jit(solution)/shard_map/ppermute | solution.py:827
  453.5 28.2 %collective-permute-start.31 = (bf16[64,2176]{1,0:T(8,128)(2,1)}, bf16[64,2176]{1,0:T(8,128)(2,1)S(1)}, u32[]{:S(2)}, u32[]{:S(2)}) collective-permute-start(bf16[64,2176]{1,0:T(8,128)(2,1)} %get-tuple-element.217), channel_id=1, source_target_pairs={{0,1},{1,2},{2,3},{3,0},{4,5},{5,6},{6,7},{7,4},{8,9},{9,10},{10,1... | collective-permute-start | bytes 835592 | tf_op jit(solution)/shard_map/ppermute | solution.py:115
  455.5 26.2 %collective-permute-start.32 = (bf16[64,2176]{1,0:T(8,128)(2,1)S(1)}, bf16[64,2176]{1,0:T(8,128)(2,1)S(1)}, u32[]{:S(2)}, u32[]{:S(2)}) collective-permute-start(bf16[64,2176]{1,0:T(8,128)(2,1)S(1)} %get-tuple-element.216), channel_id=1, source_target_pairs={{0,2},{1,3},{2,0},{3,1},{4,6},{5,7},{6,4},{7,5},{8,10},{9,11},{10,... | collective-permute-start | bytes 835592 | tf_op jit(solution)/shard_map/ppermute | solution.py:115
  456.7 25.1 %collective-permute-start.33 = (bf16[64,2176]{1,0:T(8,128)(2,1)S(1)}, bf16[64,2176]{1,0:T(8,128)(2,1)S(1)}, u32[]{:S(2)}, u32[]{:S(2)}) collective-permute-start(bf16[64,2176]{1,0:T(8,128)(2,1)S(1)} %get-tuple-element.215), channel_id=1, source_target_pairs={{0,3},{1,0},{2,1},{3,2},{4,7},{5,4},{6,5},{7,6},{8,11},{9,8},{10,9... | collective-permute-start | bytes 835592 | tf_op jit(solution)/shard_map/ppermute | solution.py:115
  481.8 35.9 %collective-permute-start.38 = (bf16[704,2048]{1,0:T(8,128)(2,1)}, bf16[704,2048]{1,0:T(8,128)(2,1)}, u32[]{:S(2)}, u32[]{:S(2)}) collective-permute-start(bf16[704,2048]{1,0:T(8,128)(2,1)} %get-tuple-element.103), channel_id=1, source_target_pairs={{0,4},{4,0},{8,12},{12,8},{16,20},{20,16},{24,28},{28,24},{1,5},{5... | collective-permute-start | bytes 8650760 | tf_op jit(solution)/shard_map/ppermute | solution.py:827
  485.4 29.7 %collective-permute-start.34 = (bf16[64,2048]{1,0:T(8,128)(2,1)S(1)}, bf16[64,2048]{1,0:T(8,128)(2,1)}, u32[]{:S(2)}, u32[]{:S(2)}) collective-permute-start(bf16[64,2048]{1,0:T(8,128)(2,1)S(1)} %get-tuple-element.195.refs_2_), channel_id=1, source_target_pairs={{0,1},{1,2},{2,3},{3,0},{4,5},{5,6},{6,7},{7,4},{8,9},{9,10},{10,1... | collective-permute-start | bytes 786440 | tf_op jit(solution)/shard_map/ppermute | solution.py:102
  487.1 29.0 %collective-permute-start.35 = (bf16[64,2048]{1,0:T(8,128)(2,1)S(1)}, bf16[64,2048]{1,0:T(8,128)(2,1)S(1)}, u32[]{:S(2)}, u32[]{:S(2)}) collective-permute-start(bf16[64,2048]{1,0:T(8,128)(2,1)S(1)} %get-tuple-element.195.refs_2_), channel_id=1, source_target_pairs={{0,2},{1,3},{2,0},{3,1},{4,6},{5,7},{6,4},{7,5},{8,10},{9,11},{10,... | collective-permute-start | bytes 786440 | tf_op jit(solution)/shard_map/ppermute | solution.py:102
  488.1 28.0 %collective-permute-start.36 = (bf16[64,2048]{1,0:T(8,128)(2,1)S(1)}, bf16[64,2048]{1,0:T(8,128)(2,1)S(1)}, u32[]{:S(2)}, u32[]{:S(2)}) collective-permute-start(bf16[64,2048]{1,0:T(8,128)(2,1)S(1)} %get-tuple-element.195.refs_2_), channel_id=1, source_target_pairs={{0,3},{1,0},{2,1},{3,2},{4,7},{5,4},{6,5},{7,6},{8,11},{9,8},{10,9... | collective-permute-start | bytes 786440 | tf_op jit(solution)/shard_map/ppermute | solution.py:102
  556.5 26.4 %collective-permute-start.39 = (bf16[128,4096]{1,0:T(8,128)(2,1)S(1)}, bf16[128,4096]{1,0:T(8,128)(2,1)S(1)}, u32[]{:S(2)}, u32[]{:S(2)}) collective-permute-start(bf16[128,4096]{1,0:T(8,128)(2,1)S(1)} %get-tuple-element.212), channel_id=1, source_target_pairs={{0,1},{1,2},{2,3},{3,0},{4,5},{5,6},{6,7},{7,4},{8,9},{9,10},{10,1... | collective-permute-start | bytes 3145736 | tf_op jit(solution)/shard_map/ppermute | solution.py:115
  556.9 49.1 %collective-permute-start.42 = (bf16[704,2048]{1,0:T(8,128)(2,1)}, bf16[704,2048]{1,0:T(8,128)(2,1)}, u32[]{:S(2)}, u32[]{:S(2)}) collective-permute-start(bf16[704,2048]{1,0:T(8,128)(2,1)} %get-tuple-element.108), channel_id=1, source_target_pairs={{0,4},{4,0},{8,12},{12,8},{16,20},{20,16},{24,28},{28,24},{1,5},{5... | collective-permute-start | bytes 8650760 | tf_op jit(solution)/shard_map/ppermute | solution.py:827
  582.9 2.7 collective-permute-start.46
  582.9 47.3 %collective-permute-start.40 = (bf16[128,4096]{1,0:T(8,128)(2,1)}, bf16[128,4096]{1,0:T(8,128)(2,1)S(1)}, u32[]{:S(2)}, u32[]{:S(2)}) collective-permute-start(bf16[128,4096]{1,0:T(8,128)(2,1)} %get-tuple-element.211), channel_id=1, source_target_pairs={{0,2},{1,3},{2,0},{3,1},{4,6},{5,7},{6,4},{7,5},{8,10},{9,11},{10,... | collective-permute-start | bytes 3145736 | tf_op jit(solution)/shard_map/ppermute | solution.py:115
  582.9 48.6 %collective-permute-start.41 = (bf16[128,4096]{1,0:T(8,128)(2,1)}, bf16[128,4096]{1,0:T(8,128)(2,1)}, u32[]{:S(2)}, u32[]{:S(2)}) collective-permute-start(bf16[128,4096]{1,0:T(8,128)(2,1)} %get-tuple-element.210), channel_id=1, source_target_pairs={{0,3},{1,0},{2,1},{3,2},{4,7},{5,4},{6,5},{7,6},{8,11},{9,8},{10,9... | collective-permute-start | bytes 3145736 | tf_op jit(solution)/shard_map/ppermute | solution.py:115
  587.0 48.0 %all-to-all-start.1 = ((bf16[3,8,88,256]{3,2,0,1:T(8,128)(2,1)}), bf16[3,8,88,256]{3,2,0,1:T(8,128)(2,1)}, u32[]{:S(2)}, u32[]{:S(2)}) async-start(bf16[3,8,88,256]{3,2,0,1:T(8,128)(2,1)} %bitcast.95), calls=%async_computation.5 | async-start | bytes 2162688 | tf_op jit(solution)/shard_map/all_to_all | solution.py:1068
  640.3 28.8 %collective-permute-start.43 = (bf16[64,640]{1,0:T(8,128)(2,1)S(1)}, bf16[64,640]{1,0:T(8,128)(2,1)S(1)}, u32[]{:S(2)}, u32[]{:S(2)}) collective-permute-start(bf16[64,640]{1,0:T(8,128)(2,1)S(1)} %get-tuple-element.236), channel_id=1, source_target_pairs={{0,1},{1,2},{2,3},{3,0},{4,5},{5,6},{6,7},{7,4},{8,9},{9,10},{10,1... | collective-permute-start | bytes 245768 | tf_op jit(solution)/shard_map/ppermute | solution.py:115
  661.5 7.7 %collective-permute-start.44 = (bf16[64,640]{1,0:T(8,128)(2,1)S(1)}, bf16[64,640]{1,0:T(8,128)(2,1)S(1)}, u32[]{:S(2)}, u32[]{:S(2)}) collective-permute-start(bf16[64,640]{1,0:T(8,128)(2,1)S(1)} %get-tuple-element.238), channel_id=1, source_target_pairs={{0,2},{1,3},{2,0},{3,1},{4,6},{5,7},{6,4},{7,5},{8,10},{9,11},{10,... | collective-permute-start | bytes 245768 | tf_op jit(solution)/shard_map/ppermute | solution.py:115
  662.9 6.2 collective-permute-start.45
  (41 other events, 420.3 us)
Sparse Core Ops, SparseCore 0:
  22.6 57.5 all-gather.4
  82.7 103.5 all-gather.6
  220.0 54.8 all-gather.8
  277.2 52.6 all-gather.10
  333.4 54.8 reduce-scatter.4
  391.8 54.8 reduce-scatter.6
  449.8 86.3 reduce-scatter.8
  551.5 86.7 reduce-scatter.10

commit v4 on v3

--- a/solution.py
+++ b/solution.py
@@ -150,17 +150,55 @@
         self.block = at // 128 * 128
         assert self.block >= self.even and self.block + 128 >= at + experts
 
-    def join(self, gate, upper):
-        return jnp.concatenate(
-            [gate[: self.even], gate[self.even :], upper[self.even :], upper[: self.even]]
-        )
-
-
-def back_kernel(plan, first_ref, mid_ref, dout_ref, meta_ref, w1_ref, wd_ref, *refs):
+    def places(self, model):
+        both, end = (2 * self.units, self.cols)
+        up_at = self.even + 2 * self.tail
+        head = self.even - both
+        gate = [(0, self.units, 0), (0, self.units, self.units), (0, end - both, both)]
+        up = [(0, self.units, up_at), (0, self.units, up_at + self.units)]
+        up.append((head, self.tail, self.cols))
+        if head:
+            up.append((0, head, up_at + both))
+        return (gate, up, gate)
+
+
+def weight_copies(plan, pieces, w1_ref, wd_ref, sems):
+    copies = ([], [], [])
+    turn = 0
+    for k, places in enumerate(plan.places(None)):
+        target = wd_ref if k == 2 else w1_ref
+        if target is None:
+            continue
+        for n, (start, rows, at) in enumerate(places):
+            source = pieces[3 * k + min(n, 2)]
+            copy = pltpu.make_async_copy(
+                source.at[pl.ds(start, rows)], target.at[pl.ds(at, rows)], sems.at[turn]
+            )
+            copies[(1, 2, 0, 0)[n]].append(copy)
+            turn += 1
+    return copies
+
+
+def back_kernel(plan, first_ref, mid_ref, dout_ref, meta_ref, *refs):
     f32, bf16 = (jnp.float32, jnp.bfloat16)
     even, tail, hidden = (plan.even, plan.tail, plan.hidden)
     rows, model = mid_ref.shape
-    rows_ref, gud_ref, act_ref = refs[-3:]
+    rows_ref, gud_ref, act_ref, w1_ref, wd_ref, sems = refs[-6:]
+    step0 = pl.program_id(0) == 0
+    copies = weight_copies(plan, refs[:9], w1_ref, wd_ref, sems)
+
+    @pl.when(step0)
+    def _():
+        for group in copies:
+            for copy in group:
+                copy.start()
+
+    def arrived(n):
+        @pl.when(step0)
+        def _():
+            for copy in copies[n]:
+                copy.wait()
+
     mid = mid_ref[...]
     dout = dout_ref[...].reshape(rows, model)
     lanes = lax.broadcasted_iota(jnp.int32, (rows, 128), 1)
@@ -196,6 +234,10 @@
             gud_ref[:, gate_at + b : gate_at + b + 128] = (da * u * slope).astype(bf16)
             gud_ref[:, up_at + b : up_at + b + 128] = (da * swish).astype(bf16)
 
+    arrived(0)
+    if even < 2 * plan.units:
+        arrived(1)
+        arrived(2)
     joint = dot_nt(mid, w1_ref[even : even + 2 * tail, :])
     at_block = plan.block - even
     sig = jax.nn.sigmoid(joint[:, at_block : at_block + 128])
@@ -214,6 +256,10 @@
     act_grad = dot_nt(dout, wd_ref[even : even + tail, :])
     elements(own, even, joint[:, :tail], joint[:, tail:], act_grad, even, even + tail)
     for at in range(0, even, 256):
+        if even >= 2 * plan.units and at == 0:
+            arrived(1)
+        if even >= 2 * plan.units and at <= plan.units < at + 256:
+            arrived(2)
         up_at = even + 2 * tail + at
         elements(
             own,
@@ -236,7 +282,7 @@
     rows_ref[:, model:] = ends.astype(bf16)
 
 
-def experts_back(plan, chunk, first, mid, dout, w1, wd, *held):
+def experts_back(plan, chunk, first, mid, dout, pieces, *held):
     tokens, model = mid.shape
     _, chunks, rows, _ = dout.shape
     tile = min(512, tokens)
@@ -246,9 +292,6 @@
 
     def slot(width):
         return pl.BlockSpec((None, tile, width), lambda i: (chunk, i, 0))
-
-    def whole(value):
-        return pl.BlockSpec(value.shape, lambda i: (0, 0), pipeline_mode=pl.Buffered(1))
 
     def outer(width, at):
         return pl.BlockSpec((tile // rows, None, rows, width), lambda i: (i, chunk, 0, at))
@@ -262,17 +305,20 @@
             row(model),
             outer(model, 0),
             outer(128, model // 128),
-            whole(w1),
-            whole(wd),
         ]
-        + [pl.BlockSpec(memory_space=pl.ANY) for _ in held],
+        + [pl.BlockSpec(memory_space=pl.ANY) for _ in (*pieces, *held)],
         out_specs=[row(model + 128), slot(2 * plan.cols), slot(plan.cols)],
         out_shape=[
             jax.ShapeDtypeStruct((tokens, model + 128), bf16),
             jax.ShapeDtypeStruct((chunks, tokens, 2 * plan.cols), bf16),
             jax.ShapeDtypeStruct((chunks, tokens, plan.cols), bf16),
         ],
-        input_output_aliases={6 + n: 1 + n for n in range(len(held))},
+        input_output_aliases={4 + len(pieces) + n: 1 + n for n in range(len(held))},
+        scratch_shapes=[
+            pltpu.VMEM((2 * plan.cols, model), bf16),
+            pltpu.VMEM((plan.cols, model), bf16),
+            pltpu.SemaphoreType.DMA((11,)),
+        ],
         compiler_params=pltpu.CompilerParams(
             dimension_semantics=("arbitrary",), vmem_limit_bytes=58 * MIB
         ),
@@ -282,33 +328,46 @@
             transcendentals=tokens * plan.cols,
         ),
         name="experts_back",
-    )(first, mid, dout, dout, w1, wd, *held)
-
-
-def out_kernel(act_ref, wd_ref, *refs):
-    out_ref = refs[-1]
-    rows, model = (act_ref.shape[0], wd_ref.shape[1])
+    )(first, mid, dout, dout, *pieces, *held)
+
+
+def out_kernel(plan, act_ref, *refs):
+    out_ref, wd_ref, sems = refs[-3:]
+    copies = weight_copies(plan, [None] * 6 + list(refs[:3]), None, wd_ref, sems)
+
+    @pl.when((pl.program_id(0) == 0) & (pl.program_id(1) == 0))
+    def _():
+        for group in copies:
+            for copy in group:
+                copy.start()
+        for group in copies:
+            for copy in group:
+                copy.wait()
+
     act = act_ref[...]
-    for at in range(0, model, 512):
+    for at in range(0, wd_ref.shape[1], 512):
         part = dot32(act, wd_ref[:, at : at + 512]).astype(jnp.bfloat16)
         out_ref[:, :, at : at + 512] = part.reshape(out_ref.shape[0], out_ref.shape[1], 512)
 
 
-def experts_out(plan, groups, lanes, start, chunks, act, wd, *others):
+def experts_out(plan, groups, lanes, start, chunks, act, down, *others):
     _, tokens, cols = act.shape
-    model = wd.shape[1]
+    model = down[0].shape[1]
     count = tokens // groups
     rows = count // lanes
     return pl.pallas_call(
-        out_kernel,
+        functools.partial(out_kernel, plan),
         grid=(chunks, groups),
         in_specs=[
             pl.BlockSpec((None, count, cols), lambda h, g: (start + h, g, 0)),
-            pl.BlockSpec(wd.shape, lambda h, g: (0, 0), pipeline_mode=pl.Buffered(1)),
         ]
-        + [pl.BlockSpec(memory_space=pl.ANY) for _ in others],
+        + [pl.BlockSpec(memory_space=pl.ANY) for _ in (*down, *others)],
         out_specs=pl.BlockSpec((None, lanes, None, rows, model), lambda h, g: (g, 0, h, 0, 0)),
         out_shape=jax.ShapeDtypeStruct((groups, lanes, chunks, rows, model), jnp.bfloat16),
+        scratch_shapes=[
+            pltpu.VMEM((plan.cols, model), jnp.bfloat16),
+            pltpu.SemaphoreType.DMA((3,)),
+        ],
         compiler_params=pltpu.CompilerParams(
             dimension_semantics=("arbitrary", "arbitrary"), vmem_limit_bytes=60 * MIB
         ),
@@ -318,7 +377,7 @@
             transcendentals=0,
         ),
         name="experts_out",
-    )(act, wd, *others).reshape(groups * lanes * chunks * rows, model)
+    )(act, *down, *others).reshape(groups * lanes * chunks * rows, model)
 
 
 def sum_kernel(plan, kind, chunks, h_ref, *refs):
@@ -858,9 +917,9 @@
     )
     small = gather_ctx(small)
     seg_all = small[:, at_seg : at_seg + seg_cols.shape[1]].astype(jnp.int32).reshape(count)
-    pieces = depth // w_expand.shape[0]
-    wide = expand_c // pieces
-    expand_blocks = [w_expand[:, k * wide : (k + 1) * wide] for k in range(pieces)]
+    folds = depth // w_expand.shape[0]
+    wide = expand_c // folds
+    expand_blocks = [w_expand[:, k * wide : (k + 1) * wide] for k in range(folds)]
     heads = Heads(width, groups, depth, small_c, wide, heads_c)
     order = heads.order()
     packed = jnp.concatenate(
@@ -891,14 +950,15 @@
     cosine, sine = (jnp.concatenate([f(angle)] * 4, axis=1) for f in (jnp.cos, jnp.sin))
     fixed = (cosine, sine, seg_all[:, None], seg_all[None, :], latent_gain[None, :])
     lane = lax.axis_index("ctx").astype(jnp.int32)[None]
+    early_pair = [swap(w.reshape(units, model_w)) for w in (expert_gate, routed_up_weight)]
     x_all, x_low, factor_in, q_low, kv_low, kr_low, latent_raw, latent_low_t, lse, heads_low, *attn = (
-        attend(heads, chunks, lane, norm_in[None, :], packed, *fixed, x_pieces)
+        attend(heads, chunks, lane, norm_in[None, :], packed, *fixed, x_pieces, *early_pair)
     )
     def pair_weights(*others):
         shared = jnp.stack([shared_gate.T, shared_up.T, shared_down]).reshape(
             3, groups, sh_units, depth
         )
-        shared, *pack = after((shared, expert_gate, routed_up_weight, expert_down), *others)
+        shared, late_down = after((shared, expert_down), *others)
         shared = lax.all_to_all(shared, "fsdp", split_axis=1, concat_axis=1, tiled=True)
         shared = shared.transpose(0, 2, 1, 3).reshape(3, sh_units, model_w)
 
@@ -906,23 +966,19 @@
             shared = jnp.pad(shared, ((0, 0), (0, plan.shared - sh_units), (0, 0)))
         shared_pair = swap(shared)
 
-        pack = [weights.reshape(units, model_w) for weights in pack]
-        pair = [swap(weights) for weights in pack]
-
-        def hidden_rows(k, router):
+        pack = [w.reshape(units, model_w) for w in (expert_gate, routed_up_weight, late_down)]
+        pair = [*early_pair, swap(pack[2])]
+
+        def rest(k, router):
             gap = jnp.zeros((plan.router - 2 * (units + plan.shared), model_w), bf16)
             end = jnp.zeros((plan.cols - plan.router - router.shape[0], model_w), bf16)
-            return jnp.concatenate([pack[k], pair[k], shared[k], shared_pair[k], gap, router, end])
+            return jnp.concatenate([shared[k], shared_pair[k], gap, router, end])
 
         none = jnp.zeros((0, model_w), bf16)
-        w1 = plan.join(
-            hidden_rows(0, router_w.T),
-            hidden_rows(1, none),
-        )
-        wd = hidden_rows(2, none)
-        return (w1, wd)
-
-    w1, wd = pair_weights(lse)
+        rests = (rest(0, router_w.T), rest(1, none), rest(2, none))
+        return [part for k in range(3) for part in (pack[k], pair[k], rests[k])]
+
+    pieces = pair_weights(lse)
 
     own_experts = group * exp_dev + jnp.arange(exp_dev, dtype=jnp.int32)
     pair_experts = (group ^ 1) * exp_dev + jnp.arange(exp_dev, dtype=jnp.int32)
@@ -940,12 +996,12 @@
         factor_mid.append(factor)
         mid_low.append(mid.astype(bf16))
         mid_part = gather_ctx(mid_low[h])
+        mid_part = after(mid_part, *pieces)
         sent = (mid_part,)
-        mid_part = after(mid_part, w1, wd)
         last = gather_half(after(mid_part, last))
         mids.append(last)
     for h in range(chunks):
-        rows_part, *held = experts_back(plan, h, first, mids[h], dout_all, w1, wd, *held)
+        rows_part, *held = experts_back(plan, h, first, mids[h], dout_all, pieces, *held)
         rows_part = after(rows_part, last)
         last = scatter_half(rows_part)
         rows_parts.append(last)
@@ -981,7 +1037,7 @@
 
     def outputs(*others):
         return [
-            experts_out(plan, half, lanes, h, 2, act, wd, *others) for h in range(0, chunks, 2)
+            experts_out(plan, half, lanes, h, 2, act, pieces[6:], *others) for h in range(0, chunks, 2)
         ]
 
     if chunks == 2:
@@ -1084,7 +1140,7 @@
     g_query = dot_nt(grads[:, : heads.query], order)
     g_expand = grads[:, at_expand:at_output].astype(f32)
     g_expand = jnp.concatenate(
-        [g_expand[k * w_expand.shape[0] : (k + 1) * w_expand.shape[0]] for k in range(pieces)],
+        [g_expand[k * w_expand.shape[0] : (k + 1) * w_expand.shape[0]] for k in range(folds)],
         axis=1,
     )
     g_output = grads[:, at_output:].astype(f32).T

time: 683 us -> 664 us (0.972)
  local copies, waits for them, and re-layouts: 50.2 us -> 36.7 us
  other arithmetic: 31.6 us -> 20.8 us
  waiting for transfers between devices: 194 us -> 201 us
    unnamed x108 -> x118, local copies, waits for them, and re-layouts: 21.6 us -> 11 us
    all_to_all x1, waiting for transfers between devices: 0.01 us -> 6.89 us  [pair_weights(): lax.all_to_all(shared, 'fsdp', split_axis=1, concat_axis=1, tiled=True)]
    concatenate x2, other arithmetic: 10 us -> 3.13 us  [rest(): return jnp.concatenate([shared[k], shared_pair[k], gap, router, end])]
  transfers between devices with their start and end apart: 57 -> 57, of which waited for: 23 -> 26; matrix products, arithmetic and copies ran while one was open for 12% -> 8% of each run, Pallas kernels for 38% -> 39%
where the time goes in v4:
time: 664 us; the launch traced here: 660 us
  Pallas kernels  257 us (39%)
  waiting for transfers between devices  201 us (30%)
  starting transfers between devices  116 us (17%)
  local copies, waits for them, and re-layouts  36.7 us (6%)
  other arithmetic  20.8 us (3%)
  between operations  15.8 us (2%)
  matrix products  12.4 us (2%)
    pallas_call x2, Pallas kernels, experts_back(): pl.pallas_call(functools.partial(back_kernel, plan), grid=(tokens // tile...  96.2 us
    ppermute x18, waiting for transfers between devices, pieces_ctx(): lax.ppermute(part, 'ctx', [(i, (i + hop) % lanes) for i in range(lanes)])  76.9 us
    pallas_call x3, Pallas kernels, weight_sum(): pl.pallas_call(functools.partial(sum_kernel, plan, kind, chunks), grid=(c...  69.2 us
    ppermute x18, waiting for transfers between devices, gather_ctx(): lax.ppermute(value, 'ctx', [(i, (i + hop) % lanes) for i in range(lanes)])  59.5 us
    ppermute x18, starting transfers between devices, pieces_ctx(): lax.ppermute(part, 'ctx', [(i, (i + hop) % lanes) for i in range(lanes)])  55.1 us
    ppermute x18, starting transfers between devices, gather_ctx(): lax.ppermute(value, 'ctx', [(i, (i + hop) % lanes) for i in range(lanes)])  36.7 us
    ppermute x3, waiting for transfers between devices, spread_ctx(): lax.ppermute(value, 'ctx', [(i, (i + hop) % lanes) for i in range(lanes)])  30.4 us
    pallas_call x1, Pallas kernels, experts_out(): pl.pallas_call(functools.partial(out_kernel, plan), grid=(chunks, groups)...  21.9 us
  transfers between devices with their start and end apart: 57, of which 26 were waited for; matrix products, arithmetic and copies ran while one was open for 8% of the time, Pallas kernels for 39%

profile of v4, /device:TPU:0, one launch (start us, length us, event | category | flops | bytes accessed | tf_op | source)
XLA Modules:
  0.0 659.8 jit_solution(9697035723074926334)
XLA Ops:
  10.0 3.1 collective-permute-start
  13.1 2.6 collective-permute-start.1
  18.2 3.0 collective-permute-done.1
  23.7 2.0 collective-permute-start.3
  25.7 1.9 collective-permute-start.4
  29.5 12.0 %collective-permute-done.3 = bf16[128,2176]{1,0:T(8,128)(2,1)} collective-permute-done((bf16[128,2176]{1,0:T(8,128)(2,1)}, bf16[128,2176]{1,0:T(8,128)(2,1)}, u32[]{:S(2)}, u32[]{:S(2)}) %collective-permute-start.3) | collective-permute-done | bytes 557088 | tf_op jit(solution)/shard_map/ppermute | solution.py:102
  42.6 21.4 %collective-permute-done.4 = bf16[128,2176]{1,0:T(8,128)(2,1)S(1)} collective-permute-done((bf16[128,2176]{1,0:T(8,128)(2,1)}, bf16[128,2176]{1,0:T(8,128)(2,1)S(1)}, u32[]{:S(2)}, u32[]{:S(2)}) %collective-permute-start.4) | collective-permute-done | bytes 557088 | tf_op jit(solution)/shard_map/ppermute | solution.py:102
  68.2 12.4 %collective-permute-start.6 = (bf16[128,2048]{1,0:T(8,128)(2,1)S(1)}, bf16[128,2048]{1,0:T(8,128)(2,1)S(1)}, u32[]{:S(2)}, u32[]{:S(2)}) collective-permute-start(bf16[128,2048]{1,0:T(8,128)(2,1)S(1)} %copy-done.4), channel_id=1, source_target_pairs={{0,1},{1,2},{2,3},{3,0},{4,5},{5,6},{6,7},{7,4},{8,9},{9,10},{10,1... | collective-permute-start | bytes 1572872 | tf_op jit(solution)/shard_map/ppermute | solution.py:133
  85.5 8.5 %collective-permute-done.6.refs_1_ = bf16[128,2048]{1,0:T(8,128)(2,1)S(1)} collective-permute-done((bf16[128,2048]{1,0:T(8,128)(2,1)S(1)}, bf16[128,2048]{1,0:T(8,128)(2,1)S(1)}, u32[]{:S(2)}, u32[]{:S(2)}) %collective-permute-start.6) | collective-permute-done | bytes 524320 | tf_op jit(solution)/shard_map/ppermute | solution.py:133
  94.0 21.9 %collective-permute-done.7.refs_2_ = bf16[128,2048]{1,0:T(8,128)(2,1)S(1)} collective-permute-done((bf16[128,2048]{1,0:T(8,128)(2,1)S(1)}, bf16[128,2048]{1,0:T(8,128)(2,1)S(1)}, u32[]{:S(2)}, u32[]{:S(2)}) %collective-permute-start.7) | collective-permute-done | bytes 524320 | tf_op jit(solution)/shard_map/ppermute | solution.py:133
  116.9 15.4 %attend.1 = (bf16[512,2048]{1,0:T(8,128)(2,1)}, bf16[512,2048]{1,0:T(8,128)(2,1)}, f32[512,128]{1,0:T(8,128)}, bf16[512,768]{1,0:T(8,128)(2,1)}, bf16[512,1024]{...) custom-call(s32[1]{0:T(128)} %bitcast.lane_ref, ...), custom_call_target="tpu_custom_call" | custom-call | flops 6174015488 | bytes 17301504 | tf_op jit(solution)/shard_map/attend/pallas_call | solution.py:729
  132.3 1.9 constant_dynamic-slice_fusion.20
  134.1 12.8 %collective-permute-start.11 = (bf16[64,2048]{1,0:T(8,128)(2,1)}, bf16[64,2048]{1,0:T(8,128)(2,1)S(1)}, u32[]{:S(2)}, u32[]{:S(2)}) collective-permute-start(bf16[64,2048]{1,0:T(8,128)(2,1)} %get-tuple-element.230), channel_id=1, source_target_pairs={{0,1},{1,2},{2,3},{3,0},{4,5},{5,6},{6,7},{7,4},{8,9},{9,10},{10,1... | collective-permute-start | bytes 786440 | tf_op jit(solution)/shard_map/ppermute | solution.py:115
  146.9 2.2 collective-permute-start.12
  150.6 3.8 all-to-all-start
  156.1 10.2 %collective-permute-done.12 = bf16[64,2048]{1,0:T(8,128)(2,1)S(1)} collective-permute-done((bf16[64,2048]{1,0:T(8,128)(2,1)S(1)}, bf16[64,2048]{1,0:T(8,128)(2,1)S(1)}, u32[]{:S(2)}, u32[]{:S(2)}) %collective-permute-start.12) | collective-permute-done | bytes 262176 | tf_op jit(solution)/shard_map/ppermute | solution.py:115
  167.8 6.1 collective-permute-start.14
  175.1 6.9 %all-to-all-done = bf16[3,8,88,256]{3,2,0,1:T(8,128)(2,1)S(1)} async-done(((bf16[3,8,88,256]{3,2,0,1:T(8,128)(2,1)}), bf16[3,8,88,256]{3,2,0,1:T(8,128)(2,1)S(1)}, u32[]{:S(2)}, u32[]{:S(2)}) %all-to-all-start) | async-done | bytes 1081376 | tf_op jit(solution)/shard_map/all_to_all | solution.py:962
  184.5 2.1 collective-permute-start.16
  186.6 1.7 constant_dynamic-update-slice_fusion.14
  188.3 3.7 collective-permute-done.15
  192.7 4.8 collective-permute-done.16
  200.8 1.9 maximum_maximum_fusion.2
  203.6 3.0 collective-permute-start.20
  206.8 7.3 %collective-permute-done.19 = bf16[64,2048]{1,0:T(8,128)(2,1)S(1)} collective-permute-done((bf16[64,2048]{1,0:T(8,128)(2,1)S(1)}, bf16[64,2048]{1,0:T(8,128)(2,1)S(1)}, u32[]{:S(2)}, u32[]{:S(2)}) %collective-permute-start.19) | collective-permute-done | bytes 262176 | tf_op jit(solution)/shard_map/ppermute | solution.py:115
  214.1 10.4 %collective-permute-done.20 = bf16[64,2048]{1,0:T(8,128)(2,1)S(1)} collective-permute-done((bf16[64,2048]{1,0:T(8,128)(2,1)S(1)}, bf16[64,2048]{1,0:T(8,128)(2,1)S(1)}, u32[]{:S(2)}, u32[]{:S(2)}) %collective-permute-start.20) | collective-permute-done | bytes 262176 | tf_op jit(solution)/shard_map/ppermute | solution.py:115
  225.0 5.5 collective-permute-start.22
  230.5 2.4 collective-permute-start.24
  232.9 4.3 collective-permute-done.22
  237.3 9.9 %collective-permute-done.23 = bf16[64,2048]{1,0:T(8,128)(2,1)S(1)} collective-permute-done((bf16[64,2048]{1,0:T(8,128)(2,1)S(1)}, bf16[64,2048]{1,0:T(8,128)(2,1)S(1)}, u32[]{:S(2)}, u32[]{:S(2)}) %collective-permute-start.23) | collective-permute-done | bytes 262176 | tf_op jit(solution)/shard_map/ppermute | solution.py:102
  247.3 8.9 %all-gather.9.cloned.1.call-done.mid_ref.refs_0_ = bf16[1024,2048]{1,0:T(8,128)(2,1)} async-done(((bf16[256,2048]{1,0:T(8,128)(2,1)}), bf16[1024,2048]{1,0:T(8,128)(2,1)}) %all-gather.9.cloned.1.call-update) | async-done | bytes 4194320 | tf_op jit(solution)/shard_map/all_gather | solution.py:889
  256.8 48.0 %experts_back.2 = (bf16[1024,2176]{1,0:T(8,128)(2,1)}, bf16[2,1024,3328]{2,1,0:T(8,128)(2,1)}, bf16[2,1024,1664]{2,1,0:T(8,128)(2,1)}) custom-call(s32[4]{0:T(128)} %pad_add_fusion.first_ref, bf16[1024,2048]{1,0:T(8,128)(2,1)} %all-gather.9.cloned.1.call-done.mid_ref.refs_0_, bf16[16,2,64,2176]{3,2,1,0:T(8,128)(2,1)} %bitcast.118, ...), custom_call_target="tpu_custom_call" | custom-call | flops 34896609280 | bytes 22806528 | tf_op jit(solution)/shard_map/experts_back/pallas_call | solution.py:300
  304.9 6.3 all-gather.11.cloned.1.call-done.mid_ref.refs_1_
  311.3 48.2 %experts_back.3 = (bf16[1024,2176]{1,0:T(8,128)(2,1)}, bf16[2,1024,3328]{2,1,0:T(8,128)(2,1)}, bf16[2,1024,1664]{2,1,0:T(8,128)(2,1)}) custom-call(s32[4]{0:T(128)} %pad_add_fusion.first_ref, bf16[1024,2048]{1,0:T(8,128)(2,1)} %all-gather.11.cloned.1.call-done.mid_ref.refs_1_, ...), custom_call_target="tpu_custom_call", output_to_operand_aliasing={{1}: (13, {}), {2}: (14, {})} | custom-call | flops 34896609280 | bytes 22806528 | tf_op jit(solution)/shard_map/experts_back/pallas_call | solution.py:300
  359.4 10.1 %reduce-scatter.5.cloned.1.call-done = bf16[256,2176]{1,0:T(8,128)(2,1)} async-done(((bf16[1024,2176]{1,0:T(8,128)(2,1)}), bf16[256,2176]{1,0:T(8,128)(2,1)}) %reduce-scatter.5.cloned.1.call-update) | async-done | bytes 1114128 | tf_op jit(solution)/shard_map/reduce_scatter | solution.py:892
  369.8 1.6 select_reduce_fusion.2
  371.6 1.5 collective-permute-start.25
  373.1 2.4 collective-permute-start.26
  377.0 22.9 %gate_sum.1 = (f32[704,2048]{1,0:T(8,128)}, f32[88,2048]{1,0:T(8,128)}, bf16[704,2048]{1,0:T(8,128)(2,1)}, bf16[88,2048]{1,0:T(8,128)(2,1)}) custom-call(bf16[2,1024,3328]{2,1,0:T(8,128)(2,1)} %get-tuple-element.87.h_ref, bf16[1024,2048]{1,0:T(8,128)(2,1)} %all-gather.9.cloned.1.call-done.mid_ref.refs_0_, ...), custom_call_target="tpu_custom_call" | custom-call | flops 13958643712 | bytes 20971520 | tf_op jit(solution)/shard_map/gate_sum/pallas_call | solution.py:449
  400.2 2.0 multiply_reduce_fusion.1
  405.3 1.9 collective-permute-start.30
  407.2 21.9 %experts_out.1 = bf16[4,4,2,64,2048]{4,3,2,1,0:T(8,128)(2,1)} custom-call(bf16[2,1024,1664]{2,1,0:T(8,128)(2,1)} %get-tuple-element.86.act_ref.h_ref, bf16[704,2048]{1,0:T(8,128)(2,1)} %bitcast.133, bf16[704,2048]{1,0:T(8,128)(2,1)} %collective-permute-done.18.refs_7_.refs_1_, bf16[256,2048]{1,0:T(8,128)(2,1)} %get-tuple-element.248.refs_8_.refs_2_, ...), custom_call_target="tpu_custom_call" | custom-call | flops 13958643712 | bytes 15204352 | tf_op jit(solution)/shard_map/experts_out/pallas_call | solution.py:358
  430.4 1.6 select_reduce_fusion.1
  432.1 1.9 fusion.54
  437.1 2.8 collective-permute-start.33
  440.0 22.9 %down_sum.1 = (f32[704,2048]{1,0:T(8,128)}, f32[88,2048]{1,0:T(8,128)}, bf16[704,2048]{1,0:T(8,128)(2,1)}, bf16[88,2048]{1,0:T(8,128)(2,1)}) custom-call(bf16[2,1024,1664]{2,1,0:T(8,128)(2,1)} %get-tuple-element.86.act_ref.h_ref, bf16[16,2,64,2176]{3,2,1,0:T(8,128)(2,1)} %bitcast.122, bf16[16,2,64,2176]{3,2,1,0:T(8,128)(2,1)} %bitcast.123, ...), custom_call_target="tpu_custom_call" | custom-call | flops 13958643712 | bytes 20971520 | tf_op jit(solution)/shard_map/down_sum/pallas_call | solution.py:449
  463.3 2.1 multiply_reduce_fusion
  467.5 1.7 collective-permute-start.35
  470.6 23.4 %up_sum.1 = (f32[704,2048]{1,0:T(8,128)}, f32[88,2048]{1,0:T(8,128)}, bf16[704,2048]{1,0:T(8,128)(2,1)}, bf16[88,2048]{1,0:T(8,128)(2,1)}) custom-call(bf16[2,1024,3328]{2,1,0:T(8,128)(2,1)} %get-tuple-element.87.h_ref, bf16[1024,2048]{1,0:T(8,128)(2,1)} %all-gather.9.cloned.1.call-done.mid_ref.refs_0_, ...), custom_call_target="tpu_custom_call" | custom-call | flops 13958643712 | bytes 20971520 | tf_op jit(solution)/shard_map/up_sum/pallas_call | solution.py:449
  497.1 1.6 pad_maximum_fusion
  498.7 1.7 copy-done.2
  500.4 19.7 %attend_back.1 = (bf16[512,1408]{1,0:T(8,128)(2,1)}, bf16[512,1024]{1,0:T(8,128)(2,1)}, bf16[512,2048]{1,0:T(8,128)(2,1)}, f32[8,2048]{1,0:T(8,128)}) custom-call(bf16[512,2048]{1,0:T(8,128)(2,1)} %bitcast.91, bf16[512,2048]{1,0:T(8,128)(2,1)} %get-tuple-element.92.x_ref, f32[512,128]{1,0:T(8,128)} %get-tuple-element.93.factor_ref, ...), custom_call_target="tpu_custom_call" | custom-call | flops 8455716864 | bytes 17301504 | tf_op jit(solution)/shard_map/attend_back/pallas_call | solution.py:844
  520.1 12.4 %packed_grads.1 = bf16[2048,2176]{1,0:T(8,128)(2,1)} custom-call(bf16[512,2048]{1,0:T(8,128)(2,1)} %get-tuple-element.108.x_ref, bf16[512,2048]{1,0:T(8,128)(2,1)} %bitcast.92, bf16[512,512]{1,0:T(8,128)(2,1)} %get-tuple-element.109.latent_ref, bf16[512,1408]{1,0:T(8,128)(2,1)} %get-tuple-element.110.qr_ref, bf16[512,512]{1,0:T(8,128)(2,1)} %get-tuple-element.111.heads_ref, ...), custom_call_target="tpu_custom_call" | custom-call | flops 4563402752 | bytes 16777216 | tf_op jit(solution)/shard_map/packed_grads/pallas_call | solution.py:509
  532.5 1.6 copy-done.18
  535.8 1.8 constant_dynamic-slice_fusion.3
  538.4 25.9 %collective-permute-done.39.refs_0_.refs_1_ = bf16[128,4096]{1,0:T(8,128)(2,1)S(1)} collective-permute-done((bf16[128,4096]{1,0:T(8,128)(2,1)S(1)}, bf16[128,4096]{1,0:T(8,128)(2,1)S(1)}, u32[]{:S(2)}, u32[]{:S(2)}) %collective-permute-start.39) | collective-permute-done | bytes 1048608 | tf_op jit(solution)/shard_map/ppermute | solution.py:115
  568.4 4.2 all-to-all-start.1
  574.3 6.6 finished.5
  580.8 5.7 finished.3
  586.5 6.2 finished.4
  592.7 18.9 %collective-permute-done.40.refs_2_ = bf16[128,4096]{1,0:T(8,128)(2,1)S(1)} collective-permute-done((bf16[128,4096]{1,0:T(8,128)(2,1)}, bf16[128,4096]{1,0:T(8,128)(2,1)S(1)}, u32[]{:S(2)}, u32[]{:S(2)}) %collective-permute-start.40) | collective-permute-done | bytes 1048608 | tf_op jit(solution)/shard_map/ppermute | solution.py:115
  612.9 3.5 ends.1
  616.4 2.6 fusion.49
  621.7 21.1 %collective-permute-start.43 = (bf16[64,640]{1,0:T(8,128)(2,1)S(1)}, bf16[64,640]{1,0:T(8,128)(2,1)S(1)}, u32[]{:S(2)}, u32[]{:S(2)}) collective-permute-start(bf16[64,640]{1,0:T(8,128)(2,1)S(1)} %get-tuple-element.233), channel_id=1, source_target_pairs={{0,1},{1,2},{2,3},{3,0},{4,5},{5,6},{6,7},{7,4},{8,9},{9,10},{10,1... | collective-permute-start | bytes 245768 | tf_op jit(solution)/shard_map/ppermute | solution.py:115
  (301 shorter events, 73.7 us)
Async XLA Ops:
  7.2 108.7 %all-gather.5.cloned.1.call-start = ((), (), s32[]{:S(2)}) async-start(), calls=%async_computation.6 | async-start | bytes 10027008 | tf_op jit(solution)/shard_map/all_gather | solution.py:928
  10.0 8.1 %collective-permute-start = (bf16[64,640]{1,0:T(8,128)(2,1)S(1)}, bf16[64,640]{1,0:T(8,128)(2,1)S(1)}, u32[]{:S(2)}, u32[]{:S(2)}) collective-permute-start(bf16[64,640]{1,0:T(8,128)(2,1)S(1)} %get-tuple-element.205), channel_id=1, source_target_pairs={{0,1},{1,2},{2,3},{3,0},{4,5},{5,6},{6,7},{7,4},{8,9},{9,10},{10,1... | collective-permute-start | bytes 245768 | tf_op jit(solution)/shard_map/ppermute | solution.py:102
  13.1 8.1 %collective-permute-start.1 = (bf16[64,640]{1,0:T(8,128)(2,1)S(1)}, bf16[64,640]{1,0:T(8,128)(2,1)S(1)}, u32[]{:S(2)}, u32[]{:S(2)}) collective-permute-start(bf16[64,640]{1,0:T(8,128)(2,1)S(1)} %get-tuple-element.205), channel_id=1, source_target_pairs={{0,2},{1,3},{2,0},{3,1},{4,6},{5,7},{6,4},{7,5},{8,10},{9,11},{10,... | collective-permute-start | bytes 245768 | tf_op jit(solution)/shard_map/ppermute | solution.py:102
  15.7 5.7 collective-permute-start.2
  22.5 180.2 %all-gather.7.cloned.1.call-start = ((), (), s32[]{:S(2)}) async-start(), calls=%async_computation.7 | async-start | bytes 11141120 | tf_op jit(solution)/shard_map/all_gather | solution.py:889
  23.7 17.8 %collective-permute-start.3 = (bf16[128,2176]{1,0:T(8,128)(2,1)}, bf16[128,2176]{1,0:T(8,128)(2,1)}, u32[]{:S(2)}, u32[]{:S(2)}) collective-permute-start(bf16[128,2176]{1,0:T(8,128)(2,1)} %concatenate.51), channel_id=1, source_target_pairs={{0,1},{1,2},{2,3},{3,0},{4,5},{5,6},{6,7},{7,4},{8,9},{9,10},{10,1... | collective-permute-start | bytes 1671176 | tf_op jit(solution)/shard_map/ppermute | solution.py:102
  25.7 38.3 %collective-permute-start.4 = (bf16[128,2176]{1,0:T(8,128)(2,1)}, bf16[128,2176]{1,0:T(8,128)(2,1)S(1)}, u32[]{:S(2)}, u32[]{:S(2)}) collective-permute-start(bf16[128,2176]{1,0:T(8,128)(2,1)} %concatenate.51), channel_id=1, source_target_pairs={{0,2},{1,3},{2,0},{3,1},{4,6},{5,7},{6,4},{7,5},{8,10},{9,11},{10,... | collective-permute-start | bytes 1671176 | tf_op jit(solution)/shard_map/ppermute | solution.py:102
  27.6 36.5 %collective-permute-start.5 = (bf16[128,2176]{1,0:T(8,128)(2,1)}, bf16[128,2176]{1,0:T(8,128)(2,1)S(1)}, u32[]{:S(2)}, u32[]{:S(2)}) collective-permute-start(bf16[128,2176]{1,0:T(8,128)(2,1)} %concatenate.51), channel_id=1, source_target_pairs={{0,3},{1,0},{2,1},{3,2},{4,7},{5,4},{6,5},{7,6},{8,11},{9,8},{10,9... | collective-permute-start | bytes 1671176 | tf_op jit(solution)/shard_map/ppermute | solution.py:102
  65.5 50.4 %collective-permute-start.10 = (bf16[704,2048]{1,0:T(8,128)(2,1)}, bf16[704,2048]{1,0:T(8,128)(2,1)}, u32[]{:S(2)}, u32[]{:S(2)}) collective-permute-start(bf16[704,2048]{1,0:T(8,128)(2,1)} %bitcast.127), channel_id=1, source_target_pairs={{0,4},{4,0},{8,12},{12,8},{16,20},{20,16},{24,28},{28,24},{1,5},{5... | collective-permute-start | bytes 8650760 | tf_op jit(solution)/shard_map/ppermute | solution.py:886
  65.6 50.3 %collective-permute-start.9 = (bf16[704,2048]{1,0:T(8,128)(2,1)}, bf16[704,2048]{1,0:T(8,128)(2,1)}, u32[]{:S(2)}, u32[]{:S(2)}) collective-permute-start(bf16[704,2048]{1,0:T(8,128)(2,1)} %bitcast.124), channel_id=1, source_target_pairs={{0,4},{4,0},{8,12},{12,8},{16,20},{20,16},{24,28},{28,24},{1,5},{5... | collective-permute-start | bytes 8650760 | tf_op jit(solution)/shard_map/ppermute | solution.py:886
  68.2 25.8 %collective-permute-start.6 = (bf16[128,2048]{1,0:T(8,128)(2,1)S(1)}, bf16[128,2048]{1,0:T(8,128)(2,1)S(1)}, u32[]{:S(2)}, u32[]{:S(2)}) collective-permute-start(bf16[128,2048]{1,0:T(8,128)(2,1)S(1)} %copy-done.4), channel_id=1, source_target_pairs={{0,1},{1,2},{2,3},{3,0},{4,5},{5,6},{6,7},{7,4},{8,9},{9,10},{10,1... | collective-permute-start | bytes 1572872 | tf_op jit(solution)/shard_map/ppermute | solution.py:133
  80.5 35.4 %collective-permute-start.7 = (bf16[128,2048]{1,0:T(8,128)(2,1)S(1)}, bf16[128,2048]{1,0:T(8,128)(2,1)S(1)}, u32[]{:S(2)}, u32[]{:S(2)}) collective-permute-start(bf16[128,2048]{1,0:T(8,128)(2,1)S(1)} %copy-done.4), channel_id=1, source_target_pairs={{0,2},{1,3},{2,0},{3,1},{4,6},{5,7},{6,4},{7,5},{8,10},{9,11},{10,... | collective-permute-start | bytes 1572872 | tf_op jit(solution)/shard_map/ppermute | solution.py:133
  81.7 34.2 %collective-permute-start.8 = (bf16[128,2048]{1,0:T(8,128)(2,1)S(1)}, bf16[128,2048]{1,0:T(8,128)(2,1)S(1)}, u32[]{:S(2)}, u32[]{:S(2)}) collective-permute-start(bf16[128,2048]{1,0:T(8,128)(2,1)S(1)} %copy-done.4), channel_id=1, source_target_pairs={{0,3},{1,0},{2,1},{3,2},{4,7},{5,4},{6,5},{7,6},{8,11},{9,8},{10,9... | collective-permute-start | bytes 1572872 | tf_op jit(solution)/shard_map/ppermute | solution.py:133
  116.9 32.6 %copy-start.36 = (bf16[704,256]{1,0:T(8,128)(2,1)S(1)}, bf16[704,256]{1,0:T(8,128)(2,1)}, u32[]{:S(2)}) copy-start(bf16[704,256]{1,0:T(8,128)(2,1)} %param.33) | copy-start | bytes 1081348
  116.9 32.6 %copy-start.37 = (bf16[256,704]{0,1:T(8,128)(2,1)S(1)}, bf16[256,704]{0,1:T(8,128)(2,1)}, u32[]{:S(2)}) copy-start(bf16[256,704]{0,1:T(8,128)(2,1)} %param.32) | copy-start | bytes 1081348
  116.9 32.6 %copy-start.38 = (bf16[256,704]{0,1:T(8,128)(2,1)S(1)}, bf16[256,704]{0,1:T(8,128)(2,1)}, u32[]{:S(2)}) copy-start(bf16[256,704]{0,1:T(8,128)(2,1)} %param.31) | copy-start | bytes 1081348
  134.1 21.9 %collective-permute-start.11 = (bf16[64,2048]{1,0:T(8,128)(2,1)}, bf16[64,2048]{1,0:T(8,128)(2,1)S(1)}, u32[]{:S(2)}, u32[]{:S(2)}) collective-permute-start(bf16[64,2048]{1,0:T(8,128)(2,1)} %get-tuple-element.230), channel_id=1, source_target_pairs={{0,1},{1,2},{2,3},{3,0},{4,5},{5,6},{6,7},{7,4},{8,9},{9,10},{10,1... | collective-permute-start | bytes 786440 | tf_op jit(solution)/shard_map/ppermute | solution.py:115
  146.9 19.3 %collective-permute-start.12 = (bf16[64,2048]{1,0:T(8,128)(2,1)S(1)}, bf16[64,2048]{1,0:T(8,128)(2,1)S(1)}, u32[]{:S(2)}, u32[]{:S(2)}) collective-permute-start(bf16[64,2048]{1,0:T(8,128)(2,1)S(1)} %get-tuple-element.232), channel_id=1, source_target_pairs={{0,2},{1,3},{2,0},{3,1},{4,6},{5,7},{6,4},{7,5},{8,10},{9,11},{10,... | collective-permute-start | bytes 786440 | tf_op jit(solution)/shard_map/ppermute | solution.py:115
  149.1 17.1 %collective-permute-start.13 = (bf16[64,2048]{1,0:T(8,128)(2,1)S(1)}, bf16[64,2048]{1,0:T(8,128)(2,1)S(1)}, u32[]{:S(2)}, u32[]{:S(2)}) collective-permute-start(bf16[64,2048]{1,0:T(8,128)(2,1)S(1)} %get-tuple-element.231), channel_id=1, source_target_pairs={{0,3},{1,0},{2,1},{3,2},{4,7},{5,4},{6,5},{7,6},{8,11},{9,8},{10,9... | collective-permute-start | bytes 786440 | tf_op jit(solution)/shard_map/ppermute | solution.py:115
  150.6 31.4 %all-to-all-start = ((bf16[3,8,88,256]{3,2,0,1:T(8,128)(2,1)}), bf16[3,8,88,256]{3,2,0,1:T(8,128)(2,1)S(1)}, u32[]{:S(2)}, u32[]{:S(2)}) async-start(bf16[3,8,88,256]{3,2,0,1:T(8,128)(2,1)} %pad_maximum_fusion.2), calls=%async_computation | async-start | bytes 2162688 | tf_op jit(solution)/shard_map/all_to_all | solution.py:962
  154.3 101.8 %all-gather.9.cloned.1.call-start = ((), (), s32[]{:S(2)}) async-start(), calls=%async_computation.8 | async-start | bytes 5242880 | tf_op jit(solution)/shard_map/all_gather | solution.py:889
  154.4 48.3 %collective-permute-start.18 = (bf16[704,2048]{1,0:T(8,128)(2,1)}, bf16[704,2048]{1,0:T(8,128)(2,1)}, u32[]{:S(2)}, u32[]{:S(2)}) collective-permute-start(bf16[704,2048]{1,0:T(8,128)(2,1)} %bitcast.130), channel_id=1, source_target_pairs={{0,4},{4,0},{8,12},{12,8},{16,20},{20,16},{24,28},{28,24},{1,5},{5... | collective-permute-start | bytes 8650760 | tf_op jit(solution)/shard_map/ppermute | solution.py:886
  167.5 234.9 %copy-start.9 = (f32[64,2048]{1,0:T(8,128)}, f32[64,2048]{1,0:T(8,128)S(1)}, u32[]{:S(2)}) copy-start(f32[64,2048]{1,0:T(8,128)S(1)} %get-tuple-element.203) | copy-start | bytes 1572868
  167.8 18.8 %collective-permute-start.14 = (bf16[64,2048]{1,0:T(8,128)(2,1)S(1)}, bf16[64,2048]{1,0:T(8,128)(2,1)}, u32[]{:S(2)}, u32[]{:S(2)}) collective-permute-start(bf16[64,2048]{1,0:T(8,128)(2,1)S(1)} %get-tuple-element.201), channel_id=1, source_target_pairs={{0,1},{1,2},{2,3},{3,0},{4,5},{5,6},{6,7},{7,4},{8,9},{9,10},{10,1... | collective-permute-start | bytes 786440 | tf_op jit(solution)/shard_map/ppermute | solution.py:102
  173.9 18.0 %collective-permute-start.15 = (bf16[64,2048]{1,0:T(8,128)(2,1)S(1)}, bf16[64,2048]{1,0:T(8,128)(2,1)S(1)}, u32[]{:S(2)}, u32[]{:S(2)}) collective-permute-start(bf16[64,2048]{1,0:T(8,128)(2,1)S(1)} %get-tuple-element.201), channel_id=1, source_target_pairs={{0,2},{1,3},{2,0},{3,1},{4,6},{5,7},{6,4},{7,5},{8,10},{9,11},{10,... | collective-permute-start | bytes 786440 | tf_op jit(solution)/shard_map/ppermute | solution.py:102
  183.1 15.2 %collective-permute-start.17 = (bf16[3,88,2048]{2,1,0:T(8,128)(2,1)}, bf16[3,88,2048]{2,1,0:T(8,128)(2,1)}, u32[]{:S(2)}, u32[]{:S(2)}) collective-permute-start(bf16[3,88,2048]{2,1,0:T(8,128)(2,1)} %bitcast.51), channel_id=1, source_target_pairs={{0,4},{4,0},{8,12},{12,8},{16,20},{20,16},{24,28},{28,24},{1,5},{5... | collective-permute-start | bytes 3244040 | tf_op jit(solution)/shard_map/ppermute | solution.py:886
  184.5 12.9 %collective-permute-start.16 = (bf16[64,2048]{1,0:T(8,128)(2,1)S(1)}, bf16[64,2048]{1,0:T(8,128)(2,1)S(1)}, u32[]{:S(2)}, u32[]{:S(2)}) collective-permute-start(bf16[64,2048]{1,0:T(8,128)(2,1)S(1)} %get-tuple-element.201), channel_id=1, source_target_pairs={{0,3},{1,0},{2,1},{3,2},{4,7},{5,4},{6,5},{7,6},{8,11},{9,8},{10,9... | collective-permute-start | bytes 786440 | tf_op jit(solution)/shard_map/ppermute | solution.py:102
  202.8 108.4 %all-gather.11.cloned.1.call-start = ((), (), s32[]{:S(2)}) async-start(), calls=%async_computation.9 | async-start | bytes 5242880 | tf_op jit(solution)/shard_map/all_gather | solution.py:889
  202.9 11.2 %collective-permute-start.19 = (bf16[64,2048]{1,0:T(8,128)(2,1)S(1)}, bf16[64,2048]{1,0:T(8,128)(2,1)S(1)}, u32[]{:S(2)}, u32[]{:S(2)}) collective-permute-start(bf16[64,2048]{1,0:T(8,128)(2,1)S(1)} %get-tuple-element.227), channel_id=1, source_target_pairs={{0,1},{1,2},{2,3},{3,0},{4,5},{5,6},{6,7},{7,4},{8,9},{9,10},{10,1... | collective-permute-start | bytes 786440 | tf_op jit(solution)/shard_map/ppermute | solution.py:115
  203.6 20.9 %collective-permute-start.20 = (bf16[64,2048]{1,0:T(8,128)(2,1)S(1)}, bf16[64,2048]{1,0:T(8,128)(2,1)S(1)}, u32[]{:S(2)}, u32[]{:S(2)}) collective-permute-start(bf16[64,2048]{1,0:T(8,128)(2,1)S(1)} %get-tuple-element.229), channel_id=1, source_target_pairs={{0,2},{1,3},{2,0},{3,1},{4,6},{5,7},{6,4},{7,5},{8,10},{9,11},{10,... | collective-permute-start | bytes 786440 | tf_op jit(solution)/shard_map/ppermute | solution.py:115
  206.5 17.9 %collective-permute-start.21 = (bf16[64,2048]{1,0:T(8,128)(2,1)S(1)}, bf16[64,2048]{1,0:T(8,128)(2,1)S(1)}, u32[]{:S(2)}, u32[]{:S(2)}) collective-permute-start(bf16[64,2048]{1,0:T(8,128)(2,1)S(1)} %get-tuple-element.228), channel_id=1, source_target_pairs={{0,3},{1,0},{2,1},{3,2},{4,7},{5,4},{6,5},{7,6},{8,11},{9,8},{10,9... | collective-permute-start | bytes 786440 | tf_op jit(solution)/shard_map/ppermute | solution.py:115
  224.8 240.7 %copy-start.10 = (f32[64,2048]{1,0:T(8,128)}, f32[64,2048]{1,0:T(8,128)S(1)}, u32[]{:S(2)}) copy-start(f32[64,2048]{1,0:T(8,128)S(1)} %get-tuple-element.199) | copy-start | bytes 1572868
  225.0 79.9 %copy-start.24 = (bf16[64,2048]{1,0:T(8,128)(2,1)}, bf16[64,2048]{1,0:T(8,128)(2,1)S(1)}, u32[]{:S(2)}) copy-start(bf16[64,2048]{1,0:T(8,128)(2,1)S(1)} %get-tuple-element.197) | copy-start | bytes 786436
  225.0 12.2 %collective-permute-start.22 = (bf16[64,2048]{1,0:T(8,128)(2,1)S(1)}, bf16[64,2048]{1,0:T(8,128)(2,1)S(1)}, u32[]{:S(2)}, u32[]{:S(2)}) collective-permute-start(bf16[64,2048]{1,0:T(8,128)(2,1)S(1)} %get-tuple-element.197), channel_id=1, source_target_pairs={{0,1},{1,2},{2,3},{3,0},{4,5},{5,6},{6,7},{7,4},{8,9},{9,10},{10,1... | collective-permute-start | bytes 786440 | tf_op jit(solution)/shard_map/ppermute | solution.py:102
  230.5 16.7 %collective-permute-start.23 = (bf16[64,2048]{1,0:T(8,128)(2,1)S(1)}, bf16[64,2048]{1,0:T(8,128)(2,1)S(1)}, u32[]{:S(2)}, u32[]{:S(2)}) collective-permute-start(bf16[64,2048]{1,0:T(8,128)(2,1)S(1)} %get-tuple-element.197), channel_id=1, source_target_pairs={{0,2},{1,3},{2,0},{3,1},{4,6},{5,7},{6,4},{7,5},{8,10},{9,11},{10,... | collective-permute-start | bytes 786440 | tf_op jit(solution)/shard_map/ppermute | solution.py:102
  230.5 16.8 %collective-permute-start.24 = (bf16[64,2048]{1,0:T(8,128)(2,1)S(1)}, bf16[64,2048]{1,0:T(8,128)(2,1)S(1)}, u32[]{:S(2)}, u32[]{:S(2)}) collective-permute-start(bf16[64,2048]{1,0:T(8,128)(2,1)S(1)} %get-tuple-element.197), channel_id=1, source_target_pairs={{0,3},{1,0},{2,1},{3,2},{4,7},{5,4},{6,5},{7,6},{8,11},{9,8},{10,9... | collective-permute-start | bytes 786440 | tf_op jit(solution)/shard_map/ppermute | solution.py:102
  256.2 113.4 %reduce-scatter.5.cloned.1.call-start = ((), (), s32[]{:S(2)}) async-start(), calls=%async_computation.10 | async-start | bytes 5570560 | tf_op jit(solution)/shard_map/reduce_scatter | solution.py:892
  311.2 118.1 %reduce-scatter.7.cloned.1.call-start = ((), (), s32[]{:S(2)}) async-start(), calls=%async_computation.11 | async-start | bytes 5570560 | tf_op jit(solution)/shard_map/reduce_scatter | solution.py:892
  369.6 162.9 %reduce-scatter.9.cloned.1.call-start = ((), (), s32[]{:S(2)}) async-start(), calls=%async_computation.12 | async-start | bytes 10485760 | tf_op jit(solution)/shard_map/reduce_scatter | solution.py:892
  371.6 28.3 %collective-permute-start.25 = (bf16[64,2176]{1,0:T(8,128)(2,1)S(1)}, bf16[64,2176]{1,0:T(8,128)(2,1)S(1)}, u32[]{:S(2)}, u32[]{:S(2)}) collective-permute-start(bf16[64,2176]{1,0:T(8,128)(2,1)S(1)} %get-tuple-element.217), channel_id=1, source_target_pairs={{0,1},{1,2},{2,3},{3,0},{4,5},{5,6},{6,7},{7,4},{8,9},{9,10},{10,1... | collective-permute-start | bytes 835592 | tf_op jit(solution)/shard_map/ppermute | solution.py:115
  373.1 26.8 %collective-permute-start.26 = (bf16[64,2176]{1,0:T(8,128)(2,1)S(1)}, bf16[64,2176]{1,0:T(8,128)(2,1)S(1)}, u32[]{:S(2)}, u32[]{:S(2)}) collective-permute-start(bf16[64,2176]{1,0:T(8,128)(2,1)S(1)} %get-tuple-element.216), channel_id=1, source_target_pairs={{0,2},{1,3},{2,0},{3,1},{4,6},{5,7},{6,4},{7,5},{8,10},{9,11},{10,... | collective-permute-start | bytes 835592 | tf_op jit(solution)/shard_map/ppermute | solution.py:115
  375.5 24.4 %collective-permute-start.27 = (bf16[64,2176]{1,0:T(8,128)(2,1)S(1)}, bf16[64,2176]{1,0:T(8,128)(2,1)S(1)}, u32[]{:S(2)}, u32[]{:S(2)}) collective-permute-start(bf16[64,2176]{1,0:T(8,128)(2,1)S(1)} %get-tuple-element.215), channel_id=1, source_target_pairs={{0,3},{1,0},{2,1},{3,2},{4,7},{5,4},{6,5},{7,6},{8,11},{9,8},{10,9... | collective-permute-start | bytes 835592 | tf_op jit(solution)/shard_map/ppermute | solution.py:115
  403.3 25.8 %collective-permute-start.28 = (bf16[64,2048]{1,0:T(8,128)(2,1)S(1)}, bf16[64,2048]{1,0:T(8,128)(2,1)S(1)}, u32[]{:S(2)}, u32[]{:S(2)}) collective-permute-start(bf16[64,2048]{1,0:T(8,128)(2,1)S(1)} %get-tuple-element.194.refs_3_), channel_id=1, source_target_pairs={{0,1},{1,2},{2,3},{3,0},{4,5},{5,6},{6,7},{7,4},{8,9},{9,10},{10,1... | collective-permute-start | bytes 786440 | tf_op jit(solution)/shard_map/ppermute | solution.py:102
  403.8 25.3 %collective-permute-start.29 = (bf16[64,2048]{1,0:T(8,128)(2,1)S(1)}, bf16[64,2048]{1,0:T(8,128)(2,1)S(1)}, u32[]{:S(2)}, u32[]{:S(2)}) collective-permute-start(bf16[64,2048]{1,0:T(8,128)(2,1)S(1)} %get-tuple-element.194.refs_3_), channel_id=1, source_target_pairs={{0,2},{1,3},{2,0},{3,1},{4,6},{5,7},{6,4},{7,5},{8,10},{9,11},{10,... | collective-permute-start | bytes 786440 | tf_op jit(solution)/shard_map/ppermute | solution.py:102
  405.3 23.9 %collective-permute-start.30 = (bf16[64,2048]{1,0:T(8,128)(2,1)S(1)}, bf16[64,2048]{1,0:T(8,128)(2,1)S(1)}, u32[]{:S(2)}, u32[]{:S(2)}) collective-permute-start(bf16[64,2048]{1,0:T(8,128)(2,1)S(1)} %get-tuple-element.194.refs_3_), channel_id=1, source_target_pairs={{0,3},{1,0},{2,1},{3,2},{4,7},{5,4},{6,5},{7,6},{8,11},{9,8},{10,9... | collective-permute-start | bytes 786440 | tf_op jit(solution)/shard_map/ppermute | solution.py:102
  430.3 189.3 %reduce-scatter.11.cloned.1.call-start = ((), (), s32[]{:S(2)}) async-start(), calls=%async_computation.13 | async-start | bytes 10027008 | tf_op jit(solution)/shard_map/reduce_scatter | solution.py:1138
  432.0 31.3 %copy-start.50 = (f32[64]{0:T(128)}, f32[64]{0:T(128)S(1)}, u32[]{:S(2)}) copy-start(f32[64]{0:T(128)S(1)} %get-tuple-element.253) | copy-start | bytes 772
  432.0 66.7 %collective-permute-start.37 = (bf16[704,2048]{1,0:T(8,128)(2,1)}, bf16[704,2048]{1,0:T(8,128)(2,1)S(1)}, u32[]{:S(2)}, u32[]{:S(2)}) collective-permute-start(bf16[704,2048]{1,0:T(8,128)(2,1)} %get-tuple-element.98), channel_id=1, source_target_pairs={{0,4},{4,0},{8,12},{12,8},{16,20},{20,16},{24,28},{28,24},{1,5},{5... | collective-permute-start | bytes 8650760 | tf_op jit(solution)/shard_map/ppermute | solution.py:886
  434.8 28.1 %collective-permute-start.31 = (bf16[64,2176]{1,0:T(8,128)(2,1)}, bf16[64,2176]{1,0:T(8,128)(2,1)S(1)}, u32[]{:S(2)}, u32[]{:S(2)}) collective-permute-start(bf16[64,2176]{1,0:T(8,128)(2,1)} %get-tuple-element.213), channel_id=1, source_target_pairs={{0,1},{1,2},{2,3},{3,0},{4,5},{5,6},{6,7},{7,4},{8,9},{9,10},{10,1... | collective-permute-start | bytes 835592 | tf_op jit(solution)/shard_map/ppermute | solution.py:115
  435.6 27.3 %collective-permute-start.32 = (bf16[64,2176]{1,0:T(8,128)(2,1)}, bf16[64,2176]{1,0:T(8,128)(2,1)S(1)}, u32[]{:S(2)}, u32[]{:S(2)}) collective-permute-start(bf16[64,2176]{1,0:T(8,128)(2,1)} %get-tuple-element.212), channel_id=1, source_target_pairs={{0,2},{1,3},{2,0},{3,1},{4,6},{5,7},{6,4},{7,5},{8,10},{9,11},{10,... | collective-permute-start | bytes 835592 | tf_op jit(solution)/shard_map/ppermute | solution.py:115
  437.1 25.8 %collective-permute-start.33 = (bf16[64,2176]{1,0:T(8,128)(2,1)S(1)}, bf16[64,2176]{1,0:T(8,128)(2,1)S(1)}, u32[]{:S(2)}, u32[]{:S(2)}) collective-permute-start(bf16[64,2176]{1,0:T(8,128)(2,1)S(1)} %get-tuple-element.211), channel_id=1, source_target_pairs={{0,3},{1,0},{2,1},{3,2},{4,7},{5,4},{6,5},{7,6},{8,11},{9,8},{10,9... | collective-permute-start | bytes 835592 | tf_op jit(solution)/shard_map/ppermute | solution.py:115
  462.9 35.8 %collective-permute-start.38 = (bf16[704,2048]{1,0:T(8,128)(2,1)}, bf16[704,2048]{1,0:T(8,128)(2,1)}, u32[]{:S(2)}, u32[]{:S(2)}) collective-permute-start(bf16[704,2048]{1,0:T(8,128)(2,1)} %get-tuple-element.99), channel_id=1, source_target_pairs={{0,4},{4,0},{8,12},{12,8},{16,20},{20,16},{24,28},{28,24},{1,5},{5... | collective-permute-start | bytes 8650760 | tf_op jit(solution)/shard_map/ppermute | solution.py:886
  466.5 29.5 %collective-permute-start.34 = (bf16[64,2048]{1,0:T(8,128)(2,1)S(1)}, bf16[64,2048]{1,0:T(8,128)(2,1)}, u32[]{:S(2)}, u32[]{:S(2)}) collective-permute-start(bf16[64,2048]{1,0:T(8,128)(2,1)S(1)} %get-tuple-element.191.refs_2_), channel_id=1, source_target_pairs={{0,1},{1,2},{2,3},{3,0},{4,5},{5,6},{6,7},{7,4},{8,9},{9,10},{10,1... | collective-permute-start | bytes 786440 | tf_op jit(solution)/shard_map/ppermute | solution.py:102
  467.5 29.5 %collective-permute-start.35 = (bf16[64,2048]{1,0:T(8,128)(2,1)S(1)}, bf16[64,2048]{1,0:T(8,128)(2,1)S(1)}, u32[]{:S(2)}, u32[]{:S(2)}) collective-permute-start(bf16[64,2048]{1,0:T(8,128)(2,1)S(1)} %get-tuple-element.191.refs_2_), channel_id=1, source_target_pairs={{0,2},{1,3},{2,0},{3,1},{4,6},{5,7},{6,4},{7,5},{8,10},{9,11},{10,... | collective-permute-start | bytes 786440 | tf_op jit(solution)/shard_map/ppermute | solution.py:102
  469.2 27.8 %collective-permute-start.36 = (bf16[64,2048]{1,0:T(8,128)(2,1)S(1)}, bf16[64,2048]{1,0:T(8,128)(2,1)S(1)}, u32[]{:S(2)}, u32[]{:S(2)}) collective-permute-start(bf16[64,2048]{1,0:T(8,128)(2,1)S(1)} %get-tuple-element.191.refs_2_), channel_id=1, source_target_pairs={{0,3},{1,0},{2,1},{3,2},{4,7},{5,4},{6,5},{7,6},{8,11},{9,8},{10,9... | collective-permute-start | bytes 786440 | tf_op jit(solution)/shard_map/ppermute | solution.py:102
  537.6 26.7 %collective-permute-start.39 = (bf16[128,4096]{1,0:T(8,128)(2,1)S(1)}, bf16[128,4096]{1,0:T(8,128)(2,1)S(1)}, u32[]{:S(2)}, u32[]{:S(2)}) collective-permute-start(bf16[128,4096]{1,0:T(8,128)(2,1)S(1)} %get-tuple-element.208), channel_id=1, source_target_pairs={{0,1},{1,2},{2,3},{3,0},{4,5},{5,6},{6,7},{7,4},{8,9},{9,10},{10,1... | collective-permute-start | bytes 3145736 | tf_op jit(solution)/shard_map/ppermute | solution.py:115
  538.3 48.2 %collective-permute-start.42 = (bf16[704,2048]{1,0:T(8,128)(2,1)}, bf16[704,2048]{1,0:T(8,128)(2,1)}, u32[]{:S(2)}, u32[]{:S(2)}) collective-permute-start(bf16[704,2048]{1,0:T(8,128)(2,1)} %get-tuple-element.104), channel_id=1, source_target_pairs={{0,4},{4,0},{8,12},{12,8},{16,20},{20,16},{24,28},{28,24},{1,5},{5... | collective-permute-start | bytes 8650760 | tf_op jit(solution)/shard_map/ppermute | solution.py:886
  564.3 2.7 collective-permute-start.46
  564.3 47.3 %collective-permute-start.40 = (bf16[128,4096]{1,0:T(8,128)(2,1)}, bf16[128,4096]{1,0:T(8,128)(2,1)S(1)}, u32[]{:S(2)}, u32[]{:S(2)}) collective-permute-start(bf16[128,4096]{1,0:T(8,128)(2,1)} %get-tuple-element.207), channel_id=1, source_target_pairs={{0,2},{1,3},{2,0},{3,1},{4,6},{5,7},{6,4},{7,5},{8,10},{9,11},{10,... | collective-permute-start | bytes 3145736 | tf_op jit(solution)/shard_map/ppermute | solution.py:115
  564.3 48.6 %collective-permute-start.41 = (bf16[128,4096]{1,0:T(8,128)(2,1)}, bf16[128,4096]{1,0:T(8,128)(2,1)}, u32[]{:S(2)}, u32[]{:S(2)}) collective-permute-start(bf16[128,4096]{1,0:T(8,128)(2,1)} %get-tuple-element.206), channel_id=1, source_target_pairs={{0,3},{1,0},{2,1},{3,2},{4,7},{5,4},{6,5},{7,6},{8,11},{9,8},{10,9... | collective-permute-start | bytes 3145736 | tf_op jit(solution)/shard_map/ppermute | solution.py:115
  568.4 48.0 %all-to-all-start.1 = ((bf16[3,8,88,256]{3,2,0,1:T(8,128)(2,1)}), bf16[3,8,88,256]{3,2,0,1:T(8,128)(2,1)}, u32[]{:S(2)}, u32[]{:S(2)}) async-start(bf16[3,8,88,256]{3,2,0,1:T(8,128)(2,1)} %bitcast.93), calls=%async_computation.5 | async-start | bytes 2162688 | tf_op jit(solution)/shard_map/all_to_all | solution.py:1124
  621.7 26.8 %collective-permute-start.43 = (bf16[64,640]{1,0:T(8,128)(2,1)S(1)}, bf16[64,640]{1,0:T(8,128)(2,1)S(1)}, u32[]{:S(2)}, u32[]{:S(2)}) collective-permute-start(bf16[64,640]{1,0:T(8,128)(2,1)S(1)} %get-tuple-element.233), channel_id=1, source_target_pairs={{0,1},{1,2},{2,3},{3,0},{4,5},{5,6},{6,7},{7,4},{8,9},{9,10},{10,1... | collective-permute-start | bytes 245768 | tf_op jit(solution)/shard_map/ppermute | solution.py:115
  642.8 7.0 %collective-permute-start.44 = (bf16[64,640]{1,0:T(8,128)(2,1)S(1)}, bf16[64,640]{1,0:T(8,128)(2,1)S(1)}, u32[]{:S(2)}, u32[]{:S(2)}) collective-permute-start(bf16[64,640]{1,0:T(8,128)(2,1)S(1)} %get-tuple-element.235), channel_id=1, source_target_pairs={{0,2},{1,3},{2,0},{3,1},{4,6},{5,7},{6,4},{7,5},{8,10},{9,11},{10,... | collective-permute-start | bytes 245768 | tf_op jit(solution)/shard_map/ppermute | solution.py:115
  644.4 5.9 collective-permute-start.45
  (48 other events, 457.4 us)
Sparse Core Ops, SparseCore 0:
  22.6 57.5 all-gather.4
  82.7 105.9 all-gather.6
  202.9 53.2 all-gather.8
  258.4 52.6 all-gather.10
  314.7 54.8 reduce-scatter.4
  373.1 54.8 reduce-scatter.6
  431.1 86.3 reduce-scatter.8
  532.6 86.9 reduce-scatter.10

commit v5 on v4

--- a/solution.py
+++ b/solution.py
@@ -893,6 +893,15 @@
             value, "fsdp", scatter_dimension=0, tiled=True, axis_index_groups=halves
         )
 
+    def direct_half(value):
+        chip, rows = (lax.axis_index("fsdp") // 2, value.shape[0] // half)
+        total = lax.dynamic_slice_in_dim(value, chip * rows, rows, 0).astype(jnp.float32)
+        for hop in range(1, half):
+            part = lax.dynamic_slice_in_dim(value, (chip ^ hop) * rows, rows, 0)
+            got = lax.ppermute(part, "fsdp", [(i, i ^ (2 * hop)) for i in range(groups)])
+            total = total + got.astype(jnp.float32)
+        return total.astype(jnp.bfloat16)
+
     group = lax.axis_index("fsdp")
     tok_dev, model_w = tokens_in.shape
     count = tok_dev * lanes
@@ -1002,6 +1011,9 @@
         mids.append(last)
     for h in range(chunks):
         rows_part, *held = experts_back(plan, h, first, mids[h], dout_all, pieces, *held)
+        if h == 0 and chunks == 2:
+            rows_parts.append(direct_half(rows_part))
+            continue
         rows_part = after(rows_part, last)
         last = scatter_half(rows_part)
         rows_parts.append(last)

time: 664 us -> 774 us (1.17)
  waiting for transfers between devices: 201 us -> 293 us
  starting transfers between devices: 116 us -> 128 us
    ppermute x0 -> x3, waiting for transfers between devices: none -> 72 us  [direct_half(): got = lax.ppermute(part, 'fsdp', [(i, i ^ 2 * hop) for i in range(groups)])]
    ppermute x18, waiting for transfers between devices: 76.9 us -> 91.7 us  [pieces_ctx(): lax.ppermute(part, 'ctx', [(i, (i + hop) % lanes) for i in range(lanes)])]
    ppermute x18, waiting for transfers between devices: 59.5 us -> 74.1 us  [gather_ctx(): lax.ppermute(value, 'ctx', [(i, (i + hop) % lanes) for i in range(lanes)])]
    reduce_scatter x3 -> x2, waiting for transfers between devices: 10.2 us -> 0.02 us  [scatter_half(): lax.psum_scatter(value, 'fsdp', scatter_dimension=0, tiled=True, axis_ind...]
  transfers between devices with their start and end apart: 57 -> 59, of which waited for: 26 -> 32; matrix products, arithmetic and copies ran while one was open for 8% -> 8% of each run, Pallas kernels for 39% -> 27%
where the time goes in v5:
time: 774 us; the launch traced here: 770 us
  waiting for transfers between devices  293 us (38%)
  Pallas kernels  257 us (33%)
  starting transfers between devices  128 us (17%)
  local copies, waits for them, and re-layouts  40 us (5%)
  other arithmetic  23.5 us (3%)
  between operations  15.8 us (2%)
  matrix products  12.3 us (2%)
    pallas_call x2, Pallas kernels, experts_back(): pl.pallas_call(functools.partial(back_kernel, plan), grid=(tokens // tile...  96.2 us
    ppermute x18, waiting for transfers between devices, pieces_ctx(): lax.ppermute(part, 'ctx', [(i, (i + hop) % lanes) for i in range(lanes)])  91.7 us
    ppermute x18, waiting for transfers between devices, gather_ctx(): lax.ppermute(value, 'ctx', [(i, (i + hop) % lanes) for i in range(lanes)])  74.1 us
    ppermute x3, waiting for transfers between devices, direct_half(): got = lax.ppermute(part, 'fsdp', [(i, i ^ 2 * hop) for i in range(groups)])  72 us
    pallas_call x3, Pallas kernels, weight_sum(): pl.pallas_call(functools.partial(sum_kernel, plan, kind, chunks), grid=(c...  69.9 us
    ppermute x18, starting transfers between devices, pieces_ctx(): lax.ppermute(part, 'ctx', [(i, (i + hop) % lanes) for i in range(lanes)])  57.8 us
    ppermute x18, starting transfers between devices, gather_ctx(): lax.ppermute(value, 'ctx', [(i, (i + hop) % lanes) for i in range(lanes)])  42.3 us
    ppermute x3, waiting for transfers between devices, spread_ctx(): lax.ppermute(value, 'ctx', [(i, (i + hop) % lanes) for i in range(lanes)])  30.5 us
  transfers between devices with their start and end apart: 59, of which 32 were waited for; matrix products, arithmetic and copies ran while one was open for 8% of the time, Pallas kernels for 27%

profile of v5, /device:TPU:0, one launch (start us, length us, event | category | flops | bytes accessed | tf_op | source)
XLA Modules:
  0.0 769.9 jit_solution(17398230338088253346)
XLA Ops:
  10.0 3.1 collective-permute-start
  13.1 2.6 collective-permute-start.1
  18.2 3.0 collective-permute-done.1
  23.7 2.0 collective-permute-start.3
  25.7 1.9 collective-permute-start.4
  29.5 12.0 %collective-permute-done.3 = bf16[128,2176]{1,0:T(8,128)(2,1)} collective-permute-done((bf16[128,2176]{1,0:T(8,128)(2,1)}, bf16[128,2176]{1,0:T(8,128)(2,1)}, u32[]{:S(2)}, u32[]{:S(2)}) %collective-permute-start.3) | collective-permute-done | bytes 557088 | tf_op jit(solution)/shard_map/ppermute | solution.py:102
  42.6 21.4 %collective-permute-done.4 = bf16[128,2176]{1,0:T(8,128)(2,1)S(1)} collective-permute-done((bf16[128,2176]{1,0:T(8,128)(2,1)}, bf16[128,2176]{1,0:T(8,128)(2,1)S(1)}, u32[]{:S(2)}, u32[]{:S(2)}) %collective-permute-start.4) | collective-permute-done | bytes 557088 | tf_op jit(solution)/shard_map/ppermute | solution.py:102
  68.2 12.4 %collective-permute-start.6 = (bf16[128,2048]{1,0:T(8,128)(2,1)S(1)}, bf16[128,2048]{1,0:T(8,128)(2,1)S(1)}, u32[]{:S(2)}, u32[]{:S(2)}) collective-permute-start(bf16[128,2048]{1,0:T(8,128)(2,1)S(1)} %copy-done.4), channel_id=1, source_target_pairs={{0,1},{1,2},{2,3},{3,0},{4,5},{5,6},{6,7},{7,4},{8,9},{9,10},{10,1... | collective-permute-start | bytes 1572872 | tf_op jit(solution)/shard_map/ppermute | solution.py:133
  85.5 8.6 %collective-permute-done.6.refs_1_ = bf16[128,2048]{1,0:T(8,128)(2,1)S(1)} collective-permute-done((bf16[128,2048]{1,0:T(8,128)(2,1)S(1)}, bf16[128,2048]{1,0:T(8,128)(2,1)S(1)}, u32[]{:S(2)}, u32[]{:S(2)}) %collective-permute-start.6) | collective-permute-done | bytes 524320 | tf_op jit(solution)/shard_map/ppermute | solution.py:133
  94.0 21.9 %collective-permute-done.7.refs_2_ = bf16[128,2048]{1,0:T(8,128)(2,1)S(1)} collective-permute-done((bf16[128,2048]{1,0:T(8,128)(2,1)S(1)}, bf16[128,2048]{1,0:T(8,128)(2,1)S(1)}, u32[]{:S(2)}, u32[]{:S(2)}) %collective-permute-start.7) | collective-permute-done | bytes 524320 | tf_op jit(solution)/shard_map/ppermute | solution.py:133
  116.9 15.4 %attend.1 = (bf16[512,2048]{1,0:T(8,128)(2,1)}, bf16[512,2048]{1,0:T(8,128)(2,1)}, f32[512,128]{1,0:T(8,128)}, bf16[512,768]{1,0:T(8,128)(2,1)}, bf16[512,1024]{...) custom-call(s32[1]{0:T(128)} %bitcast.lane_ref, ...), custom_call_target="tpu_custom_call" | custom-call | flops 6174015488 | bytes 17301504 | tf_op jit(solution)/shard_map/attend/pallas_call | solution.py:729
  132.3 1.9 constant_dynamic-slice_fusion.23
  134.1 12.8 %collective-permute-start.11 = (bf16[64,2048]{1,0:T(8,128)(2,1)}, bf16[64,2048]{1,0:T(8,128)(2,1)S(1)}, u32[]{:S(2)}, u32[]{:S(2)}) collective-permute-start(bf16[64,2048]{1,0:T(8,128)(2,1)} %get-tuple-element.231), channel_id=1, source_target_pairs={{0,1},{1,2},{2,3},{3,0},{4,5},{5,6},{6,7},{7,4},{8,9},{9,10},{10,1... | collective-permute-start | bytes 786440 | tf_op jit(solution)/shard_map/ppermute | solution.py:115
  146.9 2.2 collective-permute-start.12
  150.6 3.8 all-to-all-start
  156.1 10.1 %collective-permute-done.12 = bf16[64,2048]{1,0:T(8,128)(2,1)S(1)} collective-permute-done((bf16[64,2048]{1,0:T(8,128)(2,1)S(1)}, bf16[64,2048]{1,0:T(8,128)(2,1)S(1)}, u32[]{:S(2)}, u32[]{:S(2)}) %collective-permute-start.12) | collective-permute-done | bytes 262176 | tf_op jit(solution)/shard_map/ppermute | solution.py:115
  167.7 6.1 collective-permute-start.14
  175.1 6.9 all-to-all-done
  184.5 2.1 collective-permute-start.16
  188.2 3.7 collective-permute-done.15
  192.7 4.8 collective-permute-done.16
  200.8 1.9 maximum_maximum_fusion.2
  203.5 3.0 collective-permute-start.20
  206.7 7.3 collective-permute-done.19
  214.0 10.4 %collective-permute-done.20 = bf16[64,2048]{1,0:T(8,128)(2,1)S(1)} collective-permute-done((bf16[64,2048]{1,0:T(8,128)(2,1)S(1)}, bf16[64,2048]{1,0:T(8,128)(2,1)S(1)}, u32[]{:S(2)}, u32[]{:S(2)}) %collective-permute-start.20) | collective-permute-done | bytes 262176 | tf_op jit(solution)/shard_map/ppermute | solution.py:115
  225.0 5.5 collective-permute-start.28
  230.4 2.4 collective-permute-start.30
  232.9 4.3 collective-permute-done.28
  237.2 9.9 %collective-permute-done.29 = bf16[64,2048]{1,0:T(8,128)(2,1)S(1)} collective-permute-done((bf16[64,2048]{1,0:T(8,128)(2,1)S(1)}, bf16[64,2048]{1,0:T(8,128)(2,1)S(1)}, u32[]{:S(2)}, u32[]{:S(2)}) %collective-permute-start.29) | collective-permute-done | bytes 262176 | tf_op jit(solution)/shard_map/ppermute | solution.py:102
  247.2 8.9 %all-gather.9.cloned.1.call-done.mid_ref.refs_0_ = bf16[1024,2048]{1,0:T(8,128)(2,1)} async-done(((bf16[256,2048]{1,0:T(8,128)(2,1)}), bf16[1024,2048]{1,0:T(8,128)(2,1)}) %all-gather.9.cloned.1.call-update) | async-done | bytes 4194320 | tf_op jit(solution)/shard_map/all_gather | solution.py:889
  256.8 48.1 %experts_back.2 = (bf16[1024,2176]{1,0:T(8,128)(2,1)}, bf16[2,1024,3328]{2,1,0:T(8,128)(2,1)}, bf16[2,1024,1664]{2,1,0:T(8,128)(2,1)}) custom-call(s32[4]{0:T(128)} %pad_add_fusion.first_ref, bf16[1024,2048]{1,0:T(8,128)(2,1)} %all-gather.9.cloned.1.call-done.mid_ref.refs_0_, bf16[16,2,64,2176]{3,2,1,0:T(8,128)(2,1)} %bitcast.118, ...), custom_call_target="tpu_custom_call" | custom-call | flops 34896609280 | bytes 22806528 | tf_op jit(solution)/shard_map/experts_back/pallas_call | solution.py:300
  304.9 6.3 all-gather.11.cloned.1.call-done.mid_ref.refs_1_
  311.1 48.2 %experts_back.3 = (bf16[1024,2176]{1,0:T(8,128)(2,1)}, bf16[2,1024,3328]{2,1,0:T(8,128)(2,1)}, bf16[2,1024,1664]{2,1,0:T(8,128)(2,1)}) custom-call(s32[4]{0:T(128)} %pad_add_fusion.first_ref, bf16[1024,2048]{1,0:T(8,128)(2,1)} %all-gather.11.cloned.1.call-done.mid_ref.refs_1_, ...), custom_call_target="tpu_custom_call", output_to_operand_aliasing={{1}: (13, {}), {2}: (14, {})} | custom-call | flops 34896609280 | bytes 22806528 | tf_op jit(solution)/shard_map/experts_back/pallas_call | solution.py:300
  359.4 3.6 constant_dynamic-slice_fusion.17
  366.5 46.9 %collective-permute-done.22 = bf16[256,2176]{1,0:T(8,128)(2,1)} collective-permute-done((bf16[256,2176]{1,0:T(8,128)(2,1)}, bf16[256,2176]{1,0:T(8,128)(2,1)}, u32[]{:S(2)}, u32[]{:S(2)}) %collective-permute-start.22) | collective-permute-done | bytes 1114144 | tf_op jit(solution)/shard_map/ppermute | solution.py:901
  413.4 25.1 %collective-permute-done.23 = bf16[256,2176]{1,0:T(8,128)(2,1)} collective-permute-done((bf16[256,2176]{1,0:T(8,128)(2,1)}, bf16[256,2176]{1,0:T(8,128)(2,1)}, u32[]{:S(2)}, u32[]{:S(2)}) %collective-permute-start.23) | collective-permute-done | bytes 1114144 | tf_op jit(solution)/shard_map/ppermute | solution.py:901
  438.5 2.9 add_convert_fusion
  443.0 2.4 collective-permute-start.26
  448.5 4.5 collective-permute-done.25
  453.0 9.6 %collective-permute-done.26 = bf16[64,2176]{1,0:T(8,128)(2,1)S(1)} collective-permute-done((bf16[64,2176]{1,0:T(8,128)(2,1)S(1)}, bf16[64,2176]{1,0:T(8,128)(2,1)S(1)}, u32[]{:S(2)}, u32[]{:S(2)}) %collective-permute-start.26) | collective-permute-done | bytes 278560 | tf_op jit(solution)/shard_map/ppermute | solution.py:115
  462.9 2.0 multiply_reduce_fusion.1
  466.1 6.4 collective-permute-start.31
  474.9 5.4 collective-permute-done.31
  480.3 8.8 %collective-permute-done.32 = bf16[64,2048]{1,0:T(8,128)(2,1)S(1)} collective-permute-done((bf16[64,2048]{1,0:T(8,128)(2,1)S(1)}, bf16[64,2048]{1,0:T(8,128)(2,1)S(1)}, u32[]{:S(2)}, u32[]{:S(2)}) %collective-permute-start.32) | collective-permute-done | bytes 262176 | tf_op jit(solution)/shard_map/ppermute | solution.py:102
  489.6 23.2 %gate_sum.1 = (f32[704,2048]{1,0:T(8,128)}, f32[88,2048]{1,0:T(8,128)}, bf16[704,2048]{1,0:T(8,128)(2,1)}, bf16[88,2048]{1,0:T(8,128)(2,1)}) custom-call(bf16[2,1024,3328]{2,1,0:T(8,128)(2,1)} %get-tuple-element.85.h_ref, bf16[1024,2048]{1,0:T(8,128)(2,1)} %all-gather.9.cloned.1.call-done.mid_ref.refs_0_, ...), custom_call_target="tpu_custom_call" | custom-call | flops 13958643712 | bytes 20971520 | tf_op jit(solution)/shard_map/gate_sum/pallas_call | solution.py:449
  512.8 22.0 %experts_out.1 = bf16[4,4,2,64,2048]{4,3,2,1,0:T(8,128)(2,1)} custom-call(bf16[2,1024,1664]{2,1,0:T(8,128)(2,1)} %get-tuple-element.84.act_ref.h_ref, bf16[704,2048]{1,0:T(8,128)(2,1)} %bitcast.133, bf16[704,2048]{1,0:T(8,128)(2,1)} %collective-permute-done.18.refs_7_.refs_1_, bf16[256,2048]{1,0:T(8,128)(2,1)} %get-tuple-element.249.refs_8_.refs_2_, ...), custom_call_target="tpu_custom_call" | custom-call | flops 13958643712 | bytes 15204352 | tf_op jit(solution)/shard_map/experts_out/pallas_call | solution.py:358
  540.0 5.9 collective-permute-start.34
  545.9 3.4 collective-permute-start.35
  549.3 23.1 %down_sum.1 = (f32[704,2048]{1,0:T(8,128)}, f32[88,2048]{1,0:T(8,128)}, bf16[704,2048]{1,0:T(8,128)(2,1)}, bf16[88,2048]{1,0:T(8,128)(2,1)}) custom-call(bf16[2,1024,1664]{2,1,0:T(8,128)(2,1)} %get-tuple-element.84.act_ref.h_ref, bf16[16,2,64,2176]{3,2,1,0:T(8,128)(2,1)} %bitcast.122, bf16[16,2,64,2176]{3,2,1,0:T(8,128)(2,1)} %bitcast.123, ...), custom_call_target="tpu_custom_call" | custom-call | flops 13958643712 | bytes 20971520 | tf_op jit(solution)/shard_map/down_sum/pallas_call | solution.py:449
  572.8 2.1 multiply_reduce_fusion
  576.0 2.3 collective-permute-start.37
  578.3 2.4 collective-permute-start.39
  580.7 23.5 %up_sum.1 = (f32[704,2048]{1,0:T(8,128)}, f32[88,2048]{1,0:T(8,128)}, bf16[704,2048]{1,0:T(8,128)(2,1)}, bf16[88,2048]{1,0:T(8,128)(2,1)}) custom-call(bf16[2,1024,3328]{2,1,0:T(8,128)(2,1)} %get-tuple-element.85.h_ref, bf16[1024,2048]{1,0:T(8,128)(2,1)} %all-gather.9.cloned.1.call-done.mid_ref.refs_0_, ...), custom_call_target="tpu_custom_call" | custom-call | flops 13958643712 | bytes 20971520 | tf_op jit(solution)/shard_map/up_sum/pallas_call | solution.py:449
  610.5 19.6 %attend_back.1 = (bf16[512,1408]{1,0:T(8,128)(2,1)}, bf16[512,1024]{1,0:T(8,128)(2,1)}, bf16[512,2048]{1,0:T(8,128)(2,1)}, f32[8,2048]{1,0:T(8,128)}) custom-call(bf16[512,2048]{1,0:T(8,128)(2,1)} %bitcast.91, bf16[512,2048]{1,0:T(8,128)(2,1)} %get-tuple-element.90.x_ref, f32[512,128]{1,0:T(8,128)} %get-tuple-element.91.factor_ref, ...), custom_call_target="tpu_custom_call" | custom-call | flops 8455716864 | bytes 17301504 | tf_op jit(solution)/shard_map/attend_back/pallas_call | solution.py:844
  630.1 12.4 %packed_grads.1 = bf16[2048,2176]{1,0:T(8,128)(2,1)} custom-call(bf16[512,2048]{1,0:T(8,128)(2,1)} %get-tuple-element.106.x_ref, bf16[512,2048]{1,0:T(8,128)(2,1)} %bitcast.92, bf16[512,512]{1,0:T(8,128)(2,1)} %get-tuple-element.107.latent_ref, bf16[512,1408]{1,0:T(8,128)(2,1)} %get-tuple-element.108.qr_ref, bf16[512,512]{1,0:T(8,128)(2,1)} %get-tuple-element.109.heads_ref, ...), custom_call_target="tpu_custom_call" | custom-call | flops 4563402752 | bytes 16777216 | tf_op jit(solution)/shard_map/packed_grads/pallas_call | solution.py:509
  647.9 26.2 %collective-permute-done.42.refs_0_.refs_1_ = bf16[128,4096]{1,0:T(8,128)(2,1)S(1)} collective-permute-done((bf16[128,4096]{1,0:T(8,128)(2,1)S(1)}, bf16[128,4096]{1,0:T(8,128)(2,1)S(1)}, u32[]{:S(2)}, u32[]{:S(2)}) %collective-permute-start.42) | collective-permute-done | bytes 1048608 | tf_op jit(solution)/shard_map/ppermute | solution.py:115
  678.3 4.2 all-to-all-start.1
  684.2 6.4 finished.5
  690.6 5.7 finished.3
  696.3 6.2 finished.4
  702.5 18.8 %collective-permute-done.43.refs_2_ = bf16[128,4096]{1,0:T(8,128)(2,1)S(1)} collective-permute-done((bf16[128,4096]{1,0:T(8,128)(2,1)}, bf16[128,4096]{1,0:T(8,128)(2,1)S(1)}, u32[]{:S(2)}, u32[]{:S(2)}) %collective-permute-start.43) | collective-permute-done | bytes 1048608 | tf_op jit(solution)/shard_map/ppermute | solution.py:115
  722.8 3.4 ends.1
  726.2 2.6 fusion.49
  732.1 20.5 %collective-permute-start.46 = (bf16[64,640]{1,0:T(8,128)(2,1)S(1)}, bf16[64,640]{1,0:T(8,128)(2,1)S(1)}, u32[]{:S(2)}, u32[]{:S(2)}) collective-permute-start(bf16[64,640]{1,0:T(8,128)(2,1)S(1)} %get-tuple-element.234), channel_id=1, source_target_pairs={{0,1},{1,2},{2,3},{3,0},{4,5},{5,6},{6,7},{7,4},{8,9},{9,10},{10,1... | collective-permute-start | bytes 245768 | tf_op jit(solution)/shard_map/ppermute | solution.py:115
  (304 shorter events, 88.0 us)
Async XLA Ops:
  7.2 108.8 %all-gather.5.cloned.1.call-start = ((), (), s32[]{:S(2)}) async-start(), calls=%async_computation.5 | async-start | bytes 10027008 | tf_op jit(solution)/shard_map/all_gather | solution.py:937
  10.0 8.1 %collective-permute-start = (bf16[64,640]{1,0:T(8,128)(2,1)S(1)}, bf16[64,640]{1,0:T(8,128)(2,1)S(1)}, u32[]{:S(2)}, u32[]{:S(2)}) collective-permute-start(bf16[64,640]{1,0:T(8,128)(2,1)S(1)} %get-tuple-element.203), channel_id=1, source_target_pairs={{0,1},{1,2},{2,3},{3,0},{4,5},{5,6},{6,7},{7,4},{8,9},{9,10},{10,1... | collective-permute-start | bytes 245768 | tf_op jit(solution)/shard_map/ppermute | solution.py:102
  13.1 8.1 %collective-permute-start.1 = (bf16[64,640]{1,0:T(8,128)(2,1)S(1)}, bf16[64,640]{1,0:T(8,128)(2,1)S(1)}, u32[]{:S(2)}, u32[]{:S(2)}) collective-permute-start(bf16[64,640]{1,0:T(8,128)(2,1)S(1)} %get-tuple-element.203), channel_id=1, source_target_pairs={{0,2},{1,3},{2,0},{3,1},{4,6},{5,7},{6,4},{7,5},{8,10},{9,11},{10,... | collective-permute-start | bytes 245768 | tf_op jit(solution)/shard_map/ppermute | solution.py:102
  15.7 5.7 collective-permute-start.2
  22.5 180.1 %all-gather.7.cloned.1.call-start = ((), (), s32[]{:S(2)}) async-start(), calls=%async_computation.6 | async-start | bytes 11141120 | tf_op jit(solution)/shard_map/all_gather | solution.py:889
  23.7 17.8 %collective-permute-start.3 = (bf16[128,2176]{1,0:T(8,128)(2,1)}, bf16[128,2176]{1,0:T(8,128)(2,1)}, u32[]{:S(2)}, u32[]{:S(2)}) collective-permute-start(bf16[128,2176]{1,0:T(8,128)(2,1)} %concatenate.51), channel_id=1, source_target_pairs={{0,1},{1,2},{2,3},{3,0},{4,5},{5,6},{6,7},{7,4},{8,9},{9,10},{10,1... | collective-permute-start | bytes 1671176 | tf_op jit(solution)/shard_map/ppermute | solution.py:102
  25.7 38.3 %collective-permute-start.4 = (bf16[128,2176]{1,0:T(8,128)(2,1)}, bf16[128,2176]{1,0:T(8,128)(2,1)S(1)}, u32[]{:S(2)}, u32[]{:S(2)}) collective-permute-start(bf16[128,2176]{1,0:T(8,128)(2,1)} %concatenate.51), channel_id=1, source_target_pairs={{0,2},{1,3},{2,0},{3,1},{4,6},{5,7},{6,4},{7,5},{8,10},{9,11},{10,... | collective-permute-start | bytes 1671176 | tf_op jit(solution)/shard_map/ppermute | solution.py:102
  27.6 36.5 %collective-permute-start.5 = (bf16[128,2176]{1,0:T(8,128)(2,1)}, bf16[128,2176]{1,0:T(8,128)(2,1)S(1)}, u32[]{:S(2)}, u32[]{:S(2)}) collective-permute-start(bf16[128,2176]{1,0:T(8,128)(2,1)} %concatenate.51), channel_id=1, source_target_pairs={{0,3},{1,0},{2,1},{3,2},{4,7},{5,4},{6,5},{7,6},{8,11},{9,8},{10,9... | collective-permute-start | bytes 1671176 | tf_op jit(solution)/shard_map/ppermute | solution.py:102
  65.5 50.4 %collective-permute-start.10 = (bf16[704,2048]{1,0:T(8,128)(2,1)}, bf16[704,2048]{1,0:T(8,128)(2,1)}, u32[]{:S(2)}, u32[]{:S(2)}) collective-permute-start(bf16[704,2048]{1,0:T(8,128)(2,1)} %bitcast.127), channel_id=1, source_target_pairs={{0,4},{4,0},{8,12},{12,8},{16,20},{20,16},{24,28},{28,24},{1,5},{5... | collective-permute-start | bytes 8650760 | tf_op jit(solution)/shard_map/ppermute | solution.py:886
  65.6 50.3 %collective-permute-start.9 = (bf16[704,2048]{1,0:T(8,128)(2,1)}, bf16[704,2048]{1,0:T(8,128)(2,1)}, u32[]{:S(2)}, u32[]{:S(2)}) collective-permute-start(bf16[704,2048]{1,0:T(8,128)(2,1)} %bitcast.124), channel_id=1, source_target_pairs={{0,4},{4,0},{8,12},{12,8},{16,20},{20,16},{24,28},{28,24},{1,5},{5... | collective-permute-start | bytes 8650760 | tf_op jit(solution)/shard_map/ppermute | solution.py:886
  68.2 25.8 %collective-permute-start.6 = (bf16[128,2048]{1,0:T(8,128)(2,1)S(1)}, bf16[128,2048]{1,0:T(8,128)(2,1)S(1)}, u32[]{:S(2)}, u32[]{:S(2)}) collective-permute-start(bf16[128,2048]{1,0:T(8,128)(2,1)S(1)} %copy-done.4), channel_id=1, source_target_pairs={{0,1},{1,2},{2,3},{3,0},{4,5},{5,6},{6,7},{7,4},{8,9},{9,10},{10,1... | collective-permute-start | bytes 1572872 | tf_op jit(solution)/shard_map/ppermute | solution.py:133
  80.6 35.4 %collective-permute-start.7 = (bf16[128,2048]{1,0:T(8,128)(2,1)S(1)}, bf16[128,2048]{1,0:T(8,128)(2,1)S(1)}, u32[]{:S(2)}, u32[]{:S(2)}) collective-permute-start(bf16[128,2048]{1,0:T(8,128)(2,1)S(1)} %copy-done.4), channel_id=1, source_target_pairs={{0,2},{1,3},{2,0},{3,1},{4,6},{5,7},{6,4},{7,5},{8,10},{9,11},{10,... | collective-permute-start | bytes 1572872 | tf_op jit(solution)/shard_map/ppermute | solution.py:133
  81.7 34.2 %collective-permute-start.8 = (bf16[128,2048]{1,0:T(8,128)(2,1)S(1)}, bf16[128,2048]{1,0:T(8,128)(2,1)S(1)}, u32[]{:S(2)}, u32[]{:S(2)}) collective-permute-start(bf16[128,2048]{1,0:T(8,128)(2,1)S(1)} %copy-done.4), channel_id=1, source_target_pairs={{0,3},{1,0},{2,1},{3,2},{4,7},{5,4},{6,5},{7,6},{8,11},{9,8},{10,9... | collective-permute-start | bytes 1572872 | tf_op jit(solution)/shard_map/ppermute | solution.py:133
  134.1 21.9 %collective-permute-start.11 = (bf16[64,2048]{1,0:T(8,128)(2,1)}, bf16[64,2048]{1,0:T(8,128)(2,1)S(1)}, u32[]{:S(2)}, u32[]{:S(2)}) collective-permute-start(bf16[64,2048]{1,0:T(8,128)(2,1)} %get-tuple-element.231), channel_id=1, source_target_pairs={{0,1},{1,2},{2,3},{3,0},{4,5},{5,6},{6,7},{7,4},{8,9},{9,10},{10,1... | collective-permute-start | bytes 786440 | tf_op jit(solution)/shard_map/ppermute | solution.py:115
  146.9 19.3 %collective-permute-start.12 = (bf16[64,2048]{1,0:T(8,128)(2,1)S(1)}, bf16[64,2048]{1,0:T(8,128)(2,1)S(1)}, u32[]{:S(2)}, u32[]{:S(2)}) collective-permute-start(bf16[64,2048]{1,0:T(8,128)(2,1)S(1)} %get-tuple-element.233), channel_id=1, source_target_pairs={{0,2},{1,3},{2,0},{3,1},{4,6},{5,7},{6,4},{7,5},{8,10},{9,11},{10,... | collective-permute-start | bytes 786440 | tf_op jit(solution)/shard_map/ppermute | solution.py:115
  149.1 17.1 %collective-permute-start.13 = (bf16[64,2048]{1,0:T(8,128)(2,1)S(1)}, bf16[64,2048]{1,0:T(8,128)(2,1)S(1)}, u32[]{:S(2)}, u32[]{:S(2)}) collective-permute-start(bf16[64,2048]{1,0:T(8,128)(2,1)S(1)} %get-tuple-element.232), channel_id=1, source_target_pairs={{0,3},{1,0},{2,1},{3,2},{4,7},{5,4},{6,5},{7,6},{8,11},{9,8},{10,9... | collective-permute-start | bytes 786440 | tf_op jit(solution)/shard_map/ppermute | solution.py:115
  150.6 31.4 %all-to-all-start = ((bf16[3,8,88,256]{3,2,0,1:T(8,128)(2,1)}), bf16[3,8,88,256]{3,2,0,1:T(8,128)(2,1)S(1)}, u32[]{:S(2)}, u32[]{:S(2)}) async-start(bf16[3,8,88,256]{3,2,0,1:T(8,128)(2,1)} %pad_maximum_fusion.2), calls=%async_computation | async-start | bytes 2162688 | tf_op jit(solution)/shard_map/all_to_all | solution.py:971
  154.3 101.8 %all-gather.9.cloned.1.call-start = ((), (), s32[]{:S(2)}) async-start(), calls=%async_computation.7 | async-start | bytes 5242880 | tf_op jit(solution)/shard_map/all_gather | solution.py:889
  154.4 48.3 %collective-permute-start.18 = (bf16[704,2048]{1,0:T(8,128)(2,1)}, bf16[704,2048]{1,0:T(8,128)(2,1)}, u32[]{:S(2)}, u32[]{:S(2)}) collective-permute-start(bf16[704,2048]{1,0:T(8,128)(2,1)} %bitcast.130), channel_id=1, source_target_pairs={{0,4},{4,0},{8,12},{12,8},{16,20},{20,16},{24,28},{28,24},{1,5},{5... | collective-permute-start | bytes 8650760 | tf_op jit(solution)/shard_map/ppermute | solution.py:886
  167.5 297.6 %copy-start.9 = (f32[64,2048]{1,0:T(8,128)}, f32[64,2048]{1,0:T(8,128)S(1)}, u32[]{:S(2)}) copy-start(f32[64,2048]{1,0:T(8,128)S(1)} %get-tuple-element.201) | copy-start | bytes 1572868
  167.7 18.8 %collective-permute-start.14 = (bf16[64,2048]{1,0:T(8,128)(2,1)S(1)}, bf16[64,2048]{1,0:T(8,128)(2,1)}, u32[]{:S(2)}, u32[]{:S(2)}) collective-permute-start(bf16[64,2048]{1,0:T(8,128)(2,1)S(1)} %get-tuple-element.199), channel_id=1, source_target_pairs={{0,1},{1,2},{2,3},{3,0},{4,5},{5,6},{6,7},{7,4},{8,9},{9,10},{10,1... | collective-permute-start | bytes 786440 | tf_op jit(solution)/shard_map/ppermute | solution.py:102
  173.9 18.0 %collective-permute-start.15 = (bf16[64,2048]{1,0:T(8,128)(2,1)S(1)}, bf16[64,2048]{1,0:T(8,128)(2,1)S(1)}, u32[]{:S(2)}, u32[]{:S(2)}) collective-permute-start(bf16[64,2048]{1,0:T(8,128)(2,1)S(1)} %get-tuple-element.199), channel_id=1, source_target_pairs={{0,2},{1,3},{2,0},{3,1},{4,6},{5,7},{6,4},{7,5},{8,10},{9,11},{10,... | collective-permute-start | bytes 786440 | tf_op jit(solution)/shard_map/ppermute | solution.py:102
  183.1 15.3 %collective-permute-start.17 = (bf16[3,88,2048]{2,1,0:T(8,128)(2,1)}, bf16[3,88,2048]{2,1,0:T(8,128)(2,1)}, u32[]{:S(2)}, u32[]{:S(2)}) collective-permute-start(bf16[3,88,2048]{2,1,0:T(8,128)(2,1)} %bitcast.51), channel_id=1, source_target_pairs={{0,4},{4,0},{8,12},{12,8},{16,20},{20,16},{24,28},{28,24},{1,5},{5... | collective-permute-start | bytes 3244040 | tf_op jit(solution)/shard_map/ppermute | solution.py:886
  184.5 12.9 %collective-permute-start.16 = (bf16[64,2048]{1,0:T(8,128)(2,1)S(1)}, bf16[64,2048]{1,0:T(8,128)(2,1)S(1)}, u32[]{:S(2)}, u32[]{:S(2)}) collective-permute-start(bf16[64,2048]{1,0:T(8,128)(2,1)S(1)} %get-tuple-element.199), channel_id=1, source_target_pairs={{0,3},{1,0},{2,1},{3,2},{4,7},{5,4},{6,5},{7,6},{8,11},{9,8},{10,9... | collective-permute-start | bytes 786440 | tf_op jit(solution)/shard_map/ppermute | solution.py:102
  202.7 108.4 %all-gather.11.cloned.1.call-start = ((), (), s32[]{:S(2)}) async-start(), calls=%async_computation.8 | async-start | bytes 5242880 | tf_op jit(solution)/shard_map/all_gather | solution.py:889
  202.8 11.2 %collective-permute-start.19 = (bf16[64,2048]{1,0:T(8,128)(2,1)S(1)}, bf16[64,2048]{1,0:T(8,128)(2,1)S(1)}, u32[]{:S(2)}, u32[]{:S(2)}) collective-permute-start(bf16[64,2048]{1,0:T(8,128)(2,1)S(1)} %get-tuple-element.228), channel_id=1, source_target_pairs={{0,1},{1,2},{2,3},{3,0},{4,5},{5,6},{6,7},{7,4},{8,9},{9,10},{10,1... | collective-permute-start | bytes 786440 | tf_op jit(solution)/shard_map/ppermute | solution.py:115
  203.5 20.9 %collective-permute-start.20 = (bf16[64,2048]{1,0:T(8,128)(2,1)S(1)}, bf16[64,2048]{1,0:T(8,128)(2,1)S(1)}, u32[]{:S(2)}, u32[]{:S(2)}) collective-permute-start(bf16[64,2048]{1,0:T(8,128)(2,1)S(1)} %get-tuple-element.230), channel_id=1, source_target_pairs={{0,2},{1,3},{2,0},{3,1},{4,6},{5,7},{6,4},{7,5},{8,10},{9,11},{10,... | collective-permute-start | bytes 786440 | tf_op jit(solution)/shard_map/ppermute | solution.py:115
  206.4 17.9 %collective-permute-start.21 = (bf16[64,2048]{1,0:T(8,128)(2,1)S(1)}, bf16[64,2048]{1,0:T(8,128)(2,1)S(1)}, u32[]{:S(2)}, u32[]{:S(2)}) collective-permute-start(bf16[64,2048]{1,0:T(8,128)(2,1)S(1)} %get-tuple-element.229), channel_id=1, source_target_pairs={{0,3},{1,0},{2,1},{3,2},{4,7},{5,4},{6,5},{7,6},{8,11},{9,8},{10,9... | collective-permute-start | bytes 786440 | tf_op jit(solution)/shard_map/ppermute | solution.py:115
  224.7 350.3 %copy-start.10 = (f32[64,2048]{1,0:T(8,128)}, f32[64,2048]{1,0:T(8,128)S(1)}, u32[]{:S(2)}) copy-start(f32[64,2048]{1,0:T(8,128)S(1)} %get-tuple-element.197) | copy-start | bytes 1572868
  225.0 79.9 %copy-start.23 = (bf16[64,2048]{1,0:T(8,128)(2,1)}, bf16[64,2048]{1,0:T(8,128)(2,1)S(1)}, u32[]{:S(2)}) copy-start(bf16[64,2048]{1,0:T(8,128)(2,1)S(1)} %get-tuple-element.195) | copy-start | bytes 786436
  225.0 12.2 %collective-permute-start.28 = (bf16[64,2048]{1,0:T(8,128)(2,1)S(1)}, bf16[64,2048]{1,0:T(8,128)(2,1)S(1)}, u32[]{:S(2)}, u32[]{:S(2)}) collective-permute-start(bf16[64,2048]{1,0:T(8,128)(2,1)S(1)} %get-tuple-element.195), channel_id=1, source_target_pairs={{0,1},{1,2},{2,3},{3,0},{4,5},{5,6},{6,7},{7,4},{8,9},{9,10},{10,1... | collective-permute-start | bytes 786440 | tf_op jit(solution)/shard_map/ppermute | solution.py:102
  230.4 16.7 %collective-permute-start.29 = (bf16[64,2048]{1,0:T(8,128)(2,1)S(1)}, bf16[64,2048]{1,0:T(8,128)(2,1)S(1)}, u32[]{:S(2)}, u32[]{:S(2)}) collective-permute-start(bf16[64,2048]{1,0:T(8,128)(2,1)S(1)} %get-tuple-element.195), channel_id=1, source_target_pairs={{0,2},{1,3},{2,0},{3,1},{4,6},{5,7},{6,4},{7,5},{8,10},{9,11},{10,... | collective-permute-start | bytes 786440 | tf_op jit(solution)/shard_map/ppermute | solution.py:102
  230.4 16.8 %collective-permute-start.30 = (bf16[64,2048]{1,0:T(8,128)(2,1)S(1)}, bf16[64,2048]{1,0:T(8,128)(2,1)S(1)}, u32[]{:S(2)}, u32[]{:S(2)}) collective-permute-start(bf16[64,2048]{1,0:T(8,128)(2,1)S(1)} %get-tuple-element.195), channel_id=1, source_target_pairs={{0,3},{1,0},{2,1},{3,2},{4,7},{5,4},{6,5},{7,6},{8,11},{9,8},{10,9... | collective-permute-start | bytes 786440 | tf_op jit(solution)/shard_map/ppermute | solution.py:102
  256.1 278.7 %reduce-scatter.4.cloned.1.call-start = ((), (), s32[]{:S(2)}) async-start(), calls=%async_computation.9 | async-start | bytes 5570560 | tf_op jit(solution)/shard_map/reduce_scatter | solution.py:892
  359.3 283.2 %reduce-scatter.6.cloned.1.call-start = ((), (), s32[]{:S(2)}) async-start(), calls=%async_computation.10 | async-start | bytes 10485760 | tf_op jit(solution)/shard_map/reduce_scatter | solution.py:892
  363.0 50.4 %collective-permute-start.22 = (bf16[256,2176]{1,0:T(8,128)(2,1)}, bf16[256,2176]{1,0:T(8,128)(2,1)}, u32[]{:S(2)}, u32[]{:S(2)}) collective-permute-start(bf16[256,2176]{1,0:T(8,128)(2,1)} %get-tuple-element.204), channel_id=1, source_target_pairs={{0,8},{4,12},{8,0},{12,4},{16,24},{20,28},{24,16},{28,20},{1,9},{5... | collective-permute-start | bytes 3342344 | tf_op jit(solution)/shard_map/ppermute | solution.py:901
  364.4 74.1 %collective-permute-start.23 = (bf16[256,2176]{1,0:T(8,128)(2,1)}, bf16[256,2176]{1,0:T(8,128)(2,1)}, u32[]{:S(2)}, u32[]{:S(2)}) collective-permute-start(bf16[256,2176]{1,0:T(8,128)(2,1)} %get-tuple-element.206), channel_id=1, source_target_pairs={{0,16},{4,20},{8,24},{12,28},{16,0},{20,4},{24,8},{28,12},{1,17},{... | collective-permute-start | bytes 3342344 | tf_op jit(solution)/shard_map/ppermute | solution.py:901
  365.0 73.5 %collective-permute-start.24 = (bf16[256,2176]{1,0:T(8,128)(2,1)S(1)}, bf16[256,2176]{1,0:T(8,128)(2,1)}, u32[]{:S(2)}, u32[]{:S(2)}) collective-permute-start(bf16[256,2176]{1,0:T(8,128)(2,1)S(1)} %get-tuple-element.205), channel_id=1, source_target_pairs={{0,24},{4,28},{8,16},{12,20},{16,8},{20,12},{24,0},{28,4},{1,25},{... | collective-permute-start | bytes 3342344 | tf_op jit(solution)/shard_map/ppermute | solution.py:901
  441.5 11.5 %collective-permute-start.25 = (bf16[64,2176]{1,0:T(8,128)(2,1)S(1)}, bf16[64,2176]{1,0:T(8,128)(2,1)S(1)}, u32[]{:S(2)}, u32[]{:S(2)}) collective-permute-start(bf16[64,2176]{1,0:T(8,128)(2,1)S(1)} %get-tuple-element.218), channel_id=1, source_target_pairs={{0,1},{1,2},{2,3},{3,0},{4,5},{5,6},{6,7},{7,4},{8,9},{9,10},{10,1... | collective-permute-start | bytes 835592 | tf_op jit(solution)/shard_map/ppermute | solution.py:115
  443.0 19.6 %collective-permute-start.26 = (bf16[64,2176]{1,0:T(8,128)(2,1)S(1)}, bf16[64,2176]{1,0:T(8,128)(2,1)S(1)}, u32[]{:S(2)}, u32[]{:S(2)}) collective-permute-start(bf16[64,2176]{1,0:T(8,128)(2,1)S(1)} %get-tuple-element.217), channel_id=1, source_target_pairs={{0,2},{1,3},{2,0},{3,1},{4,6},{5,7},{6,4},{7,5},{8,10},{9,11},{10,... | collective-permute-start | bytes 835592 | tf_op jit(solution)/shard_map/ppermute | solution.py:115
  445.4 17.2 %collective-permute-start.27 = (bf16[64,2176]{1,0:T(8,128)(2,1)S(1)}, bf16[64,2176]{1,0:T(8,128)(2,1)S(1)}, u32[]{:S(2)}, u32[]{:S(2)}) collective-permute-start(bf16[64,2176]{1,0:T(8,128)(2,1)S(1)} %get-tuple-element.216), channel_id=1, source_target_pairs={{0,3},{1,0},{2,1},{3,2},{4,7},{5,4},{6,5},{7,6},{8,11},{9,8},{10,9... | collective-permute-start | bytes 835592 | tf_op jit(solution)/shard_map/ppermute | solution.py:115
  466.1 46.7 %copy-start.42 = (bf16[64,2048]{1,0:T(8,128)(2,1)}, bf16[64,2048]{1,0:T(8,128)(2,1)S(1)}, u32[]{:S(2)}) copy-start(bf16[64,2048]{1,0:T(8,128)(2,1)S(1)} %get-tuple-element.192.refs_3_) | copy-start | bytes 786436
  466.1 14.2 %collective-permute-start.31 = (bf16[64,2048]{1,0:T(8,128)(2,1)S(1)}, bf16[64,2048]{1,0:T(8,128)(2,1)S(1)}, u32[]{:S(2)}, u32[]{:S(2)}) collective-permute-start(bf16[64,2048]{1,0:T(8,128)(2,1)S(1)} %get-tuple-element.192.refs_3_), channel_id=1, source_target_pairs={{0,1},{1,2},{2,3},{3,0},{4,5},{5,6},{6,7},{7,4},{8,9},{9,10},{10,1... | collective-permute-start | bytes 786440 | tf_op jit(solution)/shard_map/ppermute | solution.py:102
  472.5 16.6 %collective-permute-start.32 = (bf16[64,2048]{1,0:T(8,128)(2,1)S(1)}, bf16[64,2048]{1,0:T(8,128)(2,1)S(1)}, u32[]{:S(2)}, u32[]{:S(2)}) collective-permute-start(bf16[64,2048]{1,0:T(8,128)(2,1)S(1)} %get-tuple-element.192.refs_3_), channel_id=1, source_target_pairs={{0,2},{1,3},{2,0},{3,1},{4,6},{5,7},{6,4},{7,5},{8,10},{9,11},{10,... | collective-permute-start | bytes 786440 | tf_op jit(solution)/shard_map/ppermute | solution.py:102
  474.0 15.6 %collective-permute-start.33 = (bf16[64,2048]{1,0:T(8,128)(2,1)S(1)}, bf16[64,2048]{1,0:T(8,128)(2,1)S(1)}, u32[]{:S(2)}, u32[]{:S(2)}) collective-permute-start(bf16[64,2048]{1,0:T(8,128)(2,1)S(1)} %get-tuple-element.192.refs_3_), channel_id=1, source_target_pairs={{0,3},{1,0},{2,1},{3,2},{4,7},{5,4},{6,5},{7,6},{8,11},{9,8},{10,9... | collective-permute-start | bytes 786440 | tf_op jit(solution)/shard_map/ppermute | solution.py:102
  534.8 195.2 %reduce-scatter.8.cloned.1.call-start = ((), (), s32[]{:S(2)}) async-start(), calls=%async_computation.11 | async-start | bytes 10027008 | tf_op jit(solution)/shard_map/reduce_scatter | solution.py:1150
  537.2 35.5 %copy-start.49 = (f32[64]{0:T(128)}, f32[64]{0:T(128)S(1)}, u32[]{:S(2)}) copy-start(f32[64]{0:T(128)S(1)} %get-tuple-element.254) | copy-start | bytes 772
  539.1 69.7 %collective-permute-start.40 = (bf16[704,2048]{1,0:T(8,128)(2,1)}, bf16[704,2048]{1,0:T(8,128)(2,1)S(1)}, u32[]{:S(2)}, u32[]{:S(2)}) collective-permute-start(bf16[704,2048]{1,0:T(8,128)(2,1)} %get-tuple-element.96), channel_id=1, source_target_pairs={{0,4},{4,0},{8,12},{12,8},{16,20},{20,16},{24,28},{28,24},{1,5},{5... | collective-permute-start | bytes 8650760 | tf_op jit(solution)/shard_map/ppermute | solution.py:886
  540.0 32.4 %collective-permute-start.34 = (bf16[64,2176]{1,0:T(8,128)(2,1)}, bf16[64,2176]{1,0:T(8,128)(2,1)S(1)}, u32[]{:S(2)}, u32[]{:S(2)}) collective-permute-start(bf16[64,2176]{1,0:T(8,128)(2,1)} %get-tuple-element.214), channel_id=1, source_target_pairs={{0,1},{1,2},{2,3},{3,0},{4,5},{5,6},{6,7},{7,4},{8,9},{9,10},{10,1... | collective-permute-start | bytes 835592 | tf_op jit(solution)/shard_map/ppermute | solution.py:115
  545.9 26.5 %collective-permute-start.35 = (bf16[64,2176]{1,0:T(8,128)(2,1)}, bf16[64,2176]{1,0:T(8,128)(2,1)S(1)}, u32[]{:S(2)}, u32[]{:S(2)}) collective-permute-start(bf16[64,2176]{1,0:T(8,128)(2,1)} %get-tuple-element.213), channel_id=1, source_target_pairs={{0,2},{1,3},{2,0},{3,1},{4,6},{5,7},{6,4},{7,5},{8,10},{9,11},{10,... | collective-permute-start | bytes 835592 | tf_op jit(solution)/shard_map/ppermute | solution.py:115
  549.3 23.1 %collective-permute-start.36 = (bf16[64,2176]{1,0:T(8,128)(2,1)S(1)}, bf16[64,2176]{1,0:T(8,128)(2,1)S(1)}, u32[]{:S(2)}, u32[]{:S(2)}) collective-permute-start(bf16[64,2176]{1,0:T(8,128)(2,1)S(1)} %get-tuple-element.212), channel_id=1, source_target_pairs={{0,3},{1,0},{2,1},{3,2},{4,7},{5,4},{6,5},{7,6},{8,11},{9,8},{10,9... | collective-permute-start | bytes 835592 | tf_op jit(solution)/shard_map/ppermute | solution.py:115
  572.4 36.5 %collective-permute-start.41 = (bf16[704,2048]{1,0:T(8,128)(2,1)}, bf16[704,2048]{1,0:T(8,128)(2,1)}, u32[]{:S(2)}, u32[]{:S(2)}) collective-permute-start(bf16[704,2048]{1,0:T(8,128)(2,1)} %get-tuple-element.97), channel_id=1, source_target_pairs={{0,4},{4,0},{8,12},{12,8},{16,20},{20,16},{24,28},{28,24},{1,5},{5... | collective-permute-start | bytes 8650760 | tf_op jit(solution)/shard_map/ppermute | solution.py:886
  576.0 30.2 %collective-permute-start.37 = (bf16[64,2048]{1,0:T(8,128)(2,1)S(1)}, bf16[64,2048]{1,0:T(8,128)(2,1)}, u32[]{:S(2)}, u32[]{:S(2)}) collective-permute-start(bf16[64,2048]{1,0:T(8,128)(2,1)S(1)} %get-tuple-element.189.refs_2_), channel_id=1, source_target_pairs={{0,1},{1,2},{2,3},{3,0},{4,5},{5,6},{6,7},{7,4},{8,9},{9,10},{10,1... | collective-permute-start | bytes 786440 | tf_op jit(solution)/shard_map/ppermute | solution.py:102
  578.3 29.0 %collective-permute-start.38 = (bf16[64,2048]{1,0:T(8,128)(2,1)S(1)}, bf16[64,2048]{1,0:T(8,128)(2,1)S(1)}, u32[]{:S(2)}, u32[]{:S(2)}) collective-permute-start(bf16[64,2048]{1,0:T(8,128)(2,1)S(1)} %get-tuple-element.189.refs_2_), channel_id=1, source_target_pairs={{0,2},{1,3},{2,0},{3,1},{4,6},{5,7},{6,4},{7,5},{8,10},{9,11},{10,... | collective-permute-start | bytes 786440 | tf_op jit(solution)/shard_map/ppermute | solution.py:102
  578.3 29.0 %collective-permute-start.39 = (bf16[64,2048]{1,0:T(8,128)(2,1)S(1)}, bf16[64,2048]{1,0:T(8,128)(2,1)S(1)}, u32[]{:S(2)}, u32[]{:S(2)}) collective-permute-start(bf16[64,2048]{1,0:T(8,128)(2,1)S(1)} %get-tuple-element.189.refs_2_), channel_id=1, source_target_pairs={{0,3},{1,0},{2,1},{3,2},{4,7},{5,4},{6,5},{7,6},{8,11},{9,8},{10,9... | collective-permute-start | bytes 786440 | tf_op jit(solution)/shard_map/ppermute | solution.py:102
  647.7 26.5 %collective-permute-start.42 = (bf16[128,4096]{1,0:T(8,128)(2,1)S(1)}, bf16[128,4096]{1,0:T(8,128)(2,1)S(1)}, u32[]{:S(2)}, u32[]{:S(2)}) collective-permute-start(bf16[128,4096]{1,0:T(8,128)(2,1)S(1)} %get-tuple-element.209), channel_id=1, source_target_pairs={{0,1},{1,2},{2,3},{3,0},{4,5},{5,6},{6,7},{7,4},{8,9},{9,10},{10,1... | collective-permute-start | bytes 3145736 | tf_op jit(solution)/shard_map/ppermute | solution.py:115
  647.7 48.6 %collective-permute-start.45 = (bf16[704,2048]{1,0:T(8,128)(2,1)}, bf16[704,2048]{1,0:T(8,128)(2,1)}, u32[]{:S(2)}, u32[]{:S(2)}) collective-permute-start(bf16[704,2048]{1,0:T(8,128)(2,1)} %get-tuple-element.102), channel_id=1, source_target_pairs={{0,4},{4,0},{8,12},{12,8},{16,20},{20,16},{24,28},{28,24},{1,5},{5... | collective-permute-start | bytes 8650760 | tf_op jit(solution)/shard_map/ppermute | solution.py:886
  674.2 2.7 collective-permute-start.49
  674.2 47.2 %collective-permute-start.43 = (bf16[128,4096]{1,0:T(8,128)(2,1)}, bf16[128,4096]{1,0:T(8,128)(2,1)S(1)}, u32[]{:S(2)}, u32[]{:S(2)}) collective-permute-start(bf16[128,4096]{1,0:T(8,128)(2,1)} %get-tuple-element.208), channel_id=1, source_target_pairs={{0,2},{1,3},{2,0},{3,1},{4,6},{5,7},{6,4},{7,5},{8,10},{9,11},{10,... | collective-permute-start | bytes 3145736 | tf_op jit(solution)/shard_map/ppermute | solution.py:115
  674.2 48.6 %collective-permute-start.44 = (bf16[128,4096]{1,0:T(8,128)(2,1)}, bf16[128,4096]{1,0:T(8,128)(2,1)}, u32[]{:S(2)}, u32[]{:S(2)}) collective-permute-start(bf16[128,4096]{1,0:T(8,128)(2,1)} %get-tuple-element.207), channel_id=1, source_target_pairs={{0,3},{1,0},{2,1},{3,2},{4,7},{5,4},{6,5},{7,6},{8,11},{9,8},{10,9... | collective-permute-start | bytes 3145736 | tf_op jit(solution)/shard_map/ppermute | solution.py:115
  678.3 48.0 %all-to-all-start.1 = ((bf16[3,8,88,256]{3,2,0,1:T(8,128)(2,1)}), bf16[3,8,88,256]{3,2,0,1:T(8,128)(2,1)}, u32[]{:S(2)}, u32[]{:S(2)}) async-start(bf16[3,8,88,256]{3,2,0,1:T(8,128)(2,1)} %bitcast.93), calls=%async_computation.4 | async-start | bytes 2162688 | tf_op jit(solution)/shard_map/all_to_all | solution.py:1136
  732.1 26.2 %collective-permute-start.46 = (bf16[64,640]{1,0:T(8,128)(2,1)S(1)}, bf16[64,640]{1,0:T(8,128)(2,1)S(1)}, u32[]{:S(2)}, u32[]{:S(2)}) collective-permute-start(bf16[64,640]{1,0:T(8,128)(2,1)S(1)} %get-tuple-element.234), channel_id=1, source_target_pairs={{0,1},{1,2},{2,3},{3,0},{4,5},{5,6},{6,7},{7,4},{8,9},{9,10},{10,1... | collective-permute-start | bytes 245768 | tf_op jit(solution)/shard_map/ppermute | solution.py:115
  752.6 7.3 collective-permute-start.47
  754.4 5.9 collective-permute-start.48
  (49 other events, 586.3 us)
Sparse Core Ops, SparseCore 0:
  22.6 57.5 all-gather.4
  82.7 105.9 all-gather.6
  202.8 53.2 all-gather.8
  258.4 52.6 all-gather.10
  359.4 101.2 reduce-scatter.3
  535.0 91.7 reduce-scatter.5
  642.6 87.3 reduce-scatter.7
